TPU v7x, 32 devices: a whole 2x2x4 slice. The times are simulated.
32 devices in a mesh: dp: 8 (over y, x, core), tensor: 4 (over z).
Axes of the slice: x: 2, y: 2, z: 4, core: 2. Of those that a mesh axis runs over, the one named last changes fastest.
Arguments:
- tokens: bfloat16 [8192, 2048], P('dp'), may hold values from -6 to 6
- cotangent: bfloat16 [8192, 2048], P('dp'), may hold values from -6 to 6
- attention_norm_gain: bfloat16 [2048], replicated, may hold values from 0.099609375 to 1.8984375
- query_key_value_weight: bfloat16 [2048, 3, 2048], P('dp', None, 'tensor'), may hold values from -0.125 to 0.125
- query_key_value_bias: bfloat16 [3, 2048], P(None, 'tensor'), may hold values from -0.59765625 to 0.59765625
- output_projection_weight: bfloat16 [2048, 2048], P('dp', 'tensor'), may hold values from -2 to 2
- feedforward_norm_gain: bfloat16 [2048], replicated, may hold values from 0.099609375 to 1.8984375
- router_matrix: bfloat16 [2048, 16], P('dp'), may hold values from -0.0625 to 0.0625
- shared_expert_gate_weight: bfloat16 [2048], P('dp'), may hold values from -0.125 to 0.125
- routed_gate_up_weight: bfloat16 [2048, 16, 2, 1408], P('dp', None, None, 'tensor'), may hold values from -0.125 to 0.125
- routed_down_weight: bfloat16 [2048, 16, 1408], P('dp', None, 'tensor'), may hold values from -4 to 4
- shared_expert_gate_up_weight: bfloat16 [2048, 2, 5632], P('dp', None, 'tensor'), may hold values from -0.125 to 0.125
- shared_expert_down_weight: bfloat16 [2048, 5632], P('dp', 'tensor'), may hold values from -0.25 to 0.25
- routes: int32 [8192, 4], P('dp'), may hold values from 0 to 15, all different within a row; in each aligned block of 1024 rows (0 to 1023, 1024 to 2047, ...) at most 384 rows name the same one
- sequence_adapter_index: int32 [8], P('dp'), may hold values from 0 to 7
- picture_piece_starts: int32 [8, 2], P('dp'), may hold values from 0 to 768, as said below
- adapter_query_key_value_lower: bfloat16 [8, 2048, 16], replicated, may hold values from -0.125 to 0.125
- adapter_query_key_value_upper: bfloat16 [8, 16, 3, 2048], P(None, None, None, 'tensor'), may hold values from -0.375 to 0.375
- adapter_output_lower: bfloat16 [8, 2048, 16], P(None, 'tensor'), may hold values from -2 to 2
- adapter_output_upper: bfloat16 [8, 16, 2048], replicated, may hold values from -0.375 to 0.375
- adapter_shared_up_lower: bfloat16 [8, 2048, 16], replicated, may hold values from -0.125 to 0.125
- adapter_shared_up_upper: bfloat16 [8, 16, 2, 5632], P(None, None, None, 'tensor'), may hold values from -0.375 to 0.375
- adapter_shared_down_lower: bfloat16 [8, 5632, 16], P(None, 'tensor'), may hold values from -0.078125 to 0.078125
- adapter_shared_down_upper: bfloat16 [8, 16, 2048], replicated, may hold values from -0.75 to 0.75
Outputs:
- output: bfloat16 [8192, 2048], P('dp')
- grad_tokens: bfloat16 [8192, 2048], P('dp')
- grad_qkv_a: float32 [8, 2048, 16], replicated
- grad_qkv_b: float32 [8, 16, 3, 2048], P(None, None, None, 'tensor')
- grad_out_a: float32 [8, 2048, 16], P(None, 'tensor')
- grad_out_b: float32 [8, 16, 2048], replicated
- grad_up_a: float32 [8, 2048, 16], replicated
- grad_up_b: float32 [8, 16, 2, 5632], P(None, None, None, 'tensor')
- grad_down_a: float32 [8, 5632, 16], P(None, 'tensor')
- grad_down_b: float32 [8, 16, 2048], replicated
Inputs may be any that keep to these rules, and one draw needn't show every extreme that they name: `routes`: in each sequence no expert is named by more than 384 of the sequence's pairs. `picture_piece_starts`: in each sequence the pieces are in rising order, do not intersect, and each of their 256 tokens lies inside the sequence.
All inputs are finite; a program needn't handle non-finite values.
Results may differ from a plain program's by a relative error of at most 0.02.
Values may be sent and summed in bfloat16 or wider, within the bound.
A program may use at most 512 MiB of HBM per device.

v0:
```python
import jax
import jax.numpy as jnp
from jax import lax
from jax.sharding import PartitionSpec as P

HEAD_SIZE = 128
TOP = 4
EXPERTS = 16
ADAPTER_SETS = 8
PIECE = 256
CAP = 384


EPSILON = 1e-06
THETA = 1000000.0
ADAPTER_SCALE = 2.0
MASKED = -1e30


def matmul(left_side, right_side):
    return jnp.dot(left_side, right_side, preferred_element_type=jnp.float32)


def contract_last(left_side, right_side):
    return lax.dot_general(
        left_side, right_side, (((1,), (1,)), ((), ())), preferred_element_type=jnp.float32
    )


def contract_first(left_side, right_side):
    return lax.dot_general(
        left_side, right_side, (((0,), (0,)), ((), ())), preferred_element_type=jnp.float32
    )


def to_low(values):
    return values.astype(jnp.bfloat16)


def rms_scale(values, gain_values):
    return (
        values * lax.rsqrt(jnp.mean(values * values, axis=1, keepdims=True) + EPSILON) * gain_values
    )


def rope_tables(length):
    half_size = HEAD_SIZE // 2
    frequency = THETA ** (-jnp.arange(half_size, dtype=jnp.float32) * 2.0 / HEAD_SIZE)
    angles = jnp.arange(length, dtype=jnp.float32)[:, None] * frequency[None, :]
    return (
        jnp.concatenate([jnp.cos(angles)] * 2, axis=1),
        jnp.concatenate([jnp.sin(angles)] * 2, axis=1),
    )


def rotate(values, cosine, sine_table):
    half_size = values.shape[-1] // 2
    turned = jnp.concatenate([-values[..., half_size:], values[..., :half_size]], axis=-1)
    return values * cosine[:, None, :] + turned * sine_table[:, None, :]


def piece_index(positions, starts):
    inside = (positions[:, None] >= starts[None, :]) & (
        positions[:, None] < starts[None, :] + PIECE
    )
    labels = jnp.arange(starts.shape[0], dtype=jnp.int32)[None, :] + 1
    return jnp.sum(jnp.where(inside, labels, 0), axis=1) - 1


def visible(row_positions, col_positions, starts):
    row_piece = piece_index(row_positions, starts)
    col_piece = piece_index(col_positions, starts)
    causal = col_positions[None, :] <= row_positions[:, None]
    together = (row_piece[:, None] == col_piece[None, :]) & (row_piece[:, None] >= 0)
    return causal | together


def slot_table(routes, length):
    flat_routes = routes.reshape(-1)
    hit_table = (flat_routes[:, None] == jnp.arange(EXPERTS, dtype=jnp.int32)[None, :]).astype(
        jnp.int32
    )
    earlier = jnp.cumsum(hit_table, axis=0) - hit_table
    slot_index = flat_routes * CAP + jnp.sum(earlier * hit_table, axis=1)
    pair_tokens = jnp.arange(length * TOP, dtype=jnp.int32) // TOP
    slot_owner = jnp.full((EXPERTS * CAP,), length, jnp.int32).at[slot_index].set(pair_tokens)
    return (slot_index, slot_owner)


def swiglu(paired):
    return jax.nn.silu(paired[..., 0, :]) * paired[..., 1, :]


def tensor_total(wide_part, narrow_part):
    return lax.psum((wide_part, narrow_part), "tensor")


def body(
    tokens,
    cotangent,
    attention_norm_gain,
    query_key_value_weight,
    query_key_value_bias,
    output_projection_weight,
    feedforward_norm_gain,
    router_matrix,
    shared_expert_gate_weight,
    routed_gate_up_weight,
    routed_down_weight,
    shared_expert_gate_up_weight,
    shared_expert_down_weight,
    routes,
    sequence_adapter_index,
    picture_piece_starts,
    adapter_query_key_value_lower,
    adapter_query_key_value_upper,
    adapter_output_lower,
    adapter_output_upper,
    adapter_shared_up_lower,
    adapter_shared_up_upper,
    adapter_shared_down_lower,
    adapter_shared_down_upper,
):
    length, width = tokens.shape
    heads_here = query_key_value_weight.shape[2] // HEAD_SIZE
    set_id = sequence_adapter_index[0]
    starts = picture_piece_starts[0]

    def selected_experts(adapter_entry):
        return lax.dynamic_index_in_dim(adapter_entry, set_id, 0, keepdims=False)

    qkv_a, qkv_b, out_a, out_b = (
        selected_experts(adapter_query_key_value_lower),
        selected_experts(adapter_query_key_value_upper),
        selected_experts(adapter_output_lower),
        selected_experts(adapter_output_upper),
    )
    up_a, up_b, down_a, down_b = (
        selected_experts(adapter_shared_up_lower),
        selected_experts(adapter_shared_up_upper),
        selected_experts(adapter_shared_down_lower),
        selected_experts(adapter_shared_down_upper),
    )
    gain_attn_f = attention_norm_gain.astype(jnp.float32)
    gain_ffn_f = feedforward_norm_gain.astype(jnp.float32)
    tokens_f = tokens.astype(jnp.float32)
    normed = to_low(rms_scale(tokens_f, gain_attn_f))
    mid_qkv = to_low(matmul(normed, qkv_a))
    columns = normed
    qkv_sum = jnp.einsum(
        "tr,rsf->tsf",
        columns,
        lax.all_gather(query_key_value_weight, "dp", axis=0, tiled=True),
        preferred_element_type=jnp.float32,
    )
    qkv_sum = qkv_sum + query_key_value_bias.astype(jnp.float32)
    qkv_sum = qkv_sum + ADAPTER_SCALE * jnp.einsum(
        "tr,rsf->tsf", mid_qkv, qkv_b, preferred_element_type=jnp.float32
    )
    cosine, sine_table = rope_tables(length)

    def position(raw_values):
        query_part = rotate(
            raw_values[:, 0].reshape(length, heads_here, HEAD_SIZE), cosine, sine_table
        )
        keys_part = rotate(
            raw_values[:, 1].reshape(length, heads_here, HEAD_SIZE), cosine, sine_table
        )
        return (query_part, keys_part)

    (query_f, keys_f), rope_pull = jax.vjp(position, qkv_sum)
    query = to_low(query_f)
    keys = to_low(keys_f)
    values = to_low(qkv_sum[:, 2].reshape(length, heads_here, HEAD_SIZE))
    block_rows = min(length, 512)
    score_scale = HEAD_SIZE ** (-0.5)
    positions = jnp.arange(length, dtype=jnp.int32)
    attended_parts = []
    logsum_parts = []
    for offset in range(0, length, block_rows):
        allowed = visible(positions[offset : offset + block_rows], positions, starts)
        scores = (
            jnp.einsum(
                "qhd,khd->hqk",
                query[offset : offset + block_rows],
                keys,
                preferred_element_type=jnp.float32,
            )
            * score_scale
        )
        scores = jnp.where(allowed[None], scores, MASKED)
        highest = jnp.max(scores, axis=-1, keepdims=True)
        weights_exp = jnp.exp(scores - highest)
        row_totals = jnp.sum(weights_exp, axis=-1, keepdims=True)
        attended_parts.append(
            jnp.einsum(
                "hqk,khd->qhd",
                to_low(weights_exp / row_totals),
                values,
                preferred_element_type=jnp.float32,
            )
        )
        logsum_parts.append(highest + jnp.log(row_totals))
    attended = to_low(jnp.concatenate(attended_parts, axis=0).reshape(length, -1))
    branch_part = contract_last(
        attended, lax.all_gather(output_projection_weight, "dp", axis=0, tiled=True)
    )
    branch_here, mid_out_here_f = tensor_total(branch_part, matmul(attended, out_a))
    mid_out_here = to_low(mid_out_here_f)
    hidden_here = tokens_f + branch_here + ADAPTER_SCALE * matmul(mid_out_here, out_b)
    normed_two_here_f, norm_ffn_pull = jax.vjp(
        lambda rows: rms_scale(rows, gain_ffn_f), hidden_here
    )
    normed_two_here = to_low(normed_two_here_f)
    normed_two, mid_out = (normed_two_here, mid_out_here)
    slot_index, slot_owner = slot_table(routes, length)
    dispatched = jnp.concatenate([normed_two, jnp.zeros((1, width), jnp.bfloat16)], axis=0)[
        slot_owner
    ]
    dispatched = dispatched.reshape(EXPERTS, CAP, width)
    up_rows = lax.all_gather(routed_gate_up_weight, "dp", axis=0, tiled=True)
    shared_rows = lax.all_gather(shared_expert_gate_up_weight, "dp", axis=0, tiled=True)
    router_rows = lax.all_gather(router_matrix, "dp", axis=0, tiled=True)
    gate_rows = lax.all_gather(shared_expert_gate_weight, "dp", axis=0, tiled=True)
    first_totals = (
        jnp.einsum("ecr,rexf->ecxf", dispatched, up_rows, preferred_element_type=jnp.float32),
        jnp.einsum("tr,rxf->txf", normed_two, shared_rows, preferred_element_type=jnp.float32),
        matmul(normed_two, router_rows),
        matmul(normed_two, gate_rows),
        router_rows,
        gate_rows,
    )
    gate_up, shared_sum, logits, gate_logit, router_full, gate_full = first_totals
    router_probs = jax.nn.softmax(logits, axis=-1)
    gates = jnp.take_along_axis(router_probs, routes, axis=1)
    gate_slot = jnp.zeros((EXPERTS * CAP,), jnp.float32).at[slot_index].set(gates.reshape(-1))
    gate_slot = gate_slot.reshape(EXPERTS, CAP)
    shared_gate = jax.nn.sigmoid(gate_logit)
    act_f, act_pull = jax.vjp(swiglu, gate_up)
    act = to_low(act_f)
    mid_up = to_low(matmul(normed_two, up_a))
    shared_gu = shared_sum + ADAPTER_SCALE * jnp.einsum(
        "tr,rxf->txf", mid_up, up_b, preferred_element_type=jnp.float32
    )
    shared_act_f, shared_pull = jax.vjp(swiglu, shared_gu)
    shared_act = to_low(shared_act_f)
    cot_f = cotangent.astype(jnp.float32)
    cot_slots = jnp.concatenate([cotangent, jnp.zeros((1, width), jnp.bfloat16)], axis=0)[
        slot_owner
    ]
    cot_slots = cot_slots.reshape(EXPERTS, CAP, width)
    down_rows = lax.all_gather(routed_down_weight, "dp", axis=0, tiled=True)
    sdown_rows = lax.all_gather(shared_expert_down_weight, "dp", axis=0, tiled=True)
    expert_cols = jnp.einsum("ecf,ref->ecr", act, down_rows, preferred_element_type=jnp.float32)
    picked = expert_cols.reshape(EXPERTS * CAP, -1)[slot_index].reshape(length, TOP, -1)
    shared_cols = contract_last(shared_act, sdown_rows)
    routed = jnp.sum(gates[:, :, None] * picked, axis=1)
    down_totals = (
        routed + shared_gate[:, None] * shared_cols,
        jnp.sum(cot_f[:, None, :] * picked, axis=2),
        jnp.sum(cot_f * shared_cols, axis=1),
    )
    combined_part, gate_pair_part, shared_gate_part = down_totals
    combined_here, mid_down_here_f = tensor_total(combined_part, matmul(shared_act, down_a))
    mid_down_here = to_low(mid_down_here_f)
    extra_here = ADAPTER_SCALE * matmul(mid_down_here, down_b)
    output_here = to_low(hidden_here + combined_here + shared_gate[:, None] * extra_here)
    output, mid_down = (output_here, mid_down_here)
    grad_shared = to_low(shared_gate[:, None] * cot_f)
    down_rows = lax.all_gather(routed_down_weight, "dp", axis=0, tiled=True)
    sdown_rows = lax.all_gather(shared_expert_down_weight, "dp", axis=0, tiled=True)
    cot_cols = cot_slots.astype(jnp.float32)
    grad_cols = to_low(gate_slot[:, :, None] * cot_cols)
    shared_cols = grad_shared
    back_totals = (
        jnp.einsum("ecr,ref->ecf", grad_cols, down_rows, preferred_element_type=jnp.float32),
        matmul(shared_cols, sdown_rows),
    )
    grad_act, grad_shared_act = back_totals
    grad_mid_down = to_low(ADAPTER_SCALE * contract_last(grad_shared, down_b))
    grad_shared_act = grad_shared_act + contract_last(grad_mid_down, down_a)
    grad_down_a_local = contract_first(shared_act, grad_mid_down)
    grad_down_b_local = ADAPTER_SCALE * contract_first(mid_down, grad_shared)
    grad_gate_up = to_low(act_pull(grad_act)[0])
    grad_shared_gu = to_low(shared_pull(grad_shared_act)[0])
    grad_mid_up_part = ADAPTER_SCALE * jnp.einsum(
        "txf,rxf->tr", grad_shared_gu, up_b, preferred_element_type=jnp.float32
    )
    grad_up_b_local = ADAPTER_SCALE * jnp.einsum(
        "tr,txf->rxf", mid_up, grad_shared_gu, preferred_element_type=jnp.float32
    )
    up_rows, shared_rows = lax.all_gather(
        (routed_gate_up_weight, shared_expert_gate_up_weight), "dp", axis=0, tiled=True
    )
    expert_cols = jnp.einsum(
        "ecxf,rexf->ecr", grad_gate_up, up_rows, preferred_element_type=jnp.float32
    )
    routed = jnp.sum(
        expert_cols.reshape(EXPERTS * CAP, -1)[slot_index].reshape(length, TOP, -1), axis=1
    )
    normed_two_part = routed + jnp.einsum(
        "txf,rxf->tr", grad_shared_gu, shared_rows, preferred_element_type=jnp.float32
    )
    narrow_part = jnp.concatenate(
        [gate_pair_part, shared_gate_part[:, None], grad_mid_up_part], axis=1
    )
    grad_normed_two, narrow_sum = tensor_total(normed_two_part, narrow_part)
    top_count = routes.shape[1]
    grad_gates = narrow_sum[:, :top_count]
    expert_ids = jnp.arange(EXPERTS, dtype=jnp.int32)
    grad_probs = jnp.sum(
        grad_gates[:, :, None]
        * (routes[:, :, None] == expert_ids[None, None, :]).astype(jnp.float32),
        axis=1,
    )
    grad_logits = to_low(
        router_probs * (grad_probs - jnp.sum(router_probs * grad_probs, axis=1, keepdims=True))
    )
    shared_gate_grad = narrow_sum[:, top_count] + jnp.sum(cot_f * extra_here, axis=1)
    grad_gate_logit = to_low(shared_gate_grad * shared_gate * (1.0 - shared_gate))
    grad_mid_up_here = to_low(narrow_sum[:, top_count + 1 :])
    grad_normed_two = grad_normed_two + contract_last(grad_logits, router_full)
    grad_normed_two = (
        grad_normed_two
        + grad_gate_logit.astype(jnp.float32)[:, None] * gate_full.astype(jnp.float32)[None, :]
    )
    grad_normed_two = grad_normed_two + contract_last(grad_mid_up_here, up_a)
    grad_hidden = cot_f + norm_ffn_pull(grad_normed_two)[0]
    grad_branch_here = to_low(grad_hidden)
    grad_branch, grad_mid_up = (grad_branch_here, grad_mid_up_here)
    grad_up_a_local = contract_first(normed_two, grad_mid_up)
    grad_mid_out = to_low(ADAPTER_SCALE * contract_last(grad_branch, out_b))
    grad_out_b_local = ADAPTER_SCALE * contract_first(mid_out, grad_branch)
    columns = grad_branch
    grad_att_sum = matmul(
        columns, lax.all_gather(output_projection_weight, "dp", axis=0, tiled=True)
    )
    grad_attended = to_low(grad_att_sum + contract_last(grad_mid_out, out_a)).reshape(
        length, heads_here, HEAD_SIZE
    )
    grad_out_a_local = contract_first(attended, grad_mid_out)
    grad_keys = jnp.zeros((length, heads_here, HEAD_SIZE), jnp.float32)
    grad_values = jnp.zeros((length, heads_here, HEAD_SIZE), jnp.float32)
    grad_query_parts = []
    for block_number, offset in enumerate(range(0, length, block_rows)):
        query_rows = query[offset : offset + block_rows]
        allowed = visible(positions[offset : offset + block_rows], positions, starts)
        scores = (
            jnp.einsum("qhd,khd->hqk", query_rows, keys, preferred_element_type=jnp.float32)
            * score_scale
        )
        scores = jnp.where(allowed[None], scores, MASKED)
        probs_f = jnp.exp(scores - logsum_parts[block_number])
        grad_rows = grad_attended[offset : offset + block_rows]
        grad_values = grad_values + jnp.einsum(
            "hqk,qhd->khd", to_low(probs_f), grad_rows, preferred_element_type=jnp.float32
        )
        grad_probs_att = jnp.einsum(
            "qhd,khd->hqk", grad_rows, values, preferred_element_type=jnp.float32
        )
        grad_scores = to_low(
            probs_f * (grad_probs_att - jnp.sum(probs_f * grad_probs_att, axis=-1, keepdims=True))
        )
        grad_query_parts.append(
            jnp.einsum("hqk,khd->qhd", grad_scores, keys, preferred_element_type=jnp.float32)
            * score_scale
        )
        grad_keys = (
            grad_keys
            + jnp.einsum(
                "hqk,qhd->khd", grad_scores, query_rows, preferred_element_type=jnp.float32
            )
            * score_scale
        )
    grad_query = jnp.concatenate(grad_query_parts, axis=0)
    grad_raw = rope_pull((grad_query, grad_keys))[0]
    grad_raw = grad_raw.at[:, 2].set(grad_values.reshape(length, -1))
    grad_qkv = to_low(grad_raw)
    grad_mid_qkv_part = ADAPTER_SCALE * jnp.einsum(
        "tsf,rsf->tr", grad_qkv, qkv_b, preferred_element_type=jnp.float32
    )
    grad_qkv_b_local = ADAPTER_SCALE * jnp.einsum(
        "tr,tsf->rsf", mid_qkv, grad_qkv, preferred_element_type=jnp.float32
    )
    normed_part = jnp.einsum(
        "tsf,rsf->tr",
        grad_qkv,
        lax.all_gather(query_key_value_weight, "dp", axis=0, tiled=True),
        preferred_element_type=jnp.float32,
    )
    grad_normed, grad_mid_qkv_f = tensor_total(normed_part, grad_mid_qkv_part)
    grad_mid_qkv_here = to_low(grad_mid_qkv_f)
    grad_normed = grad_normed + contract_last(grad_mid_qkv_here, qkv_a)
    norm_attn_pull = jax.vjp(lambda rows: rms_scale(rows, gain_attn_f), tokens_f)[1]
    grad_tokens_here = to_low(grad_hidden + norm_attn_pull(grad_normed)[0])
    grad_tokens, grad_mid_qkv = (grad_tokens_here, grad_mid_qkv_here)
    grad_qkv_a_local = contract_first(normed, grad_mid_qkv)
    marker = (jnp.arange(ADAPTER_SETS, dtype=jnp.int32) == set_id).astype(jnp.float32)

    def spread(local_grad):
        return marker.reshape((ADAPTER_SETS,) + (1,) * local_grad.ndim) * local_grad[None]

    adapter_totals = (
        lax.psum(spread(grad_qkv_a_local).astype(jnp.bfloat16), "dp").astype(jnp.float32),
        lax.psum(spread(grad_qkv_b_local).astype(jnp.bfloat16), "dp").astype(jnp.float32),
        lax.psum(spread(grad_out_a_local).astype(jnp.bfloat16), "dp").astype(jnp.float32),
        lax.psum(spread(grad_out_b_local).astype(jnp.bfloat16), "dp").astype(jnp.float32),
        lax.psum(spread(grad_up_a_local).astype(jnp.bfloat16), "dp").astype(jnp.float32),
        lax.psum(spread(grad_up_b_local).astype(jnp.bfloat16), "dp").astype(jnp.float32),
        lax.psum(spread(grad_down_a_local).astype(jnp.bfloat16), "dp").astype(jnp.float32),
        lax.psum(spread(grad_down_b_local).astype(jnp.bfloat16), "dp").astype(jnp.float32),
    )
    return (
        output,
        grad_tokens,
        adapter_totals[0],
        adapter_totals[1],
        adapter_totals[2],
        adapter_totals[3],
        adapter_totals[4],
        adapter_totals[5],
        adapter_totals[6],
        adapter_totals[7],
    )


def solution(mesh):
    return jax.shard_map(
        body,
        mesh=mesh,
        in_specs=(
            P("dp", None),
            P("dp", None),
            P(),
            P("dp", None, "tensor"),
            P(None, "tensor"),
            P("dp", "tensor"),
            P(),
            P("dp", None),
            P("dp"),
            P("dp", None, None, "tensor"),
            P("dp", None, "tensor"),
            P("dp", None, "tensor"),
            P("dp", "tensor"),
            P("dp", None),
            P("dp"),
            P("dp", None),
            P(),
            P(None, None, None, "tensor"),
            P(None, "tensor", None),
            P(),
            P(),
            P(None, None, None, "tensor"),
            P(None, "tensor", None),
            P(),
        ),
        out_specs=(
            P("dp", None),
            P("dp", None),
            P(),
            P(None, None, None, "tensor"),
            P(None, "tensor", None),
            P(),
            P(),
            P(None, None, None, "tensor"),
            P(None, "tensor", None),
            P(),
        ),
        check_vma=False,
    )
```

profile of v0, /device:TPU:0, one launch (start us, length us, event | category | flops | bytes accessed | tf_op | source)
XLA Modules:
  0.0 2302.9 jit_solution(10562421458837231954)
XLA Ops:
  13.3 3.1 fusion.13
  20.1 3.9 fusion.64
  26.3 33.6 %all-gather.8.cloned.1.call-done = bf16[2048,3,512]{0,2,1:T(8,128)(2,1)} async-done(((bf16[256,3,512]{0,2,1:T(8,128)(2,1)}), bf16[2048,3,512]{0,2,1:T(8,128)(2,1)}) %all-gather.8.cloned.1.call-update) | async-done | bytes 6291472 | tf_op jit(solution)/shard_map/all_gather | solution.py:153
  59.9 10.2 fusion.36
  78.2 2.9 copy.187
  81.1 3.8 slice_negate_fusion.2
  102.4 7.6 fusion.181
  115.4 4.6 reduce-window.6
  121.3 6.7 convert_element_type.223
  130.7 15.7 scatter_custom_fusion
  146.4 49.2 %gather_fusion.2 = bf16[6144,2048]{1,0:T(8,128)(2,1)} fusion(bf16[1025,2048]{1,0:T(8,128)(2,1)} %concatenate.47, s32[6144]{0:T(1024)S(1)} %fusion.115), kind=kCustom, calls=%fused_computation.2 | custom fusion | bytes 50356224 | tf_op jit(solution)/shard_map/gather | solution.py:248
  195.6 9.7 all-gather
  205.4 8.3 all_gather.32
  215.9 22.5 psum.113
  238.4 164.8 %all-reduce.20.cloned.1.call-done = f32[1024,2048]{1,0:T(8,128)} async-done(((f32[1024,2048]{1,0:T(8,128)}), f32[1024,2048]{1,0:T(8,128)}) %all-reduce.20.cloned.1.call-update) | async-done | bytes 8388624 | tf_op jit(solution)/shard_map/psum | solution.py:95
  403.2 5.7 multiply_reduce_fusion.7
  409.8 2.6 copy-done.6
  412.4 2.6 concatenate.46
  417.5 33.0 %gather_fusion.4 = f32[4096]{0:T(1024)S(1)} fusion(f32[1024,16]{0,1:T(8,128)S(1)} %fusion.95, s32[4096]{0:T(1024)S(1)} %reshape.446), kind=kCustom, calls=%fused_computation.4 | custom fusion | bytes 65536 | tf_op jit(solution)/shard_map/jit(take_along_axis)/gather | solution.py:235
  451.5 49.3 %gather_fusion = bf16[6144,2048]{1,0:T(8,128)(2,1)} fusion(bf16[1025,2048]{1,0:T(8,128)(2,1)} %concatenate.46, s32[6144]{0:T(1024)S(1)} %copy-done.65), kind=kCustom, calls=%fused_computation | custom fusion | bytes 50356224 | tf_op jit(solution)/shard_map/gather | solution.py:217
  501.0 15.7 scatter_custom_fusion.1
  517.4 3.5 fusion.183
  520.9 3.4 fusion.65
  526.5 14.3 fusion.166
  540.8 17.8 fusion.34
  560.3 4.2 copy-done.17
  564.4 2.5 fusion.42
  567.0 18.2 psum.115
  585.2 7.8 multiply_bitcast_fusion.1
  593.0 2.8 fusion.61
  598.2 9.7 fusion.184
  607.9 135.1 %all-gather.12.cloned.1.call-done = bf16[2048,16,2,352]{0,3,2,1:T(8,128)(2,1)} async-done(((bf16[256,16,2,352]{0,3,2,1:T(8,128)(2,1)}), bf16[2048,16,2,352]{0,3,2,1:T(8,128)(2,1)}) %all-gather.12.cloned.1.call-update) | async-done | bytes 46137360 | tf_op jit(solution)/shard_map/all_gather | solution.py:221
  743.0 35.9 %fusion.182 = f32[16,384,2,352]{1,3,2,0:T(8,128)} fusion(bf16[16,384,2048,1]{2,1,3,0:T(8,128)(2,1)} %bitcast.274, bf16[2048,16,2,352]{0,3,2,1:T(8,128)(2,1)} %all-gather.12.cloned.1.call-done), kind=kOutput, calls=%fused_computation.315 | convolution fusion | flops 17716740096 | bytes 88604672 | tf_op jit(solution)/shard_map/ecr,rexf->ecxf/dot_general | solution.py:226
  778.9 87.0 %all-gather.14.cloned.1.call-done = bf16[2048,16,352]{0,2,1:T(8,128)(2,1)} async-done(((bf16[256,16,352]{0,2,1:T(8,128)(2,1)}), bf16[2048,16,352]{0,2,1:T(8,128)(2,1)}) %all-gather.14.cloned.1.call-update) | async-done | bytes 23068688 | tf_op jit(solution)/shard_map/all_gather | solution.py:252
  865.9 34.6 %fusion.29 = f32[16,384,2048]{2,1,0:T(8,128)} fusion(bf16[2048,16,352]{0,2,1:T(8,128)(2,1)} %all-gather.14.cloned.1.call-done, f32[16,384,2,352]{1,3,2,0:T(8,128)} %fusion.182), kind=kOutput, calls=%fused_computation.88 | convolution fusion | flops 8871346176 | bytes 90701824 | tf_op jit(solution)/shard_map/ecf,ref->ecr/dot_general | solution.py:254
  900.5 46.7 %gather_fusion.1 = f32[4096,2048]{1,0:T(8,128)} fusion(f32[6144,2048]{1,0:T(8,128)} %bitcast.263, s32[4096]{0:T(1024)S(1)} %copy-done.66), kind=kCustom, calls=%fused_computation.1 | custom fusion | bytes 67125248 | tf_op jit(solution)/shard_map/gather | solution.py:255
  947.2 37.4 %reshape.407 = f32[1024,4,2048]{2,1,0:T(4,128)} reshape(f32[4096,2048]{1,0:T(8,128)} %gather_fusion.1) | data formatting | bytes 67108864 | tf_op jit(solution)/shard_map/reshape | solution.py:255
  984.7 38.0 %multiply_reduce_fusion = (f32[1024,4]{1,0:T(8,128)S(1)}, f32[1024,2048]{1,0:T(8,128)}) fusion(f32[1024,4,2048]{2,1,0:T(4,128)} %reshape.407, f32[1024,2048]{1,0:T(8,128)} %convert_element_type.223, f32[1024,4]{1,0:T(8,128)S(1)} %copy-done.30), kind=kLoop, calls=%fused_computation.11 | loop fusion | flops 31453184 | bytes 50364416 | tf_op jit(solution)/shard_map/reduce_sum | solution.py:260
  1023.5 28.7 %multiply_bitcast_fusion = (f32[16,384,1,352]{1,3,0,2:T(8,128)}, f32[16,384,1,352]{1,3,0,2:T(8,128)}) fusion(f32[16,384,2,352]{1,3,2,0:T(8,128)} %fusion.182, bf16[2048,16,352]{0,2,1:T(8,128)(2,1)} %all-gather.14.cloned.1.call-done, bf16[16,384,2048]{2,1,0:T(8,128)(2,1)} %bitcast.273, f32[16,384]{1,0:T(8,128)S(1)} %copy-done.103), kind=kOutput, calls=%fused_computation.31 | convolution fusion | flops 8922071040 | bytes 82862080 | tf_op jit(solution)/shard_map/ecr,ref->ecf/dot_general | solution.py:276
  1052.2 45.1 %fusion.1 = f32[16,384,2048,1]{2,1,0,3:T(8,128)} fusion(bf16[2048,16,2,352]{0,3,2,1:T(8,128)(2,1)} %all-gather.12.cloned.1.call-done, f32[16,384,1,352]{1,3,0,2:T(8,128)} %get-tuple-element.41, f32[16,384,1,352]{1,3,0,2:T(8,128)} %get-tuple-element.40), kind=kOutput, calls=%fused_computation.9 | convolution fusion | flops 17725390848 | bytes 113770496 | tf_op jit(solution)/shard_map/ecxf,rexf->ecr/dot_general | solution.py:295
  1097.4 47.0 %gather_fusion.3 = f32[4096,2048]{1,0:T(8,128)} fusion(f32[6144,2048]{1,0:T(8,128)} %bitcast.264, s32[4096]{0:T(1024)S(1)} %copy-done.66), kind=kCustom, calls=%fused_computation.3 | custom fusion | bytes 67125248 | tf_op jit(solution)/shard_map/gather | solution.py:299
  1144.3 37.4 %reshape.409 = f32[1024,4,2048]{2,1,0:T(4,128)} reshape(f32[4096,2048]{1,0:T(8,128)} %gather_fusion.3) | data formatting | bytes 67108864 | tf_op jit(solution)/shard_map/reshape | solution.py:299
  1181.7 25.7 %reduce_sum.225 = f32[1024,2048]{1,0:T(8,128)} reduce(f32[1024,4,2048]{2,1,0:T(4,128)} %reshape.409, f32[]{:T(128)} %constant.133.clone.1), dimensions={1}, to_apply=%region_21.22 | reduce | flops 6291456 | bytes 41943044 | tf_op jit(solution)/shard_map/reduce_sum | solution.py:298
  1207.4 12.5 multiply_reduce_fusion.5
  1220.6 21.5 bitcast_add_fusion
  1242.9 5.3 convolution_multiply_fusion
  1253.9 283.5 %all-reduce.24.cloned.1.call-done = (f32[1024,2048]{1,0:T(8,128)}, f32[1024,21]{0,1:T(8,128)}) async-done(((f32[1024,2048]{1,0:T(8,128)}, f32[1024,21]{0,1:T(8,128)}), (f32[1024,2048]{1,0:T(8,128)}, f32[1024,21]{0,1:T(8,128)})) %all-reduce.24.cloned.1.call-update) | async-done | bytes 8474640 | tf_op jit(solution)/shard_map/psum | solution.py:95
  1540.4 10.5 multiply_reduce_fusion.4
  1551.0 5.8 fusion.10
  1565.2 2.6 multiply_reduce_fusion.3
  1569.6 4.1 fusion.75
  1577.9 3.7 multiply_reduce_fusion.2
  1582.3 2.7 fusion.53
  1595.2 2.9 copy.210
  1599.9 2.8 pad_add_fusion
  1607.0 17.4 psum.119
  1624.4 3.3 fusion.120
  1631.8 11.8 convolution_bitcast_fusion
  1643.6 64.4 %all-reduce.26.cloned.1.call-done = (bf16[8,2048,16]{1,2,0:T(8,128)(2,1)}, bf16[8,16,3,512]{3,1,2,0:T(8,128)(2,1)}, bf16[8,512,16]{1,2,0:T(8,128)(2,1)}, bf16[8,...) async-done(((bf16[8,2048,16]{1,2,0:T(8,128)(2,1)}, ...) | async-done | bytes 3702800 | tf_op jit(solution)/shard_map/psum | solution.py:404
  1708.1 2.8 convert_element_type.257
  1721.1 553.0 %all-reduce.22.cloned.1.call-done = (f32[1024,2048]{1,0:T(8,128)}, f32[1024,2048]{1,0:T(8,128)}) async-done(((f32[1024,2048]{1,0:T(8,128)}, f32[1024,2048]{1,0:T(8,128)}), (f32[1024,2048]{1,0:T(8,128)}, f32[1024,2048]{1,0:T(8,128)})) %all-reduce.22.cloned.1.call-update) | async-done | bytes 16777232 | tf_op jit(solution)/shard_map/psum | solution.py:95
  2274.1 6.5 fusion.17
  2280.6 6.0 fusion.12
  2286.6 9.0 add_convert_fusion.3
  (391 shorter events, 115.6 us)
Async XLA Ops:
  7.2 207.1 %copy-start = (bf16[8,16,2,1408]{3,2,1,0:T(2,128)(2,1)S(1)}, bf16[8,16,2,1408]{3,2,1,0:T(2,128)(2,1)}, u32[]{:S(2)}) copy-start(bf16[8,16,2,1408]{3,2,1,0:T(2,128)(2,1)} %param.47) | copy-start | bytes 2162692
  7.2 9.2 copy-start.107
  7.2 9.8 copy-start.108
  7.2 52.7 %all-gather.8.cloned.1.call-start = ((), (), s32[]{:S(2)}) async-start(), calls=%async_computation | async-start | bytes 7077888 | tf_op jit(solution)/shard_map/all_gather | solution.py:153
  9.6 92.8 %all-gather.10.cloned.1.call-start = ((), (), s32[]{:S(2)}) async-start(), calls=%async_computation.1 | async-start | bytes 2359296 | tf_op jit(solution)/shard_map/all_gather | solution.py:206
  10.4 392.8 %all-reduce.20.cloned.1.call-start = ((), (), s32[]{:S(2)}) async-start(), calls=%async_computation.2 | async-start | bytes 16777216 | tf_op jit(solution)/shard_map/psum | solution.py:95
  16.4 43.5 %copy-start.104 = (f32[1024]{0:T(1024)}, f32[1024]{0:T(1024)S(1)}, u32[]{:S(2)}) copy-start(f32[1024]{0:T(1024)S(1)} %fusion.138) | copy-start | bytes 12292
  17.0 42.9 %copy-start.97 = (f32[2048]{0:T(1024)}, f32[2048]{0:T(1024)S(1)}, u32[]{:S(2)}) copy-start(f32[2048]{0:T(1024)S(1)} %convert_element_type.201) | copy-start | bytes 24580
  20.1 64.8 %copy-start.31 = (f32[1024,128]{1,0:T(8,128)}, f32[1024,128]{1,0:T(8,128)S(1)}, u32[]{:S(2)}) copy-start(f32[1024,128]{1,0:T(8,128)S(1)} %get-tuple-element.94) | copy-start | bytes 1572868
  24.0 46.2 %copy-start.67 = (bf16[1024,16,1]{0,1,2:T(8,128)(2,1)}, bf16[1024,16,1]{0,1,2:T(8,128)(2,1)S(1)}, u32[]{:S(2)}) copy-start(bf16[1024,16,1]{0,1,2:T(8,128)(2,1)S(1)} %fusion.64) | copy-start | bytes 98308
  88.2 8.5 copy-start.4
  88.2 8.5 copy-start.74
  110.1 416.4 %all-gather.18.cloned.1.call-start = ((), (), s32[]{:S(2)}) async-start(), calls=%async_computation.6 | async-start | bytes 6488064 | tf_op jit(solution)/shard_map/all_gather | solution.py:253
  110.7 430.1 %all-gather.16.cloned.1.call-start = ((), (), s32[]{:S(2)}) async-start(), calls=%async_computation.5 | async-start | bytes 12976128 | tf_op jit(solution)/shard_map/all_gather | solution.py:222
  112.7 630.3 %all-gather.12.cloned.1.call-start = ((), (), s32[]{:S(2)}) async-start(), calls=%async_computation.3 | async-start | bytes 51904512 | tf_op jit(solution)/shard_map/all_gather | solution.py:221
  113.2 752.6 %all-gather.14.cloned.1.call-start = ((), (), s32[]{:S(2)}) async-start(), calls=%async_computation.4 | async-start | bytes 25952256 | tf_op jit(solution)/shard_map/all_gather | solution.py:252
  114.0 1423.3 %all-reduce.24.cloned.1.call-start = ((), (), s32[]{:S(2)}) async-start(), calls=%async_computation.8 | async-start | bytes 16973824 | tf_op jit(solution)/shard_map/psum | solution.py:95
  114.8 294.2 %copy-start.70 = (f32[2048]{0:T(1024)}, f32[2048]{0:T(1024)S(1)}, u32[]{:S(2)}) copy-start(f32[2048]{0:T(1024)S(1)} %convert_element_type.212) | copy-start | bytes 24580
  130.6 83.0 %copy-start.82 = (s32[4096,1]{0,1:T(1,128)}, s32[4096,1]{0,1:T(1,128)S(1)}, u32[]{:S(2)}) copy-start(s32[4096,1]{0,1:T(1,128)S(1)} %compare_select_fusion) | copy-start | bytes 49156
  146.4 49.2 %copy-start.64 = (s32[6144]{0:T(1024)}, s32[6144]{0:T(1024)S(1)}, u32[]{:S(2)}) copy-start(s32[6144]{0:T(1024)S(1)} %fusion.115) | copy-start | bytes 73732
  146.4 59.0 %copy-start.106 = (bf16[256,16]{0,1:T(8,128)(2,1)S(1)}, bf16[256,16]{0,1:T(8,128)(2,1)}, u32[]{:S(2)}) copy-start(bf16[256,16]{0,1:T(8,128)(2,1)} %param.33) | copy-start | bytes 24580
  146.4 68.5 %copy-start.49 = (bf16[4,128,512]{2,1,0:T(8,128)(2,1)S(1)}, bf16[4,128,512]{2,1,0:T(8,128)(2,1)}, u32[]{:S(2)}) copy-start(bf16[4,128,512]{2,1,0:T(8,128)(2,1)} %copy-done.48) | copy-start | bytes 1572868
  146.4 68.5 %copy-start.51 = (bf16[4,128,512]{2,1,0:T(8,128)(2,1)S(1)}, bf16[4,128,512]{2,1,0:T(8,128)(2,1)}, u32[]{:S(2)}) copy-start(bf16[4,128,512]{2,1,0:T(8,128)(2,1)} %copy-done.50) | copy-start | bytes 1572868
  213.6 201.4 %copy-start.45 = (bf16[2048,16]{0,1:T(8,128)(2,1)}, bf16[2048,16]{0,1:T(8,128)(2,1)S(1)}, u32[]{:S(2)}) copy-start(bf16[2048,16]{0,1:T(8,128)(2,1)S(1)} %all_gather.32) | copy-start | bytes 196612
  238.4 170.6 %copy-start.60 = (bf16[1024,16]{0,1:T(8,128)(2,1)}, bf16[1024,16]{0,1:T(8,128)(2,1)S(1)}, u32[]{:S(2)}) copy-start(bf16[1024,16]{0,1:T(8,128)(2,1)S(1)} %psum.113) | copy-start | bytes 98308
  417.4 33.0 %copy-start.2 = (f32[1024,16]{0,1:T(8,128)}, f32[1024,16]{0,1:T(8,128)S(1)}, u32[]{:S(2)}) copy-start(f32[1024,16]{0,1:T(8,128)S(1)} %fusion.95) | copy-start | bytes 196612
  417.4 33.8 %copy-start.53 = (s32[1024,4]{0,1:T(4,128)S(1)}, s32[1024,4]{0,1:T(4,128)}, u32[]{:S(2)}) copy-start(s32[1024,4]{0,1:T(4,128)} %param.39) | copy-start | bytes 49156
  417.5 34.0 %copy-start.65 = (s32[6144]{0:T(1024)S(1)}, s32[6144]{0:T(1024)}, u32[]{:S(2)}) copy-start(s32[6144]{0:T(1024)} %copy-done.64) | copy-start | bytes 73732
  451.5 49.3 %copy-start.29 = (f32[1024,4]{1,0:T(8,128)}, f32[1024,4]{1,0:T(8,128)S(1)}, u32[]{:S(2)}) copy-start(f32[1024,4]{1,0:T(8,128)S(1)} %copy.192) | copy-start | bytes 49156
  451.5 65.8 %copy-start.72 = (bf16[8,1,256]{2,1,0:T(2,128)(2,1)S(1)}, bf16[8,1,256]{2,1,0:T(2,128)(2,1)}, u32[]{:S(2)}) copy-start(bf16[8,1,256]{2,1,0:T(2,128)(2,1)} %all-gather) | copy-start | bytes 12292
  524.3 34.2 %copy-start.58 = (bf16[1024,16,1]{0,1,2:T(8,128)(2,1)}, bf16[1024,16,1]{0,1,2:T(8,128)(2,1)S(1)}, u32[]{:S(2)}) copy-start(bf16[1024,16,1]{0,1,2:T(8,128)(2,1)S(1)} %fusion.65) | copy-start | bytes 98308
  526.4 58.8 %copy-start.95 = (bf16[1024,16]{0,1:T(8,128)(2,1)}, bf16[1024,16]{0,1:T(8,128)(2,1)S(1)}, u32[]{:S(2)}) copy-start(bf16[1024,16]{0,1:T(8,128)(2,1)S(1)} %fusion.62) | copy-start | bytes 98308
  540.8 17.8 copy-start.56
  564.4 33.8 %slice-start.8 = ((s8[5767168]{0:T(1024)(128)(4,1)}), s8[1572864]{0:T(1024)(128)(4,1)S(1)}, s32[]{:S(2)}) async-start(s8[5767168]{0:T(1024)(128)(4,1)} %bitcast.309), calls=%async_computation.18 | async-start | bytes 3145728
  585.2 13.0 slice-start.9
  778.9 121.6 %copy-start.66 = (s32[4096]{0:T(1024)S(1)}, s32[4096]{0:T(1024)}, u32[]{:S(2)}) copy-start(s32[4096]{0:T(1024)} %broadcast_clamp_fusion) | copy-start | bytes 49156
  947.2 37.5 %copy-start.30 = (f32[1024,4]{1,0:T(8,128)S(1)}, f32[1024,4]{1,0:T(8,128)}, u32[]{:S(2)}) copy-start(f32[1024,4]{1,0:T(8,128)} %copy-done.29) | copy-start | bytes 49156
  984.7 38.8 %copy-start.103 = (f32[16,384]{1,0:T(8,128)S(1)}, f32[16,384]{1,0:T(8,128)}, u32[]{:S(2)}) copy-start(f32[16,384]{1,0:T(8,128)} %mul.597) | copy-start | bytes 73732
  1181.7 25.7 %copy-start.62 = (bf16[1024,16]{0,1:T(8,128)(2,1)S(1)}, bf16[1024,16]{0,1:T(8,128)(2,1)}, u32[]{:S(2)}) copy-start(bf16[1024,16]{0,1:T(8,128)(2,1)} %psum.115) | copy-start | bytes 98308
  1181.7 25.7 %copy-start.88 = (f32[1024]{0:T(1024)S(1)}, f32[1024]{0:T(1024)}, u32[]{:S(2)}) copy-start(f32[1024]{0:T(1024)} %copy-done.87) | copy-start | bytes 12292
  1207.4 12.5 copy-start.80
  1207.4 12.5 copy-start.81
  1242.1 466.0 %all-reduce.26.cloned.1.call-start = ((), (), s32[]{:S(2)}) async-start(), calls=%async_computation.9 | async-start | bytes 7405568 | tf_op jit(solution)/shard_map/psum | solution.py:404
  1248.2 290.6 %copy-start.54 = (s32[1024,4]{0,1:T(4,128)S(1)}, s32[1024,4]{0,1:T(4,128)}, u32[]{:S(2)}) copy-start(s32[1024,4]{0,1:T(4,128)} %param.39) | copy-start | bytes 49156
  1248.2 290.7 %copy-start.44 = (f32[1024,16]{0,1:T(8,128)S(1)}, f32[1024,16]{0,1:T(8,128)}, u32[]{:S(2)}) copy-start(f32[1024,16]{0,1:T(8,128)} %copy-done.43) | copy-start | bytes 196612
  1248.2 290.7 %copy-start.79 = (f32[1024]{0:T(1024)S(1)}, f32[1024]{0:T(1024)}, u32[]{:S(2)}) copy-start(f32[1024]{0:T(1024)} %copy-done.78) | copy-start | bytes 12292
  1248.2 290.7 %copy-start.94 = (f32[1024]{0:T(1024)S(1)}, f32[1024]{0:T(1024)}, u32[]{:S(2)}) copy-start(f32[1024]{0:T(1024)} %copy-done.93) | copy-start | bytes 12292
  1248.3 290.7 %copy-start.3 = (f32[1024,16]{0,1:T(8,128)S(1)}, f32[1024,16]{0,1:T(8,128)}, u32[]{:S(2)}) copy-start(f32[1024,16]{0,1:T(8,128)} %copy-done.2) | copy-start | bytes 196612
  1248.3 290.7 %copy-start.46 = (bf16[2048,16]{0,1:T(8,128)(2,1)S(1)}, bf16[2048,16]{0,1:T(8,128)(2,1)}, u32[]{:S(2)}) copy-start(bf16[2048,16]{0,1:T(8,128)(2,1)} %copy-done.45) | copy-start | bytes 196612
  1539.0 11.9 slice-start.4
  1540.3 10.6 copy-start.92
  1540.4 10.6 slice-start.5
  1540.4 10.6 copy-start.86
  1565.2 10.8 slice-start.2
  1567.8 8.2 slice-start.3
  1602.7 21.7 copy-start.98
  1602.7 21.7 copy-start.105
  1631.7 642.3 %all-reduce.22.cloned.1.call-start = ((), (), s32[]{:S(2)}) async-start(), calls=%async_computation.7 | async-start | bytes 33554432 | tf_op jit(solution)/shard_map/psum | solution.py:95
  1708.1 9.3 copy-start.47
  1708.1 10.4 copy-start.55
  1708.1 11.4 copy-start.57
  1708.1 12.3 copy-start.69
  2274.1 12.5 slice-start.6
  2286.6 9.1 copy-start.1
  (68 other events, 249.0 us)
Sparse Core Ops, SparseCore 0:
  10.5 49.3 all-gather.7
  61.8 27.8 all-gather.9
  110.2 292.9 all-reduce.19
  405.0 42.3 all-gather.17
  449.6 67.6 all-gather.15
  519.1 223.8 all-gather.11
  744.9 120.9 all-gather.13
  1242.2 295.0 all-reduce.23
  1631.9 76.1 all-reduce.25
  1710.7 563.2 all-reduce.21
where the time goes:
time: 2310 us; the launch traced here: 2300 us
  waiting for transfers between devices  1320 us (57%)
  local copies, waits for them, and re-layouts  381 us (16%)
  matrix products  356 us (15%)
  other arithmetic  148 us (6%)
  blocking collectives  76.1 us (3%)
    psum x3, waiting for transfers between devices, tensor_total(): return lax.psum((wide_part, narrow_part), 'tensor')  1000 us
    all_gather x1, waiting for transfers between devices, body(): up_rows = lax.all_gather(routed_gate_up_weight, 'dp', axis=0, tiled=True)  135 us
    gather x2, local copies, waits for them, and re-layouts, body(): expert_cols.reshape(EXPERTS * CAP, -1)[slot_index].reshape(length, TOP, -1)  93.7 us
    all_gather x1, waiting for transfers between devices, body(): down_rows = lax.all_gather(routed_down_weight, 'dp', axis=0, tiled=True)  87 us
    reshape x2, local copies, waits for them, and re-layouts, body(): expert_cols.reshape(EXPERTS * CAP, -1)[slot_index].reshape(length, TOP, -1)  74.8 us
    psum x1, waiting for transfers between devices, body(): lax.psum(spread(grad_qkv_a_local).astype(jnp.bfloat16), 'dp')  64.4 us
    psum x3, blocking collectives, tensor_total(): return lax.psum((wide_part, narrow_part), 'tensor')  58.1 us
    dot_general x10, matrix products, matmul(): return jnp.dot(left_side, right_side, preferred_element_type=jnp.float32)  50.4 us
  transfers between devices with their start and end apart: 10, of which 7 were waited for; matrix products, arithmetic and copies ran while one was open for 17% of the time, Pallas kernels for 0%

commit v1 on v0

--- a/solution.py
+++ b/solution.py
@@ -1,6 +1,10 @@
+import functools
+
 import jax
 import jax.numpy as jnp
 from jax import lax
+from jax.experimental import pallas as pl
+from jax.experimental.pallas import tpu as pltpu
 from jax.sharding import PartitionSpec as P
 
 HEAD_SIZE = 128
@@ -8,13 +12,15 @@
 EXPERTS = 16
 ADAPTER_SETS = 8
 PIECE = 256
-CAP = 384
 
 
 EPSILON = 1e-06
 THETA = 1000000.0
 ADAPTER_SCALE = 2.0
 MASKED = -1e30
+MESH = pl.DeviceIdType.MESH
+SUM_CHUNKS = 16
+EXPERT_PARTS = 4
 
 
 def matmul(left_side, right_side):
@@ -75,24 +81,123 @@
     return causal | together
 
 
-def slot_table(routes, length):
-    flat_routes = routes.reshape(-1)
-    hit_table = (flat_routes[:, None] == jnp.arange(EXPERTS, dtype=jnp.int32)[None, :]).astype(
-        jnp.int32
-    )
-    earlier = jnp.cumsum(hit_table, axis=0) - hit_table
-    slot_index = flat_routes * CAP + jnp.sum(earlier * hit_table, axis=1)
-    pair_tokens = jnp.arange(length * TOP, dtype=jnp.int32) // TOP
-    slot_owner = jnp.full((EXPERTS * CAP,), length, jnp.int32).at[slot_index].set(pair_tokens)
-    return (slot_index, slot_owner)
+def line_sum_kernel(
+    chunks, part_ref, total_ref, from_end, pair_sum, from_pair, semaphores
+):
+    place = lax.axis_index("tensor")
+    rows = part_ref.shape[0] // chunks
+    inner = (place == 1) | (place == 2)
+    end = (place == 0) | (place == 3)
+    mate = jnp.where(place < 2, 1 - place, 5 - place)
+    other = jnp.where(inner, 3 - place, place)
+    barrier = pltpu.get_barrier_semaphore()
+    pl.semaphore_signal(barrier, inc=1, device_id={"tensor": mate}, device_id_type=MESH)
+
+    @pl.when(inner)
+    def _():
+        pl.semaphore_signal(barrier, inc=1, device_id={"tensor": other}, device_id_type=MESH)
+        pl.semaphore_wait(barrier, 2)
+
+    @pl.when(end)
+    def _():
+        pl.semaphore_wait(barrier, 1)
+
+    def span(chunk):
+        return pl.ds(pl.multiple_of(chunk * rows, rows), rows)
+
+    def copy(source, target, chunk, lane, device):
+        return pltpu.make_async_remote_copy(
+            source.at[span(chunk)],
+            target.at[span(chunk)],
+            semaphores.at[2 * lane, chunk],
+            semaphores.at[2 * lane + 1, chunk],
+            device_id={"tensor": device},
+            device_id_type=MESH,
+        )
+
+    def inward(chunk):
+        return copy(part_ref, from_end, chunk, 0, mate)
+
+    def across(chunk):
+        return copy(pair_sum, from_pair, chunk, 1, other)
+
+    def outward(chunk):
+        return copy(total_ref, total_ref, chunk, 2, mate)
+
+    def add(left_ref, right_ref, out_ref, chunk):
+        out_ref[span(chunk)] = to_low(
+            left_ref[span(chunk)].astype(jnp.float32) + right_ref[span(chunk)].astype(jnp.float32)
+        )
+
+    @pl.when(end)
+    def _():
+        @pl.loop(0, chunks)
+        def _(chunk):
+            inward(chunk).start()
+
+        @pl.loop(0, chunks)
+        def _(chunk):
+            inward(chunk).wait_send()
+
+        @pl.loop(0, chunks)
+        def _(chunk):
+            outward(chunk).wait_recv()
+
+    @pl.when(inner)
+    def _():
+        @pl.loop(0, chunks + 1)
+        def _(step):
+            @pl.when(step < chunks)
+            def _():
+                inward(step).wait_recv()
+                add(part_ref, from_end, pair_sum, step)
+                across(step).start()
+
+            @pl.when(step > 0)
+            def _():
+                across(step - 1).wait_recv()
+                add(pair_sum, from_pair, total_ref, step - 1)
+                outward(step - 1).start()
+
+        @pl.loop(0, chunks)
+        def _(chunk):
+            across(chunk).wait_send()
+            outward(chunk).wait_send()
+
+
+def tensor_sum(part, number):
+    if lax.axis_size("tensor") != 4:
+        return lax.psum(part.astype(jnp.float32), "tensor")
+    total = pl.pallas_call(
+        functools.partial(line_sum_kernel, SUM_CHUNKS),
+        out_shape=jax.ShapeDtypeStruct(part.shape, jnp.bfloat16),
+        in_specs=[pl.BlockSpec(memory_space=pltpu.VMEM)],
+        out_specs=pl.BlockSpec(memory_space=pltpu.VMEM),
+        scratch_shapes=[pltpu.VMEM(part.shape, jnp.bfloat16)] * 3
+        + [pltpu.SemaphoreType.DMA((6, SUM_CHUNKS))],
+        compiler_params=pltpu.CompilerParams(
+            collective_id=number, has_side_effects=True, vmem_limit_bytes=40 * 2**20
+        ),
+        cost_estimate=pl.CostEstimate(flops=0, bytes_accessed=300 * 2**20, transcendentals=0),
+    )(to_low(part))
+    return total.astype(jnp.float32)
+
+
+def summed(wide_part, narrow_part, number):
+    width, small = wide_part.shape[1], narrow_part.shape[1]
+    pad = jnp.zeros((wide_part.shape[0], 128 - small), jnp.bfloat16)
+    total = tensor_sum(
+        jnp.concatenate([to_low(wide_part), to_low(narrow_part), pad], axis=1), number
+    )
+    return total[:, :width], total[:, width : width + small]
 
 
 def swiglu(paired):
     return jax.nn.silu(paired[..., 0, :]) * paired[..., 1, :]
 
 
-def tensor_total(wide_part, narrow_part):
-    return lax.psum((wide_part, narrow_part), "tensor")
+def gathered(weight):
+    return lax.all_gather(weight, "dp", axis=0, tiled=True)
 
 
 def body(
@@ -147,10 +252,11 @@
     normed = to_low(rms_scale(tokens_f, gain_attn_f))
     mid_qkv = to_low(matmul(normed, qkv_a))
     columns = normed
+    qkv_rows = gathered(query_key_value_weight)
     qkv_sum = jnp.einsum(
         "tr,rsf->tsf",
         columns,
-        lax.all_gather(query_key_value_weight, "dp", axis=0, tiled=True),
+        qkv_rows,
         preferred_element_type=jnp.float32,
     )
     qkv_sum = qkv_sum + query_key_value_bias.astype(jnp.float32)
@@ -202,10 +308,9 @@
         )
         logsum_parts.append(highest + jnp.log(row_totals))
     attended = to_low(jnp.concatenate(attended_parts, axis=0).reshape(length, -1))
-    branch_part = contract_last(
-        attended, lax.all_gather(output_projection_weight, "dp", axis=0, tiled=True)
-    )
-    branch_here, mid_out_here_f = tensor_total(branch_part, matmul(attended, out_a))
+    output_rows = gathered(output_projection_weight)
+    branch_part = contract_last(attended, output_rows)
+    branch_here, mid_out_here_f = summed(branch_part, matmul(attended, out_a), 1)
     mid_out_here = to_low(mid_out_here_f)
     hidden_here = tokens_f + branch_here + ADAPTER_SCALE * matmul(mid_out_here, out_b)
     normed_two_here_f, norm_ffn_pull = jax.vjp(
@@ -213,75 +318,40 @@
     )
     normed_two_here = to_low(normed_two_here_f)
     normed_two, mid_out = (normed_two_here, mid_out_here)
-    slot_index, slot_owner = slot_table(routes, length)
-    dispatched = jnp.concatenate([normed_two, jnp.zeros((1, width), jnp.bfloat16)], axis=0)[
-        slot_owner
-    ]
-    dispatched = dispatched.reshape(EXPERTS, CAP, width)
-    up_rows = lax.all_gather(routed_gate_up_weight, "dp", axis=0, tiled=True)
-    shared_rows = lax.all_gather(shared_expert_gate_up_weight, "dp", axis=0, tiled=True)
-    router_rows = lax.all_gather(router_matrix, "dp", axis=0, tiled=True)
-    gate_rows = lax.all_gather(shared_expert_gate_weight, "dp", axis=0, tiled=True)
-    first_totals = (
-        jnp.einsum("ecr,rexf->ecxf", dispatched, up_rows, preferred_element_type=jnp.float32),
-        jnp.einsum("tr,rxf->txf", normed_two, shared_rows, preferred_element_type=jnp.float32),
-        matmul(normed_two, router_rows),
-        matmul(normed_two, gate_rows),
-        router_rows,
-        gate_rows,
-    )
-    gate_up, shared_sum, logits, gate_logit, router_full, gate_full = first_totals
-    router_probs = jax.nn.softmax(logits, axis=-1)
-    gates = jnp.take_along_axis(router_probs, routes, axis=1)
-    gate_slot = jnp.zeros((EXPERTS * CAP,), jnp.float32).at[slot_index].set(gates.reshape(-1))
-    gate_slot = gate_slot.reshape(EXPERTS, CAP)
-    shared_gate = jax.nn.sigmoid(gate_logit)
-    act_f, act_pull = jax.vjp(swiglu, gate_up)
-    act = to_low(act_f)
+    cot_f = cotangent.astype(jnp.float32)
+    down_rows = gathered(routed_down_weight)
+    sdown_rows = gathered(shared_expert_down_weight)
+    shared_rows = gathered(shared_expert_gate_up_weight)
+    small_rows = gathered(
+        jnp.concatenate(
+            [
+                router_matrix,
+                shared_expert_gate_weight[:, None],
+                jnp.full_like(shared_expert_gate_weight, set_id)[:, None],
+            ],
+            axis=1,
+        )
+    )
+    router_full, gate_full = small_rows[:, :EXPERTS], small_rows[:, EXPERTS]
+    router_probs = jax.nn.softmax(matmul(normed_two, router_full), axis=-1)
+    shared_gate = jax.nn.sigmoid(matmul(normed_two, gate_full))
+    expert_ids = jnp.arange(EXPERTS, dtype=jnp.int32)
+    chosen = jnp.sum(
+        (routes[:, :, None] == expert_ids[None, None, :]).astype(jnp.float32), axis=1
+    )
+    gate_table = (router_probs * chosen).T
+
     mid_up = to_low(matmul(normed_two, up_a))
-    shared_gu = shared_sum + ADAPTER_SCALE * jnp.einsum(
-        "tr,rxf->txf", mid_up, up_b, preferred_element_type=jnp.float32
-    )
+    shared_gu = jnp.einsum(
+        "tr,rxf->txf", normed_two, shared_rows, preferred_element_type=jnp.float32
+    ) + ADAPTER_SCALE * jnp.einsum("tr,rxf->txf", mid_up, up_b, preferred_element_type=jnp.float32)
     shared_act_f, shared_pull = jax.vjp(swiglu, shared_gu)
     shared_act = to_low(shared_act_f)
-    cot_f = cotangent.astype(jnp.float32)
-    cot_slots = jnp.concatenate([cotangent, jnp.zeros((1, width), jnp.bfloat16)], axis=0)[
-        slot_owner
-    ]
-    cot_slots = cot_slots.reshape(EXPERTS, CAP, width)
-    down_rows = lax.all_gather(routed_down_weight, "dp", axis=0, tiled=True)
-    sdown_rows = lax.all_gather(shared_expert_down_weight, "dp", axis=0, tiled=True)
-    expert_cols = jnp.einsum("ecf,ref->ecr", act, down_rows, preferred_element_type=jnp.float32)
-    picked = expert_cols.reshape(EXPERTS * CAP, -1)[slot_index].reshape(length, TOP, -1)
     shared_cols = contract_last(shared_act, sdown_rows)
-    routed = jnp.sum(gates[:, :, None] * picked, axis=1)
-    down_totals = (
-        routed + shared_gate[:, None] * shared_cols,
-        jnp.sum(cot_f[:, None, :] * picked, axis=2),
-        jnp.sum(cot_f * shared_cols, axis=1),
-    )
-    combined_part, gate_pair_part, shared_gate_part = down_totals
-    combined_here, mid_down_here_f = tensor_total(combined_part, matmul(shared_act, down_a))
-    mid_down_here = to_low(mid_down_here_f)
-    extra_here = ADAPTER_SCALE * matmul(mid_down_here, down_b)
-    output_here = to_low(hidden_here + combined_here + shared_gate[:, None] * extra_here)
-    output, mid_down = (output_here, mid_down_here)
+    shared_gate_part = jnp.sum(cot_f * shared_cols, axis=1)
     grad_shared = to_low(shared_gate[:, None] * cot_f)
-    down_rows = lax.all_gather(routed_down_weight, "dp", axis=0, tiled=True)
-    sdown_rows = lax.all_gather(shared_expert_down_weight, "dp", axis=0, tiled=True)
-    cot_cols = cot_slots.astype(jnp.float32)
-    grad_cols = to_low(gate_slot[:, :, None] * cot_cols)
-    shared_cols = grad_shared
-    back_totals = (
-        jnp.einsum("ecr,ref->ecf", grad_cols, down_rows, preferred_element_type=jnp.float32),
-        matmul(shared_cols, sdown_rows),
-    )
-    grad_act, grad_shared_act = back_totals
     grad_mid_down = to_low(ADAPTER_SCALE * contract_last(grad_shared, down_b))
-    grad_shared_act = grad_shared_act + contract_last(grad_mid_down, down_a)
-    grad_down_a_local = contract_first(shared_act, grad_mid_down)
-    grad_down_b_local = ADAPTER_SCALE * contract_first(mid_down, grad_shared)
-    grad_gate_up = to_low(act_pull(grad_act)[0])
+    grad_shared_act = matmul(grad_shared, sdown_rows) + contract_last(grad_mid_down, down_a)
     grad_shared_gu = to_low(shared_pull(grad_shared_act)[0])
     grad_mid_up_part = ADAPTER_SCALE * jnp.einsum(
         "txf,rxf->tr", grad_shared_gu, up_b, preferred_element_type=jnp.float32
@@ -289,36 +359,65 @@
     grad_up_b_local = ADAPTER_SCALE * jnp.einsum(
         "tr,txf->rxf", mid_up, grad_shared_gu, preferred_element_type=jnp.float32
     )
-    up_rows, shared_rows = lax.all_gather(
-        (routed_gate_up_weight, shared_expert_gate_up_weight), "dp", axis=0, tiled=True
-    )
-    expert_cols = jnp.einsum(
-        "ecxf,rexf->ecr", grad_gate_up, up_rows, preferred_element_type=jnp.float32
-    )
-    routed = jnp.sum(
-        expert_cols.reshape(EXPERTS * CAP, -1)[slot_index].reshape(length, TOP, -1), axis=1
-    )
-    normed_two_part = routed + jnp.einsum(
+    grad_down_a_local = contract_first(shared_act, grad_mid_down)
+    combined_part = shared_gate[:, None] * shared_cols
+    normed_two_part = jnp.einsum(
         "txf,rxf->tr", grad_shared_gu, shared_rows, preferred_element_type=jnp.float32
     )
+
+    grad_act_open = jnp.einsum(
+        "ref,tr->eft", down_rows, cotangent, preferred_element_type=jnp.float32
+    )
+    gate_grad_parts = []
+    share = EXPERTS // EXPERT_PARTS
+    for first in range(0, EXPERTS, share):
+        some = slice(first, first + share)
+        up_rows = gathered(routed_gate_up_weight[:, some])
+        gate_up = jnp.einsum(
+            "rexf,tr->exft", up_rows, normed_two, preferred_element_type=jnp.float32
+        )
+        gate_half, up_half = gate_up[:, 0], gate_up[:, 1]
+        squashed = jax.nn.sigmoid(gate_half)
+        act = to_low(gate_half * squashed * up_half).astype(jnp.float32)
+        gate_rows = gate_table[some, None, :]
+        open_part = grad_act_open[some]
+        gate_grad_parts.append(jnp.sum(act * open_part, axis=1))
+        grad_act = gate_rows * open_part
+        grad_gate_up = to_low(
+            jnp.stack(
+                [
+                    grad_act * up_half * squashed * (1.0 + gate_half * (1.0 - squashed)),
+                    grad_act * gate_half * squashed,
+                ],
+                axis=1,
+            )
+        )
+        combined_part = combined_part + jnp.einsum(
+            "eft,ref->tr",
+            to_low(gate_rows * act),
+            down_rows[:, some],
+            preferred_element_type=jnp.float32,
+        )
+        normed_two_part = normed_two_part + jnp.einsum(
+            "exft,rexf->tr", grad_gate_up, up_rows, preferred_element_type=jnp.float32
+        )
+    gate_grad_part = jnp.concatenate(gate_grad_parts, axis=0).T
     narrow_part = jnp.concatenate(
-        [gate_pair_part, shared_gate_part[:, None], grad_mid_up_part], axis=1
-    )
-    grad_normed_two, narrow_sum = tensor_total(normed_two_part, narrow_part)
-    top_count = routes.shape[1]
-    grad_gates = narrow_sum[:, :top_count]
-    expert_ids = jnp.arange(EXPERTS, dtype=jnp.int32)
-    grad_probs = jnp.sum(
-        grad_gates[:, :, None]
-        * (routes[:, :, None] == expert_ids[None, None, :]).astype(jnp.float32),
-        axis=1,
-    )
+        [gate_grad_part, shared_gate_part[:, None], grad_mid_up_part], axis=1
+    )
+    grad_normed_two, narrow_sum = summed(normed_two_part, narrow_part, 2)
+    combined_here, mid_down_here_f = summed(combined_part, matmul(shared_act, down_a), 3)
+    mid_down = to_low(mid_down_here_f)
+    extra_here = ADAPTER_SCALE * matmul(mid_down, down_b)
+    output = to_low(hidden_here + combined_here + shared_gate[:, None] * extra_here)
+    grad_down_b_local = ADAPTER_SCALE * contract_first(mid_down, grad_shared)
+    grad_probs = chosen * narrow_sum[:, :EXPERTS]
     grad_logits = to_low(
         router_probs * (grad_probs - jnp.sum(router_probs * grad_probs, axis=1, keepdims=True))
     )
-    shared_gate_grad = narrow_sum[:, top_count] + jnp.sum(cot_f * extra_here, axis=1)
+    shared_gate_grad = narrow_sum[:, EXPERTS] + jnp.sum(cot_f * extra_here, axis=1)
     grad_gate_logit = to_low(shared_gate_grad * shared_gate * (1.0 - shared_gate))
-    grad_mid_up_here = to_low(narrow_sum[:, top_count + 1 :])
+    grad_mid_up_here = to_low(narrow_sum[:, EXPERTS + 1 :])
     grad_normed_two = grad_normed_two + contract_last(grad_logits, router_full)
     grad_normed_two = (
         grad_normed_two
@@ -333,7 +432,7 @@
     grad_out_b_local = ADAPTER_SCALE * contract_first(mid_out, grad_branch)
     columns = grad_branch
     grad_att_sum = matmul(
-        columns, lax.all_gather(output_projection_weight, "dp", axis=0, tiled=True)
+        columns, output_rows
     )
     grad_attended = to_low(grad_att_sum + contract_last(grad_mid_out, out_a)).reshape(
         length, heads_here, HEAD_SIZE
@@ -385,31 +484,46 @@
     normed_part = jnp.einsum(
         "tsf,rsf->tr",
         grad_qkv,
-        lax.all_gather(query_key_value_weight, "dp", axis=0, tiled=True),
+        qkv_rows,
         preferred_element_type=jnp.float32,
     )
-    grad_normed, grad_mid_qkv_f = tensor_total(normed_part, grad_mid_qkv_part)
+    grad_normed, grad_mid_qkv_f = summed(normed_part, grad_mid_qkv_part, 4)
     grad_mid_qkv_here = to_low(grad_mid_qkv_f)
     grad_normed = grad_normed + contract_last(grad_mid_qkv_here, qkv_a)
     norm_attn_pull = jax.vjp(lambda rows: rms_scale(rows, gain_attn_f), tokens_f)[1]
     grad_tokens_here = to_low(grad_hidden + norm_attn_pull(grad_normed)[0])
     grad_tokens, grad_mid_qkv = (grad_tokens_here, grad_mid_qkv_here)
     grad_qkv_a_local = contract_first(normed, grad_mid_qkv)
-    marker = (jnp.arange(ADAPTER_SETS, dtype=jnp.int32) == set_id).astype(jnp.float32)
-
-    def spread(local_grad):
-        return marker.reshape((ADAPTER_SETS,) + (1,) * local_grad.ndim) * local_grad[None]
-
-    adapter_totals = (
-        lax.psum(spread(grad_qkv_a_local).astype(jnp.bfloat16), "dp").astype(jnp.float32),
-        lax.psum(spread(grad_qkv_b_local).astype(jnp.bfloat16), "dp").astype(jnp.float32),
-        lax.psum(spread(grad_out_a_local).astype(jnp.bfloat16), "dp").astype(jnp.float32),
-        lax.psum(spread(grad_out_b_local).astype(jnp.bfloat16), "dp").astype(jnp.float32),
-        lax.psum(spread(grad_up_a_local).astype(jnp.bfloat16), "dp").astype(jnp.float32),
-        lax.psum(spread(grad_up_b_local).astype(jnp.bfloat16), "dp").astype(jnp.float32),
-        lax.psum(spread(grad_down_a_local).astype(jnp.bfloat16), "dp").astype(jnp.float32),
-        lax.psum(spread(grad_down_b_local).astype(jnp.bfloat16), "dp").astype(jnp.float32),
-    )
+    everyone = small_rows[:: small_rows.shape[0] // lax.axis_size("dp"), EXPERTS + 1]
+    marker = to_low(
+        jnp.arange(ADAPTER_SETS, dtype=jnp.int32)[:, None] == everyone.astype(jnp.int32)[None, :]
+    )
+
+    def adapter_sums(local_grads):
+        sizes = [local_grad.size for local_grad in local_grads]
+        flat = jnp.concatenate([to_low(local_grad).reshape(-1) for local_grad in local_grads])
+        rows = lax.all_gather(flat[None], "dp", axis=0, tiled=True)
+        totals = matmul(marker, rows)
+        results, start = [], 0
+        for local_grad, size in zip(local_grads, sizes):
+            results.append(
+                totals[:, start : start + size].reshape((ADAPTER_SETS,) + local_grad.shape)
+            )
+            start += size
+        return results
+
+    early = adapter_sums(
+        [
+            grad_out_a_local,
+            grad_out_b_local,
+            grad_up_a_local,
+            grad_up_b_local,
+            grad_down_a_local,
+            grad_down_b_local,
+        ]
+    )
+    late = adapter_sums([grad_qkv_b_local, grad_qkv_a_local])
+    adapter_totals = [late[1], late[0]] + early
     return (
         output,
         grad_tokens,

time: 2310 us -> 1410 us (0.61)
  waiting for transfers between devices: 1320 us -> 209 us
  Pallas kernels: 0 us -> 450 us
  local copies, waits for them, and re-layouts: 381 us -> 139 us
  matrix products: 356 us -> 454 us
  blocking collectives: 76.1 us -> 21.5 us
  other arithmetic: 148 us -> 111 us
    psum x4 -> x0, waiting for transfers between devices: 1070 us -> none  [the longest x3 1000 us: tensor_total(): return lax.psum((wide_part, narrow_part), 'tensor')]
    pallas_call x0 -> x4, Pallas kernels: none -> 450 us  [tensor_sum(): pl.pallas_call(functools.partial(line_sum_kernel, SUM_CHUNKS), out_shape=...]
    gather x9 -> x0, local copies, waits for them, and re-layouts: 226 us -> none  [the longest x2 93.7 us: body(): expert_cols.reshape(EXPERTS * CAP, -1)[slot_index].reshape(length, TOP, -1)]
    dot_general x6 -> x15, matrix products: 166 us -> 256 us  [the longest x4 77.1 us: body(): jnp.einsum('exft,rexf->tr', grad_gate_up, up_rows, preferred_element_type...]
    reduce_sum x5 -> x2, other arithmetic: 64 us -> 0.4 us  [the longest x1 0.37 us: body(): router_probs = jax.nn.softmax(matmul(normed_two, router_full), axis=-1)]
    psum x3 -> x0, blocking collectives: 58.1 us -> none  [tensor_total(): return lax.psum((wide_part, narrow_part), 'tensor')]
    reshape x2 -> x10, local copies, waits for them, and re-layouts: 74.8 us -> 19.8 us  [the longest x4 17.3 us: adapter_sums(): totals[:, start:start + size].reshape((ADAPTER_SETS,) + local_grad.shape)]
    all_gather x6 -> x10, waiting for transfers between devices: 256 us -> 205 us  [the longest x9 205 us: gathered(): return lax.all_gather(weight, 'dp', axis=0, tiled=True)]
  transfers between devices with their start and end apart: 10 -> 10, of which waited for: 7 -> 4; matrix products, arithmetic and copies ran while one was open for 17% -> 24% of each run, Pallas kernels for 0% -> 16%
where the time goes in v1:
time: 1410 us; the launch traced here: 1400 us
  matrix products  454 us (32%)
  Pallas kernels  450 us (32%)
  waiting for transfers between devices  209 us (15%)
  local copies, waits for them, and re-layouts  139 us (10%)
  other arithmetic  111 us (8%)
  blocking collectives  21.5 us (2%)
  between operations  16.8 us (1%)
    pallas_call x4, Pallas kernels, tensor_sum(): pl.pallas_call(functools.partial(line_sum_kernel, SUM_CHUNKS), out_shape=...  450 us
    all_gather x9, waiting for transfers between devices, gathered(): return lax.all_gather(weight, 'dp', axis=0, tiled=True)  205 us
    dot_general x4, matrix products, body(): jnp.einsum('exft,rexf->tr', grad_gate_up, up_rows, preferred_element_type...  77.1 us
    dot_general x4, matrix products, body(): jnp.einsum('rexf,tr->exft', up_rows, normed_two, preferred_element_type=j...  72.3 us
    unnamed x259, local copies, waits for them, and re-layouts  56.1 us
    dot_general x9, matrix products, contract_last(): lax.dot_general(left_side, right_side, (((1,), (1,)), ((), ())), preferre...  54.5 us
    dot_general x4, matrix products, body(): jnp.einsum('eft,ref->tr', to_low(gate_rows * act), down_rows[:, some], pr...  53.1 us
    another operation x2, other arithmetic, body(): jnp.stack([grad_act * up_half * squashed * (1.0 + gate_half * (1.0 - squa...  53 us
  transfers between devices with their start and end apart: 10, of which 4 were waited for; matrix products, arithmetic and copies ran while one was open for 24% of the time, Pallas kernels for 16%

profile of v1, /device:TPU:0, one launch (start us, length us, event | category | flops | bytes accessed | tf_op | source)
XLA Modules:
  0.0 1402.2 jit_solution(12808058560459981030)
XLA Ops:
  13.9 5.3 fusion.254
  23.0 10.8 all_gather.38
  39.0 3.3 fusion.11
  47.7 12.5 all-gather.13.cloned.1.call-done
  60.1 10.2 fusion.71
  80.7 3.8 slice_negate_fusion.2
  99.7 6.5 convolution_convert_fusion
  106.2 7.9 concatenate.65.part_ref
  116.7 114.8 %shard_map.303 = bf16[1024,2176]{1,0:T(8,128)(2,1)S(1)} custom-call(bf16[1024,2176]{1,0:T(8,128)(2,1)S(1)} %copy-done.6), custom_call_target="tpu_custom_call" | custom-call | bytes 314572800 | tf_op jit(solution)/shard_map/pallas_call | solution.py:171
  231.6 3.1 multiply_reduce_fusion.3
  246.5 3.5 fusion.210
  251.3 3.4 fusion.149
  256.8 12.4 fusion.247
  269.2 17.9 %fusion.69 = f32[1024,2,1408]{2,0,1:T(8,128)S(1)} fusion(bf16[2048,2,1408]{2,0,1:T(8,128)(2,1)} %all-gather.17.cloned.1.call-done, bf16[1024,2048]{1,0:T(8,128)(2,1)} %copy-done.11), kind=kOutput, calls=%fused_computation.156 | convolution fusion | flops 11811160064 | bytes 27262976 | tf_op jit(solution)/shard_map/tr,rxf->txf/dot_general | solution.py:345
  288.8 10.3 multiply_bitcast_fusion
  304.2 5.9 fusion.145
  314.6 7.1 fusion.139
  321.8 8.9 fusion.265
  330.7 18.1 %fusion.80 = f32[4,2,352,1024]{3,2,0,1:T(8,128)} fusion(bf16[2048,4,2,352]{0,3,2,1:T(8,128)(2,1)} %all-gather.25.cloned.1.call-done, bf16[1024,2048]{1,0:T(8,128)(2,1)} %copy-done.11), kind=kOutput, calls=%fused_computation.165 | convolution fusion | flops 11811160064 | bytes 27262976 | tf_op jit(solution)/shard_map/rexf,tr->exft/dot_general | solution.py:376
  348.7 18.3 %fusion.85 = f32[4,2,352,1024]{3,2,0,1:T(8,128)} fusion(bf16[2048,4,2,352]{0,3,2,1:T(8,128)(2,1)} %all-gather.27.cloned.1.call-done, bf16[1024,2048]{1,0:T(8,128)(2,1)} %copy-done.11), kind=kOutput, calls=%fused_computation.166 | convolution fusion | flops 11811160064 | bytes 27262976 | tf_op jit(solution)/shard_map/rexf,tr->exft/dot_general | solution.py:376
  367.0 53.3 %all-gather.29.cloned.1.call-done = bf16[2048,4,2,352]{0,3,2,1:T(8,128)(2,1)} async-done(((bf16[256,4,2,352]{0,3,2,1:T(8,128)(2,1)}), bf16[2048,4,2,352]{0,3,2,1:T(8,128)(2,1)}) %all-gather.29.cloned.1.call-update) | async-done | bytes 11534352 | tf_op jit(solution)/shard_map/all_gather | solution.py:200
  420.4 18.0 %fusion.90 = f32[4,2,352,1024]{3,2,0,1:T(8,128)} fusion(bf16[2048,4,2,352]{0,3,2,1:T(8,128)(2,1)} %all-gather.29.cloned.1.call-done, bf16[1024,2048]{1,0:T(8,128)(2,1)} %copy-done.11), kind=kOutput, calls=%fused_computation.167 | convolution fusion | flops 11811160064 | bytes 27262976 | tf_op jit(solution)/shard_map/rexf,tr->exft/dot_general | solution.py:376
  438.4 53.8 %all-gather.21.cloned.1.call-done = bf16[2048,4,2,352]{0,3,2,1:T(8,128)(2,1)} async-done(((bf16[256,4,2,352]{0,3,2,1:T(8,128)(2,1)}), bf16[2048,4,2,352]{0,3,2,1:T(8,128)(2,1)}) %all-gather.21.cloned.1.call-update) | async-done | bytes 11534352 | tf_op jit(solution)/shard_map/all_gather | solution.py:200
  492.2 18.0 %fusion.77 = f32[4,2,352,1024]{3,2,1,0:T(8,128)} fusion(bf16[2048,4,2,352]{0,3,2,1:T(8,128)(2,1)} %all-gather.21.cloned.1.call-done, bf16[1024,2048]{1,0:T(8,128)(2,1)} %copy-done.11), kind=kOutput, calls=%fused_computation.164 | convolution fusion | flops 11811160064 | bytes 27262976 | tf_op jit(solution)/shard_map/rexf,tr->exft/dot_general | solution.py:376
  510.2 20.0 %fusion.252 = f32[1024,2048,1]{1,0,2:T(8,128)} fusion(bf16[2048,2,1408]{2,0,1:T(8,128)(2,1)} %all-gather.17.cloned.1.call-done, f32[1024,1,1408]{2,0,1:T(8,128)} %copy-done.42, f32[1024,1,1408]{2,0,1:T(8,128)} %copy-done.41), kind=kOutput, calls=%fused_computation.385 | convolution fusion | flops 11816927232 | bytes 31457280 | tf_op jit(solution)/shard_map/txf,rxf->tr/dot_general | solution.py:364
  530.1 84.9 %all-gather.23.cloned.1.call-done = bf16[2048,16,352]{0,2,1:T(8,128)(2,1)} async-done(((bf16[256,16,352]{0,2,1:T(8,128)(2,1)}), bf16[2048,16,352]{0,2,1:T(8,128)(2,1)}) %all-gather.23.cloned.1.call-update) | async-done | bytes 23068688 | tf_op jit(solution)/shard_map/all_gather | solution.py:200
  615.1 31.1 %fusion.64 = f32[16,352,1024]{2,1,0:T(8,128)} fusion(bf16[2048,16,352]{0,2,1:T(8,128)(2,1)} %all-gather.23.cloned.1.call-done, bf16[1024,2048]{1,0:T(8,128)(2,1)} %param.27), kind=kOutput, calls=%fused_computation.151 | convolution fusion | flops 23622320128 | bytes 50331648 | tf_op jit(solution)/shard_map/ref,tr->eft/dot_general | solution.py:368
  646.2 27.4 %fusion.109 = (bf16[4,1,352,1024]{3,2,0,1:T(8,128)(2,1)}, bf16[4,1,352,1024]{3,2,0,1:T(8,128)(2,1)}, bf16[4,1024]{1,0:T(4,128)(2,1)S(1)}, bf16[4,352,1024]{2,1,0...) fusion(f32[4,2,352,1024]{3,2,1,0:T(8,128)} %fusion.77, ...), kind=kLoop, calls=%fused_computation.179 | loop fusion | flops 67747840 | bytes 86556672 | tf_op jit(solution)/shard_map/stack | solution.py:387
  673.7 25.6 %fusion.110 = (bf16[4,1,352,1024]{3,2,0,1:T(8,128)(2,1)}, bf16[4,1,352,1024]{3,2,0,1:T(8,128)(2,1)}, bf16[4,1,352,1024]{3,2,0,1:T(8,128)(2,1)}, bf16[4,1,352,102...) fusion(f32[4,2,352,1024]{3,2,0,1:T(8,128)} %fusion.80, ...), kind=kLoop, calls=%fused_computation.180 | loop fusion | flops 60555264 | bytes 69255168 | tf_op jit(solution)/shard_map/stack | solution.py:387
  699.2 10.8 fusion.36
  710.0 10.8 fusion.38
  720.8 10.9 fusion.40
  731.7 20.6 %fusion.20 = bf16[1024,2048]{1,0:T(8,128)(2,1)} fusion(f32[1024,2048,1]{1,0,2:T(8,128)} %fusion.36, f32[1024,2048,1]{1,0,2:T(8,128)} %fusion.38, f32[1024,2048,1]{1,0,2:T(8,128)} %fusion.40, f32[1024,2048]{1,0:T(8,128)} %fusion.265, f32[1024]{0:T(1024)S(1)} %copy-done.99, bf16[2048,16,352]{0,2,1:T(8,128)(2,1)} %all-gather.23.cloned.1.call-done, ...), kind=kOutput, calls=%fused_computation.41 | convolution fusion | flops 5922488320 | bytes 46419968 | tf_op jit(solution)/shard_map/eft,ref->tr/dot_general | solution.py:395
  752.3 7.8 concatenate.67.part_ref
  762.3 114.2 %shard_map.304 = bf16[1024,2176]{1,0:T(8,128)(2,1)S(1)} custom-call(bf16[1024,2176]{1,0:T(8,128)(2,1)S(1)} %copy-done.7), custom_call_target="tpu_custom_call" | custom-call | bytes 314572800 | tf_op jit(solution)/shard_map/pallas_call | solution.py:171
  876.6 8.2 fusion.10
  886.1 18.9 %fusion.50 = f32[1024,2048,1,1]{1,0,3,2:T(8,128)} fusion(bf16[2048,4,2,352]{0,3,2,1:T(8,128)(2,1)} %all-gather.27.cloned.1.call-done, bf16[4,1,352,1024]{3,2,0,1:T(8,128)(2,1)} %get-tuple-element.102, bf16[4,1,352,1024]{3,2,0,1:T(8,128)(2,1)} %get-tuple-element.103), kind=kOutput, calls=%fused_computation.118 | convolution fusion | flops 11814043648 | bytes 25690112 | tf_op jit(solution)/shard_map/exft,rexf->tr/dot_general | solution.py:401
  905.0 17.8 %fusion.48 = f32[1024,2048,1,1]{1,0,3,2:T(8,128)} fusion(bf16[2048,4,2,352]{0,3,2,1:T(8,128)(2,1)} %all-gather.29.cloned.1.call-done, bf16[4,1,352,1024]{3,2,0,1:T(8,128)(2,1)S(1)} %copy-done.60, bf16[4,1,352,1024]{3,2,0,1:T(8,128)(2,1)S(1)} %copy-done.61), kind=kOutput, calls=%fused_computation.116 | convolution fusion | flops 11814043648 | bytes 25690112 | tf_op jit(solution)/shard_map/exft,rexf->tr/dot_general | solution.py:401
  922.9 17.6 %fusion.52 = f32[1024,2048,1,1]{1,0,3,2:T(8,128)} fusion(bf16[2048,4,2,352]{0,3,2,1:T(8,128)(2,1)} %all-gather.25.cloned.1.call-done, bf16[4,1,352,1024]{3,2,0,1:T(8,128)(2,1)S(1)} %copy-done.59, bf16[4,1,352,1024]{3,2,0,1:T(8,128)(2,1)S(1)} %copy-done.58), kind=kOutput, calls=%fused_computation.120 | convolution fusion | flops 11814043648 | bytes 25690112 | tf_op jit(solution)/shard_map/exft,rexf->tr/dot_general | solution.py:401
  940.5 22.8 %fusion.19 = bf16[1024,2048]{1,0:T(8,128)(2,1)} fusion(f32[1024,2048,1,1]{1,0,3,2:T(8,128)} %fusion.48, f32[1024,2048,1,1]{1,0,3,2:T(8,128)} %fusion.50, f32[1024,2048,1,1]{1,0,3,2:T(8,128)} %fusion.52, f32[1024,2048,1]{1,0,2:T(8,128)} %fusion.252, bf16[2048,4,2,352]{0,3,2,1:T(8,128)(2,1)} %all-gather.21.cloned.1.call-done, ...), kind=kOutput, calls=%fused_computation.35 | convolution fusion | flops 11824529408 | bytes 55050240 | tf_op jit(solution)/shard_map/exft,rexf->tr/dot_general | solution.py:401
  963.3 7.8 concatenate.69.part_ref
  973.4 112.4 %shard_map.305 = bf16[1024,2176]{1,0:T(8,128)(2,1)S(1)} custom-call(bf16[1024,2176]{1,0:T(8,128)(2,1)S(1)} %copy-done.4), custom_call_target="tpu_custom_call" | custom-call | bytes 314572800 | tf_op jit(solution)/shard_map/pallas_call | solution.py:171
  1088.3 5.1 fusion.162
  1094.3 12.3 multiply_reduce_fusion.2
  1106.8 14.8 %convert_add_fusion.1 = (f32[1024,2048]{1,0:T(8,128)}, bf16[1024,2048]{1,0:T(8,128)(2,1)}) fusion(bf16[1024,2048]{1,0:T(8,128)(2,1)S(1)} %copy-done.19, f32[1024,2048]{1,0:T(8,128)} %copy-done.14, f32[1024,2048]{1,0:T(8,128)} %get-tuple-element.154, f32[1024]{0:T(1024)S(1)} %multiply_multiply_fusion.1, f32[1024]{0:T(1024)S(1)} %copy-done.91, ...), kind=kLoop, calls=%fused_computation.5 | loop fusion | flops 23068672 | bytes 46149632 | tf_op jit(solution)/shard_map/add | solution.py:427
  1121.6 4.3 fusion.142
  1139.7 3.6 fusion.129
  1143.3 3.0 fusion.159
  1148.5 5.0 multiply_reduce_fusion
  1156.0 6.1 fusion.125
  1162.2 4.6 multiply_convert_fusion
  1182.8 12.5 bitcast_convert_fusion
  1197.1 7.7 concatenate.71.part_ref
  1207.1 108.9 %shard_map.306 = bf16[1024,2176]{1,0:T(8,128)(2,1)S(1)} custom-call(bf16[1024,2176]{1,0:T(8,128)(2,1)S(1)} %copy-done.5), custom_call_target="tpu_custom_call" | custom-call | bytes 314572800 | tf_op jit(solution)/shard_map/pallas_call | solution.py:171
  1319.3 3.4 convolution_convert_fusion.3
  1323.3 10.6 all-gather
  1336.2 6.1 reshape.351
  1342.3 6.1 copy.331
  1348.4 5.8 fusion.15
  1354.5 6.6 fusion.7
  1373.5 4.4 reshape.363
  1377.9 5.1 copy.337
  1383.0 6.1 reshape.361
  1389.1 6.0 copy.335
  (409 shorter events, 140.4 us)
Async XLA Ops:
  7.2 35.6 %copy-start = (bf16[8,16,2,1408]{3,2,1,0:T(2,128)(2,1)S(1)}, bf16[8,16,2,1408]{3,2,1,0:T(2,128)(2,1)}, u32[]{:S(2)}) copy-start(bf16[8,16,2,1408]{3,2,1,0:T(2,128)(2,1)} %param.47) | copy-start | bytes 2162692
  7.2 52.9 %all-gather.13.cloned.1.call-start = ((), (), s32[]{:S(2)}) async-start(), calls=%async_computation | async-start | bytes 7077888 | tf_op jit(solution)/shard_map/all_gather | solution.py:200
  9.6 90.1 %all-gather.15.cloned.1.call-start = ((), (), s32[]{:S(2)}) async-start(), calls=%async_computation.1 | async-start | bytes 2359296 | tf_op jit(solution)/shard_map/all_gather | solution.py:200
  10.4 246.4 %all-gather.19.cloned.1.call-start = ((), (), s32[]{:S(2)}) async-start(), calls=%async_computation.3 | async-start | bytes 6488064 | tf_op jit(solution)/shard_map/all_gather | solution.py:200
  11.1 258.1 %all-gather.17.cloned.1.call-start = ((), (), s32[]{:S(2)}) async-start(), calls=%async_computation.2 | async-start | bytes 12976128 | tf_op jit(solution)/shard_map/all_gather | solution.py:200
  13.8 316.8 %all-gather.25.cloned.1.call-start = ((), (), s32[]{:S(2)}) async-start(), calls=%async_computation.6 | async-start | bytes 12976128 | tf_op jit(solution)/shard_map/all_gather | solution.py:200
  19.2 14.8 %copy-start.104 = (bf16[2048]{0:T(1024)(128)(2,1)S(1)}, bf16[2048]{0:T(1024)(128)(2,1)}, u32[]{:S(2)}) copy-start(bf16[2048]{0:T(1024)(128)(2,1)} %param.28) | copy-start | bytes 12292
  19.2 14.8 %copy-start.105 = (bf16[2048]{0:T(1024)(128)(2,1)S(1)}, bf16[2048]{0:T(1024)(128)(2,1)}, u32[]{:S(2)}) copy-start(bf16[2048]{0:T(1024)(128)(2,1)} %param.32) | copy-start | bytes 12292
  19.2 14.8 %copy-start.106 = (bf16[3,512]{1,0:T(4,128)(2,1)S(1)}, bf16[3,512]{1,0:T(4,128)(2,1)}, u32[]{:S(2)}) copy-start(bf16[3,512]{1,0:T(4,128)(2,1)} %param.30) | copy-start | bytes 9220
  19.2 14.8 %copy-start.100 = (s32[1024,4]{0,1:T(4,128)S(1)}, s32[1024,4]{0,1:T(4,128)}, u32[]{:S(2)}) copy-start(s32[1024,4]{0,1:T(4,128)} %param.39) | copy-start | bytes 49156
  19.2 15.7 %copy-start.108 = (s32[1,2]{1,0:T(1,128)S(1)}, s32[1,2]{1,0:T(1,128)}, u32[]{:S(2)}) copy-start(s32[1,2]{1,0:T(1,128)} %param.41) | copy-start | bytes 28
  19.3 329.5 %all-gather.27.cloned.1.call-start = ((), (), s32[]{:S(2)}) async-start(), calls=%async_computation.7 | async-start | bytes 12976128 | tf_op jit(solution)/shard_map/all_gather | solution.py:200
  19.9 400.5 %all-gather.29.cloned.1.call-start = ((), (), s32[]{:S(2)}) async-start(), calls=%async_computation.8 | async-start | bytes 12976128 | tf_op jit(solution)/shard_map/all_gather | solution.py:200
  20.6 471.5 %all-gather.21.cloned.1.call-start = ((), (), s32[]{:S(2)}) async-start(), calls=%async_computation.4 | async-start | bytes 12976128 | tf_op jit(solution)/shard_map/all_gather | solution.py:200
  21.4 593.7 %all-gather.23.cloned.1.call-start = ((), (), s32[]{:S(2)}) async-start(), calls=%async_computation.5 | async-start | bytes 25952256 | tf_op jit(solution)/shard_map/all_gather | solution.py:200
  22.1 1339.0 %all-gather.31.cloned.1.call-start = ((), (), s32[]{:S(2)}) async-start(), calls=%async_computation.9 | async-start | bytes 3133440 | tf_op jit(solution)/shard_map/all_gather | solution.py:505
  33.8 212.7 %copy-start.66 = (bf16[2048,18]{0,1:T(8,128)(2,1)}, bf16[2048,18]{0,1:T(8,128)(2,1)S(1)}, u32[]{:S(2)}) copy-start(bf16[2048,18]{0,1:T(8,128)(2,1)S(1)} %all_gather.38) | copy-start | bytes 221188
  34.0 26.1 %copy-start.82 = (f32[2048]{0:T(1024)}, f32[2048]{0:T(1024)S(1)}, u32[]{:S(2)}) copy-start(f32[2048]{0:T(1024)S(1)} %convert_element_type.226) | copy-start | bytes 24580
  34.0 200.7 %copy-start.80 = (f32[2048]{0:T(1024)}, f32[2048]{0:T(1024)S(1)}, u32[]{:S(2)}) copy-start(f32[2048]{0:T(1024)S(1)} %convert_element_type.238) | copy-start | bytes 24580
  34.9 207.6 %copy-start.29 = (f32[1024,16]{1,0:T(8,128)}, f32[1024,16]{1,0:T(8,128)S(1)}, u32[]{:S(2)}) copy-start(f32[1024,16]{1,0:T(8,128)S(1)} %copy.286) | copy-start | bytes 196612
  34.9 10.6 copy-start.20
  42.8 17.4 %copy-start.96 = (f32[1024]{0:T(1024)}, f32[1024]{0:T(1024)S(1)}, u32[]{:S(2)}) copy-start(f32[1024]{0:T(1024)S(1)} %fusion.216) | copy-start | bytes 12292
  47.7 22.7 %copy-start.76 = (bf16[1024,16,1]{0,1,2:T(8,128)(2,1)}, bf16[1024,16,1]{0,1,2:T(8,128)(2,1)S(1)}, u32[]{:S(2)}) copy-start(bf16[1024,16,1]{0,1,2:T(8,128)(2,1)S(1)} %fusion.148) | copy-start | bytes 98308
  106.2 125.4 %copy-start.48 = (bf16[1024,112]{1,0:T(8,128)(2,1)}, bf16[1024,112]{1,0:T(8,128)(2,1)S(1)}, u32[]{:S(2)}) copy-start(bf16[1024,112]{1,0:T(8,128)(2,1)S(1)} %broadcast.288) | copy-start | bytes 688132
  116.7 114.9 %copy-start.21 = (bf16[1024,2048]{1,0:T(8,128)(2,1)S(1)}, bf16[1024,2048]{1,0:T(8,128)(2,1)}, u32[]{:S(2)}) copy-start(bf16[1024,2048]{1,0:T(8,128)(2,1)} %param.26) | copy-start | bytes 12582916
  241.9 8.1 copy-start.70
  242.1 7.9 copy-start.25
  246.5 8.2 copy-start.17
  288.8 10.4 copy-start.31
  310.9 10.8 slice-start.9
  530.1 116.0 %copy-start.87 = (f32[4,1024]{1,0:T(4,128)S(1)}, f32[4,1024]{1,0:T(4,128)}, u32[]{:S(2)}) copy-start(f32[4,1024]{1,0:T(4,128)} %copy.287) | copy-start | bytes 49156
  646.2 27.5 %copy-start.84 = (f32[4,1024]{1,0:T(4,128)S(1)}, f32[4,1024]{1,0:T(4,128)}, u32[]{:S(2)}) copy-start(f32[4,1024]{1,0:T(4,128)} %copy.291) | copy-start | bytes 49156
  646.2 27.5 %copy-start.85 = (f32[4,1024]{1,0:T(4,128)S(1)}, f32[4,1024]{1,0:T(4,128)}, u32[]{:S(2)}) copy-start(f32[4,1024]{1,0:T(4,128)} %copy.289) | copy-start | bytes 49156
  646.2 27.5 %copy-start.86 = (f32[4,1024]{1,0:T(4,128)S(1)}, f32[4,1024]{1,0:T(4,128)}, u32[]{:S(2)}) copy-start(f32[4,1024]{1,0:T(4,128)} %copy.293) | copy-start | bytes 49156
  720.8 10.9 copy-start.99
  731.7 20.6 %copy-start.49 = (bf16[1024,112]{1,0:T(8,128)(2,1)S(1)}, bf16[1024,112]{1,0:T(8,128)(2,1)}, u32[]{:S(2)}) copy-start(bf16[1024,112]{1,0:T(8,128)(2,1)} %copy-done.48) | copy-start | bytes 688132
  731.7 20.6 %copy-start.65 = (bf16[1024,16]{1,0:T(8,128)(2,1)S(1)}, bf16[1024,16]{1,0:T(8,128)(2,1)}, u32[]{:S(2)}) copy-start(bf16[1024,16]{1,0:T(8,128)(2,1)} %copy.295) | copy-start | bytes 98308
  762.3 114.2 %copy-start.18 = (bf16[1024,2048]{1,0:T(8,128)(2,1)S(1)}, bf16[1024,2048]{1,0:T(8,128)(2,1)}, u32[]{:S(2)}) copy-start(bf16[1024,2048]{1,0:T(8,128)(2,1)} %param.27) | copy-start | bytes 12582916
  876.6 8.2 copy-start.2
  886.1 19.0 %copy-start.60 = (bf16[4,1,352,1024]{3,2,0,1:T(8,128)(2,1)S(1)}, bf16[4,1,352,1024]{3,2,0,1:T(8,128)(2,1)}, u32[]{:S(2)}) copy-start(bf16[4,1,352,1024]{3,2,0,1:T(8,128)(2,1)} %get-tuple-element.100) | copy-start | bytes 8650756
  886.1 19.0 %copy-start.61 = (bf16[4,1,352,1024]{3,2,0,1:T(8,128)(2,1)S(1)}, bf16[4,1,352,1024]{3,2,0,1:T(8,128)(2,1)}, u32[]{:S(2)}) copy-start(bf16[4,1,352,1024]{3,2,0,1:T(8,128)(2,1)} %get-tuple-element.101) | copy-start | bytes 8650756
  905.0 17.8 %copy-start.58 = (bf16[4,1,352,1024]{3,2,0,1:T(8,128)(2,1)S(1)}, bf16[4,1,352,1024]{3,2,0,1:T(8,128)(2,1)}, u32[]{:S(2)}) copy-start(bf16[4,1,352,1024]{3,2,0,1:T(8,128)(2,1)} %get-tuple-element.86) | copy-start | bytes 8650756
  905.0 17.8 %copy-start.59 = (bf16[4,1,352,1024]{3,2,0,1:T(8,128)(2,1)S(1)}, bf16[4,1,352,1024]{3,2,0,1:T(8,128)(2,1)}, u32[]{:S(2)}) copy-start(bf16[4,1,352,1024]{3,2,0,1:T(8,128)(2,1)} %get-tuple-element.87) | copy-start | bytes 8650756
  922.8 17.6 %copy-start.56 = (bf16[4,1,352,1024]{3,2,0,1:T(8,128)(2,1)S(1)}, bf16[4,1,352,1024]{3,2,0,1:T(8,128)(2,1)}, u32[]{:S(2)}) copy-start(bf16[4,1,352,1024]{3,2,0,1:T(8,128)(2,1)} %get-tuple-element.84) | copy-start | bytes 8650756
  922.8 17.6 %copy-start.57 = (bf16[4,1,352,1024]{3,2,0,1:T(8,128)(2,1)S(1)}, bf16[4,1,352,1024]{3,2,0,1:T(8,128)(2,1)}, u32[]{:S(2)}) copy-start(bf16[4,1,352,1024]{3,2,0,1:T(8,128)(2,1)} %get-tuple-element.85) | copy-start | bytes 8650756
  940.5 22.8 %copy-start.72 = (bf16[1024,16]{1,0:T(8,128)(2,1)S(1)}, bf16[1024,16]{1,0:T(8,128)(2,1)}, u32[]{:S(2)}) copy-start(bf16[1024,16]{1,0:T(8,128)(2,1)} %fusion.139) | copy-start | bytes 98308
  973.4 112.4 %copy-start.12 = (bf16[1024,2048]{1,0:T(8,128)(2,1)S(1)}, bf16[1024,2048]{1,0:T(8,128)(2,1)}, u32[]{:S(2)}) copy-start(bf16[1024,2048]{1,0:T(8,128)(2,1)} %copy-done.11) | copy-start | bytes 12582916
  1088.3 18.4 %slice-start = ((s8[4456448]{0:T(1024)(128)(4,1)}), s8[4194304]{0:T(1024)(128)(4,1)S(1)}, s32[]{:S(2)}) async-start(s8[4456448]{0:T(1024)(128)(4,1)} %bitcast.393), calls=%async_computation.10 | async-start | bytes 8388608
  1094.3 12.4 copy-start.102
  1094.3 12.4 slice-start.1
  1094.3 12.4 copy-start.19
  1094.3 12.4 copy-start.91
  1135.3 11.0 slice-start.4
  1137.9 8.4 slice-start.5
  1182.7 12.5 copy-start.27
  1182.7 14.3 %copy-start.50 = (bf16[1024,112]{1,0:T(8,128)(2,1)S(1)}, bf16[1024,112]{1,0:T(8,128)(2,1)}, u32[]{:S(2)}) copy-start(bf16[1024,112]{1,0:T(8,128)(2,1)} %copy-done.48) | copy-start | bytes 688132
  1207.1 111.1 %copy-start.28 = (bf16[1024,3,512]{0,2,1:T(8,128)(2,1)S(1)}, bf16[1024,3,512]{0,2,1:T(8,128)(2,1)}, u32[]{:S(2)}) copy-start(bf16[1024,3,512]{0,2,1:T(8,128)(2,1)} %copy-done.27) | copy-start | bytes 9437188
  1207.1 111.1 %copy-start.77 = (bf16[1024,16,1]{0,1,2:T(8,128)(2,1)S(1)}, bf16[1024,16,1]{0,1,2:T(8,128)(2,1)}, u32[]{:S(2)}) copy-start(bf16[1024,16,1]{0,1,2:T(8,128)(2,1)} %copy-done.76) | copy-start | bytes 98308
  1207.1 112.1 %copy-start.83 = (f32[2048]{0:T(1024)S(1)}, f32[2048]{0:T(1024)}, u32[]{:S(2)}) copy-start(f32[2048]{0:T(1024)} %copy-done.82) | copy-start | bytes 24580
  1207.1 112.1 %copy-start.97 = (f32[1024]{0:T(1024)S(1)}, f32[1024]{0:T(1024)}, u32[]{:S(2)}) copy-start(f32[1024]{0:T(1024)} %copy-done.96) | copy-start | bytes 12292
  1319.2 15.0 %copy-start.107 = (s32[8]{0:T(128)S(1)}, s32[8]{0:T(128)}, u32[]{:S(2)}) copy-start(s32[8]{0:T(128)} %bitcast_convert_fusion.1) | copy-start | bytes 100
  1342.3 12.0 slice-start.2
  1373.5 9.5 copy-start.54
  1383.0 12.1 copy-start.1
  (68 other events, 265.8 us)
Sparse Core Ops, SparseCore 0:
  10.5 49.6 all-gather.12
  62.0 27.8 all-gather.14
  91.8 43.3 all-gather.18
  137.0 67.6 all-gather.16
  206.4 69.8 all-gather.24
  278.1 69.8 all-gather.26
  350.4 69.8 all-gather.28
  422.2 69.8 all-gather.20
  494.0 120.9 all-gather.22
  1156.1 29.8 all-gather.30

commit v2 on v1

--- a/solution.py
+++ b/solution.py
@@ -20,7 +20,9 @@
 MASKED = -1e30
 MESH = pl.DeviceIdType.MESH
 SUM_CHUNKS = 16
-EXPERT_PARTS = 4
+AHEAD = 2
+PAIR = 2
+EXPERT_PARTS = (8, 4, 4)
 
 
 def matmul(left_side, right_side):
@@ -81,26 +83,13 @@
     return causal | together
 
 
-def line_sum_kernel(
-    chunks, part_ref, total_ref, from_end, pair_sum, from_pair, semaphores
-):
+def line_sum_steps(chunks, part_ref, total_ref, from_end, pair_sum, from_pair, semaphores):
     place = lax.axis_index("tensor")
     rows = part_ref.shape[0] // chunks
     inner = (place == 1) | (place == 2)
     end = (place == 0) | (place == 3)
     mate = jnp.where(place < 2, 1 - place, 5 - place)
     other = jnp.where(inner, 3 - place, place)
-    barrier = pltpu.get_barrier_semaphore()
-    pl.semaphore_signal(barrier, inc=1, device_id={"tensor": mate}, device_id_type=MESH)
-
-    @pl.when(inner)
-    def _():
-        pl.semaphore_signal(barrier, inc=1, device_id={"tensor": other}, device_id_type=MESH)
-        pl.semaphore_wait(barrier, 2)
-
-    @pl.when(end)
-    def _():
-        pl.semaphore_wait(barrier, 1)
 
     def span(chunk):
         return pl.ds(pl.multiple_of(chunk * rows, rows), rows)
@@ -129,44 +118,203 @@
             left_ref[span(chunk)].astype(jnp.float32) + right_ref[span(chunk)].astype(jnp.float32)
         )
 
-    @pl.when(end)
-    def _():
-        @pl.loop(0, chunks)
-        def _(chunk):
-            inward(chunk).start()
-
-        @pl.loop(0, chunks)
-        def _(chunk):
-            inward(chunk).wait_send()
-
-        @pl.loop(0, chunks)
-        def _(chunk):
-            outward(chunk).wait_recv()
-
-    @pl.when(inner)
-    def _():
-        @pl.loop(0, chunks + 1)
-        def _(step):
-            @pl.when(step < chunks)
-            def _():
-                inward(step).wait_recv()
-                add(part_ref, from_end, pair_sum, step)
-                across(step).start()
-
-            @pl.when(step > 0)
-            def _():
-                across(step - 1).wait_recv()
-                add(pair_sum, from_pair, total_ref, step - 1)
-                outward(step - 1).start()
-
-        @pl.loop(0, chunks)
-        def _(chunk):
-            across(chunk).wait_send()
-            outward(chunk).wait_send()
+    def greet(extra):
+        barrier = pltpu.get_barrier_semaphore()
+        pl.semaphore_signal(barrier, inc=1, device_id={"tensor": mate}, device_id_type=MESH)
+
+        @pl.when(inner)
+        def _():
+            pl.semaphore_signal(barrier, inc=1, device_id={"tensor": other}, device_id_type=MESH)
+            pl.semaphore_wait(barrier, 2 + extra)
+
+        @pl.when(end)
+        def _():
+            pl.semaphore_wait(barrier, 1 + extra)
+
+    def begin():
+        @pl.when(end)
+        def _():
+            @pl.loop(0, chunks)
+            def _(chunk):
+                inward(chunk).start()
+
+    def advance(step):
+        @pl.when(inner & (step < chunks))
+        def _():
+            inward(step).wait_recv()
+            add(part_ref, from_end, pair_sum, step)
+            across(step).start()
+
+        @pl.when(inner & (step > 0) & (step <= chunks))
+        def _():
+            across(step - 1).wait_recv()
+            add(pair_sum, from_pair, total_ref, step - 1)
+            outward(step - 1).start()
+
+    def finish():
+        @pl.when(end)
+        def _():
+            @pl.loop(0, chunks)
+            def _(chunk):
+                inward(chunk).wait_send()
+                outward(chunk).wait_recv()
+
+        @pl.when(inner)
+        def _():
+            @pl.loop(0, chunks)
+            def _(chunk):
+                across(chunk).wait_send()
+                outward(chunk).wait_send()
+
+    return greet, begin, advance, finish
+
+
+def plane_gather_steps(pieces, block_ref, whole_ref, semaphores, local_semaphore):
+    spot = lax.axis_index("dp")
+    depth = block_ref.shape[1]
+    rows = block_ref.shape[0] // pieces
+    core_mate = spot + 1 - 2 * (spot % 2)
+    x_mate = spot + 2 - 4 * ((spot // 2) % 2)
+    y_mate = spot + 4 - 8 * (spot // 4)
+    x_y_mate = x_mate + 4 - 8 * (spot // 4)
+    lanes = {
+        "core": (spot, core_mate, 0, 1),
+        "x": (spot, x_mate, 0, 1),
+        "y": (spot, y_mate, 0, 1),
+        "x_core": (x_mate, core_mate, 0, 1),
+        "x_y": (x_mate, y_mate, 0, 2),
+        "y_core": (y_mate, core_mate, 0, 1),
+        "y_x": (y_mate, x_mate, 1, 2),
+        "xy_core": (x_y_mate, core_mate, 0, 2),
+        "yx_core": (x_y_mate, core_mate, 1, 2),
+    }
+    order = list(lanes)
+
+    def send(name, piece):
+        owner, device, part, parts = lanes[name]
+        lane = order.index(name)
+        span = pl.ds(
+            pl.multiple_of(piece * rows + part * (rows // parts), rows // parts), rows // parts
+        )
+        columns = pl.ds(pl.multiple_of(owner * depth, depth), depth)
+        target = whole_ref.at[span, columns]
+        source = block_ref.at[span] if name in ("core", "x", "y") else target
+        return pltpu.make_async_remote_copy(
+            source,
+            target,
+            semaphores.at[2 * lane, piece],
+            semaphores.at[2 * lane + 1, piece],
+            device_id={"dp": device},
+            device_id_type=MESH,
+        )
+
+    def own():
+        columns = pl.ds(pl.multiple_of(spot * depth, depth), depth)
+        return pltpu.make_async_copy(block_ref, whole_ref.at[:, columns], local_semaphore)
+
+    def greet():
+        barrier = pltpu.get_barrier_semaphore()
+        for device in (core_mate, x_mate, y_mate):
+            pl.semaphore_signal(barrier, inc=1, device_id={"dp": device}, device_id_type=MESH)
+
+    def begin():
+        own().start()
+
+    def advance(step):
+        @pl.when(step < pieces)
+        def _():
+            for name in ("x", "y", "core"):
+                send(name, step).start()
+
+        @pl.when((step >= AHEAD) & (step < pieces + AHEAD))
+        def _():
+            piece = step - AHEAD
+            send("x", piece).wait_recv()
+            send("x_y", piece).start()
+            send("x_core", piece).start()
+            send("y", piece).wait_recv()
+            send("y_x", piece).start()
+            send("y_core", piece).start()
+
+        @pl.when((step >= 2 * AHEAD) & (step < pieces + 2 * AHEAD))
+        def _():
+            piece = step - 2 * AHEAD
+            send("x_y", piece).wait_recv()
+            send("xy_core", piece).start()
+            send("y_x", piece).wait_recv()
+            send("yx_core", piece).start()
+
+    def finish():
+        own().wait()
+
+        @pl.loop(0, pieces)
+        def _(piece):
+            for name in order:
+                send(name, piece).wait_send()
+            for name in ("core", "x_core", "y_core", "xy_core", "yx_core"):
+                send(name, piece).wait_recv()
+
+    return greet, begin, advance, finish
+
+
+def line_sum_kernel(chunks, part_ref, total_ref, from_end, pair_sum, from_pair, semaphores):
+    greet, begin, advance, finish = line_sum_steps(
+        chunks, part_ref, total_ref, from_end, pair_sum, from_pair, semaphores
+    )
+    greet(0)
+    begin()
+
+    @pl.loop(0, chunks + 1)
+    def _(step):
+        advance(step)
+
+    finish()
+
+
+def sum_gather_kernel(
+    chunks,
+    pieces,
+    part_ref,
+    block_ref,
+    total_ref,
+    whole_ref,
+    from_end,
+    pair_sum,
+    from_pair,
+    semaphores,
+    gather_semaphores,
+    local_semaphore,
+):
+    greet, begin, advance, finish = line_sum_steps(
+        chunks, part_ref, total_ref, from_end, pair_sum, from_pair, semaphores
+    )
+    gather_greet, gather_begin, gather_advance, gather_finish = plane_gather_steps(
+        pieces, block_ref, whole_ref, gather_semaphores, local_semaphore.at[0]
+    )
+    gather_greet()
+    greet(3)
+    begin()
+    gather_begin()
+
+    @pl.loop(0, max(chunks + 1, pieces + 2 * AHEAD))
+    def _(step):
+        gather_advance(step)
+        advance(step)
+
+    gather_finish()
+    finish()
+
+
+def on_line():
+    return lax.axis_size("tensor") == 4
+
+
+def in_plane():
+    return lax.axis_size("dp") == 8
 
 
 def tensor_sum(part, number):
-    if lax.axis_size("tensor") != 4:
+    if not on_line():
         return lax.psum(part.astype(jnp.float32), "tensor")
     total = pl.pallas_call(
         functools.partial(line_sum_kernel, SUM_CHUNKS),
@@ -179,17 +327,152 @@
             collective_id=number, has_side_effects=True, vmem_limit_bytes=40 * 2**20
         ),
         cost_estimate=pl.CostEstimate(flops=0, bytes_accessed=300 * 2**20, transcendentals=0),
-    )(to_low(part))
+    )(part)
     return total.astype(jnp.float32)
+
+
+def packed(wide_part, narrow_part):
+    pad = jnp.zeros((wide_part.shape[0], 128 - narrow_part.shape[1]), jnp.bfloat16)
+    return jnp.concatenate([to_low(wide_part), to_low(narrow_part), pad], axis=1)
 
 
 def summed(wide_part, narrow_part, number):
     width, small = wide_part.shape[1], narrow_part.shape[1]
-    pad = jnp.zeros((wide_part.shape[0], 128 - small), jnp.bfloat16)
-    total = tensor_sum(
-        jnp.concatenate([to_low(wide_part), to_low(narrow_part), pad], axis=1), number
-    )
+    total = tensor_sum(packed(wide_part, narrow_part), number)
     return total[:, :width], total[:, width : width + small]
+
+
+def summed_and_gathered(wide_part, narrow_part, block, number):
+    if not (on_line() and in_plane()):
+        whole = lax.all_gather(block, "dp", axis=1, tiled=True)
+        return summed(wide_part, narrow_part, number) + (whole,)
+    width, small = wide_part.shape[1], narrow_part.shape[1]
+    part = packed(wide_part, narrow_part)
+    pieces = EXPERTS
+    total, whole = pl.pallas_call(
+        functools.partial(sum_gather_kernel, SUM_CHUNKS, pieces),
+        out_shape=[
+            jax.ShapeDtypeStruct(part.shape, jnp.bfloat16),
+            jax.ShapeDtypeStruct((block.shape[0], 8 * block.shape[1]), jnp.bfloat16),
+        ],
+        in_specs=[pl.BlockSpec(memory_space=pltpu.VMEM), pl.BlockSpec(memory_space=pltpu.HBM)],
+        out_specs=[pl.BlockSpec(memory_space=pltpu.VMEM), pl.BlockSpec(memory_space=pltpu.HBM)],
+        scratch_shapes=[pltpu.VMEM(part.shape, jnp.bfloat16)] * 3
+        + [
+            pltpu.SemaphoreType.DMA((6, SUM_CHUNKS)),
+            pltpu.SemaphoreType.DMA((18, pieces)),
+            pltpu.SemaphoreType.DMA((1,)),
+        ],
+        compiler_params=pltpu.CompilerParams(
+            collective_id=number, has_side_effects=True, vmem_limit_bytes=40 * 2**20
+        ),
+        cost_estimate=pl.CostEstimate(flops=0, bytes_accessed=360 * 2**20, transcendentals=0),
+    )(part, block)
+    total = total.astype(jnp.float32)
+    return total[:, :width], total[:, width : width + small], whole
+
+
+def experts_kernel(
+    tile,
+    inputs_ref,
+    cotangent_ref,
+    gate_ref,
+    up_ref,
+    down_ref,
+    out_start,
+    grad_start,
+    out_ref,
+    grad_ref,
+    gate_grad_ref,
+    act_rows,
+    grad_rows,
+    semaphores,
+):
+    @pl.when(pl.program_id(0) == 0)
+    def _():
+        loads = [
+            pltpu.make_async_copy(out_start, out_ref, semaphores.at[0]),
+            pltpu.make_async_copy(grad_start, grad_ref, semaphores.at[1]),
+        ]
+        for load in loads:
+            load.start()
+        for load in loads:
+            load.wait()
+
+    pair = gate_ref.shape[1]
+    hidden = down_ref.shape[1] // pair
+
+    @pl.loop(0, inputs_ref.shape[1] // tile)
+    def _(index):
+        column = pl.ds(pl.multiple_of(index * tile, tile), tile)
+        inputs = inputs_ref[:, column]
+        cotangents = cotangent_ref[:, column]
+        for member in range(pair):
+            gate_from, up_from = 2 * hidden * member, 2 * hidden * member + hidden
+            gate_up = matmul(up_ref[0, gate_from : gate_from + 2 * hidden], inputs)
+            open_part = matmul(down_ref[0, hidden * member : hidden * (member + 1)], cotangents)
+            gate_half, up_half = gate_up[:hidden], gate_up[hidden:]
+            squashed = 1.0 / (1.0 + jnp.exp(-gate_half))
+            act = to_low(gate_half * squashed * up_half).astype(jnp.float32)
+            gate_row = gate_ref[0, member : member + 1, column]
+            gate_grad_ref[0, member : member + 1, column] = jnp.sum(
+                act * open_part, axis=0, keepdims=True
+            )
+            act_rows[hidden * member : hidden * (member + 1)] = to_low(gate_row * act)
+            grad_act = gate_row * open_part
+            grad_rows[gate_from : gate_from + hidden] = to_low(
+                grad_act * up_half * squashed * (1.0 + gate_half * (1.0 - squashed))
+            )
+            grad_rows[up_from : up_from + hidden] = to_low(grad_act * gate_half * squashed)
+        out_ref[column] += contract_first(act_rows[...], down_ref[0])
+        grad_ref[column] += contract_first(grad_rows[...], up_ref[0])
+
+
+def experts_step(inputs, cotangents, gates, up_rows, down_rows, out_start, grad_start, first):
+    groups, pair, length = up_rows.shape[0], gates.shape[1], inputs.shape[1]
+    width, hidden = inputs.shape[0], down_rows.shape[1] // gates.shape[1]
+    tile = min(512, length)
+    once = pl.Buffered(1)
+
+    def still(shape):
+        return pl.BlockSpec(shape, lambda group: (0, 0), pipeline_mode=once)
+
+    return pl.pallas_call(
+        functools.partial(experts_kernel, tile),
+        grid=(groups,),
+        in_specs=[
+            still((width, length)),
+            still((width, length)),
+            pl.BlockSpec((1, pair, length), lambda group: (group + first, 0, 0)),
+            pl.BlockSpec((1, 2 * pair * hidden, width), lambda group: (group, 0, 0)),
+            pl.BlockSpec((1, pair * hidden, width), lambda group: (group + first, 0, 0)),
+            pl.BlockSpec(memory_space=pltpu.HBM),
+            pl.BlockSpec(memory_space=pltpu.HBM),
+        ],
+        out_specs=[
+            still((length, width)),
+            still((length, width)),
+            pl.BlockSpec((1, pair, length), lambda group: (group, 0, 0)),
+        ],
+        out_shape=[
+            jax.ShapeDtypeStruct((length, width), jnp.float32),
+            jax.ShapeDtypeStruct((length, width), jnp.float32),
+            jax.ShapeDtypeStruct((groups, pair, length), jnp.float32),
+        ],
+        scratch_shapes=[
+            pltpu.VMEM((pair * hidden, tile), jnp.bfloat16),
+            pltpu.VMEM((2 * pair * hidden, tile), jnp.bfloat16),
+            pltpu.SemaphoreType.DMA((2,)),
+        ],
+        compiler_params=pltpu.CompilerParams(
+            vmem_limit_bytes=60 * 2**20, dimension_semantics=("arbitrary",)
+        ),
+        cost_estimate=pl.CostEstimate(
+            flops=18 * groups * pair * hidden * width * length,
+            bytes_accessed=64 * 2**20,
+            transcendentals=0,
+        ),
+    )(inputs, cotangents, gates, up_rows, down_rows, out_start, grad_start)
 
 
 def swiglu(paired):
@@ -252,7 +535,10 @@
     normed = to_low(rms_scale(tokens_f, gain_attn_f))
     mid_qkv = to_low(matmul(normed, qkv_a))
     columns = normed
-    qkv_rows = gathered(query_key_value_weight)
+    attention_rows = gathered(
+        jnp.concatenate([query_key_value_weight, output_projection_weight[:, None]], axis=1)
+    )
+    qkv_rows, output_rows = attention_rows[:, :3], attention_rows[:, 3]
     qkv_sum = jnp.einsum(
         "tr,rsf->tsf",
         columns,
@@ -308,9 +594,14 @@
         )
         logsum_parts.append(highest + jnp.log(row_totals))
     attended = to_low(jnp.concatenate(attended_parts, axis=0).reshape(length, -1))
-    output_rows = gathered(output_projection_weight)
     branch_part = contract_last(attended, output_rows)
-    branch_here, mid_out_here_f = summed(branch_part, matmul(attended, out_a), 1)
+    down_block = jnp.transpose(routed_down_weight, (1, 2, 0))
+    branch_here, mid_out_here_f, down_rows = summed_and_gathered(
+        branch_part,
+        matmul(attended, out_a),
+        down_block.reshape(-1, down_block.shape[2]),
+        1,
+    )
     mid_out_here = to_low(mid_out_here_f)
     hidden_here = tokens_f + branch_here + ADAPTER_SCALE * matmul(mid_out_here, out_b)
     normed_two_here_f, norm_ffn_pull = jax.vjp(
@@ -319,9 +610,10 @@
     normed_two_here = to_low(normed_two_here_f)
     normed_two, mid_out = (normed_two_here, mid_out_here)
     cot_f = cotangent.astype(jnp.float32)
-    down_rows = gathered(routed_down_weight)
-    sdown_rows = gathered(shared_expert_down_weight)
-    shared_rows = gathered(shared_expert_gate_up_weight)
+    shared_three = gathered(
+        jnp.concatenate([shared_expert_gate_up_weight, shared_expert_down_weight[:, None]], axis=1)
+    )
+    shared_rows, sdown_rows = shared_three[:, :2], shared_three[:, 2]
     small_rows = gathered(
         jnp.concatenate(
             [
@@ -359,48 +651,32 @@
     grad_up_b_local = ADAPTER_SCALE * jnp.einsum(
         "tr,txf->rxf", mid_up, grad_shared_gu, preferred_element_type=jnp.float32
     )
-    grad_down_a_local = contract_first(shared_act, grad_mid_down)
+    grad_down_a_local = contract_first(grad_mid_down, shared_act)
     combined_part = shared_gate[:, None] * shared_cols
     normed_two_part = jnp.einsum(
         "txf,rxf->tr", grad_shared_gu, shared_rows, preferred_element_type=jnp.float32
     )
 
-    grad_act_open = jnp.einsum(
-        "ref,tr->eft", down_rows, cotangent, preferred_element_type=jnp.float32
-    )
+    up_block = jnp.transpose(routed_gate_up_weight, (1, 2, 3, 0))
+    inputs_t, cotangents_t = normed_two.T, cotangent.T
+    gates = gate_table.reshape(EXPERTS // PAIR, PAIR, length)
+    down_rows = down_rows.reshape(EXPERTS // PAIR, -1, width)
     gate_grad_parts = []
-    share = EXPERTS // EXPERT_PARTS
-    for first in range(0, EXPERTS, share):
-        some = slice(first, first + share)
-        up_rows = gathered(routed_gate_up_weight[:, some])
-        gate_up = jnp.einsum(
-            "rexf,tr->exft", up_rows, normed_two, preferred_element_type=jnp.float32
-        )
-        gate_half, up_half = gate_up[:, 0], gate_up[:, 1]
-        squashed = jax.nn.sigmoid(gate_half)
-        act = to_low(gate_half * squashed * up_half).astype(jnp.float32)
-        gate_rows = gate_table[some, None, :]
-        open_part = grad_act_open[some]
-        gate_grad_parts.append(jnp.sum(act * open_part, axis=1))
-        grad_act = gate_rows * open_part
-        grad_gate_up = to_low(
-            jnp.stack(
-                [
-                    grad_act * up_half * squashed * (1.0 + gate_half * (1.0 - squashed)),
-                    grad_act * gate_half * squashed,
-                ],
-                axis=1,
-            )
-        )
-        combined_part = combined_part + jnp.einsum(
-            "eft,ref->tr",
-            to_low(gate_rows * act),
-            down_rows[:, some],
-            preferred_element_type=jnp.float32,
-        )
-        normed_two_part = normed_two_part + jnp.einsum(
-            "exft,rexf->tr", grad_gate_up, up_rows, preferred_element_type=jnp.float32
-        )
+    first = 0
+    for count in EXPERT_PARTS:
+        up_rows = lax.all_gather(up_block[first : first + count], "dp", axis=3, tiled=True)
+        combined_part, normed_two_part, gate_grads = experts_step(
+            inputs_t,
+            cotangents_t,
+            gates,
+            up_rows.reshape(count // PAIR, -1, width),
+            down_rows,
+            combined_part,
+            normed_two_part,
+            first // PAIR,
+        )
+        gate_grad_parts.append(gate_grads.reshape(count, length))
+        first += count
     gate_grad_part = jnp.concatenate(gate_grad_parts, axis=0).T
     narrow_part = jnp.concatenate(
         [gate_grad_part, shared_gate_part[:, None], grad_mid_up_part], axis=1
@@ -427,7 +703,7 @@
     grad_hidden = cot_f + norm_ffn_pull(grad_normed_two)[0]
     grad_branch_here = to_low(grad_hidden)
     grad_branch, grad_mid_up = (grad_branch_here, grad_mid_up_here)
-    grad_up_a_local = contract_first(normed_two, grad_mid_up)
+    grad_up_a_local = contract_first(grad_mid_up, normed_two)
     grad_mid_out = to_low(ADAPTER_SCALE * contract_last(grad_branch, out_b))
     grad_out_b_local = ADAPTER_SCALE * contract_first(mid_out, grad_branch)
     columns = grad_branch
@@ -437,7 +713,7 @@
     grad_attended = to_low(grad_att_sum + contract_last(grad_mid_out, out_a)).reshape(
         length, heads_here, HEAD_SIZE
     )
-    grad_out_a_local = contract_first(attended, grad_mid_out)
+    grad_out_a_local = contract_first(grad_mid_out, attended)
     grad_keys = jnp.zeros((length, heads_here, HEAD_SIZE), jnp.float32)
     grad_values = jnp.zeros((length, heads_here, HEAD_SIZE), jnp.float32)
     grad_query_parts = []
@@ -493,48 +769,53 @@
     norm_attn_pull = jax.vjp(lambda rows: rms_scale(rows, gain_attn_f), tokens_f)[1]
     grad_tokens_here = to_low(grad_hidden + norm_attn_pull(grad_normed)[0])
     grad_tokens, grad_mid_qkv = (grad_tokens_here, grad_mid_qkv_here)
-    grad_qkv_a_local = contract_first(normed, grad_mid_qkv)
+    grad_qkv_a_local = contract_first(grad_mid_qkv, normed)
     everyone = small_rows[:: small_rows.shape[0] // lax.axis_size("dp"), EXPERTS + 1]
     marker = to_low(
         jnp.arange(ADAPTER_SETS, dtype=jnp.int32)[:, None] == everyone.astype(jnp.int32)[None, :]
     )
 
     def adapter_sums(local_grads):
-        sizes = [local_grad.size for local_grad in local_grads]
-        flat = jnp.concatenate([to_low(local_grad).reshape(-1) for local_grad in local_grads])
-        rows = lax.all_gather(flat[None], "dp", axis=0, tiled=True)
-        totals = matmul(marker, rows)
+        sizes = [local_grad.shape[1] for local_grad in local_grads]
+        flat = jnp.concatenate([to_low(local_grad) for local_grad in local_grads], axis=1)
+        rows = lax.all_gather(flat, "dp", axis=0, tiled=False)
+        totals = jnp.einsum("cj,jrn->crn", marker, rows, preferred_element_type=jnp.float32)
         results, start = [], 0
-        for local_grad, size in zip(local_grads, sizes):
-            results.append(
-                totals[:, start : start + size].reshape((ADAPTER_SETS,) + local_grad.shape)
-            )
+        for size in sizes:
+            results.append(totals[:, :, start : start + size])
             start += size
         return results
 
-    early = adapter_sums(
+    def flipped(total):
+        return jnp.swapaxes(total, 1, 2)
+
+    def opened(total, count):
+        return total.reshape(total.shape[0], total.shape[1], count, -1)
+
+    total_out_a, total_out_b, total_up_a, total_up_b, total_down_a, total_down_b = adapter_sums(
         [
             grad_out_a_local,
             grad_out_b_local,
             grad_up_a_local,
-            grad_up_b_local,
+            grad_up_b_local.reshape(grad_up_b_local.shape[0], -1),
             grad_down_a_local,
             grad_down_b_local,
         ]
     )
-    late = adapter_sums([grad_qkv_b_local, grad_qkv_a_local])
-    adapter_totals = [late[1], late[0]] + early
+    total_qkv_b, total_qkv_a = adapter_sums(
+        [grad_qkv_b_local.reshape(grad_qkv_b_local.shape[0], -1), grad_qkv_a_local]
+    )
     return (
         output,
         grad_tokens,
-        adapter_totals[0],
-        adapter_totals[1],
-        adapter_totals[2],
-        adapter_totals[3],
-        adapter_totals[4],
-        adapter_totals[5],
-        adapter_totals[6],
-        adapter_totals[7],
+        flipped(total_qkv_a),
+        opened(total_qkv_b, 3),
+        flipped(total_out_a),
+        total_out_b,
+        flipped(total_up_a),
+        opened(total_up_b, 2),
+        flipped(total_down_a),
+        total_down_b,
     )
 
 

time: 1410 us -> 1210 us (0.86)
  Pallas kernels: 450 us -> 730 us
  matrix products: 454 us -> 224 us
  waiting for transfers between devices: 209 us -> 15.3 us
  local copies, waits for them, and re-layouts: 139 us -> 108 us
  other arithmetic: 111 us -> 86.8 us
    pallas_call x0 -> x4, Pallas kernels: none -> 389 us  [the longest x3 221 us: experts_step(): pl.pallas_call(functools.partial(experts_kernel, tile), grid=(groups,), i...]
    dot_general x13 -> x2, matrix products: 234 us -> 3.71 us  [adapter_sums(): jnp.einsum('cj,jrn->crn', marker, rows, preferred_element_type=jnp.float32)]
    all_gather x9 -> x2, waiting for transfers between devices: 205 us -> 14.6 us  [gathered(): return lax.all_gather(weight, 'dp', axis=0, tiled=True)]
    pallas_call x4 -> x3, Pallas kernels: 450 us -> 341 us  [tensor_sum(): pl.pallas_call(functools.partial(line_sum_kernel, SUM_CHUNKS), out_shape=...]
    another operation x2 -> x3, other arithmetic: 53 us -> 0.03 us  [body(): jnp.stack([grad_act * up_half * squashed * (1.0 + gate_half * (1.0 - squa...]
    convert_element_type x5 -> x8, other arithmetic: 15.3 us -> 36 us  [to_low(): return values.astype(jnp.bfloat16)]
    reshape x10 -> x4, local copies, waits for them, and re-layouts: 19.8 us -> 0.73 us  [the longest x1 0.69 us: body(): gates = gate_table.reshape(EXPERTS // PAIR, PAIR, length)]
    unnamed x259 -> x239, local copies, waits for them, and re-layouts: 56.1 us -> 43.1 us
  transfers between devices with their start and end apart: 10 -> 6, of which waited for: 4 -> 1; matrix products, arithmetic and copies ran while one was open for 24% -> 22% of each run, Pallas kernels for 16% -> 37%
where the time goes in v2:
time: 1210 us; the launch traced here: 1200 us
  Pallas kernels  730 us (60%)
  matrix products  224 us (19%)
  local copies, waits for them, and re-layouts  108 us (9%)
  other arithmetic  86.8 us (7%)
  blocking collectives  21.5 us (2%)
  between operations  16.8 us (1%)
  waiting for transfers between devices  15.3 us (1%)
    pallas_call x3, Pallas kernels, tensor_sum(): pl.pallas_call(functools.partial(line_sum_kernel, SUM_CHUNKS), out_shape=...  341 us
    pallas_call x3, Pallas kernels, experts_step(): pl.pallas_call(functools.partial(experts_kernel, tile), grid=(groups,), i...  221 us
    pallas_call x1, Pallas kernels, summed_and_gathered(): pl.pallas_call(functools.partial(sum_gather_kernel, SUM_CHUNKS, pieces),...  168 us
    dot_general x9, matrix products, contract_last(): lax.dot_general(left_side, right_side, (((1,), (1,)), ((), ())), preferre...  55 us
    unnamed x239, local copies, waits for them, and re-layouts  43.1 us
    dot_general x10, matrix products, matmul(): return jnp.dot(left_side, right_side, preferred_element_type=jnp.float32)  37.9 us
    convert_element_type x8, other arithmetic, to_low(): return values.astype(jnp.bfloat16)  36 us
    concatenate x4, local copies, waits for them, and re-layouts, packed(): jnp.concatenate([to_low(wide_part), to_low(narrow_part), pad], axis=1)  31.4 us
  transfers between devices with their start and end apart: 6, of which 1 were waited for; matrix products, arithmetic and copies ran while one was open for 22% of the time, Pallas kernels for 37%

profile of v2, /device:TPU:0, one launch (start us, length us, event | category | flops | bytes accessed | tf_op | source)
XLA Modules:
  0.0 1202.5 jit_solution(6817926245934445870)
XLA Ops:
  11.2 2.7 pad_maximum_fusion
  14.0 3.6 slice.247
  17.6 3.6 fusion.205
  23.0 11.5 all_gather.31
  34.6 3.1 fusion.11
  40.0 6.7 copy.262
  49.8 3.4 fusion.99
  55.4 14.6 %all-gather.9.cloned.1.call-done = bf16[2048,4,512]{0,2,1:T(8,128)(2,1)} async-done(((bf16[256,4,512]{0,2,1:T(8,128)(2,1)}), bf16[2048,4,512]{0,2,1:T(8,128)(2,1)}) %all-gather.9.cloned.1.call-update) | async-done | bytes 8388624 | tf_op jit(solution)/shard_map/all_gather | solution.py:483
  70.1 10.2 fusion.32
  82.3 2.3 fusion.204
  87.7 3.1 copy.258
  90.8 3.8 slice_negate_fusion.2
  101.9 2.3 fusion.87
  106.0 2.7 fusion.86
  110.6 6.0 convolution_convert_fusion
  117.4 8.0 concatenate.71.part_ref
  125.4 2.3 copy-done.3
  127.6 168.0 %shard_map.303 = (bf16[1024,2176]{1,0:T(8,128)(2,1)S(1)}, bf16[5632,2048]{1,0:T(8,128)(2,1)}) custom-call(bf16[1024,2176]{1,0:T(8,128)(2,1)S(1)} %copy-done.3, bf16[5632,256]{1,0:T(8,128)(2,1)S(1)} %bitcast.245), custom_call_target="tpu_custom_call" | custom-call | bytes 377487360 | tf_op jit(solution)/shard_map/pallas_call | solution.py:352
  295.7 3.0 multiply_reduce_fusion.3
  301.9 2.8 fusion.247
  310.4 6.5 copy.271.inputs_ref
  317.0 6.0 fusion.126
  326.3 12.0 %fusion.34 = f32[1024,1408]{1,0:T(8,128)} fusion(bf16[2048,3,1408]{2,0,1:T(8,128)(2,1)} %all-gather.17.cloned.1.call-done, bf16[1024,2048]{1,0:T(8,128)(2,1)} %param.27, f32[1024]{0:T(1024)S(1)} %add_divide_fusion), kind=kOutput, calls=%fused_computation.75 | convolution fusion | flops 5911871488 | bytes 15732736 | tf_op jit(solution)/shard_map/dot_general | solution.py:29
  338.3 19.7 %multiply_add_fusion = f32[1024,2,1408]{2,0,1:T(8,128)} fusion(f32[1024,2,1408]{2,0,1:T(8,128)} %fusion.126, bf16[2048,3,1408]{2,0,1:T(8,128)(2,1)} %all-gather.17.cloned.1.call-done, bf16[1024,2048]{1,0:T(8,128)(2,1)S(1)} %copy-done.12), kind=kOutput, calls=%fused_computation.12 | convolution fusion | flops 11816927232 | bytes 38797312 | tf_op jit(solution)/shard_map/tr,rxf->txf/dot_general | solution.py:637
  358.0 7.9 multiply_bitcast_fusion
  368.9 2.7 copy-done.38
  371.7 2.3 fusion.91
  379.6 12.3 %broadcast_multiply_fusion = (f32[1024,2048]{1,0:T(8,128)}, f32[1024,2048]{1,0:T(8,128)}) fusion(f32[1024]{0:T(1024)S(1)} %add_divide_fusion, bf16[2048,3,1408]{2,0,1:T(8,128)(2,1)} %all-gather.17.cloned.1.call-done, bf16[1024,1,1408]{2,0,1:T(8,128)(2,1)S(1)} %multiply_convert_fusion.3), kind=kOutput, calls=%fused_computation.85 | convolution fusion | flops 5907677184 | bytes 25432064 | tf_op jit(solution)/shard_map/dot_general | solution.py:33
  391.9 20.2 %fusion.36.grad_start = f32[1024,2048]{1,0:T(8,128)} fusion(bf16[2048,3,1408]{2,0,1:T(8,128)(2,1)} %all-gather.17.cloned.1.call-done, f32[1024,1,1408]{2,0,1:T(8,128)} %copy-done.38, f32[1024,1,1408]{2,0,1:T(8,128)} %copy-done.37), kind=kOutput, calls=%fused_computation.78 | convolution fusion | flops 11816927232 | bytes 31457280 | tf_op jit(solution)/shard_map/txf,rxf->tr/dot_general | solution.py:656
  412.1 100.9 %shard_map.304 = (f32[1024,2048]{1,0:T(8,128)}, f32[1024,2048]{1,0:T(8,128)}, f32[4,2,1024]{2,1,0:T(2,128)}) custom-call(bf16[2048,1024]{1,0:T(8,128)(2,1)} %copy.271.inputs_ref, bf16[2048,1024]{1,0:T(8,128)(2,1)} %bitcast.274, f32[8,2,1024]{2,1,0:T(2,128)} %reshape.337.gate_ref, bf16[4,1408,2048]{2,1,0:T(8,128)(2,1)} %bitcast.296, ...), custom_call_target="tpu_custom_call" | custom-call | flops 106300440576 | bytes 67108864 | tf_op jit(solution)/shard_map/pallas_call | solution.py:440
  513.0 60.2 %shard_map.305 = (f32[1024,2048]{1,0:T(8,128)}, f32[1024,2048]{1,0:T(8,128)}, f32[2,2,1024]{2,1,0:T(2,128)}) custom-call(bf16[2048,1024]{1,0:T(8,128)(2,1)} %copy.271.inputs_ref, bf16[2048,1024]{1,0:T(8,128)(2,1)} %bitcast.275, f32[8,2,1024]{2,1,0:T(2,128)} %reshape.337.gate_ref, bf16[2,1408,2048]{2,1,0:T(8,128)(2,1)} %bitcast.300, ...), custom_call_target="tpu_custom_call" | custom-call | flops 53150220288 | bytes 67108864 | tf_op jit(solution)/shard_map/pallas_call | solution.py:440
  573.2 59.9 %shard_map.306 = (f32[1024,2048]{1,0:T(8,128)}, f32[1024,2048]{1,0:T(8,128)}, f32[2,2,1024]{2,1,0:T(2,128)}) custom-call(bf16[2048,1024]{1,0:T(8,128)(2,1)} %copy.271.inputs_ref, bf16[2048,1024]{1,0:T(8,128)(2,1)} %bitcast.276, f32[8,2,1024]{2,1,0:T(2,128)} %reshape.337.gate_ref, bf16[2,1408,2048]{2,1,0:T(8,128)(2,1)} %bitcast.301, ...), custom_call_target="tpu_custom_call" | custom-call | flops 53150220288 | bytes 67108864 | tf_op jit(solution)/shard_map/pallas_call | solution.py:440
  633.1 6.1 convert_element_type.216
  639.2 7.8 concatenate.74.part_ref
  649.2 115.3 %shard_map.307 = bf16[1024,2176]{1,0:T(8,128)(2,1)S(1)} custom-call(bf16[1024,2176]{1,0:T(8,128)(2,1)S(1)} %copy-done.6), custom_call_target="tpu_custom_call" | custom-call | bytes 314572800 | tf_op jit(solution)/shard_map/pallas_call | solution.py:319
  764.5 8.1 fusion.10
  773.2 6.1 convert_element_type.219
  779.4 7.8 concatenate.76.part_ref
  789.5 112.0 %shard_map.308 = bf16[1024,2176]{1,0:T(8,128)(2,1)S(1)} custom-call(bf16[1024,2176]{1,0:T(8,128)(2,1)S(1)} %copy-done.4), custom_call_target="tpu_custom_call" | custom-call | bytes 314572800 | tf_op jit(solution)/shard_map/pallas_call | solution.py:319
  903.6 5.5 fusion.113
  912.1 9.8 multiply_reduce_fusion.2
  921.9 16.0 %convert_add_fusion.1 = (f32[1024,2048]{1,0:T(8,128)}, bf16[1024,2048]{1,0:T(8,128)(2,1)}) fusion(bf16[1024,2048]{1,0:T(8,128)(2,1)} %param.27, f32[1024,2048]{1,0:T(8,128)} %copy-done.14, f32[1024,2048]{1,0:T(8,128)} %get-tuple-element.143, f32[1024]{0:T(1024)S(1)} %multiply_multiply_fusion.1, f32[1024]{0:T(1024)S(1)} %copy-done.73, ...), kind=kLoop, calls=%fused_computation.5 | loop fusion | flops 23068672 | bytes 46149632 | tf_op jit(solution)/shard_map/add | solution.py:703
  938.0 4.7 fusion.94
  943.8 4.2 fusion.79
  949.4 4.4 multiply_reduce_fusion.1
  953.9 6.2 multiply_convert_fusion.1
  960.1 5.3 fusion.110
  967.7 3.0 fusion.39
  970.6 4.4 multiply_reduce_fusion
  976.1 2.5 fusion.61
  980.7 6.0 fusion.67
  988.2 6.6 fusion.81
  994.8 7.1 multiply_convert_fusion
  1008.1 2.5 fusion.76
  1010.5 2.9 copy.286
  1015.2 2.8 pad_add_fusion
  1018.1 11.2 bitcast_convert_fusion
  1029.3 2.5 fusion.90
  1031.8 7.8 concatenate.78.part_ref
  1041.9 113.7 %shard_map.309 = bf16[1024,2176]{1,0:T(8,128)(2,1)S(1)} custom-call(bf16[1024,2176]{1,0:T(8,128)(2,1)S(1)} %copy-done.5), custom_call_target="tpu_custom_call" | custom-call | bytes 314572800 | tf_op jit(solution)/shard_map/pallas_call | solution.py:319
  1157.7 10.0 all-gather
  1171.7 5.3 fusion.15
  1177.0 6.4 fusion.7
  1183.4 2.8 fusion.56
  (360 shorter events, 94.7 us)
Async XLA Ops:
  7.2 41.8 %copy-start = (bf16[8,16,2,1408]{3,2,1,0:T(2,128)(2,1)S(1)}, bf16[8,16,2,1408]{3,2,1,0:T(2,128)(2,1)}, u32[]{:S(2)}) copy-start(bf16[8,16,2,1408]{3,2,1,0:T(2,128)(2,1)} %param.47) | copy-start | bytes 2162692
  7.2 62.8 %all-gather.9.cloned.1.call-start = ((), (), s32[]{:S(2)}) async-start(), calls=%async_computation | async-start | bytes 9437184 | tf_op jit(solution)/shard_map/all_gather | solution.py:483
  11.0 315.3 %all-gather.17.cloned.1.call-start = ((), (), s32[]{:S(2)}) async-start(), calls=%async_computation.4 | async-start | bytes 19464192 | tf_op jit(solution)/shard_map/all_gather | solution.py:483
  13.9 398.2 %all-gather.15.cloned.1.call-start = ((), (), s32[]{:S(2)}) async-start(), calls=%async_computation.3 | async-start | bytes 25952256 | tf_op jit(solution)/shard_map/all_gather | solution.py:667
  17.5 17.1 %copy-start.90 = (bf16[2048]{0:T(1024)(128)(2,1)S(1)}, bf16[2048]{0:T(1024)(128)(2,1)}, u32[]{:S(2)}) copy-start(bf16[2048]{0:T(1024)(128)(2,1)} %param.28) | copy-start | bytes 12292
  17.5 20.2 %copy-start.91 = (bf16[3,512]{1,0:T(4,128)(2,1)S(1)}, bf16[3,512]{1,0:T(4,128)(2,1)}, u32[]{:S(2)}) copy-start(bf16[3,512]{1,0:T(4,128)(2,1)} %param.30) | copy-start | bytes 9220
  17.6 22.2 %copy-start.92 = (bf16[2048]{0:T(1024)(128)(2,1)S(1)}, bf16[2048]{0:T(1024)(128)(2,1)}, u32[]{:S(2)}) copy-start(bf16[2048]{0:T(1024)(128)(2,1)} %param.32) | copy-start | bytes 12292
  17.6 22.2 %copy-start.84 = (s32[1024,4]{0,1:T(4,128)S(1)}, s32[1024,4]{0,1:T(4,128)}, u32[]{:S(2)}) copy-start(s32[1024,4]{0,1:T(4,128)} %param.39) | copy-start | bytes 49156
  17.6 495.4 %all-gather.13.cloned.1.call-start = ((), (), s32[]{:S(2)}) async-start(), calls=%async_computation.2 | async-start | bytes 12976128 | tf_op jit(solution)/shard_map/all_gather | solution.py:667
  21.2 551.9 %all-gather.11.cloned.1.call-start = ((), (), s32[]{:S(2)}) async-start(), calls=%async_computation.1 | async-start | bytes 12976128 | tf_op jit(solution)/shard_map/all_gather | solution.py:667
  21.8 1161.6 %all-gather.19.cloned.1.call-start = ((), (), s32[]{:S(2)}) async-start(), calls=%async_computation.5 | async-start | bytes 3133440 | tf_op jit(solution)/shard_map/all_gather | solution.py:781
  34.5 266.2 %copy-start.51 = (bf16[2048,18]{0,1:T(8,128)(2,1)}, bf16[2048,18]{0,1:T(8,128)(2,1)S(1)}, u32[]{:S(2)}) copy-start(bf16[2048,18]{0,1:T(8,128)(2,1)S(1)} %all_gather.31) | copy-start | bytes 221188
  34.6 35.4 %copy-start.70 = (f32[2048]{0:T(1024)}, f32[2048]{0:T(1024)S(1)}, u32[]{:S(2)}) copy-start(f32[2048]{0:T(1024)S(1)} %convert_element_type.194) | copy-start | bytes 24580
  37.7 11.3 copy-start.76
  37.7 32.3 %copy-start.80 = (f32[1024]{0:T(1024)}, f32[1024]{0:T(1024)S(1)}, u32[]{:S(2)}) copy-start(f32[1024]{0:T(1024)S(1)} %fusion.169) | copy-start | bytes 12292
  39.8 262.1 %copy-start.68 = (f32[2048]{0:T(1024)}, f32[2048]{0:T(1024)S(1)}, u32[]{:S(2)}) copy-start(f32[2048]{0:T(1024)S(1)} %convert_element_type.205) | copy-start | bytes 24580
  40.0 268.6 %copy-start.26 = (f32[1024,16]{1,0:T(8,128)}, f32[1024,16]{1,0:T(8,128)S(1)}, u32[]{:S(2)}) copy-start(f32[1024,16]{1,0:T(8,128)S(1)} %copy.265) | copy-start | bytes 196612
  49.0 45.6 %copy-start.39 = (f32[1024,128]{1,0:T(8,128)}, f32[1024,128]{1,0:T(8,128)S(1)}, u32[]{:S(2)}) copy-start(f32[1024,128]{1,0:T(8,128)S(1)} %get-tuple-element.153) | copy-start | bytes 1572868
  53.2 27.0 %copy-start.64 = (bf16[1024,16,1]{0,1,2:T(8,128)(2,1)}, bf16[1024,16,1]{0,1,2:T(8,128)(2,1)S(1)}, u32[]{:S(2)}) copy-start(bf16[1024,16,1]{0,1,2:T(8,128)(2,1)S(1)} %fusion.99) | copy-start | bytes 98308
  98.0 6.2 copy-start.10
  99.8 6.2 copy-start.9
  104.2 6.5 copy-start.53
  116.6 8.8 copy-start.7
  127.6 168.0 %copy-start.20 = (bf16[1024,2048]{1,0:T(8,128)(2,1)S(1)}, bf16[1024,2048]{1,0:T(8,128)(2,1)}, u32[]{:S(2)}) copy-start(bf16[1024,2048]{1,0:T(8,128)(2,1)} %param.26) | copy-start | bytes 12582916
  299.5 6.5 copy-start.11
  300.7 7.3 copy-start.74
  301.9 6.7 copy-start.59
  308.0 71.6 %copy-start.82 = (f32[1024]{0:T(1024)}, f32[1024]{0:T(1024)S(1)}, u32[]{:S(2)}) copy-start(f32[1024]{0:T(1024)S(1)} %add_divide_fusion) | copy-start | bytes 12292
  308.0 9.0 copy-start.57
  308.2 14.8 %copy-start.23 = (f32[1024,16]{1,0:T(8,128)}, f32[1024,16]{1,0:T(8,128)S(1)}, u32[]{:S(2)}) copy-start(f32[1024,16]{1,0:T(8,128)S(1)} %copy.263) | copy-start | bytes 196612
  325.2 32.9 %copy-start.96 = (bf16[1024,16]{0,1:T(8,128)(2,1)}, bf16[1024,16]{0,1:T(8,128)(2,1)S(1)}, u32[]{:S(2)}) copy-start(bf16[1024,16]{0,1:T(8,128)(2,1)S(1)} %fusion.93) | copy-start | bytes 98308
  326.3 12.0 %copy-start.12 = (bf16[1024,2048]{1,0:T(8,128)(2,1)S(1)}, bf16[1024,2048]{1,0:T(8,128)(2,1)}, u32[]{:S(2)}) copy-start(bf16[1024,2048]{1,0:T(8,128)(2,1)} %copy-done.11) | copy-start | bytes 12582916
  366.0 8.0 slice-start.12
  366.0 8.0 slice-start.13
  649.2 115.3 %copy-start.17 = (bf16[1024,2048]{1,0:T(8,128)(2,1)S(1)}, bf16[1024,2048]{1,0:T(8,128)(2,1)}, u32[]{:S(2)}) copy-start(bf16[1024,2048]{1,0:T(8,128)(2,1)} %param.27) | copy-start | bytes 12582916
  764.5 8.2 copy-start.2
  764.5 8.4 copy-start.88
  764.5 8.4 copy-start.87
  764.5 8.4 copy-start.79
  773.2 6.1 copy-start.61
  902.7 8.5 copy-start.19
  902.7 8.5 slice-start.6
  903.6 7.6 copy-start.75
  903.6 8.5 slice-start.7
  903.6 8.5 copy-start.69
  903.6 8.4 copy-start.78
  903.6 18.3 %slice-start = ((s8[4456448]{0:T(1024)(128)(4,1)}), s8[4194304]{0:T(1024)(128)(4,1)S(1)}, s32[]{:S(2)}) async-start(s8[4456448]{0:T(1024)(128)(4,1)} %bitcast.243), calls=%async_computation.6 | async-start | bytes 8388608
  912.0 9.8 copy-start.86
  912.1 9.9 slice-start.1
  912.1 9.9 copy-start.73
  938.0 11.4 slice-start.4
  949.4 18.2 %slice-start.2 = ((s8[8388608]{0:T(1024)(128)(4,1)}), s8[4194304]{0:T(1024)(128)(4,1)S(1)}, s32[]{:S(2)}) async-start(s8[8388608]{0:T(1024)(128)(4,1)} %bitcast.246), calls=%async_computation.8 | async-start | bytes 8388608
  953.9 6.2 copy-start.32
  953.9 13.8 %slice-start.3 = ((s8[8388608]{0:T(1024)(128)(4,1)}), s8[4194304]{0:T(1024)(128)(4,1)S(1)}, s32[]{:S(2)}) async-start(s8[8388608]{0:T(1024)(128)(4,1)} %bitcast.246), calls=%async_computation.9 | async-start | bytes 8388608
  960.1 7.5 copy-start.66
  967.7 8.4 slice-start.8
  994.8 7.1 copy-start.30
  1041.9 113.7 %copy-start.65 = (bf16[1024,16,1]{0,1,2:T(8,128)(2,1)S(1)}, bf16[1024,16,1]{0,1,2:T(8,128)(2,1)}, u32[]{:S(2)}) copy-start(bf16[1024,16,1]{0,1,2:T(8,128)(2,1)} %copy-done.64) | copy-start | bytes 98308
  1041.9 114.6 %copy-start.21 = (bf16[1024,2048]{1,0:T(8,128)(2,1)S(1)}, bf16[1024,2048]{1,0:T(8,128)(2,1)}, u32[]{:S(2)}) copy-start(bf16[1024,2048]{1,0:T(8,128)(2,1)} %param.26) | copy-start | bytes 12582916
  1041.9 114.6 %copy-start.71 = (f32[2048]{0:T(1024)S(1)}, f32[2048]{0:T(1024)}, u32[]{:S(2)}) copy-start(f32[2048]{0:T(1024)} %copy-done.70) | copy-start | bytes 24580
  1041.9 114.7 %copy-start.81 = (f32[1024]{0:T(1024)S(1)}, f32[1024]{0:T(1024)}, u32[]{:S(2)}) copy-start(f32[1024]{0:T(1024)} %copy-done.80) | copy-start | bytes 12292
  1155.6 12.1 %copy-start.93 = (s32[8]{0:T(128)S(1)}, s32[8]{0:T(128)}, u32[]{:S(2)}) copy-start(s32[8]{0:T(128)} %bitcast_convert_fusion.1) | copy-start | bytes 100
  1168.7 8.2 slice-start.10
  1186.7 8.5 copy-start.1
  (55 other events, 190.1 us)
Sparse Core Ops, SparseCore 0:
  11.1 58.9 all-gather.8
  71.9 121.7 all-gather.16
  195.6 158.7 all-gather.14
  356.7 69.8 all-gather.12
  428.4 69.8 all-gather.10
  988.3 30.3 all-gather.18

commit v3 on v2

--- a/solution.py
+++ b/solution.py
@@ -18,9 +18,12 @@
 THETA = 1000000.0
 ADAPTER_SCALE = 2.0
 MASKED = -1e30
+QUERY_ROWS = 256
+NARROW = 128
 MESH = pl.DeviceIdType.MESH
 SUM_CHUNKS = 16
 AHEAD = 2
+GATHER_PIECES = 16
 PAIR = 2
 EXPERT_PARTS = (8, 4, 4)
 
@@ -61,12 +64,6 @@
     )
 
 
-def rotate(values, cosine, sine_table):
-    half_size = values.shape[-1] // 2
-    turned = jnp.concatenate([-values[..., half_size:], values[..., :half_size]], axis=-1)
-    return values * cosine[:, None, :] + turned * sine_table[:, None, :]
-
-
 def piece_index(positions, starts):
     inside = (positions[:, None] >= starts[None, :]) & (
         positions[:, None] < starts[None, :] + PIECE
@@ -75,16 +72,11 @@
     return jnp.sum(jnp.where(inside, labels, 0), axis=1) - 1
 
 
-def visible(row_positions, col_positions, starts):
-    row_piece = piece_index(row_positions, starts)
-    col_piece = piece_index(col_positions, starts)
-    causal = col_positions[None, :] <= row_positions[:, None]
-    together = (row_piece[:, None] == col_piece[None, :]) & (row_piece[:, None] >= 0)
-    return causal | together
-
-
-def line_sum_steps(chunks, part_ref, total_ref, from_end, pair_sum, from_pair, semaphores):
+def line_sum_steps(
+    chunks, wide_ref, narrow_ref, total_ref, part_ref, from_end, pair_sum, from_pair, semaphores
+):
     place = lax.axis_index("tensor")
+    width = wide_ref.shape[1]
     rows = part_ref.shape[0] // chunks
     inner = (place == 1) | (place == 2)
     end = (place == 0) | (place == 3)
@@ -118,6 +110,11 @@
             left_ref[span(chunk)].astype(jnp.float32) + right_ref[span(chunk)].astype(jnp.float32)
         )
 
+    def stage(chunk):
+        part_ref[span(chunk), :width] = to_low(wide_ref[span(chunk)])
+        if narrow_ref is not None:
+            part_ref[span(chunk), width:] = narrow_ref[span(chunk)]
+
     def greet(extra):
         barrier = pltpu.get_barrier_semaphore()
         pl.semaphore_signal(barrier, inc=1, device_id={"tensor": mate}, device_id_type=MESH)
@@ -136,11 +133,13 @@
         def _():
             @pl.loop(0, chunks)
             def _(chunk):
+                stage(chunk)
                 inward(chunk).start()
 
     def advance(step):
         @pl.when(inner & (step < chunks))
         def _():
+            stage(step)
             inward(step).wait_recv()
             add(part_ref, from_end, pair_sum, step)
             across(step).start()
@@ -257,10 +256,8 @@
     return greet, begin, advance, finish
 
 
-def line_sum_kernel(chunks, part_ref, total_ref, from_end, pair_sum, from_pair, semaphores):
-    greet, begin, advance, finish = line_sum_steps(
-        chunks, part_ref, total_ref, from_end, pair_sum, from_pair, semaphores
-    )
+def line_sum_kernel(chunks, *refs):
+    greet, begin, advance, finish = line_sum_steps(chunks, *refs)
     greet(0)
     begin()
 
@@ -272,22 +269,12 @@
 
 
 def sum_gather_kernel(
-    chunks,
-    pieces,
-    part_ref,
-    block_ref,
-    total_ref,
-    whole_ref,
-    from_end,
-    pair_sum,
-    from_pair,
-    semaphores,
-    gather_semaphores,
-    local_semaphore,
+    chunks, pieces, wide_ref, narrow_ref, block_ref, total_ref, whole_ref, *scratch
 ):
     greet, begin, advance, finish = line_sum_steps(
-        chunks, part_ref, total_ref, from_end, pair_sum, from_pair, semaphores
-    )
+        chunks, wide_ref, narrow_ref, total_ref, *scratch[:5]
+    )
+    gather_semaphores, local_semaphore = scratch[5:]
     gather_greet, gather_begin, gather_advance, gather_finish = plane_gather_steps(
         pieces, block_ref, whole_ref, gather_semaphores, local_semaphore.at[0]
     )
@@ -305,6 +292,30 @@
     finish()
 
 
+def attend_back_sum_kernel(chunks, wide_ref, *refs):
+    inputs, (total_ref, grad_qkv_ref), scratch = refs[:8], refs[8:10], refs[10:]
+    greet, begin, advance, finish = line_sum_steps(
+        chunks, wide_ref, None, total_ref, *scratch[:5]
+    )
+    head_block = attend_back_steps(*inputs, grad_qkv_ref, *scratch[5:])
+    length, heads_width = inputs[0].shape
+    heads, blocks = heads_width // HEAD_SIZE, length // QUERY_ROWS
+    greet(0)
+    begin()
+
+    @pl.loop(0, heads)
+    def _(head):
+        for block in range(blocks):
+            advance(head * blocks + block)
+            head_block(head, block * QUERY_ROWS)
+
+    @pl.loop(heads * blocks, max(heads * blocks, chunks + 1))
+    def _(step):
+        advance(step)
+
+    finish()
+
+
 def on_line():
     return lax.axis_size("tensor") == 4
 
@@ -313,63 +324,223 @@
     return lax.axis_size("dp") == 8
 
 
-def tensor_sum(part, number):
+def in_vmem(count):
+    return [pl.BlockSpec(memory_space=pltpu.VMEM)] * count
+
+
+def sum_scratch(shape):
+    return [pltpu.VMEM(shape, jnp.bfloat16)] * 4 + [pltpu.SemaphoreType.DMA((6, SUM_CHUNKS))]
+
+
+def narrowed(narrow_part):
+    pad = jnp.zeros((narrow_part.shape[0], NARROW - narrow_part.shape[1]), jnp.bfloat16)
+    return jnp.concatenate([to_low(narrow_part), pad], axis=1)
+
+
+def parts_of(total, wide_part, narrow_part):
+    width, small = wide_part.shape[1], narrow_part.shape[1]
+    total = total.astype(jnp.float32)
+    return total[:, :width], total[:, width : width + small]
+
+
+def summed(wide_part, narrow_part, number):
     if not on_line():
-        return lax.psum(part.astype(jnp.float32), "tensor")
+        return lax.psum((wide_part, narrow_part), "tensor")
+    shape = (wide_part.shape[0], wide_part.shape[1] + NARROW)
     total = pl.pallas_call(
         functools.partial(line_sum_kernel, SUM_CHUNKS),
-        out_shape=jax.ShapeDtypeStruct(part.shape, jnp.bfloat16),
-        in_specs=[pl.BlockSpec(memory_space=pltpu.VMEM)],
+        out_shape=jax.ShapeDtypeStruct(shape, jnp.bfloat16),
+        in_specs=in_vmem(2),
         out_specs=pl.BlockSpec(memory_space=pltpu.VMEM),
-        scratch_shapes=[pltpu.VMEM(part.shape, jnp.bfloat16)] * 3
-        + [pltpu.SemaphoreType.DMA((6, SUM_CHUNKS))],
+        scratch_shapes=sum_scratch(shape),
         compiler_params=pltpu.CompilerParams(
-            collective_id=number, has_side_effects=True, vmem_limit_bytes=40 * 2**20
+            collective_id=number, has_side_effects=True, vmem_limit_bytes=48 * 2**20
         ),
         cost_estimate=pl.CostEstimate(flops=0, bytes_accessed=300 * 2**20, transcendentals=0),
-    )(part)
-    return total.astype(jnp.float32)
-
-
-def packed(wide_part, narrow_part):
-    pad = jnp.zeros((wide_part.shape[0], 128 - narrow_part.shape[1]), jnp.bfloat16)
-    return jnp.concatenate([to_low(wide_part), to_low(narrow_part), pad], axis=1)
-
-
-def summed(wide_part, narrow_part, number):
-    width, small = wide_part.shape[1], narrow_part.shape[1]
-    total = tensor_sum(packed(wide_part, narrow_part), number)
-    return total[:, :width], total[:, width : width + small]
+    )(wide_part, narrowed(narrow_part))
+    return parts_of(total, wide_part, narrow_part)
 
 
 def summed_and_gathered(wide_part, narrow_part, block, number):
     if not (on_line() and in_plane()):
         whole = lax.all_gather(block, "dp", axis=1, tiled=True)
         return summed(wide_part, narrow_part, number) + (whole,)
-    width, small = wide_part.shape[1], narrow_part.shape[1]
-    part = packed(wide_part, narrow_part)
-    pieces = EXPERTS
+    shape = (wide_part.shape[0], wide_part.shape[1] + NARROW)
+    pieces = GATHER_PIECES
     total, whole = pl.pallas_call(
         functools.partial(sum_gather_kernel, SUM_CHUNKS, pieces),
         out_shape=[
-            jax.ShapeDtypeStruct(part.shape, jnp.bfloat16),
+            jax.ShapeDtypeStruct(shape, jnp.bfloat16),
             jax.ShapeDtypeStruct((block.shape[0], 8 * block.shape[1]), jnp.bfloat16),
         ],
-        in_specs=[pl.BlockSpec(memory_space=pltpu.VMEM), pl.BlockSpec(memory_space=pltpu.HBM)],
+        in_specs=in_vmem(2) + [pl.BlockSpec(memory_space=pltpu.HBM)],
         out_specs=[pl.BlockSpec(memory_space=pltpu.VMEM), pl.BlockSpec(memory_space=pltpu.HBM)],
-        scratch_shapes=[pltpu.VMEM(part.shape, jnp.bfloat16)] * 3
-        + [
-            pltpu.SemaphoreType.DMA((6, SUM_CHUNKS)),
-            pltpu.SemaphoreType.DMA((18, pieces)),
-            pltpu.SemaphoreType.DMA((1,)),
-        ],
+        scratch_shapes=sum_scratch(shape)
+        + [pltpu.SemaphoreType.DMA((18, pieces)), pltpu.SemaphoreType.DMA((1,))],
         compiler_params=pltpu.CompilerParams(
-            collective_id=number, has_side_effects=True, vmem_limit_bytes=40 * 2**20
+            collective_id=number, has_side_effects=True, vmem_limit_bytes=48 * 2**20
         ),
         cost_estimate=pl.CostEstimate(flops=0, bytes_accessed=360 * 2**20, transcendentals=0),
-    )(part, block)
-    total = total.astype(jnp.float32)
-    return total[:, :width], total[:, width : width + small], whole
+    )(wide_part, narrowed(narrow_part), block)
+    return parts_of(total, wide_part, narrow_part) + (whole,)
+
+
+def block_mask(first, rows, extent, row_piece_ref, col_piece_ref):
+    row_place = lax.broadcasted_iota(jnp.int32, (rows, extent), 0) + first
+    col_place = lax.broadcasted_iota(jnp.int32, (rows, extent), 1)
+    row_piece = row_piece_ref[first : first + rows, 0:1]
+    together = (row_piece == col_piece_ref[0:1, :extent]) & (row_piece >= 0)
+    return (col_place <= row_place) | together
+
+
+def block_probs(query_rows, keys, allowed):
+    scores = jnp.where(allowed, contract_last(query_rows, keys) * HEAD_SIZE**-0.5, MASKED)
+    raised = jnp.exp(scores - jnp.max(scores, axis=1, keepdims=True))
+    return raised * (1.0 / jnp.sum(raised, axis=1, keepdims=True))
+
+
+def half_turn(values, signed_sine):
+    return pltpu.roll(values, HEAD_SIZE // 2, 1) * signed_sine
+
+
+def attend_kernel(
+    qkv_ref,
+    cosine_ref,
+    sine_ref,
+    row_piece_ref,
+    col_piece_ref,
+    query_ref,
+    keys_ref,
+    values_ref,
+    attended_ref,
+):
+    length = qkv_ref.shape[1]
+
+    @pl.loop(0, qkv_ref.shape[2] // HEAD_SIZE)
+    def _(head):
+        column = pl.ds(pl.multiple_of(head * HEAD_SIZE, HEAD_SIZE), HEAD_SIZE)
+        for source, target in ((0, query_ref), (1, keys_ref)):
+            raw = qkv_ref[source, :, column]
+            target[:, column] = to_low(raw * cosine_ref[...] + half_turn(raw, sine_ref[...]))
+        values_ref[:, column] = to_low(qkv_ref[2, :, column])
+        for first in range(0, length, QUERY_ROWS):
+            extent = min(length, first + QUERY_ROWS + PIECE)
+            allowed = block_mask(first, QUERY_ROWS, extent, row_piece_ref, col_piece_ref)
+            probs = block_probs(
+                query_ref[first : first + QUERY_ROWS, column], keys_ref[:extent, column], allowed
+            )
+            attended_ref[first : first + QUERY_ROWS, column] = to_low(
+                matmul(to_low(probs), values_ref[:extent, column])
+            )
+
+
+def attend(qkv, cosine, signed_sine, row_piece, col_piece):
+    length, heads_width = qkv.shape[1:]
+    shape = jax.ShapeDtypeStruct((length, heads_width), jnp.bfloat16)
+    return pl.pallas_call(
+        attend_kernel,
+        out_shape=[shape] * 4,
+        in_specs=[pl.BlockSpec(memory_space=pltpu.VMEM)] * 5,
+        out_specs=[pl.BlockSpec(memory_space=pltpu.VMEM)] * 4,
+        compiler_params=pltpu.CompilerParams(vmem_limit_bytes=48 * 2**20),
+        cost_estimate=pl.CostEstimate(
+            flops=4 * length * length * heads_width,
+            bytes_accessed=16 * 2**20,
+            transcendentals=length * length * heads_width // HEAD_SIZE,
+        ),
+    )(qkv, cosine, signed_sine, row_piece, col_piece)
+
+
+def attend_back_steps(
+    query_ref,
+    keys_ref,
+    values_ref,
+    grad_ref,
+    cosine_ref,
+    sine_ref,
+    row_piece_ref,
+    col_piece_ref,
+    grad_qkv_ref,
+    grad_keys,
+    grad_values,
+):
+    length = query_ref.shape[0]
+
+    def turned_back(grad, first):
+        span = slice(first, first + grad.shape[0])
+        scaled = grad * HEAD_SIZE**-0.5
+        return to_low(scaled * cosine_ref[span] - half_turn(scaled, sine_ref[span]))
+
+    def head_block(head, first):
+        column = pl.ds(pl.multiple_of(head * HEAD_SIZE, HEAD_SIZE), HEAD_SIZE)
+        span = slice(first, first + QUERY_ROWS)
+        extent = min(length, first + QUERY_ROWS + PIECE)
+        if first == 0:
+            grad_keys[...] = jnp.zeros_like(grad_keys)
+            grad_values[...] = jnp.zeros_like(grad_values)
+        allowed = block_mask(first, QUERY_ROWS, extent, row_piece_ref, col_piece_ref)
+        query_rows = query_ref[span, column]
+        keys = keys_ref[:extent, column]
+        grad_rows = grad_ref[span, column]
+        probs = block_probs(query_rows, keys, allowed)
+        grad_probs = contract_last(grad_rows, values_ref[:extent, column])
+        shift = jnp.sum(probs * grad_probs, axis=1, keepdims=True)
+        grad_scores = to_low(probs * (grad_probs - shift))
+        grad_values[:extent] += contract_first(to_low(probs), grad_rows)
+        grad_keys[:extent] += contract_first(grad_scores, query_rows)
+        grad_qkv_ref[0, span, column] = turned_back(matmul(grad_scores, keys), first)
+        if first + QUERY_ROWS >= length:
+            grad_qkv_ref[1, :, column] = turned_back(grad_keys[...], 0)
+            grad_qkv_ref[2, :, column] = to_low(grad_values[...])
+
+    return head_block
+
+
+def attend_back_kernel(*refs):
+    head_block = attend_back_steps(*refs)
+
+    @pl.loop(0, refs[0].shape[1] // HEAD_SIZE)
+    def _(head):
+        for first in range(0, refs[0].shape[0], QUERY_ROWS):
+            head_block(head, first)
+
+
+def attend_back(query, keys, values, grads, cosine, signed_sine, row_piece, col_piece):
+    length, heads_width = query.shape
+    return pl.pallas_call(
+        attend_back_kernel,
+        out_shape=jax.ShapeDtypeStruct((3, length, heads_width), jnp.bfloat16),
+        in_specs=[pl.BlockSpec(memory_space=pltpu.VMEM)] * 8,
+        out_specs=pl.BlockSpec(memory_space=pltpu.VMEM),
+        scratch_shapes=[pltpu.VMEM((length, HEAD_SIZE), jnp.float32)] * 2,
+        compiler_params=pltpu.CompilerParams(vmem_limit_bytes=48 * 2**20),
+        cost_estimate=pl.CostEstimate(
+            flops=10 * length * length * heads_width,
+            bytes_accessed=16 * 2**20,
+            transcendentals=length * length * heads_width // HEAD_SIZE,
+        ),
+    )(query, keys, values, grads, cosine, signed_sine, row_piece, col_piece)
+
+
+def summed_and_attended_back(wide_part, attention_inputs, number):
+    if not on_line():
+        return lax.psum(wide_part, "tensor"), attend_back(*attention_inputs)
+    shape = wide_part.shape
+    length, heads_width = attention_inputs[0].shape
+    return pl.pallas_call(
+        functools.partial(attend_back_sum_kernel, SUM_CHUNKS),
+        out_shape=[
+            jax.ShapeDtypeStruct(shape, jnp.bfloat16),
+            jax.ShapeDtypeStruct((3, length, heads_width), jnp.bfloat16),
+        ],
+        in_specs=in_vmem(1 + len(attention_inputs)),
+        out_specs=in_vmem(2),
+        scratch_shapes=sum_scratch(shape) + [pltpu.VMEM((length, HEAD_SIZE), jnp.float32)] * 2,
+        compiler_params=pltpu.CompilerParams(
+            collective_id=number, has_side_effects=True, vmem_limit_bytes=58 * 2**20
+        ),
+        cost_estimate=pl.CostEstimate(flops=0, bytes_accessed=300 * 2**20, transcendentals=0),
+    )(wide_part, *attention_inputs)
 
 
 def experts_kernel(
@@ -443,7 +614,7 @@
         in_specs=[
             still((width, length)),
             still((width, length)),
-            pl.BlockSpec((1, pair, length), lambda group: (group + first, 0, 0)),
+            pl.BlockSpec((1, pair, length), lambda group: (group, 0, 0)),
             pl.BlockSpec((1, 2 * pair * hidden, width), lambda group: (group, 0, 0)),
             pl.BlockSpec((1, pair * hidden, width), lambda group: (group + first, 0, 0)),
             pl.BlockSpec(memory_space=pltpu.HBM),
@@ -510,7 +681,6 @@
     adapter_shared_down_upper,
 ):
     length, width = tokens.shape
-    heads_here = query_key_value_weight.shape[2] // HEAD_SIZE
     set_id = sequence_adapter_index[0]
     starts = picture_piece_starts[0]
 
@@ -534,74 +704,30 @@
     tokens_f = tokens.astype(jnp.float32)
     normed = to_low(rms_scale(tokens_f, gain_attn_f))
     mid_qkv = to_low(matmul(normed, qkv_a))
-    columns = normed
     attention_rows = gathered(
         jnp.concatenate([query_key_value_weight, output_projection_weight[:, None]], axis=1)
     )
     qkv_rows, output_rows = attention_rows[:, :3], attention_rows[:, 3]
-    qkv_sum = jnp.einsum(
-        "tr,rsf->tsf",
-        columns,
-        qkv_rows,
-        preferred_element_type=jnp.float32,
-    )
-    qkv_sum = qkv_sum + query_key_value_bias.astype(jnp.float32)
+    qkv_sum = jnp.einsum("tr,rsf->stf", normed, qkv_rows, preferred_element_type=jnp.float32)
+    qkv_sum = qkv_sum + query_key_value_bias.astype(jnp.float32)[:, None, :]
     qkv_sum = qkv_sum + ADAPTER_SCALE * jnp.einsum(
-        "tr,rsf->tsf", mid_qkv, qkv_b, preferred_element_type=jnp.float32
+        "tr,rsf->stf", mid_qkv, qkv_b, preferred_element_type=jnp.float32
     )
     cosine, sine_table = rope_tables(length)
-
-    def position(raw_values):
-        query_part = rotate(
-            raw_values[:, 0].reshape(length, heads_here, HEAD_SIZE), cosine, sine_table
-        )
-        keys_part = rotate(
-            raw_values[:, 1].reshape(length, heads_here, HEAD_SIZE), cosine, sine_table
-        )
-        return (query_part, keys_part)
-
-    (query_f, keys_f), rope_pull = jax.vjp(position, qkv_sum)
-    query = to_low(query_f)
-    keys = to_low(keys_f)
-    values = to_low(qkv_sum[:, 2].reshape(length, heads_here, HEAD_SIZE))
-    block_rows = min(length, 512)
-    score_scale = HEAD_SIZE ** (-0.5)
-    positions = jnp.arange(length, dtype=jnp.int32)
-    attended_parts = []
-    logsum_parts = []
-    for offset in range(0, length, block_rows):
-        allowed = visible(positions[offset : offset + block_rows], positions, starts)
-        scores = (
-            jnp.einsum(
-                "qhd,khd->hqk",
-                query[offset : offset + block_rows],
-                keys,
-                preferred_element_type=jnp.float32,
-            )
-            * score_scale
-        )
-        scores = jnp.where(allowed[None], scores, MASKED)
-        highest = jnp.max(scores, axis=-1, keepdims=True)
-        weights_exp = jnp.exp(scores - highest)
-        row_totals = jnp.sum(weights_exp, axis=-1, keepdims=True)
-        attended_parts.append(
-            jnp.einsum(
-                "hqk,khd->qhd",
-                to_low(weights_exp / row_totals),
-                values,
-                preferred_element_type=jnp.float32,
-            )
-        )
-        logsum_parts.append(highest + jnp.log(row_totals))
-    attended = to_low(jnp.concatenate(attended_parts, axis=0).reshape(length, -1))
+    signs = jnp.where(jnp.arange(HEAD_SIZE) < HEAD_SIZE // 2, -1.0, 1.0)
+    piece_ids = piece_index(jnp.arange(length, dtype=jnp.int32), starts)
+    places = (cosine, sine_table * signs[None, :], piece_ids[:, None], piece_ids[None, :])
+    query, keys, values, attended = attend(qkv_sum, *places)
     branch_part = contract_last(attended, output_rows)
     down_block = jnp.transpose(routed_down_weight, (1, 2, 0))
-    branch_here, mid_out_here_f, down_rows = summed_and_gathered(
+    early = EXPERT_PARTS[0]
+    branch_here, mid_out_here_f, down_early = summed_and_gathered(
         branch_part,
         matmul(attended, out_a),
-        down_block.reshape(-1, down_block.shape[2]),
+        down_block[:early].reshape(-1, down_block.shape[2]),
         1,
     )
+    down_late = lax.all_gather(down_block[early:], "dp", axis=2, tiled=True)
     mid_out_here = to_low(mid_out_here_f)
     hidden_here = tokens_f + branch_here + ADAPTER_SCALE * matmul(mid_out_here, out_b)
     normed_two_here_f, norm_ffn_pull = jax.vjp(
@@ -642,6 +768,7 @@
     shared_cols = contract_last(shared_act, sdown_rows)
     shared_gate_part = jnp.sum(cot_f * shared_cols, axis=1)
     grad_shared = to_low(shared_gate[:, None] * cot_f)
+    cotangent_down = ADAPTER_SCALE * contract_last(cotangent, down_b)
     grad_mid_down = to_low(ADAPTER_SCALE * contract_last(grad_shared, down_b))
     grad_shared_act = matmul(grad_shared, sdown_rows) + contract_last(grad_mid_down, down_a)
     grad_shared_gu = to_low(shared_pull(grad_shared_act)[0])
@@ -660,7 +787,8 @@
     up_block = jnp.transpose(routed_gate_up_weight, (1, 2, 3, 0))
     inputs_t, cotangents_t = normed_two.T, cotangent.T
     gates = gate_table.reshape(EXPERTS // PAIR, PAIR, length)
-    down_rows = down_rows.reshape(EXPERTS // PAIR, -1, width)
+    down_early = down_early.reshape(early // PAIR, -1, width)
+    down_late = down_late.reshape((EXPERTS - early) // PAIR, -1, width)
     gate_grad_parts = []
     first = 0
     for count in EXPERT_PARTS:
@@ -668,97 +796,64 @@
         combined_part, normed_two_part, gate_grads = experts_step(
             inputs_t,
             cotangents_t,
-            gates,
+            gates[first // PAIR : (first + count) // PAIR],
             up_rows.reshape(count // PAIR, -1, width),
-            down_rows,
+            down_early if first < early else down_late,
             combined_part,
             normed_two_part,
-            first // PAIR,
+            (first if first < early else first - early) // PAIR,
         )
         gate_grad_parts.append(gate_grads.reshape(count, length))
         first += count
     gate_grad_part = jnp.concatenate(gate_grad_parts, axis=0).T
     narrow_part = jnp.concatenate(
-        [gate_grad_part, shared_gate_part[:, None], grad_mid_up_part], axis=1
+        [
+            gate_grad_part,
+            shared_gate_part[:, None],
+            grad_mid_up_part,
+            matmul(shared_act, down_a),
+        ],
+        axis=1,
     )
     grad_normed_two, narrow_sum = summed(normed_two_part, narrow_part, 2)
-    combined_here, mid_down_here_f = summed(combined_part, matmul(shared_act, down_a), 3)
-    mid_down = to_low(mid_down_here_f)
+    rank = up_a.shape[1]
+    mid_down = to_low(narrow_sum[:, EXPERTS + 1 + rank :])
+    grad_mid_up = to_low(narrow_sum[:, EXPERTS + 1 : EXPERTS + 1 + rank])
+    grad_probs = chosen * narrow_sum[:, :EXPERTS]
+    grad_logits = to_low(
+        router_probs * (grad_probs - jnp.sum(router_probs * grad_probs, axis=1, keepdims=True))
+    )
+    shared_gate_grad = narrow_sum[:, EXPERTS] + jnp.sum(
+        mid_down.astype(jnp.float32) * cotangent_down, axis=1
+    )
+    grad_gate_logit = to_low(shared_gate_grad * shared_gate * (1.0 - shared_gate))
+    grad_normed_two = grad_normed_two + contract_last(
+        jnp.concatenate([grad_logits, grad_gate_logit[:, None], grad_mid_up], axis=1),
+        jnp.concatenate([router_full, gate_full[:, None], up_a], axis=1),
+    )
+    grad_hidden = cot_f + norm_ffn_pull(grad_normed_two)[0]
+    grad_branch = to_low(grad_hidden)
+    grad_mid_out = to_low(ADAPTER_SCALE * contract_last(grad_branch, out_b))
+    grad_attended = to_low(
+        matmul(grad_branch, output_rows) + contract_last(grad_mid_out, out_a)
+    )
+    combined_here, grad_qkv = summed_and_attended_back(
+        combined_part, (query, keys, values, grad_attended) + places, 3
+    )
     extra_here = ADAPTER_SCALE * matmul(mid_down, down_b)
     output = to_low(hidden_here + combined_here + shared_gate[:, None] * extra_here)
     grad_down_b_local = ADAPTER_SCALE * contract_first(mid_down, grad_shared)
-    grad_probs = chosen * narrow_sum[:, :EXPERTS]
-    grad_logits = to_low(
-        router_probs * (grad_probs - jnp.sum(router_probs * grad_probs, axis=1, keepdims=True))
-    )
-    shared_gate_grad = narrow_sum[:, EXPERTS] + jnp.sum(cot_f * extra_here, axis=1)
-    grad_gate_logit = to_low(shared_gate_grad * shared_gate * (1.0 - shared_gate))
-    grad_mid_up_here = to_low(narrow_sum[:, EXPERTS + 1 :])
-    grad_normed_two = grad_normed_two + contract_last(grad_logits, router_full)
-    grad_normed_two = (
-        grad_normed_two
-        + grad_gate_logit.astype(jnp.float32)[:, None] * gate_full.astype(jnp.float32)[None, :]
-    )
-    grad_normed_two = grad_normed_two + contract_last(grad_mid_up_here, up_a)
-    grad_hidden = cot_f + norm_ffn_pull(grad_normed_two)[0]
-    grad_branch_here = to_low(grad_hidden)
-    grad_branch, grad_mid_up = (grad_branch_here, grad_mid_up_here)
     grad_up_a_local = contract_first(grad_mid_up, normed_two)
-    grad_mid_out = to_low(ADAPTER_SCALE * contract_last(grad_branch, out_b))
     grad_out_b_local = ADAPTER_SCALE * contract_first(mid_out, grad_branch)
-    columns = grad_branch
-    grad_att_sum = matmul(
-        columns, output_rows
-    )
-    grad_attended = to_low(grad_att_sum + contract_last(grad_mid_out, out_a)).reshape(
-        length, heads_here, HEAD_SIZE
-    )
     grad_out_a_local = contract_first(grad_mid_out, attended)
-    grad_keys = jnp.zeros((length, heads_here, HEAD_SIZE), jnp.float32)
-    grad_values = jnp.zeros((length, heads_here, HEAD_SIZE), jnp.float32)
-    grad_query_parts = []
-    for block_number, offset in enumerate(range(0, length, block_rows)):
-        query_rows = query[offset : offset + block_rows]
-        allowed = visible(positions[offset : offset + block_rows], positions, starts)
-        scores = (
-            jnp.einsum("qhd,khd->hqk", query_rows, keys, preferred_element_type=jnp.float32)
-            * score_scale
-        )
-        scores = jnp.where(allowed[None], scores, MASKED)
-        probs_f = jnp.exp(scores - logsum_parts[block_number])
-        grad_rows = grad_attended[offset : offset + block_rows]
-        grad_values = grad_values + jnp.einsum(
-            "hqk,qhd->khd", to_low(probs_f), grad_rows, preferred_element_type=jnp.float32
-        )
-        grad_probs_att = jnp.einsum(
-            "qhd,khd->hqk", grad_rows, values, preferred_element_type=jnp.float32
-        )
-        grad_scores = to_low(
-            probs_f * (grad_probs_att - jnp.sum(probs_f * grad_probs_att, axis=-1, keepdims=True))
-        )
-        grad_query_parts.append(
-            jnp.einsum("hqk,khd->qhd", grad_scores, keys, preferred_element_type=jnp.float32)
-            * score_scale
-        )
-        grad_keys = (
-            grad_keys
-            + jnp.einsum(
-                "hqk,qhd->khd", grad_scores, query_rows, preferred_element_type=jnp.float32
-            )
-            * score_scale
-        )
-    grad_query = jnp.concatenate(grad_query_parts, axis=0)
-    grad_raw = rope_pull((grad_query, grad_keys))[0]
-    grad_raw = grad_raw.at[:, 2].set(grad_values.reshape(length, -1))
-    grad_qkv = to_low(grad_raw)
     grad_mid_qkv_part = ADAPTER_SCALE * jnp.einsum(
-        "tsf,rsf->tr", grad_qkv, qkv_b, preferred_element_type=jnp.float32
+        "stf,rsf->tr", grad_qkv, qkv_b, preferred_element_type=jnp.float32
     )
     grad_qkv_b_local = ADAPTER_SCALE * jnp.einsum(
-        "tr,tsf->rsf", mid_qkv, grad_qkv, preferred_element_type=jnp.float32
+        "tr,stf->rsf", mid_qkv, grad_qkv, preferred_element_type=jnp.float32
     )
     normed_part = jnp.einsum(
-        "tsf,rsf->tr",
+        "stf,rsf->tr",
         grad_qkv,
         qkv_rows,
         preferred_element_type=jnp.float32,

time: 1210 us -> 1070 us (0.88)
  other arithmetic: 86.8 us -> 33.6 us
  local copies, waits for them, and re-layouts: 108 us -> 59.8 us
  matrix products: 224 us -> 187 us
  waiting for transfers between devices: 15.3 us -> 46.5 us
  Pallas kernels: 730 us -> 704 us
    pallas_call x1, Pallas kernels: 168 us -> 123 us  [summed_and_gathered(): pl.pallas_call(functools.partial(sum_gather_kernel, SUM_CHUNKS, pieces),...]
    dot_general x17 -> x5, matrix products: 64.5 us -> 29.8 us  [the longest x1 10.8 us: body(): jnp.einsum('stf,rsf->tr', grad_qkv, qkv_rows, preferred_element_type=jnp....]
    all_gather x3, waiting for transfers between devices: 0.04 us -> 32.9 us  [body(): lax.all_gather(up_block[first:first + count], 'dp', axis=3, tiled=True)]
    concatenate x5 -> x4, local copies, waits for them, and re-layouts: 31.6 us -> 0.35 us  [the longest x1 0.18 us: body(): jnp.concatenate([gate_grad_part, shared_gate_part[:, None], grad_mid_up_p...]
    convert_element_type x8 -> x3, other arithmetic: 36 us -> 12.7 us  [to_low(): return values.astype(jnp.bfloat16)]
    pallas_call x3 -> x4, Pallas kernels: 341 us -> 360 us  [the longest x2 231 us: summed(): pl.pallas_call(functools.partial(line_sum_kernel, SUM_CHUNKS), out_shape=...]
    unnamed x239 -> x183, local copies, waits for them, and re-layouts: 43.1 us -> 33.1 us
  transfers between devices with their start and end apart: 6 -> 7, of which waited for: 1 -> 3; matrix products, arithmetic and copies ran while one was open for 22% -> 20% of each run, Pallas kernels for 37% -> 49%
where the time goes in v3:
time: 1070 us
  Pallas kernels  704 us (66%)
  matrix products  187 us (17%)
  local copies, waits for them, and re-layouts  59.8 us (6%)
  waiting for transfers between devices  46.5 us (4%)
  other arithmetic  33.6 us (3%)
  blocking collectives  21.6 us (2%)
  between operations  16.3 us (2%)
    pallas_call x2, Pallas kernels, summed(): pl.pallas_call(functools.partial(line_sum_kernel, SUM_CHUNKS), out_shape=...  231 us
    pallas_call x3, Pallas kernels, experts_step(): pl.pallas_call(functools.partial(experts_kernel, tile), grid=(groups,), i...  221 us
    pallas_call x1, Pallas kernels, summed_and_gathered(): pl.pallas_call(functools.partial(sum_gather_kernel, SUM_CHUNKS, pieces),...  123 us
    pallas_call x1, Pallas kernels, summed_and_attended_back(): pl.pallas_call(functools.partial(attend_back_sum_kernel, SUM_CHUNKS), out...  114 us
    dot_general x9, matrix products, contract_last(): lax.dot_general(left_side, right_side, (((1,), (1,)), ((), ())), preferre...  49.2 us
    dot_general x10, matrix products, matmul(): return jnp.dot(left_side, right_side, preferred_element_type=jnp.float32)  36.8 us
    unnamed x183, local copies, waits for them, and re-layouts  33.1 us
    all_gather x3, waiting for transfers between devices, body(): lax.all_gather(up_block[first:first + count], 'dp', axis=3, tiled=True)  32.9 us
  transfers between devices with their start and end apart: 7, of which 3 were waited for; matrix products, arithmetic and copies ran while one was open for 20% of the time, Pallas kernels for 49%

profile of v3, /device:TPU:0, one launch (start us, length us, event | category | flops | bytes accessed | tf_op | source)
XLA Modules:
  0.0 1069.3 jit_solution(6462560025217427961)
XLA Ops:
  7.2 1.5 copy.193
  11.2 2.7 pad_maximum_fusion
  13.9 3.6 slice.178
  17.6 3.1 fusion.166
  20.8 3.9 fusion.164
  26.0 3.1 fusion.10
  29.2 1.9 fusion.77
  33.4 10.7 %all_gather.34 = bf16[2048,18]{0,1:T(8,128)(2,1)S(1)} all-gather(bf16[256,18]{0,1:T(8,128)(2,1)S(1)} %maximum_maximum_fusion), channel_id=1, replica_groups=mesh['dp'=8,'tensor'=4] {'dp'}, dimensions={0}, use_global_device_ids=true | all-gather | bytes 82944 | tf_op jit(solution)/shard_map/all_gather | solution.py:654
  45.2 6.4 copy.198
  52.2 3.5 fusion.72
  56.8 13.0 %all-gather.10.cloned.1.call-done = bf16[2048,4,512]{0,2,1:T(8,128)(2,1)} async-done(((bf16[256,4,512]{0,2,1:T(8,128)(2,1)}), bf16[2048,4,512]{0,2,1:T(8,128)(2,1)}) %all-gather.10.cloned.1.call-update) | async-done | bytes 8388624 | tf_op jit(solution)/shard_map/all_gather | solution.py:654
  69.8 10.6 fusion.34
  80.5 4.8 add_bitcast_fusion.qkv_ref
  85.3 14.5 %shard_map.303 = (bf16[1024,512]{1,0:T(8,128)(2,1)S(1)}, bf16[1024,512]{1,0:T(8,128)(2,1)S(1)}, bf16[1024,512]{1,0:T(8,128)(2,1)S(1)}, bf16[1024,512]{1,0:T(8,128)(2,1)S(1)}) custom-call(f32[3,1024,512]{2,1,0:T(8,128)} %add_bitcast_fusion.qkv_ref, f32[1024,128]{1,0:T(8,128)S(1)} %get-tuple-element.119.cosine_ref.refs_4_, f32[1024,128]{1,0:T(8,128)S(1)} %copy-done.6, ...), custom_call_target="tpu_custom_call" | custom-call | flops 2147483648 | bytes 16777216 | tf_op jit(solution)/shard_map/pallas_call | solution.py:440
  104.1 7.2 fusion.57.wide_ref
  111.2 123.4 %shard_map.304 = (bf16[1024,2176]{1,0:T(8,128)(2,1)S(1)}, bf16[2816,2048]{1,0:T(8,128)(2,1)}) custom-call(f32[1024,2048]{1,0:T(8,128)} %fusion.57.wide_ref, bf16[1024,128]{1,0:T(8,128)(2,1)S(1)} %concatenate.48.narrow_ref, bf16[2816,256]{1,0:T(8,128)(2,1)S(1)} %bitcast.212), custom_call_target="tpu_custom_call" | custom-call | bytes 377487360 | tf_op jit(solution)/shard_map/pallas_call | solution.py:370
  234.7 3.1 multiply_reduce_fusion.1
  239.8 1.2 fusion.168
  241.1 2.8 fusion.192
  247.3 6.8 copy.209.inputs_ref
  255.7 7.6 fusion.92
  263.3 2.1 fusion.65
  265.4 22.1 %multiply_add_fusion = f32[1024,2,1408]{2,0,1:T(8,128)} fusion(f32[1024,2,1408]{2,0,1:T(8,128)} %fusion.92, bf16[2048,3,1408]{2,0,1:T(8,128)(2,1)} %all-gather.20.cloned.1.call-done, bf16[1024,2048]{1,0:T(8,128)(2,1)} %copy-done.14), kind=kOutput, calls=%fused_computation.11 | convolution fusion | flops 11816927232 | bytes 38797312 | tf_op jit(solution)/shard_map/tr,rxf->txf/dot_general | solution.py:763
  287.5 5.5 multiply_convert_fusion.1
  293.5 10.6 fusion.25
  304.2 6.5 multiply_bitcast_fusion
  310.7 3.7 fusion.44
  315.1 11.0 %fusion.7 = (bf16[1024]{0:T(1024)(128)(2,1)S(1)}, f32[1024,2048]{1,0:T(8,128)}) fusion(bf16[1024,2048]{1,0:T(8,128)(2,1)S(1)} %copy-done.18, f32[1024]{0:T(1024)S(1)} %add_divide_fusion, bf16[2048,3,1408]{2,0,1:T(8,128)(2,1)} %all-gather.20.cloned.1.call-done, bf16[1024,1,1408]{2,0,1:T(8,128)(2,1)S(1)} %multiply_convert_fusion.1), kind=kOutput, calls=%fused_computation.18 | convolution fusion | flops 5913967616 | bytes 21239808 | tf_op jit(solution)/shard_map/dot_general | solution.py:36
  326.7 2.3 fusion.69
  329.0 2.2 fusion.66
  331.2 18.7 %fusion.30.grad_start = f32[1024,2048]{1,0:T(8,128)} fusion(bf16[2048,3,1408]{2,0,1:T(8,128)(2,1)} %all-gather.20.cloned.1.call-done, f32[1024,1,1408]{2,0,1:T(8,128)} %get-tuple-element.95, f32[1024,1,1408]{2,0,1:T(8,128)S(1)} %get-tuple-element.94), kind=kOutput, calls=%fused_computation.55 | convolution fusion | flops 11816927232 | bytes 31457280 | tf_op jit(solution)/shard_map/txf,rxf->tr/dot_general | solution.py:783
  349.9 100.1 %shard_map.305 = (f32[1024,2048]{1,0:T(8,128)}, f32[1024,2048]{1,0:T(8,128)}, f32[4,2,1024]{2,1,0:T(2,128)}) custom-call(bf16[2048,1024]{1,0:T(8,128)(2,1)} %copy.209.inputs_ref, bf16[2048,1024]{1,0:T(8,128)(2,1)} %bitcast.230, f32[4,2,1024]{2,1,0:T(2,128)} %slice.144.gate_ref, bf16[4,1408,2048]{2,1,0:T(8,128)(2,1)} %bitcast.245, ...), custom_call_target="tpu_custom_call" | custom-call | flops 106300440576 | bytes 67108864 | tf_op jit(solution)/shard_map/pallas_call | solution.py:611
  450.0 22.3 %all-gather.16.cloned.1.call-done = bf16[4,2,352,2048]{3,2,1,0:T(8,128)(2,1)} async-done(((bf16[4,2,352,256]{3,2,1,0:T(8,128)(2,1)}), bf16[4,2,352,2048]{3,2,1,0:T(8,128)(2,1)}) %all-gather.16.cloned.1.call-update) | async-done | bytes 11534352 | tf_op jit(solution)/shard_map/all_gather | solution.py:795
  472.4 61.1 %shard_map.306 = (f32[1024,2048]{1,0:T(8,128)}, f32[1024,2048]{1,0:T(8,128)}, f32[2,2,1024]{2,1,0:T(2,128)}) custom-call(bf16[2048,1024]{1,0:T(8,128)(2,1)} %copy.209.inputs_ref, bf16[2048,1024]{1,0:T(8,128)(2,1)} %bitcast.231, f32[2,2,1024]{2,1,0:T(2,128)} %slice.141.gate_ref, bf16[2,1408,2048]{2,1,0:T(8,128)(2,1)} %bitcast.249, ...), custom_call_target="tpu_custom_call" | custom-call | flops 53150220288 | bytes 67108864 | tf_op jit(solution)/shard_map/pallas_call | solution.py:611
  533.5 10.5 all-gather.12.cloned.1.call-done
  544.0 60.3 %shard_map.307 = (f32[1024,2048]{1,0:T(8,128)}, f32[1024,2048]{1,0:T(8,128)}, f32[2,2,1024]{2,1,0:T(2,128)}) custom-call(bf16[2048,1024]{1,0:T(8,128)(2,1)} %copy.209.inputs_ref, bf16[2048,1024]{1,0:T(8,128)(2,1)} %bitcast.232, f32[2,2,1024]{2,1,0:T(2,128)} %slice.137.gate_ref, bf16[2,1408,2048]{2,1,0:T(8,128)(2,1)} %bitcast.248, ...), custom_call_target="tpu_custom_call" | custom-call | flops 53150220288 | bytes 67108864 | tf_op jit(solution)/shard_map/pallas_call | solution.py:611
  605.5 117.6 %shard_map.308 = bf16[1024,2176]{1,0:T(8,128)(2,1)S(1)} custom-call(f32[1024,2048]{1,0:T(8,128)} %get-tuple-element.38.refs_0_, bf16[1024,128]{1,0:T(8,128)(2,1)S(1)} %concatenate.53.refs_1_), custom_call_target="tpu_custom_call" | custom-call | bytes 314572800 | tf_op jit(solution)/shard_map/pallas_call | solution.py:350
  726.0 3.4 copy-done.19
  729.4 2.2 fusion.62
  732.5 10.6 multiply_reduce_fusion
  743.2 1.8 copy-done.20
  745.0 4.4 convert_add_fusion.1
  749.5 2.2 fusion.67
  751.9 2.8 fusion.46
  755.0 1.7 fusion.55
  756.8 5.3 fusion.52
  762.0 1.9 fusion.48
  764.7 6.3 fusion.56
  771.0 2.1 add_convert_fusion.2.refs_3_
  773.2 114.2 %shard_map.309 = (bf16[1024,2048]{1,0:T(8,128)(2,1)}, bf16[3,1024,512]{2,1,0:T(8,128)(2,1)}) custom-call(f32[1024,2048]{1,0:T(8,128)} %get-tuple-element.34.wide_ref, bf16[1024,512]{1,0:T(8,128)(2,1)} %copy-done.8, bf16[1024,512]{1,0:T(8,128)(2,1)} %copy-done.9, bf16[1024,512]{1,0:T(8,128)(2,1)} %copy-done.10, bf16[1024,512]{1,0:T(8,128)(2,1)} %add_convert_fusion.2.refs_3_, ...), custom_call_target="tpu_custom_call" | custom-call | bytes 314572800 | tf_op jit(solution)/shard_map/pallas_call | solution.py:530
  887.4 3.0 fusion.61
  890.5 10.8 %fusion.27.refs_0_ = f32[1024,2048]{1,0:T(8,128)} fusion(bf16[3,1024,512]{2,1,0:T(8,128)(2,1)S(1)} %copy-done.29, bf16[2048,4,512]{0,2,1:T(8,128)(2,1)} %all-gather.10.cloned.1.call-done), kind=kOutput, calls=%fused_computation.54 | convolution fusion | flops 6442450944 | bytes 17825792 | tf_op jit(solution)/shard_map/stf,rsf->tr/dot_general | solution.py:855
  901.9 113.1 %shard_map.310 = bf16[1024,2176]{1,0:T(8,128)(2,1)S(1)} custom-call(f32[1024,2048]{1,0:T(8,128)} %fusion.27.refs_0_, bf16[1024,128]{1,0:T(8,128)(2,1)S(1)} %concatenate.56.refs_1_), custom_call_target="tpu_custom_call" | custom-call | bytes 314572800 | tf_op jit(solution)/shard_map/pallas_call | solution.py:350
  1016.2 10.9 %all-gather = bf16[128,3584]{1,0:T(8,128)(2,1)S(1)} all-gather(bf16[16,3584]{1,0:T(8,128)(2,1)S(1)} %pad_maximum_fusion.4), channel_id=2, replica_groups=mesh['dp'=8,'tensor'=4] {'dp'}, dimensions={0}, use_global_device_ids=true | all-gather | bytes 1032192 | tf_op jit(solution)/shard_map/all_gather | solution.py:876
  1028.2 1.6 copy.224
  1029.8 1.3 copy.225
  1031.1 5.2 fusion.14
  1036.4 6.3 add_convert_fusion.1
  1043.9 6.4 fusion.9
  1050.4 2.8 fusion.41
  1053.8 1.6 copy.227
  1055.4 1.6 copy.228
  1056.9 1.6 copy.231
  1058.5 1.8 copy.229
  (272 shorter events, 33.8 us)
Async XLA Ops:
  7.2 26.0 %copy-start = (bf16[8,16,2,1408]{3,2,1,0:T(2,128)(2,1)S(1)}, bf16[8,16,2,1408]{3,2,1,0:T(2,128)(2,1)}, u32[]{:S(2)}) copy-start(bf16[8,16,2,1408]{3,2,1,0:T(2,128)(2,1)} %param.45) | copy-start | bytes 2162692
  7.2 62.6 %all-gather.10.cloned.1.call-start = ((), (), s32[]{:S(2)}) async-start(), calls=%async_computation | async-start | bytes 9437184 | tf_op jit(solution)/shard_map/all_gather | solution.py:654
  11.0 254.4 %all-gather.20.cloned.1.call-start = ((), (), s32[]{:S(2)}) async-start(), calls=%async_computation.5 | async-start | bytes 19464192 | tf_op jit(solution)/shard_map/all_gather | solution.py:654
  13.9 336.0 %all-gather.18.cloned.1.call-start = ((), (), s32[]{:S(2)}) async-start(), calls=%async_computation.4 | async-start | bytes 25952256 | tf_op jit(solution)/shard_map/all_gather | solution.py:795
  17.5 432.5 %all-gather.14.cloned.1.call-start = ((), (), s32[]{:S(2)}) async-start(), calls=%async_computation.2 | async-start | bytes 12976128 | tf_op jit(solution)/shard_map/all_gather | solution.py:730
  20.7 5.3 copy-start.66
  20.7 8.4 copy-start.67
  20.7 10.4 copy-start.70
  20.7 451.7 %all-gather.16.cloned.1.call-start = ((), (), s32[]{:S(2)}) async-start(), calls=%async_computation.3 | async-start | bytes 12976128 | tf_op jit(solution)/shard_map/all_gather | solution.py:795
  24.7 7.6 copy-start.68
  24.7 8.6 copy-start.71
  24.7 8.7 copy-start.65
  24.7 19.5 %copy-start.60 = (s32[1024,4]{0,1:T(4,128)S(1)}, s32[1024,4]{0,1:T(4,128)}, u32[]{:S(2)}) copy-start(s32[1024,4]{0,1:T(4,128)} %param.37) | copy-start | bytes 49156
  24.7 519.3 %all-gather.12.cloned.1.call-start = ((), (), s32[]{:S(2)}) async-start(), calls=%async_computation.1 | async-start | bytes 12976128 | tf_op jit(solution)/shard_map/all_gather | solution.py:795
  25.3 1025.1 %all-gather.22.cloned.1.call-start = ((), (), s32[]{:S(2)}) async-start(), calls=%async_computation.6 | async-start | bytes 3133440 | tf_op jit(solution)/shard_map/all_gather | solution.py:876
  26.0 43.8 %copy-start.44 = (f32[2048]{0:T(1024)}, f32[2048]{0:T(1024)S(1)}, u32[]{:S(2)}) copy-start(f32[2048]{0:T(1024)S(1)} %convert_element_type.136) | copy-start | bytes 24580
  29.1 40.7 %copy-start.56 = (f32[1024]{0:T(1024)}, f32[1024]{0:T(1024)S(1)}, u32[]{:S(2)}) copy-start(f32[1024]{0:T(1024)S(1)} %fusion.135) | copy-start | bytes 12292
  31.2 54.0 %copy-start.11 = (s32[1024]{0:T(1024)}, s32[1024]{0:T(1024)S(1)}, u32[]{:S(2)}) copy-start(s32[1024]{0:T(1024)S(1)} %broadcast_add_fusion) | copy-start | bytes 12292
  32.3 208.8 %copy-start.40 = (f32[2048]{0:T(1024)}, f32[2048]{0:T(1024)S(1)}, u32[]{:S(2)}) copy-start(f32[2048]{0:T(1024)S(1)} %convert_element_type.141) | copy-start | bytes 24580
  33.1 210.8 %copy-start.33 = (bf16[2048,16]{0,1:T(8,128)(2,1)}, bf16[2048,16]{0,1:T(8,128)(2,1)S(1)}, u32[]{:S(2)}) copy-start(bf16[2048,16]{0,1:T(8,128)(2,1)S(1)} %dynamic-slice_bitcast_fusion) | copy-start | bytes 196612
  44.1 195.7 %copy-start.31 = (bf16[2048,18]{0,1:T(8,128)(2,1)}, bf16[2048,18]{0,1:T(8,128)(2,1)S(1)}, u32[]{:S(2)}) copy-start(bf16[2048,18]{0,1:T(8,128)(2,1)S(1)} %all_gather.34) | copy-start | bytes 221188
  55.6 24.8 %copy-start.38 = (bf16[1024,16,1]{0,1,2:T(8,128)(2,1)}, bf16[1024,16,1]{0,1,2:T(8,128)(2,1)S(1)}, u32[]{:S(2)}) copy-start(bf16[1024,16,1]{0,1,2:T(8,128)(2,1)S(1)} %fusion.72) | copy-start | bytes 98308
  56.8 28.5 %copy-start.5 = (f32[1024,128]{1,0:T(8,128)}, f32[1024,128]{1,0:T(8,128)S(1)}, u32[]{:S(2)}) copy-start(f32[1024,128]{1,0:T(8,128)S(1)} %get-tuple-element.119.cosine_ref.refs_4_) | copy-start | bytes 1572868
  102.7 8.5 copy-start.3
  111.2 123.5 %copy-start.22 = (bf16[1024,2048]{1,0:T(8,128)(2,1)S(1)}, bf16[1024,2048]{1,0:T(8,128)(2,1)}, u32[]{:S(2)}) copy-start(bf16[1024,2048]{1,0:T(8,128)(2,1)} %param.24) | copy-start | bytes 12582916
  245.1 69.9 %copy-start.58 = (f32[1024]{0:T(1024)}, f32[1024]{0:T(1024)S(1)}, u32[]{:S(2)}) copy-start(f32[1024]{0:T(1024)S(1)} %add_divide_fusion) | copy-start | bytes 12292
  245.3 8.7 copy-start.25
  245.7 8.3 copy-start.48
  255.7 7.6 copy-start.17
  265.4 38.8 %copy-start.72 = (bf16[1024,16]{0,1:T(8,128)(2,1)}, bf16[1024,16]{0,1:T(8,128)(2,1)S(1)}, u32[]{:S(2)}) copy-start(bf16[1024,16]{0,1:T(8,128)(2,1)S(1)} %fusion.65) | copy-start | bytes 98308
  287.5 6.0 copy-start.18
  287.5 16.7 %slice-start.6 = ((s8[11534336]{0:T(1024)(128)(4,1)}), s8[4194304]{0:T(1024)(128)(4,1)S(1)}, s32[]{:S(2)}) async-start(s8[11534336]{0:T(1024)(128)(4,1)} %bitcast.222), calls=%async_computation.13 | async-start | bytes 8388608
  293.5 10.6 slice-start.7
  293.5 10.6 slice-start.8
  310.7 18.2 %slice-start.9 = ((s8[5767168]{0:T(1024)(128)(4,1)}), s8[4194304]{0:T(1024)(128)(4,1)S(1)}, s32[]{:S(2)}) async-start(s8[5767168]{0:T(1024)(128)(4,1)} %bitcast.227), calls=%async_computation.16 | async-start | bytes 8388608
  315.1 13.9 %slice-start.10 = ((s8[5767168]{0:T(1024)(128)(4,1)}), s8[1572864]{0:T(1024)(128)(4,1)S(1)}, s32[]{:S(2)}) async-start(s8[5767168]{0:T(1024)(128)(4,1)} %bitcast.227), calls=%async_computation.17 | async-start | bytes 3145728
  544.0 61.0 %copy-start.64 = (f32[2,2,1024]{2,1,0:T(2,128)S(1)}, f32[2,2,1024]{2,1,0:T(2,128)}, u32[]{:S(2)}) copy-start(f32[2,2,1024]{2,1,0:T(2,128)} %get-tuple-element.40) | copy-start | bytes 49156
  544.0 61.0 %copy-start.54 = (f32[4,2,1024]{2,1,0:T(2,128)S(1)}, f32[4,2,1024]{2,1,0:T(2,128)}, u32[]{:S(2)}) copy-start(f32[4,2,1024]{2,1,0:T(2,128)} %get-tuple-element.39) | copy-start | bytes 98308
  544.0 61.1 %copy-start.37 = (bf16[1024,16]{0,1:T(8,128)(2,1)S(1)}, bf16[1024,16]{0,1:T(8,128)(2,1)}, u32[]{:S(2)}) copy-start(bf16[1024,16]{0,1:T(8,128)(2,1)} %fusion.69) | copy-start | bytes 98308
  544.0 61.1 %copy-start.55 = (bf16[1024,16]{0,1:T(8,128)(2,1)S(1)}, bf16[1024,16]{0,1:T(8,128)(2,1)}, u32[]{:S(2)}) copy-start(bf16[1024,16]{0,1:T(8,128)(2,1)} %fusion.66) | copy-start | bytes 98308
  544.0 61.1 %copy-start.63 = (bf16[1024,1]{0,1:T(2,128)(2,1)S(1)}, bf16[1024,1]{0,1:T(2,128)(2,1)}, u32[]{:S(2)}) copy-start(bf16[1024,1]{0,1:T(2,128)(2,1)} %broadcast_in_dim.83) | copy-start | bytes 6148
  723.1 8.4 copy-start.2
  723.2 6.2 copy-start.19
  725.1 6.6 copy-start.21
  725.1 7.2 copy-start.51
  725.1 7.4 copy-start.32
  725.1 7.4 copy-start.34
  725.1 7.4 copy-start.41
  732.4 10.7 %slice-start = ((s8[8388608]{0:T(1024)(128)(4,1)}), s8[4194304]{0:T(1024)(128)(4,1)S(1)}, s32[]{:S(2)}) async-start(s8[8388608]{0:T(1024)(128)(4,1)} %bitcast.216), calls=%async_computation.7 | async-start | bytes 8388608
  732.5 10.7 copy-start.62
  732.5 10.7 slice-start.1
  732.5 12.5 %copy-start.20 = (bf16[1024,2048]{1,0:T(8,128)(2,1)S(1)}, bf16[1024,2048]{1,0:T(8,128)(2,1)}, u32[]{:S(2)}) copy-start(bf16[1024,2048]{1,0:T(8,128)(2,1)} %param.25) | copy-start | bytes 12582916
  732.5 12.5 %copy-start.47 = (f32[1024]{0:T(1024)S(1)}, f32[1024]{0:T(1024)}, u32[]{:S(2)}) copy-start(f32[1024]{0:T(1024)} %copy-done.46) | copy-start | bytes 12292
  749.5 5.3 copy-start.16
  890.5 10.9 %copy-start.39 = (bf16[1024,16,1]{0,1,2:T(8,128)(2,1)S(1)}, bf16[1024,16,1]{0,1,2:T(8,128)(2,1)}, u32[]{:S(2)}) copy-start(bf16[1024,16,1]{0,1,2:T(8,128)(2,1)} %copy-done.38) | copy-start | bytes 98308
  901.9 113.2 %copy-start.23 = (bf16[1024,2048]{1,0:T(8,128)(2,1)S(1)}, bf16[1024,2048]{1,0:T(8,128)(2,1)}, u32[]{:S(2)}) copy-start(bf16[1024,2048]{1,0:T(8,128)(2,1)} %param.24) | copy-start | bytes 12582916
  901.9 113.2 %copy-start.45 = (f32[2048]{0:T(1024)S(1)}, f32[2048]{0:T(1024)}, u32[]{:S(2)}) copy-start(f32[2048]{0:T(1024)} %copy-done.44) | copy-start | bytes 24580
  901.9 113.2 %copy-start.57 = (f32[1024]{0:T(1024)S(1)}, f32[1024]{0:T(1024)}, u32[]{:S(2)}) copy-start(f32[1024]{0:T(1024)} %copy-done.56) | copy-start | bytes 12292
  1015.1 12.1 %copy-start.69 = (s32[8]{0:T(128)S(1)}, s32[8]{0:T(128)}, u32[]{:S(2)}) copy-start(s32[8]{0:T(128)} %bitcast_convert_fusion) | copy-start | bytes 100
  1028.2 8.2 slice-start.2
  1036.4 6.4 slice-start.4
  1036.4 6.3 slice-start.5
  1036.4 7.5 copy-start.24
  1053.7 8.5 copy-start.1
  (28 other events, 87.8 us)
Sparse Core Ops, SparseCore 0:
  11.1 58.6 all-gather.9
  71.7 133.4 all-gather.19
  207.0 121.3 all-gather.17
  330.7 69.9 all-gather.13
  402.4 69.8 all-gather.15
  474.1 69.8 all-gather.11
  764.8 28.9 all-gather.21

commit v4 on v3

--- a/solution.py
+++ b/solution.py
@@ -23,8 +23,6 @@
 MESH = pl.DeviceIdType.MESH
 SUM_CHUNKS = 16
 AHEAD = 2
-GATHER_PIECES = 16
-PAIR = 2
 EXPERT_PARTS = (8, 4, 4)
 
 
@@ -243,17 +241,21 @@
             send("y_x", piece).wait_recv()
             send("yx_core", piece).start()
 
+    def arrive(piece):
+        @pl.when(piece == 0)
+        def _():
+            own().wait()
+
+        for name in ("core", "x_core", "y_core", "xy_core", "yx_core"):
+            send(name, piece).wait_recv()
+
     def finish():
-        own().wait()
-
         @pl.loop(0, pieces)
         def _(piece):
             for name in order:
                 send(name, piece).wait_send()
-            for name in ("core", "x_core", "y_core", "xy_core", "yx_core"):
-                send(name, piece).wait_recv()
-
-    return greet, begin, advance, finish
+
+    return greet, begin, advance, arrive, finish
 
 
 def line_sum_kernel(chunks, *refs):
@@ -269,26 +271,145 @@
 
 
 def sum_gather_kernel(
-    chunks, pieces, wide_ref, narrow_ref, block_ref, total_ref, whole_ref, *scratch
+    chunks,
+    pieces,
+    wide_ref,
+    narrow_ref,
+    block_ref,
+    cotangent_ref,
+    total_ref,
+    whole_ref,
+    open_ref,
+    *scratch,
 ):
     greet, begin, advance, finish = line_sum_steps(
         chunks, wide_ref, narrow_ref, total_ref, *scratch[:5]
     )
-    gather_semaphores, local_semaphore = scratch[5:]
-    gather_greet, gather_begin, gather_advance, gather_finish = plane_gather_steps(
-        pieces, block_ref, whole_ref, gather_semaphores, local_semaphore.at[0]
-    )
+    gather_semaphores, local_semaphores, piece_rows, open_rows = scratch[5:]
+    gather_greet, gather_begin, gather_advance, gather_arrive, gather_finish = plane_gather_steps(
+        pieces, block_ref, whole_ref, gather_semaphores, local_semaphores.at[0]
+    )
+    rows = piece_rows.shape[1]
+
+    def load(piece):
+        slot = piece % 2
+        span = pl.ds(pl.multiple_of(piece * rows, rows), rows)
+        return pltpu.make_async_copy(
+            whole_ref.at[span], piece_rows.at[slot], local_semaphores.at[1 + slot]
+        )
+
+    def store(piece):
+        slot = piece % 2
+        span = pl.ds(pl.multiple_of(piece * rows, rows), rows)
+        return pltpu.make_async_copy(
+            open_rows.at[slot], open_ref.at[span], local_semaphores.at[3 + slot]
+        )
+
     gather_greet()
     greet(3)
     begin()
     gather_begin()
 
-    @pl.loop(0, max(chunks + 1, pieces + 2 * AHEAD))
+    @pl.loop(0, max(chunks + 1, pieces + 3 * AHEAD + 1))
     def _(step):
         gather_advance(step)
         advance(step)
 
+        @pl.when((step >= 3 * AHEAD) & (step < pieces + 3 * AHEAD))
+        def _():
+            gather_arrive(step - 3 * AHEAD)
+            load(step - 3 * AHEAD).start()
+
+        @pl.when((step > 3 * AHEAD) & (step <= pieces + 3 * AHEAD))
+        def _():
+            piece = step - 3 * AHEAD - 1
+            load(piece).wait()
+
+            @pl.when(piece >= 2)
+            def _():
+                store(piece - 2).wait()
+
+            open_rows[piece % 2] = to_low(matmul(piece_rows[piece % 2], cotangent_ref[...]))
+            store(piece).start()
+
+    store(pieces - 2).wait()
+    store(pieces - 1).wait()
     gather_finish()
+    finish()
+
+
+def sum_down_kernel(
+    chunks,
+    wide_ref,
+    narrow_ref,
+    start_ref,
+    down_ref,
+    *refs,
+):
+    act_refs, (total_ref, out_ref), scratch = refs[:-11], refs[-11:-9], refs[-9:]
+    greet, begin, advance, finish = line_sum_steps(
+        chunks, wide_ref, narrow_ref, total_ref, *scratch[:5]
+    )
+    semaphores, act_rows, down_rows, out_rows = scratch[5:]
+    rows = act_rows.shape[1]
+    blocks = down_ref.shape[0] // rows
+
+    def load_down(block):
+        slot = block % 2
+        span = pl.ds(pl.multiple_of(block * rows, rows), rows)
+        return pltpu.make_async_copy(
+            down_ref.at[span], down_rows.at[slot], semaphores.at[1, slot]
+        )
+
+    def load_act(act_ref, block, slot):
+        span = pl.ds(pl.multiple_of(block * rows, rows), rows)
+        return pltpu.make_async_copy(act_ref.at[span], act_rows.at[slot], semaphores.at[0, slot])
+
+    def load_start(block):
+        load_down(block).start()
+        first = 0
+        for act_ref in act_refs:
+            count = act_ref.shape[0] // rows
+            from_here = block - first
+
+            @pl.when((from_here >= 0) & (from_here < count))
+            def _():
+                load_act(act_ref, from_here, block % 2).start()
+
+            first += count
+
+    def load_wait(block):
+        load_down(block).wait()
+        load_act(act_refs[0], 0, block % 2).wait()
+
+    first = pltpu.make_async_copy(start_ref, out_rows, semaphores.at[2, 0])
+    first.start()
+    load_start(0)
+    greet(0)
+    begin()
+    first.wait()
+
+    @pl.loop(0, max(blocks, chunks + 1))
+    def _(step):
+        advance(step)
+
+        @pl.when(step < blocks)
+        def _():
+            @pl.when(step + 1 < blocks)
+            def _():
+                load_start(step + 1)
+
+            load_wait(step)
+            tile = min(256, out_rows.shape[0])
+
+            @pl.loop(0, out_rows.shape[0] // tile)
+            def _(index):
+                span = pl.ds(pl.multiple_of(index * tile, tile), tile)
+                out_rows[span] += contract_first(
+                    act_rows[step % 2, :, span], down_rows[step % 2]
+                )
+
+    out_ref[...] = to_low(out_rows[...])
     finish()
 
 
@@ -361,28 +482,69 @@
     return parts_of(total, wide_part, narrow_part)
 
 
-def summed_and_gathered(wide_part, narrow_part, block, number):
+def summed_and_gathered(wide_part, narrow_part, block, cotangents, number):
+    length, width = wide_part.shape
     if not (on_line() and in_plane()):
         whole = lax.all_gather(block, "dp", axis=1, tiled=True)
-        return summed(wide_part, narrow_part, number) + (whole,)
-    shape = (wide_part.shape[0], wide_part.shape[1] + NARROW)
-    pieces = GATHER_PIECES
-    total, whole = pl.pallas_call(
+        open_rows = to_low(matmul(whole, cotangents))
+        return summed(wide_part, narrow_part, number) + (whole, open_rows)
+    shape = (length, width + NARROW)
+    pieces = EXPERTS
+    rows = block.shape[0] // pieces
+    in_hbm = pl.BlockSpec(memory_space=pltpu.HBM)
+    total, whole, open_rows = pl.pallas_call(
         functools.partial(sum_gather_kernel, SUM_CHUNKS, pieces),
         out_shape=[
             jax.ShapeDtypeStruct(shape, jnp.bfloat16),
-            jax.ShapeDtypeStruct((block.shape[0], 8 * block.shape[1]), jnp.bfloat16),
+            jax.ShapeDtypeStruct((block.shape[0], width), jnp.bfloat16),
+            jax.ShapeDtypeStruct((block.shape[0], length), jnp.bfloat16),
         ],
-        in_specs=in_vmem(2) + [pl.BlockSpec(memory_space=pltpu.HBM)],
-        out_specs=[pl.BlockSpec(memory_space=pltpu.VMEM), pl.BlockSpec(memory_space=pltpu.HBM)],
+        in_specs=in_vmem(2) + [in_hbm] + in_vmem(1),
+        out_specs=in_vmem(1) + [in_hbm] * 2,
         scratch_shapes=sum_scratch(shape)
-        + [pltpu.SemaphoreType.DMA((18, pieces)), pltpu.SemaphoreType.DMA((1,))],
+        + [
+            pltpu.SemaphoreType.DMA((18, pieces)),
+            pltpu.SemaphoreType.DMA((5,)),
+            pltpu.VMEM((2, rows, width), jnp.bfloat16),
+            pltpu.VMEM((2, rows, length), jnp.bfloat16),
+        ],
         compiler_params=pltpu.CompilerParams(
-            collective_id=number, has_side_effects=True, vmem_limit_bytes=48 * 2**20
+            collective_id=number, has_side_effects=True, vmem_limit_bytes=58 * 2**20
         ),
         cost_estimate=pl.CostEstimate(flops=0, bytes_accessed=360 * 2**20, transcendentals=0),
-    )(wide_part, narrowed(narrow_part), block)
-    return parts_of(total, wide_part, narrow_part) + (whole,)
+    )(wide_part, narrowed(narrow_part), block, cotangents)
+    return parts_of(total, wide_part, narrow_part) + (whole, open_rows)
+
+
+def summed_and_down(wide_part, narrow_part, start, act_parts, down_rows, number):
+    length, width = wide_part.shape
+    if not on_line():
+        out = start + contract_first(jnp.concatenate(act_parts, axis=0), down_rows)
+        return summed(wide_part, narrow_part, number) + (out,)
+    shape = (length, width + NARROW)
+    rows = 2 * down_rows.shape[0] // EXPERTS
+    in_hbm = pl.BlockSpec(memory_space=pltpu.HBM)
+    total, out = pl.pallas_call(
+        functools.partial(sum_down_kernel, SUM_CHUNKS),
+        out_shape=[
+            jax.ShapeDtypeStruct(shape, jnp.bfloat16),
+            jax.ShapeDtypeStruct((length, width), jnp.bfloat16),
+        ],
+        in_specs=in_vmem(2) + [in_hbm] * (2 + len(act_parts)),
+        out_specs=in_vmem(2),
+        scratch_shapes=sum_scratch(shape)
+        + [
+            pltpu.SemaphoreType.DMA((3, 2)),
+            pltpu.VMEM((2, rows, length), jnp.bfloat16),
+            pltpu.VMEM((2, rows, width), jnp.bfloat16),
+            pltpu.VMEM((length, width), jnp.float32),
+        ],
+        compiler_params=pltpu.CompilerParams(
+            collective_id=number, has_side_effects=True, vmem_limit_bytes=58 * 2**20
+        ),
+        cost_estimate=pl.CostEstimate(flops=0, bytes_accessed=300 * 2**20, transcendentals=0),
+    )(wide_part, narrowed(narrow_part), start, down_rows, *act_parts)
+    return parts_of(total, wide_part, narrow_part) + (out,)
 
 
 def block_mask(first, rows, extent, row_piece_ref, col_piece_ref):
@@ -544,106 +706,83 @@
 
 
 def experts_kernel(
-    tile,
     inputs_ref,
-    cotangent_ref,
     gate_ref,
     up_ref,
-    down_ref,
-    out_start,
+    open_ref,
     grad_start,
-    out_ref,
     grad_ref,
+    act_ref,
     gate_grad_ref,
-    act_rows,
     grad_rows,
-    semaphores,
+    semaphore,
 ):
     @pl.when(pl.program_id(0) == 0)
     def _():
-        loads = [
-            pltpu.make_async_copy(out_start, out_ref, semaphores.at[0]),
-            pltpu.make_async_copy(grad_start, grad_ref, semaphores.at[1]),
-        ]
-        for load in loads:
-            load.start()
-        for load in loads:
-            load.wait()
-
-    pair = gate_ref.shape[1]
-    hidden = down_ref.shape[1] // pair
-
-    @pl.loop(0, inputs_ref.shape[1] // tile)
-    def _(index):
-        column = pl.ds(pl.multiple_of(index * tile, tile), tile)
-        inputs = inputs_ref[:, column]
-        cotangents = cotangent_ref[:, column]
-        for member in range(pair):
-            gate_from, up_from = 2 * hidden * member, 2 * hidden * member + hidden
-            gate_up = matmul(up_ref[0, gate_from : gate_from + 2 * hidden], inputs)
-            open_part = matmul(down_ref[0, hidden * member : hidden * (member + 1)], cotangents)
-            gate_half, up_half = gate_up[:hidden], gate_up[hidden:]
-            squashed = 1.0 / (1.0 + jnp.exp(-gate_half))
-            act = to_low(gate_half * squashed * up_half).astype(jnp.float32)
-            gate_row = gate_ref[0, member : member + 1, column]
-            gate_grad_ref[0, member : member + 1, column] = jnp.sum(
-                act * open_part, axis=0, keepdims=True
-            )
-            act_rows[hidden * member : hidden * (member + 1)] = to_low(gate_row * act)
-            grad_act = gate_row * open_part
-            grad_rows[gate_from : gate_from + hidden] = to_low(
-                grad_act * up_half * squashed * (1.0 + gate_half * (1.0 - squashed))
-            )
-            grad_rows[up_from : up_from + hidden] = to_low(grad_act * gate_half * squashed)
-        out_ref[column] += contract_first(act_rows[...], down_ref[0])
-        grad_ref[column] += contract_first(grad_rows[...], up_ref[0])
-
-
-def experts_step(inputs, cotangents, gates, up_rows, down_rows, out_start, grad_start, first):
-    groups, pair, length = up_rows.shape[0], gates.shape[1], inputs.shape[1]
-    width, hidden = inputs.shape[0], down_rows.shape[1] // gates.shape[1]
-    tile = min(512, length)
+        load = pltpu.make_async_copy(grad_start, grad_ref, semaphore.at[0])
+        load.start()
+        load.wait()
+
+    hidden = open_ref.shape[1]
+    gate_up = matmul(up_ref[0], inputs_ref[...])
+    open_part = open_ref[0].astype(jnp.float32)
+    gate_half, up_half = gate_up[:hidden], gate_up[hidden:]
+    squashed = 1.0 / (1.0 + jnp.exp(-gate_half))
+    act = to_low(gate_half * squashed * up_half).astype(jnp.float32)
+    gate_row = gate_ref[0]
+    gate_grad_ref[0] = jnp.sum(act * open_part, axis=0, keepdims=True)
+    act_ref[0] = to_low(gate_row * act)
+    grad_act = gate_row * open_part
+    grad_rows[:hidden] = to_low(
+        grad_act * up_half * squashed * (1.0 + gate_half * (1.0 - squashed))
+    )
+    grad_rows[hidden:] = to_low(grad_act * gate_half * squashed)
+    grad_ref[...] += contract_first(grad_rows[...], up_ref[0])
+
+
+def experts_step(inputs, gates, up_rows, open_rows, grad_start, first):
+    count, length, width = up_rows.shape[0], inputs.shape[1], inputs.shape[0]
+    hidden = open_rows.shape[1]
     once = pl.Buffered(1)
 
     def still(shape):
-        return pl.BlockSpec(shape, lambda group: (0, 0), pipeline_mode=once)
+        return pl.BlockSpec(shape, lambda expert: (0, 0), pipeline_mode=once)
+
+    def here(rows):
+        return pl.BlockSpec((1, rows, length), lambda expert: (expert, 0, 0))
+
+    def ahead(rows):
+        return pl.BlockSpec((1, rows, length), lambda expert: (expert + first, 0, 0))
 
     return pl.pallas_call(
-        functools.partial(experts_kernel, tile),
-        grid=(groups,),
+        experts_kernel,
+        grid=(count,),
         in_specs=[
             still((width, length)),
-            still((width, length)),
-            pl.BlockSpec((1, pair, length), lambda group: (group, 0, 0)),
-            pl.BlockSpec((1, 2 * pair * hidden, width), lambda group: (group, 0, 0)),
-            pl.BlockSpec((1, pair * hidden, width), lambda group: (group + first, 0, 0)),
-            pl.BlockSpec(memory_space=pltpu.HBM),
+            ahead(1),
+            pl.BlockSpec((1, 2 * hidden, width), lambda expert: (expert, 0, 0)),
+            ahead(hidden),
             pl.BlockSpec(memory_space=pltpu.HBM),
         ],
-        out_specs=[
-            still((length, width)),
-            still((length, width)),
-            pl.BlockSpec((1, pair, length), lambda group: (group, 0, 0)),
-        ],
+        out_specs=[still((length, width)), here(hidden), here(1)],
         out_shape=[
             jax.ShapeDtypeStruct((length, width), jnp.float32),
-            jax.ShapeDtypeStruct((length, width), jnp.float32),
-            jax.ShapeDtypeStruct((groups, pair, length), jnp.float32),
+            jax.ShapeDtypeStruct((count, hidden, length), jnp.bfloat16),
+            jax.ShapeDtypeStruct((count, 1, length), jnp.float32),
         ],
         scratch_shapes=[
-            pltpu.VMEM((pair * hidden, tile), jnp.bfloat16),
-            pltpu.VMEM((2 * pair * hidden, tile), jnp.bfloat16),
-            pltpu.SemaphoreType.DMA((2,)),
+            pltpu.VMEM((2 * hidden, length), jnp.bfloat16),
+            pltpu.SemaphoreType.DMA((1,)),
         ],
         compiler_params=pltpu.CompilerParams(
-            vmem_limit_bytes=60 * 2**20, dimension_semantics=("arbitrary",)
+            vmem_limit_bytes=58 * 2**20, dimension_semantics=("arbitrary",)
         ),
         cost_estimate=pl.CostEstimate(
-            flops=18 * groups * pair * hidden * width * length,
-            bytes_accessed=64 * 2**20,
+            flops=12 * count * hidden * width * length,
+            bytes_accessed=32 * 2**20,
             transcendentals=0,
         ),
-    )(inputs, cotangents, gates, up_rows, down_rows, out_start, grad_start)
+    )(inputs, gates, up_rows, open_rows, grad_start)
 
 
 def swiglu(paired):
@@ -720,21 +859,20 @@
     query, keys, values, attended = attend(qkv_sum, *places)
     branch_part = contract_last(attended, output_rows)
     down_block = jnp.transpose(routed_down_weight, (1, 2, 0))
-    early = EXPERT_PARTS[0]
-    branch_here, mid_out_here_f, down_early = summed_and_gathered(
+    branch_here, mid_out_here_f, down_rows, open_rows = summed_and_gathered(
         branch_part,
         matmul(attended, out_a),
-        down_block[:early].reshape(-1, down_block.shape[2]),
+        down_block.reshape(-1, down_block.shape[2]),
+        cotangent.T,
         1,
     )
-    down_late = lax.all_gather(down_block[early:], "dp", axis=2, tiled=True)
-    mid_out_here = to_low(mid_out_here_f)
-    hidden_here = tokens_f + branch_here + ADAPTER_SCALE * matmul(mid_out_here, out_b)
+    mid_out = to_low(mid_out_here_f)
+    hidden_here = tokens_f + branch_here + ADAPTER_SCALE * matmul(mid_out, out_b)
     normed_two_here_f, norm_ffn_pull = jax.vjp(
         lambda rows: rms_scale(rows, gain_ffn_f), hidden_here
     )
     normed_two_here = to_low(normed_two_here_f)
-    normed_two, mid_out = (normed_two_here, mid_out_here)
+    normed_two = normed_two_here
     cot_f = cotangent.astype(jnp.float32)
     shared_three = gathered(
         jnp.concatenate([shared_expert_gate_up_weight, shared_expert_down_weight[:, None]], axis=1)
@@ -785,24 +923,23 @@
     )
 
     up_block = jnp.transpose(routed_gate_up_weight, (1, 2, 3, 0))
-    inputs_t, cotangents_t = normed_two.T, cotangent.T
-    gates = gate_table.reshape(EXPERTS // PAIR, PAIR, length)
-    down_early = down_early.reshape(early // PAIR, -1, width)
-    down_late = down_late.reshape((EXPERTS - early) // PAIR, -1, width)
+    inputs_t = normed_two.T
+    gates = gate_table.reshape(EXPERTS, 1, length)
+    open_rows = open_rows.reshape(EXPERTS, -1, length)
     gate_grad_parts = []
+    act_parts = []
     first = 0
     for count in EXPERT_PARTS:
         up_rows = lax.all_gather(up_block[first : first + count], "dp", axis=3, tiled=True)
-        combined_part, normed_two_part, gate_grads = experts_step(
+        normed_two_part, act_part, gate_grads = experts_step(
             inputs_t,
-            cotangents_t,
-            gates[first // PAIR : (first + count) // PAIR],
-            up_rows.reshape(count // PAIR, -1, width),
-            down_early if first < early else down_late,
-            combined_part,
+            gates,
+            up_rows.reshape(count, -1, width),
+            open_rows,
             normed_two_part,
-            (first if first < early else first - early) // PAIR,
+            first,
         )
+        act_parts.append(act_part.reshape(-1, length))
         gate_grad_parts.append(gate_grads.reshape(count, length))
         first += count
     gate_grad_part = jnp.concatenate(gate_grad_parts, axis=0).T
@@ -815,7 +952,9 @@
         ],
         axis=1,
     )
-    grad_normed_two, narrow_sum = summed(normed_two_part, narrow_part, 2)
+    grad_normed_two, narrow_sum, combined_part = summed_and_down(
+        normed_two_part, narrow_part, combined_part, act_parts, down_rows, 2
+    )
     rank = up_a.shape[1]
     mid_down = to_low(narrow_sum[:, EXPERTS + 1 + rank :])
     grad_mid_up = to_low(narrow_sum[:, EXPERTS + 1 : EXPERTS + 1 + rank])

time: 1070 us -> 1060 us (level)
  waiting for transfers between devices: 46.5 us -> 18.3 us
    pallas_call x2 -> x1, Pallas kernels: 231 us -> 110 us  [summed(): pl.pallas_call(functools.partial(line_sum_kernel, SUM_CHUNKS), out_shape=...]
    pallas_call x1, Pallas kernels: 123 us -> 216 us  [summed_and_gathered(): pl.pallas_call(functools.partial(sum_gather_kernel, SUM_CHUNKS, pieces),...]
    pallas_call x3 -> x4, Pallas kernels: 221 us -> 264 us  [the longest x3 148 us: experts_step(): pl.pallas_call(experts_kernel, grid=(count,), in_specs=[still((width, len...]
    all_gather x3, waiting for transfers between devices: 32.9 us -> 0.04 us  [body(): lax.all_gather(up_block[first:first + count], 'dp', axis=3, tiled=True)]
    unnamed x183 -> x180, local copies, waits for them, and re-layouts: 33.1 us -> 28.2 us
  transfers between devices with their start and end apart: 7 -> 6, of which waited for: 3 -> 1; matrix products, arithmetic and copies ran while one was open for 20% -> 20% of each run, Pallas kernels for 49% -> 53%
where the time goes in v4:
time: 1060 us; the launch traced here: 1050 us
  Pallas kernels  714 us (67%)
  matrix products  193 us (18%)
  local copies, waits for them, and re-layouts  50.3 us (5%)
  other arithmetic  31.9 us (3%)
  blocking collectives  25.6 us (2%)
  waiting for transfers between devices  18.3 us (2%)
  between operations  16.4 us (2%)
    pallas_call x1, Pallas kernels, summed_and_gathered(): pl.pallas_call(functools.partial(sum_gather_kernel, SUM_CHUNKS, pieces),...  216 us
    pallas_call x3, Pallas kernels, experts_step(): pl.pallas_call(experts_kernel, grid=(count,), in_specs=[still((width, len...  148 us
    pallas_call x1, Pallas kernels, summed_and_down(): pl.pallas_call(functools.partial(sum_down_kernel, SUM_CHUNKS), out_shape=...  116 us
    pallas_call x1, Pallas kernels, summed(): pl.pallas_call(functools.partial(line_sum_kernel, SUM_CHUNKS), out_shape=...  110 us
    pallas_call x1, Pallas kernels, summed_and_attended_back(): pl.pallas_call(functools.partial(attend_back_sum_kernel, SUM_CHUNKS), out...  109 us
    dot_general x9, matrix products, contract_last(): lax.dot_general(left_side, right_side, (((1,), (1,)), ((), ())), preferre...  49.6 us
    dot_general x10, matrix products, matmul(): return jnp.dot(left_side, right_side, preferred_element_type=jnp.float32)  38.3 us
    unnamed x180, local copies, waits for them, and re-layouts  28.2 us
  transfers between devices with their start and end apart: 6, of which 1 were waited for; matrix products, arithmetic and copies ran while one was open for 20% of the time, Pallas kernels for 53%

profile of v4, /device:TPU:0, one launch (start us, length us, event | category | flops | bytes accessed | tf_op | source)
XLA Modules:
  0.0 1049.6 jit_solution(14135035135039288935)
XLA Ops:
  7.2 1.5 copy.233
  11.2 2.7 pad_maximum_fusion
  13.9 3.7 slice.141
  17.7 3.5 fusion.164
  22.6 3.3 fusion.10
  26.0 1.9 fusion.77
  28.3 6.6 copy.238
  36.0 11.4 %all_gather.31 = bf16[2048,18]{0,1:T(8,128)(2,1)S(1)} all-gather(bf16[256,18]{0,1:T(8,128)(2,1)S(1)} %maximum_maximum_fusion), channel_id=1, replica_groups=mesh['dp'=8,'tensor'=4] {'dp'}, dimensions={0}, use_global_device_ids=true | all-gather | bytes 82944 | tf_op jit(solution)/shard_map/all_gather | solution.py:793
  48.4 3.5 fusion.72
  52.2 17.7 %all-gather.9.cloned.1.call-done = bf16[2048,4,512]{0,2,1:T(8,128)(2,1)} async-done(((bf16[256,4,512]{0,2,1:T(8,128)(2,1)}), bf16[2048,4,512]{0,2,1:T(8,128)(2,1)}) %all-gather.9.cloned.1.call-update) | async-done | bytes 8388624 | tf_op jit(solution)/shard_map/all_gather | solution.py:793
  69.9 10.7 %fusion.34 = f32[3,512,1024]{1,2,0:T(8,128)S(1)} fusion(bf16[2048,4,512]{0,2,1:T(8,128)(2,1)} %all-gather.9.cloned.1.call-done, bf16[1024,2048]{1,0:T(8,128)(2,1)} %param.24, f32[2048]{0:T(1024)S(1)} %convert_element_type.136, f32[1024]{0:T(1024)S(1)} %fusion.135), kind=kOutput, calls=%fused_computation.57 | convolution fusion | flops 6450839552 | bytes 18886656 | tf_op jit(solution)/shard_map/tr,rsf->stf/dot_general | solution.py:850
  80.5 4.6 add_bitcast_fusion.qkv_ref
  85.2 14.6 %shard_map.303 = (bf16[1024,512]{1,0:T(8,128)(2,1)S(1)}, bf16[1024,512]{1,0:T(8,128)(2,1)S(1)}, bf16[1024,512]{1,0:T(8,128)(2,1)S(1)}, bf16[1024,512]{1,0:T(8,128)(2,1)S(1)}) custom-call(f32[3,1024,512]{2,1,0:T(8,128)} %add_bitcast_fusion.qkv_ref, f32[1024,128]{1,0:T(8,128)S(1)} %get-tuple-element.131.cosine_ref.refs_4_, ...), custom_call_target="tpu_custom_call" | custom-call | flops 2147483648 | bytes 16777216 | tf_op jit(solution)/shard_map/pallas_call | solution.py:602
  104.7 7.2 fusion.57.wide_ref
  111.9 216.4 %shard_map.304 = (bf16[1024,2176]{1,0:T(8,128)(2,1)}, bf16[5632,2048]{1,0:T(8,128)(2,1)}, bf16[5632,1024]{1,0:T(8,128)(2,1)}) custom-call(f32[1024,2048]{1,0:T(8,128)} %fusion.57.wide_ref, bf16[1024,128]{1,0:T(8,128)(2,1)} %concatenate.48.narrow_ref, bf16[5632,256]{1,0:T(8,128)(2,1)} %bitcast.245, bf16[2048,1024]{1,0:T(8,128)(2,1)} %bitcast.234), custom_call_target="tpu_custom_call" | custom-call | bytes 377487360 | tf_op jit(solution)/shard_map/pallas_call | solution.py:495
  328.4 4.4 multiply_reduce_fusion.1
  333.6 1.2 fusion.129
  334.7 1.2 fusion.166
  336.1 2.8 fusion.190
  338.9 1.2 fusion.73
  341.9 6.8 copy.248.inputs_ref
  348.6 6.0 fusion.92
  354.6 2.1 fusion.65
  356.7 23.0 %multiply_add_fusion = f32[1024,2,1408]{2,0,1:T(8,128)} fusion(f32[1024,2,1408]{2,0,1:T(8,128)} %fusion.92, bf16[2048,3,1408]{2,0,1:T(8,128)(2,1)} %all-gather.17.cloned.1.call-done, bf16[1024,2048]{1,0:T(8,128)(2,1)} %copy-done.12), kind=kOutput, calls=%fused_computation.11 | convolution fusion | flops 11816927232 | bytes 38797312 | tf_op jit(solution)/shard_map/tr,rxf->txf/dot_general | solution.py:901
  379.8 10.7 %fusion.26 = f32[1024,1408]{1,0:T(8,128)} fusion(bf16[2048,3,1408]{2,0,1:T(8,128)(2,1)} %all-gather.17.cloned.1.call-done, bf16[1024,2048]{1,0:T(8,128)(2,1)S(1)} %copy-done.16, f32[1024]{0:T(1024)S(1)} %add_divide_fusion), kind=kOutput, calls=%fused_computation.52 | convolution fusion | flops 5911871488 | bytes 15732736 | tf_op jit(solution)/shard_map/dot_general | solution.py:30
  390.5 6.4 multiply_bitcast_fusion
  396.9 5.6 fusion.44
  403.1 1.8 multiply_convert_fusion.1
  404.9 11.1 %broadcast_multiply_fusion = (f32[1024,2048]{1,0:T(8,128)}, bf16[1024]{0:T(1024)(128)(2,1)S(1)}) fusion(f32[1024]{0:T(1024)S(1)} %add_divide_fusion, bf16[1024,2048]{1,0:T(8,128)(2,1)S(1)} %copy-done.16, bf16[2048,3,1408]{2,0,1:T(8,128)(2,1)} %all-gather.17.cloned.1.call-done, bf16[1024,1,1408]{2,0,1:T(8,128)(2,1)S(1)} %multiply_convert_fusion.1), kind=kOutput, calls=%fused_computation.59 | convolution fusion | flops 5913967616 | bytes 21239808 | tf_op jit(solution)/shard_map/dot_general | solution.py:34
  416.7 2.4 fusion.69
  419.1 5.0 fusion.66
  424.0 18.7 %fusion.30.grad_start = f32[1024,2048]{1,0:T(8,128)} fusion(bf16[2048,3,1408]{2,0,1:T(8,128)(2,1)} %all-gather.17.cloned.1.call-done, f32[1024,1,1408]{2,0,1:T(8,128)S(1)} %bitcast.239, f32[1024,1,1408]{2,0,1:T(8,128)} %copy-done.28), kind=kOutput, calls=%fused_computation.55 | convolution fusion | flops 11816927232 | bytes 31457280 | tf_op jit(solution)/shard_map/txf,rxf->tr/dot_general | solution.py:921
  442.8 68.7 %shard_map.305 = (f32[1024,2048]{1,0:T(8,128)}, bf16[8,352,1024]{2,1,0:T(8,128)(2,1)}, f32[8,1,1024]{2,1,0:T(1,128)}) custom-call(bf16[2048,1024]{1,0:T(8,128)(2,1)} %copy.248.inputs_ref, f32[16,1,1024]{2,1,0:T(1,128)} %copy.249.gate_ref, bf16[8,704,2048]{2,1,0:T(8,128)(2,1)} %bitcast.258, bf16[16,352,1024]{2,1,0:T(8,128)(2,1)} %bitcast.261, ...), custom_call_target="tpu_custom_call" | custom-call | flops 70866960384 | bytes 33554432 | tf_op jit(solution)/shard_map/pallas_call | solution.py:757
  511.5 39.2 %shard_map.306 = (f32[1024,2048]{1,0:T(8,128)}, bf16[4,352,1024]{2,1,0:T(8,128)(2,1)}, f32[4,1,1024]{2,1,0:T(1,128)}) custom-call(bf16[2048,1024]{1,0:T(8,128)(2,1)} %copy.248.inputs_ref, f32[16,1,1024]{2,1,0:T(1,128)} %copy.249.gate_ref, bf16[4,704,2048]{2,1,0:T(8,128)(2,1)} %bitcast.259, bf16[16,352,1024]{2,1,0:T(8,128)(2,1)} %bitcast.262, ...), custom_call_target="tpu_custom_call" | custom-call | flops 35433480192 | bytes 33554432 | tf_op jit(solution)/shard_map/pallas_call | solution.py:757
  550.8 39.7 %shard_map.307 = (f32[1024,2048]{1,0:T(8,128)}, bf16[4,352,1024]{2,1,0:T(8,128)(2,1)}, f32[4,1,1024]{2,1,0:T(1,128)}) custom-call(bf16[2048,1024]{1,0:T(8,128)(2,1)} %copy.248.inputs_ref, f32[16,1,1024]{2,1,0:T(1,128)} %copy.249.gate_ref, bf16[4,704,2048]{2,1,0:T(8,128)(2,1)} %bitcast.260, bf16[16,352,1024]{2,1,0:T(8,128)(2,1)} %bitcast.263, ...), custom_call_target="tpu_custom_call" | custom-call | flops 35433480192 | bytes 33554432 | tf_op jit(solution)/shard_map/pallas_call | solution.py:757
  592.4 116.1 %shard_map.308 = (bf16[1024,2176]{1,0:T(8,128)(2,1)}, bf16[1024,2048]{1,0:T(8,128)(2,1)}) custom-call(f32[1024,2048]{1,0:T(8,128)} %get-tuple-element.35.wide_ref, bf16[1024,128]{1,0:T(8,128)(2,1)} %concatenate.53.narrow_ref, f32[1024,2048]{1,0:T(8,128)} %get-tuple-element.112.start_ref, bf16[5632,2048]{1,0:T(8,128)(2,1)} %get-tuple-element.39.down_ref, ...), custom_call_target="tpu_custom_call" | custom-call | bytes 314572800 | tf_op jit(solution)/shard_map/pallas_call | solution.py:527
  708.6 3.0 convert_element_type.152
  712.6 2.6 fusion.62
  717.1 10.6 %multiply_reduce_fusion = (f32[1024]{0:T(1024)S(1)}, f32[1024,2048]{1,0:T(8,128)}) fusion(f32[1024,2048]{1,0:T(8,128)} %copy-done.11, f32[2048]{0:T(1024)S(1)} %copy-done.41, bf16[2048,16]{0,1:T(8,128)(2,1)S(1)} %copy-done.34, bf16[2048,17]{0,1:T(8,128)(2,1)S(1)} %bitcast.248, bf16[1024,16]{0,1:T(8,128)(2,1)S(1)} %copy.255, ...), kind=kOutput, calls=%fused_computation.30 | convolution fusion | flops 147272704 | bytes 25380864 | tf_op jit(solution)/shard_map/dot_general | solution.py:34
  727.7 1.8 copy-done.18
  729.6 4.4 convert_add_fusion.1
  734.0 2.2 fusion.67
  736.5 2.8 fusion.46
  739.6 1.7 fusion.55
  741.3 5.3 fusion.52
  746.6 1.9 fusion.48
  749.2 6.3 fusion.56
  755.6 2.2 add_convert_fusion.2.refs_3_
  757.7 109.4 %shard_map.309 = (bf16[1024,2048]{1,0:T(8,128)(2,1)}, bf16[3,1024,512]{2,1,0:T(8,128)(2,1)}) custom-call(bf16[1024,2048]{1,0:T(8,128)(2,1)} %get-tuple-element.43.wide_ref, bf16[1024,512]{1,0:T(8,128)(2,1)} %copy-done.7, bf16[1024,512]{1,0:T(8,128)(2,1)} %copy-done.8, bf16[1024,512]{1,0:T(8,128)(2,1)} %copy-done.9, ...), custom_call_target="tpu_custom_call" | custom-call | bytes 314572800 | tf_op jit(solution)/shard_map/pallas_call | solution.py:692
  867.1 3.0 fusion.61
  870.2 10.9 %fusion.27.refs_0_ = f32[1024,2048]{1,0:T(8,128)} fusion(bf16[3,1024,512]{2,1,0:T(8,128)(2,1)S(1)} %copy-done.29, bf16[2048,4,512]{0,2,1:T(8,128)(2,1)} %all-gather.9.cloned.1.call-done), kind=kOutput, calls=%fused_computation.54 | convolution fusion | flops 6442450944 | bytes 17825792 | tf_op jit(solution)/shard_map/stf,rsf->tr/dot_general | solution.py:994
  881.7 110.3 %shard_map.310 = bf16[1024,2176]{1,0:T(8,128)(2,1)S(1)} custom-call(f32[1024,2048]{1,0:T(8,128)} %fusion.27.refs_0_, bf16[1024,128]{1,0:T(8,128)(2,1)S(1)} %concatenate.56.refs_1_), custom_call_target="tpu_custom_call" | custom-call | bytes 314572800 | tf_op jit(solution)/shard_map/pallas_call | solution.py:471
  993.2 14.2 %all-gather = bf16[128,3584]{1,0:T(8,128)(2,1)S(1)} all-gather(bf16[16,3584]{1,0:T(8,128)(2,1)S(1)} %pad_maximum_fusion.4), channel_id=2, replica_groups=mesh['dp'=8,'tensor'=4] {'dp'}, dimensions={0}, use_global_device_ids=true | all-gather | bytes 1032192 | tf_op jit(solution)/shard_map/all_gather | solution.py:1015
  1008.4 1.6 copy.264
  1010.0 1.3 copy.265
  1011.4 5.3 fusion.14
  1016.7 6.3 add_convert_fusion.1
  1023.0 1.2 copy-done.22
  1024.2 6.4 fusion.9
  1030.6 2.8 fusion.41
  1034.1 1.6 copy.267
  1035.6 1.6 copy.268
  1037.2 1.6 copy.271
  1038.8 1.8 copy.269
  (255 shorter events, 26.0 us)
Async XLA Ops:
  7.2 28.6 %copy-start = (bf16[8,16,2,1408]{3,2,1,0:T(2,128)(2,1)S(1)}, bf16[8,16,2,1408]{3,2,1,0:T(2,128)(2,1)}, u32[]{:S(2)}) copy-start(bf16[8,16,2,1408]{3,2,1,0:T(2,128)(2,1)} %param.45) | copy-start | bytes 2162692
  7.2 62.7 %all-gather.9.cloned.1.call-start = ((), (), s32[]{:S(2)}) async-start(), calls=%async_computation | async-start | bytes 9437184 | tf_op jit(solution)/shard_map/all_gather | solution.py:793
  11.0 345.8 %all-gather.17.cloned.1.call-start = ((), (), s32[]{:S(2)}) async-start(), calls=%async_computation.4 | async-start | bytes 19464192 | tf_op jit(solution)/shard_map/all_gather | solution.py:793
  13.9 428.9 %all-gather.15.cloned.1.call-start = ((), (), s32[]{:S(2)}) async-start(), calls=%async_computation.3 | async-start | bytes 25952256 | tf_op jit(solution)/shard_map/all_gather | solution.py:933
  17.6 8.3 copy-start.67
  17.6 10.3 copy-start.70
  17.7 493.9 %all-gather.13.cloned.1.call-start = ((), (), s32[]{:S(2)}) async-start(), calls=%async_computation.2 | async-start | bytes 12976128 | tf_op jit(solution)/shard_map/all_gather | solution.py:933
  21.3 529.5 %all-gather.11.cloned.1.call-start = ((), (), s32[]{:S(2)}) async-start(), calls=%async_computation.1 | async-start | bytes 12976128 | tf_op jit(solution)/shard_map/all_gather | solution.py:933
  21.9 1008.8 %all-gather.19.cloned.1.call-start = ((), (), s32[]{:S(2)}) async-start(), calls=%async_computation.5 | async-start | bytes 3133440 | tf_op jit(solution)/shard_map/all_gather | solution.py:1015
  22.6 47.3 %copy-start.44 = (f32[2048]{0:T(1024)}, f32[2048]{0:T(1024)S(1)}, u32[]{:S(2)}) copy-start(f32[2048]{0:T(1024)S(1)} %convert_element_type.136) | copy-start | bytes 24580
  25.9 9.0 copy-start.68
  25.9 10.0 copy-start.71
  25.9 10.1 copy-start.65
  25.9 21.5 %copy-start.60 = (s32[1024,4]{0,1:T(4,128)S(1)}, s32[1024,4]{0,1:T(4,128)}, u32[]{:S(2)}) copy-start(s32[1024,4]{0,1:T(4,128)} %param.37) | copy-start | bytes 49156
  26.0 43.9 %copy-start.56 = (f32[1024]{0:T(1024)}, f32[1024]{0:T(1024)S(1)}, u32[]{:S(2)}) copy-start(f32[1024]{0:T(1024)S(1)} %fusion.135) | copy-start | bytes 12292
  28.1 57.1 %copy-start.10 = (s32[1024]{0:T(1024)}, s32[1024]{0:T(1024)S(1)}, u32[]{:S(2)}) copy-start(s32[1024]{0:T(1024)S(1)} %broadcast_add_fusion) | copy-start | bytes 12292
  28.3 56.9 %copy-start.6 = (s32[1024,1]{1,0:T(8,128)}, s32[1024,1]{1,0:T(8,128)S(1)}, u32[]{:S(2)}) copy-start(s32[1024,1]{1,0:T(8,128)S(1)} %copy.236.row_piece_ref.refs_6_) | copy-start | bytes 12292
  34.9 301.1 %copy-start.40 = (f32[2048]{0:T(1024)}, f32[2048]{0:T(1024)S(1)}, u32[]{:S(2)}) copy-start(f32[2048]{0:T(1024)S(1)} %convert_element_type.141) | copy-start | bytes 24580
  35.8 303.1 %copy-start.33 = (bf16[2048,16]{0,1:T(8,128)(2,1)}, bf16[2048,16]{0,1:T(8,128)(2,1)S(1)}, u32[]{:S(2)}) copy-start(bf16[2048,16]{0,1:T(8,128)(2,1)S(1)} %dynamic-slice_bitcast_fusion) | copy-start | bytes 196612
  47.4 287.3 %copy-start.31 = (bf16[2048,18]{0,1:T(8,128)(2,1)}, bf16[2048,18]{0,1:T(8,128)(2,1)S(1)}, u32[]{:S(2)}) copy-start(bf16[2048,18]{0,1:T(8,128)(2,1)S(1)} %all_gather.31) | copy-start | bytes 221188
  47.7 293.0 %copy-start.26 = (f32[1024,16]{1,0:T(8,128)}, f32[1024,16]{1,0:T(8,128)S(1)}, u32[]{:S(2)}) copy-start(f32[1024,16]{1,0:T(8,128)S(1)} %copy.241) | copy-start | bytes 196612
  51.8 28.7 %copy-start.38 = (bf16[1024,16,1]{0,1,2:T(8,128)(2,1)}, bf16[1024,16,1]{0,1,2:T(8,128)(2,1)S(1)}, u32[]{:S(2)}) copy-start(bf16[1024,16,1]{0,1,2:T(8,128)(2,1)S(1)} %fusion.72) | copy-start | bytes 98308
  52.2 33.0 %copy-start.4 = (f32[1024,128]{1,0:T(8,128)}, f32[1024,128]{1,0:T(8,128)S(1)}, u32[]{:S(2)}) copy-start(f32[1024,128]{1,0:T(8,128)S(1)} %get-tuple-element.131.cosine_ref.refs_4_) | copy-start | bytes 1572868
  52.2 33.0 %copy-start.5 = (f32[1024,128]{1,0:T(8,128)}, f32[1024,128]{1,0:T(8,128)S(1)}, u32[]{:S(2)}) copy-start(f32[1024,128]{1,0:T(8,128)S(1)} %get-tuple-element.132.sine_ref.refs_5_) | copy-start | bytes 1572868
  102.7 9.2 copy-start.2
  111.9 216.5 %copy-start.20 = (bf16[1024,2048]{1,0:T(8,128)(2,1)S(1)}, bf16[1024,2048]{1,0:T(8,128)(2,1)}, u32[]{:S(2)}) copy-start(bf16[1024,2048]{1,0:T(8,128)(2,1)} %param.24) | copy-start | bytes 12582916
  333.5 5.3 copy-start.12
  334.7 5.3 copy-start.50
  340.1 64.9 %copy-start.58 = (f32[1024]{0:T(1024)}, f32[1024]{0:T(1024)S(1)}, u32[]{:S(2)}) copy-start(f32[1024]{0:T(1024)S(1)} %add_divide_fusion) | copy-start | bytes 12292
  340.3 14.3 %copy-start.23 = (f32[1024,16]{1,0:T(8,128)}, f32[1024,16]{1,0:T(8,128)S(1)}, u32[]{:S(2)}) copy-start(f32[1024,16]{1,0:T(8,128)S(1)} %copy.239) | copy-start | bytes 196612
  340.7 13.9 %copy-start.48 = (f32[1024]{0:T(1024)}, f32[1024]{0:T(1024)S(1)}, u32[]{:S(2)}) copy-start(f32[1024]{0:T(1024)S(1)} %fusion.80) | copy-start | bytes 12292
  348.6 6.0 copy-start.15
  356.7 33.8 %copy-start.72 = (bf16[1024,16]{0,1:T(8,128)(2,1)}, bf16[1024,16]{0,1:T(8,128)(2,1)S(1)}, u32[]{:S(2)}) copy-start(bf16[1024,16]{0,1:T(8,128)(2,1)S(1)} %fusion.65) | copy-start | bytes 98308
  356.7 23.0 %copy-start.16 = (bf16[1024,2048]{1,0:T(8,128)(2,1)S(1)}, bf16[1024,2048]{1,0:T(8,128)(2,1)}, u32[]{:S(2)}) copy-start(bf16[1024,2048]{1,0:T(8,128)(2,1)} %param.25) | copy-start | bytes 12582916
  379.8 10.7 %copy-start.25 = (f32[1024,2,1408]{2,0,1:T(8,128)S(1)}, f32[1024,2,1408]{2,0,1:T(8,128)}, u32[]{:S(2)}) copy-start(f32[1024,2,1408]{2,0,1:T(8,128)} %multiply_add_fusion) | copy-start | bytes 34603012
  396.9 22.2 %copy-start.28 = (f32[1024,1,1408]{2,0,1:T(8,128)}, f32[1024,1,1408]{2,0,1:T(8,128)S(1)}, u32[]{:S(2)}) copy-start(f32[1024,1,1408]{2,0,1:T(8,128)S(1)} %get-tuple-element.110) | copy-start | bytes 17301508
  416.7 7.4 slice-start.6
  550.8 40.5 %copy-start.64 = (f32[4,1,1024]{2,1,0:T(1,128)S(1)}, f32[4,1,1024]{2,1,0:T(1,128)}, u32[]{:S(2)}) copy-start(f32[4,1,1024]{2,1,0:T(1,128)} %get-tuple-element.37) | copy-start | bytes 49156
  550.8 40.5 %copy-start.54 = (f32[8,1,1024]{2,1,0:T(1,128)S(1)}, f32[8,1,1024]{2,1,0:T(1,128)}, u32[]{:S(2)}) copy-start(f32[8,1,1024]{2,1,0:T(1,128)} %get-tuple-element.36) | copy-start | bytes 98308
  550.8 40.6 %copy-start.37 = (bf16[1024,16]{0,1:T(8,128)(2,1)S(1)}, bf16[1024,16]{0,1:T(8,128)(2,1)}, u32[]{:S(2)}) copy-start(bf16[1024,16]{0,1:T(8,128)(2,1)} %fusion.69) | copy-start | bytes 98308
  550.8 40.6 %copy-start.55 = (bf16[1024,16]{0,1:T(8,128)(2,1)S(1)}, bf16[1024,16]{0,1:T(8,128)(2,1)}, u32[]{:S(2)}) copy-start(bf16[1024,16]{0,1:T(8,128)(2,1)} %fusion.66) | copy-start | bytes 98308
  550.8 40.6 %copy-start.63 = (bf16[1024,1]{0,1:T(2,128)(2,1)S(1)}, bf16[1024,1]{0,1:T(2,128)(2,1)}, u32[]{:S(2)}) copy-start(bf16[1024,1]{0,1:T(2,128)(2,1)} %broadcast_in_dim.83) | copy-start | bytes 6148
  711.6 5.4 copy-start.32
  711.6 5.4 copy-start.34
  711.6 5.4 copy-start.41
  717.0 10.7 %slice-start = ((s8[8388608]{0:T(1024)(128)(4,1)}), s8[4194304]{0:T(1024)(128)(4,1)S(1)}, s32[]{:S(2)}) async-start(s8[8388608]{0:T(1024)(128)(4,1)} %bitcast.228), calls=%async_computation.6 | async-start | bytes 8388608
  717.0 10.7 %copy-start.62 = (f32[1024]{0:T(1024)S(1)}, f32[1024]{0:T(1024)}, u32[]{:S(2)}) copy-start(f32[1024]{0:T(1024)} %copy-done.61) | copy-start | bytes 12292
  717.1 10.7 %slice-start.1 = ((s8[8388608]{0:T(1024)(128)(4,1)}), s8[4194304]{0:T(1024)(128)(4,1)S(1)}, s32[]{:S(2)}) async-start(s8[8388608]{0:T(1024)(128)(4,1)} %bitcast.228), calls=%async_computation.7 | async-start | bytes 8388608
  717.1 12.5 %copy-start.18 = (bf16[1024,2048]{1,0:T(8,128)(2,1)S(1)}, bf16[1024,2048]{1,0:T(8,128)(2,1)}, u32[]{:S(2)}) copy-start(bf16[1024,2048]{1,0:T(8,128)(2,1)} %param.25) | copy-start | bytes 12582916
  717.1 12.5 %copy-start.47 = (f32[1024]{0:T(1024)S(1)}, f32[1024]{0:T(1024)}, u32[]{:S(2)}) copy-start(f32[1024]{0:T(1024)} %copy-done.46) | copy-start | bytes 12292
  734.0 5.3 copy-start.14
  741.3 5.3 copy-start.59
  870.2 10.9 %copy-start.39 = (bf16[1024,16,1]{0,1,2:T(8,128)(2,1)S(1)}, bf16[1024,16,1]{0,1,2:T(8,128)(2,1)}, u32[]{:S(2)}) copy-start(bf16[1024,16,1]{0,1,2:T(8,128)(2,1)} %copy-done.38) | copy-start | bytes 98308
  881.6 110.3 %copy-start.21 = (bf16[1024,2048]{1,0:T(8,128)(2,1)S(1)}, bf16[1024,2048]{1,0:T(8,128)(2,1)}, u32[]{:S(2)}) copy-start(bf16[1024,2048]{1,0:T(8,128)(2,1)} %param.24) | copy-start | bytes 12582916
  881.7 110.3 %copy-start.45 = (f32[2048]{0:T(1024)S(1)}, f32[2048]{0:T(1024)}, u32[]{:S(2)}) copy-start(f32[2048]{0:T(1024)} %copy-done.44) | copy-start | bytes 24580
  881.7 110.3 %copy-start.57 = (f32[1024]{0:T(1024)S(1)}, f32[1024]{0:T(1024)}, u32[]{:S(2)}) copy-start(f32[1024]{0:T(1024)} %copy-done.56) | copy-start | bytes 12292
  992.0 15.4 %copy-start.69 = (s32[8]{0:T(128)S(1)}, s32[8]{0:T(128)}, u32[]{:S(2)}) copy-start(s32[8]{0:T(128)} %bitcast_convert_fusion) | copy-start | bytes 100
  1008.4 8.2 slice-start.2
  1011.4 5.3 copy-start.53
  1011.4 5.3 slice-start.3
  1016.6 6.4 slice-start.4
  1016.7 6.3 slice-start.5
  1016.7 7.5 copy-start.22
  1034.0 8.5 copy-start.1
  (24 other events, 76.0 us)
Sparse Core Ops, SparseCore 0:
  11.1 58.7 all-gather.8
  71.8 128.7 all-gather.16
  202.5 165.5 all-gather.14
  370.4 69.9 all-gather.12
  442.1 69.8 all-gather.10
  749.4 30.2 all-gather.18

commit v5 on v4

--- a/solution.py
+++ b/solution.py
@@ -23,7 +23,8 @@
 MESH = pl.DeviceIdType.MESH
 SUM_CHUNKS = 16
 AHEAD = 2
-EXPERT_PARTS = (8, 4, 4)
+SHARED = 4
+HALVES = 2
 
 
 def matmul(left_side, right_side):
@@ -217,15 +218,15 @@
     def begin():
         own().start()
 
-    def advance(step):
-        @pl.when(step < pieces)
+    def launch(piece):
+        @pl.when((piece >= 0) & (piece < pieces))
         def _():
             for name in ("x", "y", "core"):
-                send(name, step).start()
-
-        @pl.when((step >= AHEAD) & (step < pieces + AHEAD))
-        def _():
-            piece = step - AHEAD
+                send(name, piece).start()
+
+    def forward(piece):
+        @pl.when((piece >= 0) & (piece < pieces))
+        def _():
             send("x", piece).wait_recv()
             send("x_y", piece).start()
             send("x_core", piece).start()
@@ -233,13 +234,18 @@
             send("y_x", piece).start()
             send("y_core", piece).start()
 
-        @pl.when((step >= 2 * AHEAD) & (step < pieces + 2 * AHEAD))
-        def _():
-            piece = step - 2 * AHEAD
+    def hand_over(piece):
+        @pl.when((piece >= 0) & (piece < pieces))
+        def _():
             send("x_y", piece).wait_recv()
             send("xy_core", piece).start()
             send("y_x", piece).wait_recv()
             send("yx_core", piece).start()
+
+    def advance(step):
+        launch(step)
+        forward(step - AHEAD)
+        hand_over(step - 2 * AHEAD)
 
     def arrive(piece):
         @pl.when(piece == 0)
@@ -255,7 +261,7 @@
             for name in order:
                 send(name, piece).wait_send()
 
-    return greet, begin, advance, arrive, finish
+    return greet, begin, advance, arrive, finish, (launch, forward, hand_over)
 
 
 def line_sum_kernel(chunks, *refs):
@@ -286,8 +292,10 @@
         chunks, wide_ref, narrow_ref, total_ref, *scratch[:5]
     )
     gather_semaphores, local_semaphores, piece_rows, open_rows = scratch[5:]
-    gather_greet, gather_begin, gather_advance, gather_arrive, gather_finish = plane_gather_steps(
-        pieces, block_ref, whole_ref, gather_semaphores, local_semaphores.at[0]
+    gather_greet, gather_begin, gather_advance, gather_arrive, gather_finish, _ = (
+        plane_gather_steps(
+            pieces, block_ref, whole_ref, gather_semaphores, local_semaphores.at[0]
+        )
     )
     rows = piece_rows.shape[1]
 
@@ -339,14 +347,8 @@
 
 
 def sum_down_kernel(
-    chunks,
-    wide_ref,
-    narrow_ref,
-    start_ref,
-    down_ref,
-    *refs,
+    chunks, wide_ref, narrow_ref, act_ref, down_ref, total_ref, out_ref, *scratch
 ):
-    act_refs, (total_ref, out_ref), scratch = refs[:-11], refs[-11:-9], refs[-9:]
     greet, begin, advance, finish = line_sum_steps(
         chunks, wide_ref, narrow_ref, total_ref, *scratch[:5]
     )
@@ -354,40 +356,19 @@
     rows = act_rows.shape[1]
     blocks = down_ref.shape[0] // rows
 
-    def load_down(block):
+    def loads(block):
         slot = block % 2
         span = pl.ds(pl.multiple_of(block * rows, rows), rows)
-        return pltpu.make_async_copy(
-            down_ref.at[span], down_rows.at[slot], semaphores.at[1, slot]
-        )
-
-    def load_act(act_ref, block, slot):
-        span = pl.ds(pl.multiple_of(block * rows, rows), rows)
-        return pltpu.make_async_copy(act_ref.at[span], act_rows.at[slot], semaphores.at[0, slot])
-
-    def load_start(block):
-        load_down(block).start()
-        first = 0
-        for act_ref in act_refs:
-            count = act_ref.shape[0] // rows
-            from_here = block - first
-
-            @pl.when((from_here >= 0) & (from_here < count))
-            def _():
-                load_act(act_ref, from_here, block % 2).start()
-
-            first += count
-
-    def load_wait(block):
-        load_down(block).wait()
-        load_act(act_refs[0], 0, block % 2).wait()
-
-    first = pltpu.make_async_copy(start_ref, out_rows, semaphores.at[2, 0])
-    first.start()
-    load_start(0)
+        return [
+            pltpu.make_async_copy(act_ref.at[span], act_rows.at[slot], semaphores.at[0, slot]),
+            pltpu.make_async_copy(down_ref.at[span], down_rows.at[slot], semaphores.at[1, slot]),
+        ]
+
+    for load in loads(0):
+        load.start()
     greet(0)
     begin()
-    first.wait()
+    out_rows[...] = jnp.zeros_like(out_rows)
 
     @pl.loop(0, max(blocks, chunks + 1))
     def _(step):
@@ -397,9 +378,11 @@
         def _():
             @pl.when(step + 1 < blocks)
             def _():
-                load_start(step + 1)
-
-            load_wait(step)
+                for load in loads(step + 1):
+                    load.start()
+
+            for load in loads(step):
+                load.wait()
             tile = min(256, out_rows.shape[0])
 
             @pl.loop(0, out_rows.shape[0] // tile)
@@ -447,6 +430,10 @@
 
 def in_vmem(count):
     return [pl.BlockSpec(memory_space=pltpu.VMEM)] * count
+
+
+def in_hbm(count):
+    return [pl.BlockSpec(memory_space=pltpu.HBM)] * count
 
 
 def sum_scratch(shape):
@@ -489,9 +476,8 @@
         open_rows = to_low(matmul(whole, cotangents))
         return summed(wide_part, narrow_part, number) + (whole, open_rows)
     shape = (length, width + NARROW)
-    pieces = EXPERTS
+    pieces = SHARED + EXPERTS
     rows = block.shape[0] // pieces
-    in_hbm = pl.BlockSpec(memory_space=pltpu.HBM)
     total, whole, open_rows = pl.pallas_call(
         functools.partial(sum_gather_kernel, SUM_CHUNKS, pieces),
         out_shape=[
@@ -499,8 +485,8 @@
             jax.ShapeDtypeStruct((block.shape[0], width), jnp.bfloat16),
             jax.ShapeDtypeStruct((block.shape[0], length), jnp.bfloat16),
         ],
-        in_specs=in_vmem(2) + [in_hbm] + in_vmem(1),
-        out_specs=in_vmem(1) + [in_hbm] * 2,
+        in_specs=in_vmem(2) + in_hbm(1) + in_vmem(1),
+        out_specs=in_vmem(1) + in_hbm(2),
         scratch_shapes=sum_scratch(shape)
         + [
             pltpu.SemaphoreType.DMA((18, pieces)),
@@ -516,25 +502,24 @@
     return parts_of(total, wide_part, narrow_part) + (whole, open_rows)
 
 
-def summed_and_down(wide_part, narrow_part, start, act_parts, down_rows, number):
+def summed_and_down(wide_part, narrow_part, act_rows, down_rows, number):
     length, width = wide_part.shape
     if not on_line():
-        out = start + contract_first(jnp.concatenate(act_parts, axis=0), down_rows)
+        out = contract_first(act_rows, down_rows)
         return summed(wide_part, narrow_part, number) + (out,)
     shape = (length, width + NARROW)
-    rows = 2 * down_rows.shape[0] // EXPERTS
-    in_hbm = pl.BlockSpec(memory_space=pltpu.HBM)
+    rows = 2 * down_rows.shape[0] // (SHARED + EXPERTS)
     total, out = pl.pallas_call(
         functools.partial(sum_down_kernel, SUM_CHUNKS),
         out_shape=[
             jax.ShapeDtypeStruct(shape, jnp.bfloat16),
             jax.ShapeDtypeStruct((length, width), jnp.bfloat16),
         ],
-        in_specs=in_vmem(2) + [in_hbm] * (2 + len(act_parts)),
+        in_specs=in_vmem(2) + in_hbm(2),
         out_specs=in_vmem(2),
         scratch_shapes=sum_scratch(shape)
         + [
-            pltpu.SemaphoreType.DMA((3, 2)),
+            pltpu.SemaphoreType.DMA((2, 2)),
             pltpu.VMEM((2, rows, length), jnp.bfloat16),
             pltpu.VMEM((2, rows, width), jnp.bfloat16),
             pltpu.VMEM((length, width), jnp.float32),
@@ -543,7 +528,7 @@
             collective_id=number, has_side_effects=True, vmem_limit_bytes=58 * 2**20
         ),
         cost_estimate=pl.CostEstimate(flops=0, bytes_accessed=300 * 2**20, transcendentals=0),
-    )(wide_part, narrowed(narrow_part), start, down_rows, *act_parts)
+    )(wide_part, narrowed(narrow_part), act_rows, down_rows)
     return parts_of(total, wide_part, narrow_part) + (out,)
 
 
@@ -705,88 +690,245 @@
     )(wide_part, *attention_inputs)
 
 
+def hidden_step(gate_up, open_part, gate_row, extra):
+    hidden = open_part.shape[0]
+    gate_half, up_half = gate_up[:hidden], gate_up[hidden:]
+    squashed = 1.0 / (1.0 + jnp.exp(-gate_half))
+    act = to_low(gate_half * squashed * up_half)
+    act_f = act.astype(jnp.float32)
+    gate_grad = jnp.sum(act_f * open_part, axis=0, keepdims=True)
+    grad_act = gate_row * open_part
+    if extra is not None:
+        grad_act = grad_act + extra
+    grad_gate = to_low(grad_act * up_half * squashed * (1.0 + gate_half * (1.0 - squashed)))
+    grad_up = to_low(grad_act * gate_half * squashed)
+    return act, to_low(gate_row * act_f), gate_grad, grad_gate, grad_up
+
+
 def experts_kernel(
+    pieces,
     inputs_ref,
     gate_ref,
-    up_ref,
+    mid_up_ref,
+    grad_mid_ref,
+    up_extra_ref,
+    down_extra_ref,
+    shared_up_ref,
+    block_ref,
     open_ref,
-    grad_start,
     grad_ref,
+    gate_grad_ref,
+    mid_down_ref,
+    grad_mid_up_ref,
+    grad_down_a_ref,
+    grad_up_b_ref,
     act_ref,
-    gate_grad_ref,
+    whole_ref,
+    grad_total,
+    up_rows,
+    open_rows,
+    act_rows,
     grad_rows,
-    semaphore,
+    gather_semaphores,
+    semaphores,
 ):
-    @pl.when(pl.program_id(0) == 0)
-    def _():
-        load = pltpu.make_async_copy(grad_start, grad_ref, semaphore.at[0])
-        load.start()
-        load.wait()
-
-    hidden = open_ref.shape[1]
-    gate_up = matmul(up_ref[0], inputs_ref[...])
-    open_part = open_ref[0].astype(jnp.float32)
-    gate_half, up_half = gate_up[:hidden], gate_up[hidden:]
-    squashed = 1.0 / (1.0 + jnp.exp(-gate_half))
-    act = to_low(gate_half * squashed * up_half).astype(jnp.float32)
-    gate_row = gate_ref[0]
-    gate_grad_ref[0] = jnp.sum(act * open_part, axis=0, keepdims=True)
-    act_ref[0] = to_low(gate_row * act)
-    grad_act = gate_row * open_part
-    grad_rows[:hidden] = to_low(
-        grad_act * up_half * squashed * (1.0 + gate_half * (1.0 - squashed))
-    )
-    grad_rows[hidden:] = to_low(grad_act * gate_half * squashed)
-    grad_ref[...] += contract_first(grad_rows[...], up_ref[0])
-
-
-def experts_step(inputs, gates, up_rows, open_rows, grad_start, first):
-    count, length, width = up_rows.shape[0], inputs.shape[1], inputs.shape[0]
+    greet, begin, _, arrive, finish, (launch, forward, hand_over) = plane_gather_steps(
+        pieces, block_ref, whole_ref, gather_semaphores, semaphores.at[0, 0]
+    )
     hidden = open_rows.shape[1]
-    once = pl.Buffered(1)
-
-    def still(shape):
-        return pl.BlockSpec(shape, lambda expert: (0, 0), pipeline_mode=once)
-
-    def here(rows):
-        return pl.BlockSpec((1, rows, length), lambda expert: (expert, 0, 0))
-
-    def ahead(rows):
-        return pl.BlockSpec((1, rows, length), lambda expert: (expert + first, 0, 0))
-
+    count = SHARED + EXPERTS
+    each = pieces // EXPERTS
+
+    def span(expert, rows):
+        return pl.ds(pl.multiple_of(expert * rows, rows), rows)
+
+    def load_open(expert):
+        slot = expert % 2
+        return pltpu.make_async_copy(
+            open_ref.at[span(expert, hidden)], open_rows.at[slot], semaphores.at[1, slot]
+        )
+
+    def load_shared(expert):
+        slot = expert % 2
+        return pltpu.make_async_copy(
+            shared_up_ref.at[span(expert, 2 * hidden)], up_rows.at[slot], semaphores.at[2, slot]
+        )
+
+    def load_routed(expert):
+        slot = expert % 2
+        return pltpu.make_async_copy(
+            whole_ref.at[span(expert - SHARED, 2 * hidden)],
+            up_rows.at[slot],
+            semaphores.at[2, slot],
+        )
+
+    def store_act(expert):
+        slot = expert % 2
+        return pltpu.make_async_copy(
+            act_rows.at[slot], act_ref.at[span(expert, hidden)], semaphores.at[3, slot]
+        )
+
+    def advance(expert):
+        for part in range(each):
+            launch(each * expert + part)
+        for part in range(each):
+            forward(each * (expert - 2) + part + 1)
+        for part in range(each):
+            hand_over(each * (expert - 3) + part + 1)
+
+        @pl.when(expert + 1 < count)
+        def _():
+            load_open(expert + 1).start()
+
+        @pl.when(expert + 1 < SHARED)
+        def _():
+            load_shared(expert + 1).start()
+
+        @pl.when((expert + 1 >= SHARED) & (expert + 1 < count))
+        def _():
+            for part in range(each):
+                arrive(each * (expert + 1 - SHARED) + part)
+            load_routed(expert + 1).start()
+
+        load_open(expert).wait()
+        load_shared(0 * expert + expert % 2).wait()
+
+        @pl.when(expert >= 2)
+        def _():
+            store_act(expert - 2).wait()
+
+    def compute(expert, shared):
+        slot = expert % 2
+        gate_up = matmul(up_rows[slot], inputs_ref[...])
+        extra = None
+        if shared:
+            gate_up = gate_up + matmul(up_extra_ref[expert], mid_up_ref[...])
+            extra = matmul(down_extra_ref[expert], grad_mid_ref[...])
+        act, act_gated, gate_grad, grad_gate, grad_up = hidden_step(
+            gate_up,
+            open_rows[slot].astype(jnp.float32),
+            gate_ref[pl.ds(expert, 1)],
+            extra,
+        )
+        gate_grad_ref[pl.ds(expert, 1)] = gate_grad
+        act_rows[slot] = act_gated
+        grad_rows[:hidden] = grad_gate
+        grad_rows[hidden:] = grad_up
+        store_act(expert).start()
+        grad_total[...] += contract_first(grad_rows[...], up_rows[slot])
+        if shared:
+            mid_down_ref[...] += contract_first(down_extra_ref[expert], act)
+            grad_mid_up_ref[...] += contract_first(up_extra_ref[expert], grad_rows[...])
+            grad_down_a_ref[expert] = contract_last(grad_mid_ref[...], act)
+            grad_up_b_ref[expert] = ADAPTER_SCALE * contract_last(mid_up_ref[...], grad_rows[...])
+
+    greet()
+    pl.semaphore_wait(pltpu.get_barrier_semaphore(), 3)
+    begin()
+    load_open(0).start()
+    load_shared(0).start()
+    grad_total[...] = jnp.zeros_like(grad_total)
+    mid_down_ref[...] = jnp.zeros_like(mid_down_ref)
+    grad_mid_up_ref[...] = jnp.zeros_like(grad_mid_up_ref)
+
+    @pl.loop(0, SHARED)
+    def _(expert):
+        advance(expert)
+        compute(expert, True)
+
+    @pl.loop(SHARED, count)
+    def _(expert):
+        advance(expert)
+        compute(expert, False)
+
+    grad_ref[...] = to_low(grad_total[...])
+    store_act(count - 2).wait()
+    store_act(count - 1).wait()
+    finish()
+
+
+def experts_plain(inputs, gates, mid_up, grad_mid, up_extra, down_extra, up_rows, open_rows):
+    count, length = gates.shape
+    hidden = open_rows.shape[0] // count
+    width = inputs.shape[0]
+    grad_total = jnp.zeros((length, width), jnp.float32)
+    act_parts, gate_grads, down_parts, up_parts = [], [], [], []
+    mid_down = jnp.zeros((NARROW, length), jnp.float32)
+    grad_mid_up = jnp.zeros((NARROW, length), jnp.float32)
+    for expert in range(count):
+        weights = up_rows[2 * hidden * expert : 2 * hidden * (expert + 1)]
+        gate_up = matmul(weights, inputs)
+        extra = None
+        if expert < SHARED:
+            gate_up = gate_up + matmul(up_extra[expert], mid_up)
+            extra = matmul(down_extra[expert], grad_mid)
+        act, act_gated, gate_grad, grad_gate, grad_up = hidden_step(
+            gate_up,
+            open_rows[hidden * expert : hidden * (expert + 1)].astype(jnp.float32),
+            gates[expert : expert + 1],
+            extra,
+        )
+        grad = jnp.concatenate([grad_gate, grad_up], axis=0)
+        act_parts.append(act_gated)
+        gate_grads.append(gate_grad)
+        grad_total = grad_total + contract_first(grad, weights)
+        if expert < SHARED:
+            mid_down = mid_down + contract_first(down_extra[expert], act)
+            grad_mid_up = grad_mid_up + contract_first(up_extra[expert], grad)
+            down_parts.append(contract_last(grad_mid, act))
+            up_parts.append(ADAPTER_SCALE * contract_last(mid_up, grad))
+    return (
+        grad_total,
+        jnp.concatenate(gate_grads, axis=0),
+        mid_down,
+        grad_mid_up,
+        jnp.stack(down_parts),
+        jnp.stack(up_parts),
+        jnp.concatenate(act_parts, axis=0),
+    )
+
+
+def experts_step(
+    inputs, gates, mid_up, grad_mid, up_extra, down_extra, shared_up, block, open_rows, number
+):
+    width, length = inputs.shape
+    count = SHARED + EXPERTS
+    hidden = open_rows.shape[0] // count
+    if not in_plane():
+        whole = lax.all_gather(block, "dp", axis=1, tiled=True)
+        up_rows = jnp.concatenate([shared_up, whole], axis=0)
+        return experts_plain(
+            inputs, gates, mid_up, grad_mid, up_extra, down_extra, up_rows, open_rows
+        )
+    pieces = HALVES * EXPERTS
     return pl.pallas_call(
-        experts_kernel,
-        grid=(count,),
-        in_specs=[
-            still((width, length)),
-            ahead(1),
-            pl.BlockSpec((1, 2 * hidden, width), lambda expert: (expert, 0, 0)),
-            ahead(hidden),
-            pl.BlockSpec(memory_space=pltpu.HBM),
-        ],
-        out_specs=[still((length, width)), here(hidden), here(1)],
+        functools.partial(experts_kernel, pieces),
+        in_specs=in_vmem(6) + in_hbm(3),
+        out_specs=in_vmem(6) + in_hbm(2),
         out_shape=[
-            jax.ShapeDtypeStruct((length, width), jnp.float32),
-            jax.ShapeDtypeStruct((count, hidden, length), jnp.bfloat16),
-            jax.ShapeDtypeStruct((count, 1, length), jnp.float32),
+            jax.ShapeDtypeStruct((length, width), jnp.bfloat16),
+            jax.ShapeDtypeStruct((count, length), jnp.float32),
+            jax.ShapeDtypeStruct((NARROW, length), jnp.float32),
+            jax.ShapeDtypeStruct((NARROW, length), jnp.float32),
+            jax.ShapeDtypeStruct((SHARED, NARROW, hidden), jnp.float32),
+            jax.ShapeDtypeStruct((SHARED, NARROW, 2 * hidden), jnp.float32),
+            jax.ShapeDtypeStruct((count * hidden, length), jnp.bfloat16),
+            jax.ShapeDtypeStruct((EXPERTS * 2 * hidden, width), jnp.bfloat16),
         ],
         scratch_shapes=[
+            pltpu.VMEM((length, width), jnp.float32),
+            pltpu.VMEM((2, 2 * hidden, width), jnp.bfloat16),
+            pltpu.VMEM((2, hidden, length), jnp.bfloat16),
+            pltpu.VMEM((2, hidden, length), jnp.bfloat16),
             pltpu.VMEM((2 * hidden, length), jnp.bfloat16),
-            pltpu.SemaphoreType.DMA((1,)),
+            pltpu.SemaphoreType.DMA((18, pieces)),
+            pltpu.SemaphoreType.DMA((4, 2)),
         ],
         compiler_params=pltpu.CompilerParams(
-            vmem_limit_bytes=58 * 2**20, dimension_semantics=("arbitrary",)
+            collective_id=number, has_side_effects=True, vmem_limit_bytes=60 * 2**20
         ),
-        cost_estimate=pl.CostEstimate(
-            flops=12 * count * hidden * width * length,
-            bytes_accessed=32 * 2**20,
-            transcendentals=0,
-        ),
-    )(inputs, gates, up_rows, open_rows, grad_start)
-
-
-def swiglu(paired):
-    return jax.nn.silu(paired[..., 0, :]) * paired[..., 1, :]
+        cost_estimate=pl.CostEstimate(flops=0, bytes_accessed=600 * 2**20, transcendentals=0),
+    )(inputs, gates, mid_up, grad_mid, up_extra, down_extra, shared_up, block, open_rows)[:7]
 
 
 def gathered(weight):
@@ -859,10 +1001,14 @@
     query, keys, values, attended = attend(qkv_sum, *places)
     branch_part = contract_last(attended, output_rows)
     down_block = jnp.transpose(routed_down_weight, (1, 2, 0))
+    depth = down_block.shape[2]
+    down_block = jnp.concatenate(
+        [shared_expert_down_weight.T, down_block.reshape(-1, depth)], axis=0
+    )
     branch_here, mid_out_here_f, down_rows, open_rows = summed_and_gathered(
         branch_part,
         matmul(attended, out_a),
-        down_block.reshape(-1, down_block.shape[2]),
+        down_block,
         cotangent.T,
         1,
     )
@@ -874,10 +1020,6 @@
     normed_two_here = to_low(normed_two_here_f)
     normed_two = normed_two_here
     cot_f = cotangent.astype(jnp.float32)
-    shared_three = gathered(
-        jnp.concatenate([shared_expert_gate_up_weight, shared_expert_down_weight[:, None]], axis=1)
-    )
-    shared_rows, sdown_rows = shared_three[:, :2], shared_three[:, 2]
     small_rows = gathered(
         jnp.concatenate(
             [
@@ -895,67 +1037,66 @@
     chosen = jnp.sum(
         (routes[:, :, None] == expert_ids[None, None, :]).astype(jnp.float32), axis=1
     )
-    gate_table = (router_probs * chosen).T
-
+    gates = jnp.concatenate(
+        [jnp.broadcast_to(shared_gate[None], (SHARED, length)), (router_probs * chosen).T], axis=0
+    )
+    hidden = shared_expert_down_weight.shape[1] // SHARED
+    rank = up_a.shape[1]
+
+    def fill(rows):
+        return jnp.pad(to_low(rows), ((0, NARROW - rows.shape[0]), (0, 0)))
+
+    def fill_last(rows):
+        return jnp.pad(to_low(rows), ((0, 0), (0, 0), (0, NARROW - rows.shape[2])))
+
+    cotangent_down = ADAPTER_SCALE * contract_last(cotangent, down_b)
     mid_up = to_low(matmul(normed_two, up_a))
-    shared_gu = jnp.einsum(
-        "tr,rxf->txf", normed_two, shared_rows, preferred_element_type=jnp.float32
-    ) + ADAPTER_SCALE * jnp.einsum("tr,rxf->txf", mid_up, up_b, preferred_element_type=jnp.float32)
-    shared_act_f, shared_pull = jax.vjp(swiglu, shared_gu)
-    shared_act = to_low(shared_act_f)
-    shared_cols = contract_last(shared_act, sdown_rows)
-    shared_gate_part = jnp.sum(cot_f * shared_cols, axis=1)
-    grad_shared = to_low(shared_gate[:, None] * cot_f)
-    cotangent_down = ADAPTER_SCALE * contract_last(cotangent, down_b)
-    grad_mid_down = to_low(ADAPTER_SCALE * contract_last(grad_shared, down_b))
-    grad_shared_act = matmul(grad_shared, sdown_rows) + contract_last(grad_mid_down, down_a)
-    grad_shared_gu = to_low(shared_pull(grad_shared_act)[0])
-    grad_mid_up_part = ADAPTER_SCALE * jnp.einsum(
-        "txf,rxf->tr", grad_shared_gu, up_b, preferred_element_type=jnp.float32
-    )
-    grad_up_b_local = ADAPTER_SCALE * jnp.einsum(
-        "tr,txf->rxf", mid_up, grad_shared_gu, preferred_element_type=jnp.float32
-    )
-    grad_down_a_local = contract_first(grad_mid_down, shared_act)
-    combined_part = shared_gate[:, None] * shared_cols
-    normed_two_part = jnp.einsum(
-        "txf,rxf->tr", grad_shared_gu, shared_rows, preferred_element_type=jnp.float32
-    )
-
+    grad_mid_down = shared_gate[:, None] * cotangent_down
+    up_extra = ADAPTER_SCALE * up_b.reshape(rank, 2, SHARED, hidden).transpose(2, 1, 3, 0)
+    shared_block = shared_expert_gate_up_weight.reshape(-1, 2, SHARED, hidden)
+    shared_up = lax.all_gather(
+        shared_block.transpose(2, 1, 3, 0).reshape(-1, depth), "dp", axis=1, tiled=True
+    )
     up_block = jnp.transpose(routed_gate_up_weight, (1, 2, 3, 0))
-    inputs_t = normed_two.T
-    gates = gate_table.reshape(EXPERTS, 1, length)
-    open_rows = open_rows.reshape(EXPERTS, -1, length)
-    gate_grad_parts = []
-    act_parts = []
-    first = 0
-    for count in EXPERT_PARTS:
-        up_rows = lax.all_gather(up_block[first : first + count], "dp", axis=3, tiled=True)
-        normed_two_part, act_part, gate_grads = experts_step(
-            inputs_t,
-            gates,
-            up_rows.reshape(count, -1, width),
-            open_rows,
-            normed_two_part,
-            first,
-        )
-        act_parts.append(act_part.reshape(-1, length))
-        gate_grad_parts.append(gate_grads.reshape(count, length))
-        first += count
-    gate_grad_part = jnp.concatenate(gate_grad_parts, axis=0).T
+    (
+        normed_two_part,
+        gate_grads,
+        mid_down_part,
+        grad_mid_up_part,
+        grad_down_a_parts,
+        grad_up_b_parts,
+        act_rows,
+    ) = experts_step(
+        normed_two.T,
+        gates,
+        fill(mid_up.T),
+        fill(grad_mid_down.T),
+        fill_last(up_extra.reshape(SHARED, 2 * hidden, rank)),
+        fill_last(down_a.reshape(SHARED, hidden, rank)),
+        shared_up,
+        up_block.reshape(-1, depth),
+        open_rows,
+        5,
+    )
+    grad_down_a_local = grad_down_a_parts[:, :rank].transpose(1, 0, 2).reshape(rank, -1)
+    grad_up_b_local = (
+        grad_up_b_parts[:, :rank]
+        .reshape(SHARED, rank, 2, hidden)
+        .transpose(1, 2, 0, 3)
+        .reshape(rank, 2, -1)
+    )
     narrow_part = jnp.concatenate(
         [
-            gate_grad_part,
-            shared_gate_part[:, None],
-            grad_mid_up_part,
-            matmul(shared_act, down_a),
+            gate_grads[SHARED:],
+            jnp.sum(gate_grads[:SHARED], axis=0, keepdims=True),
+            grad_mid_up_part[:rank],
+            mid_down_part[:rank],
         ],
-        axis=1,
-    )
+        axis=0,
+    ).T
     grad_normed_two, narrow_sum, combined_part = summed_and_down(
-        normed_two_part, narrow_part, combined_part, act_parts, down_rows, 2
-    )
-    rank = up_a.shape[1]
+        normed_two_part, narrow_part, act_rows, down_rows, 2
+    )
     mid_down = to_low(narrow_sum[:, EXPERTS + 1 + rank :])
     grad_mid_up = to_low(narrow_sum[:, EXPERTS + 1 : EXPERTS + 1 + rank])
     grad_probs = chosen * narrow_sum[:, :EXPERTS]
@@ -981,7 +1122,9 @@
     )
     extra_here = ADAPTER_SCALE * matmul(mid_down, down_b)
     output = to_low(hidden_here + combined_here + shared_gate[:, None] * extra_here)
-    grad_down_b_local = ADAPTER_SCALE * contract_first(mid_down, grad_shared)
+    grad_down_b_local = ADAPTER_SCALE * contract_first(
+        to_low(shared_gate[:, None] * mid_down.astype(jnp.float32)), cotangent
+    )
     grad_up_a_local = contract_first(grad_mid_up, normed_two)
     grad_out_b_local = ADAPTER_SCALE * contract_first(mid_out, grad_branch)
     grad_out_a_local = contract_first(grad_mid_out, attended)

time: 1060 us -> 1200 us (1.13)
  Pallas kernels: 714 us -> 946 us
  matrix products: 193 us -> 97.2 us
    pallas_call x3 -> x1, Pallas kernels: 148 us -> 371 us  [experts_step(): pl.pallas_call(functools.partial(experts_kernel, pieces), in_specs=in_vme...]
    dot_general x5 -> x0, matrix products: 58.3 us -> none  [the longest x1 23 us: body(): jnp.einsum('tr,rxf->txf', normed_two, shared_rows, preferred_element_type...]
    dot_general x9 -> x6, matrix products: 49.6 us -> 27.6 us  [contract_last(): lax.dot_general(left_side, right_side, (((1,), (1,)), ((), ())), preferre...]
    dot_general x10 -> x8, matrix products: 38.3 us -> 27.5 us  [matmul(): return jnp.dot(left_side, right_side, preferred_element_type=jnp.float32)]
    unnamed x180 -> x117, local copies, waits for them, and re-layouts: 28.2 us -> 32.5 us
  transfers between devices with their start and end apart: 6 -> 3, of which waited for: 1 -> 1; matrix products, arithmetic and copies ran while one was open for 20% -> 11% of each run, Pallas kernels for 53% -> 38%
where the time goes in v5:
time: 1200 us
  Pallas kernels  946 us (79%)
  matrix products  97.2 us (8%)
  local copies, waits for them, and re-layouts  61.3 us (5%)
  other arithmetic  38 us (3%)
  blocking collectives  21.4 us (2%)
  waiting for transfers between devices  17.1 us (1%)
  between operations  15.5 us (1%)
    pallas_call x1, Pallas kernels, experts_step(): pl.pallas_call(functools.partial(experts_kernel, pieces), in_specs=in_vme...  371 us
    pallas_call x1, Pallas kernels, summed_and_gathered(): pl.pallas_call(functools.partial(sum_gather_kernel, SUM_CHUNKS, pieces),...  214 us
    pallas_call x1, Pallas kernels, summed_and_down(): pl.pallas_call(functools.partial(sum_down_kernel, SUM_CHUNKS), out_shape=...  120 us
    pallas_call x1, Pallas kernels, summed(): pl.pallas_call(functools.partial(line_sum_kernel, SUM_CHUNKS), out_shape=...  114 us
    pallas_call x1, Pallas kernels, summed_and_attended_back(): pl.pallas_call(functools.partial(attend_back_sum_kernel, SUM_CHUNKS), out...  112 us
    unnamed x117, local copies, waits for them, and re-layouts  32.5 us
    dot_general x6, matrix products, contract_last(): lax.dot_general(left_side, right_side, (((1,), (1,)), ((), ())), preferre...  27.6 us
    dot_general x8, matrix products, matmul(): return jnp.dot(left_side, right_side, preferred_element_type=jnp.float32)  27.5 us
  transfers between devices with their start and end apart: 3, of which 1 were waited for; matrix products, arithmetic and copies ran while one was open for 11% of the time, Pallas kernels for 38%

profile of v5, /device:TPU:0, one launch (start us, length us, event | category | flops | bytes accessed | tf_op | source)
XLA Modules:
  0.0 1196.3 jit_solution(9131211169328577294)
XLA Ops:
  7.3 1.5 copy.179
  8.8 1.1 copy.178
  9.9 1.1 pad_maximum_fusion.1
  11.0 3.7 copy.192
  14.7 1.2 copy.193
  17.4 6.5 copy.185
  23.9 1.0 copy.188
  24.9 1.0 dynamic-slice_multiply_fusion
  27.5 1.0 pad.20.up_extra_ref
  29.5 10.8 all_gather.22
  40.9 4.4 fusion.3
  46.2 1.9 fusion.36
  48.5 2.3 fusion.30
  50.9 2.1 pad_maximum_fusion.block_ref
  52.9 17.0 %all-gather.6.cloned.1.call-done = bf16[2048,4,512]{0,2,1:T(8,128)(2,1)} async-done(((bf16[256,4,512]{0,2,1:T(8,128)(2,1)}), bf16[2048,4,512]{0,2,1:T(8,128)(2,1)}) %all-gather.6.cloned.1.call-update) | async-done | bytes 8388624 | tf_op jit(solution)/shard_map/all_gather | solution.py:935
  70.0 10.9 fusion.14
  80.8 4.5 add_bitcast_fusion.qkv_ref
  85.4 14.6 %shard_map.303 = (bf16[1024,512]{1,0:T(8,128)(2,1)S(1)}, bf16[1024,512]{1,0:T(8,128)(2,1)S(1)}, bf16[1024,512]{1,0:T(8,128)(2,1)S(1)}, bf16[1024,512]{1,0:T(8,128)(2,1)S(1)}) custom-call(f32[3,1024,512]{2,1,0:T(8,128)} %add_bitcast_fusion.qkv_ref, f32[1024,128]{1,0:T(8,128)S(1)} %get-tuple-element.113.cosine_ref.refs_4_, ...), custom_call_target="tpu_custom_call" | custom-call | flops 2147483648 | bytes 16777216 | tf_op jit(solution)/shard_map/pallas_call | solution.py:587
  100.9 1.0 copy-done.5
  101.9 1.0 copy-done.6
  102.9 1.1 convolution_convert_fusion.3
  104.9 7.7 fusion.24.wide_ref
  112.6 214.3 %shard_map.304 = (bf16[1024,2176]{1,0:T(8,128)(2,1)}, bf16[7040,2048]{1,0:T(8,128)(2,1)}, bf16[7040,1024]{1,0:T(8,128)(2,1)}) custom-call(f32[1024,2048]{1,0:T(8,128)} %fusion.24.wide_ref, bf16[1024,128]{1,0:T(8,128)(2,1)} %concatenate.47.narrow_ref, bf16[7040,256]{1,0:T(8,128)(2,1)} %pad_maximum_fusion.block_ref, bf16[2048,1024]{1,0:T(8,128)(2,1)} %bitcast.141), custom_call_target="tpu_custom_call" | custom-call | bytes 377487360 | tf_op jit(solution)/shard_map/pallas_call | solution.py:481
  326.9 5.7 multiply_reduce_fusion.1
  333.9 1.9 copy-done.8
  335.9 1.2 fusion.110
  339.1 3.5 fusion.81
  343.2 3.4 multiply_convert_fusion.1
  347.3 1.2 convolution_convert_fusion.2
  349.2 6.1 fusion.129
  355.4 6.8 copy.194.inputs_ref
  363.1 370.7 %shard_map.305 = (bf16[1024,2048]{1,0:T(8,128)(2,1)}, f32[20,1024]{1,0:T(8,128)}, f32[128,1024]{1,0:T(8,128)}, f32[128,1024]{1,0:T(8,128)}, f32[4,128,352]{2,1,0...) custom-call(bf16[2048,1024]{1,0:T(8,128)(2,1)} %copy.194.inputs_ref, ...), custom_call_target="tpu_custom_call" | custom-call | bytes 629145600 | tf_op jit(solution)/shard_map/pallas_call | solution.py:904
  737.9 1.1 copy.195
  739.7 119.6 %shard_map.306 = (bf16[1024,2176]{1,0:T(8,128)(2,1)}, bf16[1024,2048]{1,0:T(8,128)(2,1)}) custom-call(bf16[1024,2048]{1,0:T(8,128)(2,1)} %get-tuple-element.31.wide_ref, bf16[1024,128]{1,0:T(8,128)(2,1)} %concatenate.52.narrow_ref, bf16[7040,1024]{1,0:T(8,128)(2,1)} %get-tuple-element.35.act_ref, bf16[7040,2048]{1,0:T(8,128)(2,1)} %get-tuple-element.36.down_ref), custom_call_target="tpu_custom_call" | custom-call | bytes 314572800 | tf_op jit(solution)/shard_map/pallas_call | solution.py:512
  859.3 2.8 convert_element_type.157
  862.7 1.4 slice_reduce_fusion
  864.2 2.0 slice.122
  866.8 1.3 fusion.34
  868.8 1.1 copy.200
  869.8 6.9 multiply_reduce_fusion
  876.9 4.4 fusion
  881.3 2.1 fusion.28
  883.7 2.5 fusion.19
  886.5 1.7 fusion.22
  890.6 3.1 fusion.21
  894.4 6.3 fusion.23
  900.7 2.2 add_convert_fusion.1.refs_3_
  902.9 112.4 %shard_map.307 = (bf16[1024,2048]{1,0:T(8,128)(2,1)}, bf16[3,1024,512]{2,1,0:T(8,128)(2,1)}) custom-call(bf16[1024,2048]{1,0:T(8,128)(2,1)} %get-tuple-element.37.wide_ref, bf16[1024,512]{1,0:T(8,128)(2,1)} %copy-done.4, bf16[1024,512]{1,0:T(8,128)(2,1)} %copy-done.5, bf16[1024,512]{1,0:T(8,128)(2,1)} %copy-done.6, ...), custom_call_target="tpu_custom_call" | custom-call | bytes 314572800 | tf_op jit(solution)/shard_map/pallas_call | solution.py:677
  1015.3 3.0 fusion.26
  1018.4 10.9 fusion.11.refs_0_
  1029.8 114.2 %shard_map.308 = bf16[1024,2176]{1,0:T(8,128)(2,1)S(1)} custom-call(f32[1024,2048]{1,0:T(8,128)} %fusion.11.refs_0_, bf16[1024,128]{1,0:T(8,128)(2,1)S(1)} %concatenate.55.refs_1_), custom_call_target="tpu_custom_call" | custom-call | bytes 314572800 | tf_op jit(solution)/shard_map/pallas_call | solution.py:458
  1144.0 1.1 convolution_convert_fusion.1
  1145.2 10.6 all-gather
  1156.9 1.6 copy.210
  1158.5 1.3 copy.211
  1159.8 5.2 fusion.7
  1165.1 6.2 add_convert_fusion
  1171.3 6.4 fusion.2
  1177.8 2.8 fusion.16
  1181.2 1.6 copy.213
  1182.7 1.6 copy.214
  1184.3 1.6 copy.217
  1185.9 1.8 copy.215
  1187.7 1.0 copy.216
  (184 shorter events, 26.9 us)
Async XLA Ops:
  7.2 336.0 %copy-start = (bf16[8,16,2048]{2,1,0:T(8,128)(2,1)S(1)}, bf16[8,16,2048]{2,1,0:T(8,128)(2,1)}, u32[]{:S(2)}) copy-start(bf16[8,16,2048]{2,1,0:T(8,128)(2,1)} %param.47) | copy-start | bytes 1572868
  7.2 9.4 copy-start.41
  7.2 9.5 copy-start.42
  7.2 9.5 copy-start.45
  7.2 9.8 copy-start.21
  7.2 62.7 %all-gather.6.cloned.1.call-start = ((), (), s32[]{:S(2)}) async-start(), calls=%async_computation | async-start | bytes 9437184 | tf_op jit(solution)/shard_map/all_gather | solution.py:935
  11.0 352.2 %all-gather.8.cloned.1.call-start = ((), (), s32[]{:S(2)}) async-start(), calls=%async_computation.1 | async-start | bytes 12976128 | tf_op jit(solution)/shard_map/all_gather | solution.py:1057
  15.9 8.0 copy-start.43
  15.9 8.0 copy-start.46
  15.9 8.0 copy-start.37
  15.9 1161.8 %all-gather.10.cloned.1.call-start = ((), (), s32[]{:S(2)}) async-start(), calls=%async_computation.2 | async-start | bytes 3133440 | tf_op jit(solution)/shard_map/all_gather | solution.py:1158
  16.7 53.3 %copy-start.24 = (f32[2048]{0:T(1024)}, f32[2048]{0:T(1024)S(1)}, u32[]{:S(2)}) copy-start(f32[2048]{0:T(1024)S(1)} %convert_element_type.144) | copy-start | bytes 24580
  16.8 68.5 %copy-start.7 = (s32[1024]{0:T(1024)}, s32[1024]{0:T(1024)S(1)}, u32[]{:S(2)}) copy-start(s32[1024]{0:T(1024)S(1)} %broadcast_add_fusion) | copy-start | bytes 12292
  17.1 68.3 %copy-start.3 = (s32[1024,1]{1,0:T(8,128)}, s32[1024,1]{1,0:T(8,128)S(1)}, u32[]{:S(2)}) copy-start(s32[1024,1]{1,0:T(8,128)S(1)} %copy.182.row_piece_ref.refs_6_) | copy-start | bytes 12292
  17.4 12.0 %copy-start.40 = (bf16[256,16]{0,1:T(8,128)(2,1)S(1)}, bf16[256,16]{0,1:T(8,128)(2,1)}, u32[]{:S(2)}) copy-start(bf16[256,16]{0,1:T(8,128)(2,1)} %param.31) | copy-start | bytes 24580
  40.4 8.1 copy-start.15
  45.3 2.8 copy-start.31
  45.3 24.7 %copy-start.35 = (f32[1024]{0:T(1024)}, f32[1024]{0:T(1024)S(1)}, u32[]{:S(2)}) copy-start(f32[1024]{0:T(1024)S(1)} %fusion.87) | copy-start | bytes 12292
  46.2 301.1 %copy-start.22 = (bf16[2048,16]{0,1:T(8,128)(2,1)}, bf16[2048,16]{0,1:T(8,128)(2,1)S(1)}, u32[]{:S(2)}) copy-start(bf16[2048,16]{0,1:T(8,128)(2,1)S(1)} %dynamic-slice_bitcast_fusion) | copy-start | bytes 196612
  48.5 36.9 %copy-start.1 = (f32[1024,128]{1,0:T(8,128)}, f32[1024,128]{1,0:T(8,128)S(1)}, u32[]{:S(2)}) copy-start(f32[1024,128]{1,0:T(8,128)S(1)} %get-tuple-element.113.cosine_ref.refs_4_) | copy-start | bytes 1572868
  48.5 36.9 %copy-start.2 = (f32[1024,128]{1,0:T(8,128)}, f32[1024,128]{1,0:T(8,128)S(1)}, u32[]{:S(2)}) copy-start(f32[1024,128]{1,0:T(8,128)S(1)} %get-tuple-element.114.sine_ref.refs_5_) | copy-start | bytes 1572868
  48.5 2.4 copy-start.20
  99.9 1.0 copy-start.4
  100.9 1.0 copy-start.5
  101.9 1.0 copy-start.6
  332.6 0.6 copy-start.38
  332.6 3.3 copy-start.8
  335.9 2.0 copy-start.10
  335.9 2.6 copy-start.18
  338.5 10.0 copy-start.26
  339.1 8.3 copy-start.11
  342.6 0.6 copy-start.28
  343.2 12.2 %copy-start.33 = (f32[1024]{0:T(1024)}, f32[1024]{0:T(1024)S(1)}, u32[]{:S(2)}) copy-start(f32[1024]{0:T(1024)S(1)} %get-tuple-element.99) | copy-start | bytes 12292
  343.2 19.3 %copy-start.29 = (f32[1024]{0:T(1024)}, f32[1024]{0:T(1024)S(1)}, u32[]{:S(2)}) copy-start(f32[1024]{0:T(1024)S(1)} %get-tuple-element.100) | copy-start | bytes 12292
  859.3 2.9 copy-start.27
  862.2 4.0 copy-start.14
  869.8 7.0 copy-start.39
  869.8 7.1 copy-start.13
  881.3 4.9 copy-start.9
  883.4 3.0 copy-start.12
  883.7 6.9 copy-start.30
  893.6 0.7 copy-start.23
  1015.3 3.1 copy-start.19
  1029.8 114.2 %copy-start.16 = (bf16[1024,2048]{1,0:T(8,128)(2,1)S(1)}, bf16[1024,2048]{1,0:T(8,128)(2,1)}, u32[]{:S(2)}) copy-start(bf16[1024,2048]{1,0:T(8,128)(2,1)} %param.24) | copy-start | bytes 12582916
  1029.8 114.2 %copy-start.25 = (f32[2048]{0:T(1024)S(1)}, f32[2048]{0:T(1024)}, u32[]{:S(2)}) copy-start(f32[2048]{0:T(1024)} %copy-done.24) | copy-start | bytes 24580
  1029.8 114.2 %copy-start.36 = (f32[1024]{0:T(1024)S(1)}, f32[1024]{0:T(1024)}, u32[]{:S(2)}) copy-start(f32[1024]{0:T(1024)} %copy-done.35) | copy-start | bytes 12292
  1144.0 11.8 copy-start.44
  1156.9 8.2 slice-start
  1159.8 5.3 copy-start.32
  1159.8 5.3 slice-start.1
  1159.8 5.3 copy-start.34
  1159.8 11.5 slice-start.2
  1165.1 6.2 slice-start.3
  1165.1 6.2 copy-start.17
Sparse Core Ops, SparseCore 0:
  11.1 58.8 all-gather.5
  72.4 87.6 all-gather.7
  894.5 28.9 all-gather.9

commit v6 on v5

--- a/solution.py
+++ b/solution.py
@@ -215,9 +215,6 @@
         for device in (core_mate, x_mate, y_mate):
             pl.semaphore_signal(barrier, inc=1, device_id={"dp": device}, device_id_type=MESH)
 
-    def begin():
-        own().start()
-
     def launch(piece):
         @pl.when((piece >= 0) & (piece < pieces))
         def _():
@@ -247,11 +244,27 @@
         forward(step - AHEAD)
         hand_over(step - 2 * AHEAD)
 
+    def load(first, count, target, semaphore):
+        span = pl.ds(pl.multiple_of(first, rows), count)
+
+        def columns(owner):
+            return pl.ds(pl.multiple_of(owner * depth, depth), depth)
+
+        here = columns(spot)
+        copies = [pltpu.make_async_copy(block_ref.at[span], target.at[:, here], semaphore)]
+        for shift in range(1, 8):
+            there = columns((spot + shift) % 8)
+            copies.append(
+                pltpu.make_async_copy(
+                    whole_ref.at[span, there], target.at[:, there], semaphore
+                )
+            )
+        return copies
+
+    def load_wait(count, target, semaphore):
+        pltpu.make_async_copy(whole_ref.at[pl.ds(0, count)], target, semaphore).wait()
+
     def arrive(piece):
-        @pl.when(piece == 0)
-        def _():
-            own().wait()
-
         for name in ("core", "x_core", "y_core", "xy_core", "yx_core"):
             send(name, piece).wait_recv()
 
@@ -261,7 +274,7 @@
             for name in order:
                 send(name, piece).wait_send()
 
-    return greet, begin, advance, arrive, finish, (launch, forward, hand_over)
+    return greet, advance, arrive, finish, own, load, load_wait, (launch, forward, hand_over)
 
 
 def line_sum_kernel(chunks, *refs):
@@ -292,19 +305,12 @@
         chunks, wide_ref, narrow_ref, total_ref, *scratch[:5]
     )
     gather_semaphores, local_semaphores, piece_rows, open_rows = scratch[5:]
-    gather_greet, gather_begin, gather_advance, gather_arrive, gather_finish, _ = (
+    gather_greet, gather_advance, gather_arrive, gather_finish, own, load, load_wait, _ = (
         plane_gather_steps(
             pieces, block_ref, whole_ref, gather_semaphores, local_semaphores.at[0]
         )
     )
     rows = piece_rows.shape[1]
-
-    def load(piece):
-        slot = piece % 2
-        span = pl.ds(pl.multiple_of(piece * rows, rows), rows)
-        return pltpu.make_async_copy(
-            whole_ref.at[span], piece_rows.at[slot], local_semaphores.at[1 + slot]
-        )
 
     def store(piece):
         slot = piece % 2
@@ -316,7 +322,7 @@
     gather_greet()
     greet(3)
     begin()
-    gather_begin()
+    own().start()
 
     @pl.loop(0, max(chunks + 1, pieces + 3 * AHEAD + 1))
     def _(step):
@@ -325,13 +331,17 @@
 
         @pl.when((step >= 3 * AHEAD) & (step < pieces + 3 * AHEAD))
         def _():
-            gather_arrive(step - 3 * AHEAD)
-            load(step - 3 * AHEAD).start()
+            piece = step - 3 * AHEAD
+            gather_arrive(piece)
+            slot = piece % 2
+            for copy in load(piece * rows, rows, piece_rows.at[slot], local_semaphores.at[1 + slot]):
+                copy.start()
 
         @pl.when((step > 3 * AHEAD) & (step <= pieces + 3 * AHEAD))
         def _():
             piece = step - 3 * AHEAD - 1
-            load(piece).wait()
+            slot = piece % 2
+            load_wait(rows, piece_rows.at[slot], local_semaphores.at[1 + slot])
 
             @pl.when(piece >= 2)
             def _():
@@ -342,6 +352,7 @@
 
     store(pieces - 2).wait()
     store(pieces - 1).wait()
+    own().wait()
     gather_finish()
     finish()
 
@@ -732,8 +743,8 @@
     gather_semaphores,
     semaphores,
 ):
-    greet, begin, _, arrive, finish, (launch, forward, hand_over) = plane_gather_steps(
-        pieces, block_ref, whole_ref, gather_semaphores, semaphores.at[0, 0]
+    greet, _, arrive, finish, _, load, load_wait, (launch, forward, hand_over) = (
+        plane_gather_steps(pieces, block_ref, whole_ref, gather_semaphores, None)
     )
     hidden = open_rows.shape[1]
     count = SHARED + EXPERTS
@@ -752,14 +763,6 @@
         slot = expert % 2
         return pltpu.make_async_copy(
             shared_up_ref.at[span(expert, 2 * hidden)], up_rows.at[slot], semaphores.at[2, slot]
-        )
-
-    def load_routed(expert):
-        slot = expert % 2
-        return pltpu.make_async_copy(
-            whole_ref.at[span(expert - SHARED, 2 * hidden)],
-            up_rows.at[slot],
-            semaphores.at[2, slot],
         )
 
     def store_act(expert):
@@ -788,10 +791,13 @@
         def _():
             for part in range(each):
                 arrive(each * (expert + 1 - SHARED) + part)
-            load_routed(expert + 1).start()
+            slot = (expert + 1) % 2
+            first = (expert + 1 - SHARED) * 2 * hidden
+            for copy in load(first, 2 * hidden, up_rows.at[slot], semaphores.at[2, slot]):
+                copy.start()
 
         load_open(expert).wait()
-        load_shared(0 * expert + expert % 2).wait()
+        load_wait(2 * hidden, up_rows.at[expert % 2], semaphores.at[2, expert % 2])
 
         @pl.when(expert >= 2)
         def _():
@@ -824,7 +830,6 @@
 
     greet()
     pl.semaphore_wait(pltpu.get_barrier_semaphore(), 3)
-    begin()
     load_open(0).start()
     load_shared(0).start()
     grad_total[...] = jnp.zeros_like(grad_total)

time: 1200 us -> 1000 us (0.83)
  Pallas kernels: 946 us -> 746 us
    pallas_call x1, Pallas kernels: 371 us -> 231 us  [experts_step(): pl.pallas_call(functools.partial(experts_kernel, pieces), in_specs=in_vme...]
    pallas_call x1, Pallas kernels: 214 us -> 156 us  [summed_and_gathered(): pl.pallas_call(functools.partial(sum_gather_kernel, SUM_CHUNKS, pieces),...]
  transfers between devices with their start and end apart: 3 -> 3, of which waited for: 1 -> 1; matrix products, arithmetic and copies ran while one was open for 11% -> 13% of each run, Pallas kernels for 38% -> 40%
where the time goes in v6:
time: 1000 us; the launch traced here: 997 us
  Pallas kernels  746 us (75%)
  matrix products  97.2 us (10%)
  local copies, waits for them, and re-layouts  61.3 us (6%)
  other arithmetic  38 us (4%)
  blocking collectives  21.6 us (2%)
  waiting for transfers between devices  17.1 us (2%)
  between operations  15.5 us (2%)
    pallas_call x1, Pallas kernels, experts_step(): pl.pallas_call(functools.partial(experts_kernel, pieces), in_specs=in_vme...  231 us
    pallas_call x1, Pallas kernels, summed_and_gathered(): pl.pallas_call(functools.partial(sum_gather_kernel, SUM_CHUNKS, pieces),...  156 us
    pallas_call x1, Pallas kernels, summed_and_down(): pl.pallas_call(functools.partial(sum_down_kernel, SUM_CHUNKS), out_shape=...  118 us
    pallas_call x1, Pallas kernels, summed_and_attended_back(): pl.pallas_call(functools.partial(attend_back_sum_kernel, SUM_CHUNKS), out...  113 us
    pallas_call x1, Pallas kernels, summed(): pl.pallas_call(functools.partial(line_sum_kernel, SUM_CHUNKS), out_shape=...  112 us
    unnamed x117, local copies, waits for them, and re-layouts  32.5 us
    dot_general x6, matrix products, contract_last(): lax.dot_general(left_side, right_side, (((1,), (1,)), ((), ())), preferre...  27.6 us
    dot_general x8, matrix products, matmul(): return jnp.dot(left_side, right_side, preferred_element_type=jnp.float32)  27.5 us
  transfers between devices with their start and end apart: 3, of which 1 were waited for; matrix products, arithmetic and copies ran while one was open for 13% of the time, Pallas kernels for 40%

profile of v6, /device:TPU:0, one launch (start us, length us, event | category | flops | bytes accessed | tf_op | source)
XLA Modules:
  0.0 996.9 jit_solution(17082607399172262583)
XLA Ops:
  7.3 1.5 copy.179
  8.8 1.1 copy.178
  9.9 1.1 pad_maximum_fusion.1
  11.0 3.7 copy.192
  14.7 1.2 copy.193
  17.4 6.5 copy.185
  23.9 1.0 copy.188
  24.9 1.0 dynamic-slice_multiply_fusion
  27.5 1.0 pad.20.up_extra_ref
  29.5 10.8 %all_gather.22 = bf16[2048,18]{0,1:T(8,128)(2,1)S(1)} all-gather(bf16[256,18]{0,1:T(8,128)(2,1)S(1)} %maximum_maximum_fusion), channel_id=1, replica_groups=mesh['dp'=8,'tensor'=4] {'dp'}, dimensions={0}, use_global_device_ids=true | all-gather | bytes 82944 | tf_op jit(solution)/shard_map/all_gather | solution.py:940
  40.9 4.4 fusion.3
  46.2 1.9 fusion.36
  48.5 2.3 fusion.30
  50.9 2.1 pad_maximum_fusion.block_ref
  52.9 17.0 %all-gather.6.cloned.1.call-done = bf16[2048,4,512]{0,2,1:T(8,128)(2,1)} async-done(((bf16[256,4,512]{0,2,1:T(8,128)(2,1)}), bf16[2048,4,512]{0,2,1:T(8,128)(2,1)}) %all-gather.6.cloned.1.call-update) | async-done | bytes 8388624 | tf_op jit(solution)/shard_map/all_gather | solution.py:940
  70.0 10.9 %fusion.14 = f32[3,512,1024]{1,2,0:T(8,128)S(1)} fusion(bf16[2048,4,512]{0,2,1:T(8,128)(2,1)} %all-gather.6.cloned.1.call-done, bf16[1024,2048]{1,0:T(8,128)(2,1)} %param.24, f32[2048]{0:T(1024)S(1)} %convert_element_type.144, f32[1024]{0:T(1024)S(1)} %fusion.87), kind=kOutput, calls=%fused_computation.26 | convolution fusion | flops 6450839552 | bytes 18886656 | tf_op jit(solution)/shard_map/tr,rsf->stf/dot_general | solution.py:997
  80.8 4.5 add_bitcast_fusion.qkv_ref
  85.4 14.6 %shard_map.303 = (bf16[1024,512]{1,0:T(8,128)(2,1)S(1)}, bf16[1024,512]{1,0:T(8,128)(2,1)S(1)}, bf16[1024,512]{1,0:T(8,128)(2,1)S(1)}, bf16[1024,512]{1,0:T(8,128)(2,1)S(1)}) custom-call(f32[3,1024,512]{2,1,0:T(8,128)} %add_bitcast_fusion.qkv_ref, f32[1024,128]{1,0:T(8,128)S(1)} %get-tuple-element.113.cosine_ref.refs_4_, ...), custom_call_target="tpu_custom_call" | custom-call | flops 2147483648 | bytes 16777216 | tf_op jit(solution)/shard_map/pallas_call | solution.py:598
  100.9 1.0 copy-done.5
  101.9 1.0 copy-done.6
  102.9 1.1 convolution_convert_fusion.3
  104.9 7.7 fusion.24.wide_ref
  112.6 156.2 %shard_map.304 = (bf16[1024,2176]{1,0:T(8,128)(2,1)}, bf16[7040,2048]{1,0:T(8,128)(2,1)}, bf16[7040,1024]{1,0:T(8,128)(2,1)}) custom-call(f32[1024,2048]{1,0:T(8,128)} %fusion.24.wide_ref, bf16[1024,128]{1,0:T(8,128)(2,1)} %concatenate.47.narrow_ref, bf16[7040,256]{1,0:T(8,128)(2,1)} %pad_maximum_fusion.block_ref, bf16[2048,1024]{1,0:T(8,128)(2,1)} %bitcast.141), custom_call_target="tpu_custom_call" | custom-call | bytes 377487360 | tf_op jit(solution)/shard_map/pallas_call | solution.py:492
  268.9 5.7 multiply_reduce_fusion.1
  275.9 1.9 copy-done.8
  277.8 1.2 fusion.110
  281.0 3.5 fusion.81
  285.1 3.4 multiply_convert_fusion.1
  289.2 1.2 convolution_convert_fusion.2
  291.2 6.1 fusion.129
  297.3 6.8 copy.194.inputs_ref
  305.0 231.3 %shard_map.305 = (bf16[1024,2048]{1,0:T(8,128)(2,1)}, f32[20,1024]{1,0:T(8,128)}, f32[128,1024]{1,0:T(8,128)}, f32[128,1024]{1,0:T(8,128)}, f32[4,128,352]{2,1,0...) custom-call(bf16[2048,1024]{1,0:T(8,128)(2,1)} %copy.194.inputs_ref, ...), custom_call_target="tpu_custom_call" | custom-call | bytes 629145600 | tf_op jit(solution)/shard_map/pallas_call | solution.py:909
  540.4 1.1 copy.195
  542.3 118.5 %shard_map.306 = (bf16[1024,2176]{1,0:T(8,128)(2,1)}, bf16[1024,2048]{1,0:T(8,128)(2,1)}) custom-call(bf16[1024,2048]{1,0:T(8,128)(2,1)} %get-tuple-element.31.wide_ref, bf16[1024,128]{1,0:T(8,128)(2,1)} %concatenate.52.narrow_ref, bf16[7040,1024]{1,0:T(8,128)(2,1)} %get-tuple-element.35.act_ref, bf16[7040,2048]{1,0:T(8,128)(2,1)} %get-tuple-element.36.down_ref), custom_call_target="tpu_custom_call" | custom-call | bytes 314572800 | tf_op jit(solution)/shard_map/pallas_call | solution.py:523
  660.8 2.8 convert_element_type.157
  664.2 1.4 slice_reduce_fusion
  665.6 2.0 slice.122
  668.2 1.3 fusion.34
  670.2 1.1 copy.200
  671.3 6.9 multiply_reduce_fusion
  678.3 4.4 fusion
  682.8 2.1 fusion.28
  685.1 2.5 fusion.19
  687.9 1.7 fusion.22
  692.0 3.1 fusion.21
  695.8 6.3 fusion.23
  702.2 2.2 add_convert_fusion.1.refs_3_
  704.3 113.2 %shard_map.307 = (bf16[1024,2048]{1,0:T(8,128)(2,1)}, bf16[3,1024,512]{2,1,0:T(8,128)(2,1)}) custom-call(bf16[1024,2048]{1,0:T(8,128)(2,1)} %get-tuple-element.37.wide_ref, bf16[1024,512]{1,0:T(8,128)(2,1)} %copy-done.4, bf16[1024,512]{1,0:T(8,128)(2,1)} %copy-done.5, bf16[1024,512]{1,0:T(8,128)(2,1)} %copy-done.6, ...), custom_call_target="tpu_custom_call" | custom-call | bytes 314572800 | tf_op jit(solution)/shard_map/pallas_call | solution.py:688
  817.6 3.0 fusion.26
  820.7 10.9 %fusion.11.refs_0_ = f32[1024,2048]{1,0:T(8,128)} fusion(bf16[3,1024,512]{2,1,0:T(8,128)(2,1)S(1)} %copy-done.19, bf16[2048,4,512]{0,2,1:T(8,128)(2,1)} %all-gather.6.cloned.1.call-done), kind=kOutput, calls=%fused_computation.25 | convolution fusion | flops 6442450944 | bytes 17825792 | tf_op jit(solution)/shard_map/stf,rsf->tr/dot_general | solution.py:1142
  832.1 112.3 %shard_map.308 = bf16[1024,2176]{1,0:T(8,128)(2,1)S(1)} custom-call(f32[1024,2048]{1,0:T(8,128)} %fusion.11.refs_0_, bf16[1024,128]{1,0:T(8,128)(2,1)S(1)} %concatenate.55.refs_1_), custom_call_target="tpu_custom_call" | custom-call | bytes 314572800 | tf_op jit(solution)/shard_map/pallas_call | solution.py:469
  944.5 1.1 convolution_convert_fusion.1
  945.6 10.8 %all-gather = bf16[128,3584]{1,0:T(8,128)(2,1)S(1)} all-gather(bf16[16,3584]{1,0:T(8,128)(2,1)S(1)} %pad_maximum_fusion.4), channel_id=2, replica_groups=mesh['dp'=8,'tensor'=4] {'dp'}, dimensions={0}, use_global_device_ids=true | all-gather | bytes 1032192 | tf_op jit(solution)/shard_map/all_gather | solution.py:1163
  957.5 1.6 copy.210
  959.1 1.3 copy.211
  960.5 5.2 fusion.7
  965.8 6.2 add_convert_fusion
  972.0 6.4 fusion.2
  978.4 2.8 fusion.16
  981.8 1.6 copy.213
  983.4 1.6 copy.214
  985.0 1.6 copy.217
  986.5 1.8 copy.215
  988.4 1.0 copy.216
  (184 shorter events, 26.9 us)
Async XLA Ops:
  7.2 277.9 %copy-start = (bf16[8,16,2048]{2,1,0:T(8,128)(2,1)S(1)}, bf16[8,16,2048]{2,1,0:T(8,128)(2,1)}, u32[]{:S(2)}) copy-start(bf16[8,16,2048]{2,1,0:T(8,128)(2,1)} %param.47) | copy-start | bytes 1572868
  7.2 9.4 copy-start.41
  7.2 9.5 copy-start.42
  7.2 9.5 copy-start.45
  7.2 9.8 copy-start.21
  7.2 62.7 %all-gather.6.cloned.1.call-start = ((), (), s32[]{:S(2)}) async-start(), calls=%async_computation | async-start | bytes 9437184 | tf_op jit(solution)/shard_map/all_gather | solution.py:940
  11.0 294.1 %all-gather.8.cloned.1.call-start = ((), (), s32[]{:S(2)}) async-start(), calls=%async_computation.1 | async-start | bytes 12976128 | tf_op jit(solution)/shard_map/all_gather | solution.py:1062
  15.9 8.0 copy-start.43
  15.9 8.0 copy-start.46
  15.9 8.0 copy-start.37
  15.9 962.5 %all-gather.10.cloned.1.call-start = ((), (), s32[]{:S(2)}) async-start(), calls=%async_computation.2 | async-start | bytes 3133440 | tf_op jit(solution)/shard_map/all_gather | solution.py:1163
  16.7 53.3 %copy-start.24 = (f32[2048]{0:T(1024)}, f32[2048]{0:T(1024)S(1)}, u32[]{:S(2)}) copy-start(f32[2048]{0:T(1024)S(1)} %convert_element_type.144) | copy-start | bytes 24580
  16.8 68.5 %copy-start.7 = (s32[1024]{0:T(1024)}, s32[1024]{0:T(1024)S(1)}, u32[]{:S(2)}) copy-start(s32[1024]{0:T(1024)S(1)} %broadcast_add_fusion) | copy-start | bytes 12292
  17.1 68.3 %copy-start.3 = (s32[1024,1]{1,0:T(8,128)}, s32[1024,1]{1,0:T(8,128)S(1)}, u32[]{:S(2)}) copy-start(s32[1024,1]{1,0:T(8,128)S(1)} %copy.182.row_piece_ref.refs_6_) | copy-start | bytes 12292
  17.4 12.0 %copy-start.40 = (bf16[256,16]{0,1:T(8,128)(2,1)S(1)}, bf16[256,16]{0,1:T(8,128)(2,1)}, u32[]{:S(2)}) copy-start(bf16[256,16]{0,1:T(8,128)(2,1)} %param.31) | copy-start | bytes 24580
  40.4 8.1 copy-start.15
  45.3 2.8 copy-start.31
  45.3 24.7 %copy-start.35 = (f32[1024]{0:T(1024)}, f32[1024]{0:T(1024)S(1)}, u32[]{:S(2)}) copy-start(f32[1024]{0:T(1024)S(1)} %fusion.87) | copy-start | bytes 12292
  46.2 243.1 %copy-start.22 = (bf16[2048,16]{0,1:T(8,128)(2,1)}, bf16[2048,16]{0,1:T(8,128)(2,1)S(1)}, u32[]{:S(2)}) copy-start(bf16[2048,16]{0,1:T(8,128)(2,1)S(1)} %dynamic-slice_bitcast_fusion) | copy-start | bytes 196612
  48.5 36.9 %copy-start.1 = (f32[1024,128]{1,0:T(8,128)}, f32[1024,128]{1,0:T(8,128)S(1)}, u32[]{:S(2)}) copy-start(f32[1024,128]{1,0:T(8,128)S(1)} %get-tuple-element.113.cosine_ref.refs_4_) | copy-start | bytes 1572868
  48.5 36.9 %copy-start.2 = (f32[1024,128]{1,0:T(8,128)}, f32[1024,128]{1,0:T(8,128)S(1)}, u32[]{:S(2)}) copy-start(f32[1024,128]{1,0:T(8,128)S(1)} %get-tuple-element.114.sine_ref.refs_5_) | copy-start | bytes 1572868
  48.5 2.4 copy-start.20
  99.9 1.0 copy-start.4
  100.9 1.0 copy-start.5
  101.9 1.0 copy-start.6
  274.5 0.6 copy-start.38
  274.5 3.3 copy-start.8
  277.8 2.0 copy-start.10
  277.8 2.6 copy-start.18
  280.5 10.0 %copy-start.26 = (f32[1024]{0:T(1024)}, f32[1024]{0:T(1024)S(1)}, u32[]{:S(2)}) copy-start(f32[1024]{0:T(1024)S(1)} %fusion.39) | copy-start | bytes 12292
  281.0 8.3 copy-start.11
  284.5 0.6 copy-start.28
  285.1 12.2 %copy-start.33 = (f32[1024]{0:T(1024)}, f32[1024]{0:T(1024)S(1)}, u32[]{:S(2)}) copy-start(f32[1024]{0:T(1024)S(1)} %get-tuple-element.99) | copy-start | bytes 12292
  285.1 19.3 %copy-start.29 = (f32[1024]{0:T(1024)}, f32[1024]{0:T(1024)S(1)}, u32[]{:S(2)}) copy-start(f32[1024]{0:T(1024)S(1)} %get-tuple-element.100) | copy-start | bytes 12292
  660.8 2.9 copy-start.27
  663.6 4.0 copy-start.14
  671.3 7.0 copy-start.39
  671.3 7.1 copy-start.13
  682.8 4.9 copy-start.9
  684.9 3.0 copy-start.12
  685.1 6.9 copy-start.30
  695.1 0.7 copy-start.23
  817.6 3.1 copy-start.19
  832.1 112.4 %copy-start.16 = (bf16[1024,2048]{1,0:T(8,128)(2,1)S(1)}, bf16[1024,2048]{1,0:T(8,128)(2,1)}, u32[]{:S(2)}) copy-start(bf16[1024,2048]{1,0:T(8,128)(2,1)} %param.24) | copy-start | bytes 12582916
  832.1 112.4 %copy-start.25 = (f32[2048]{0:T(1024)S(1)}, f32[2048]{0:T(1024)}, u32[]{:S(2)}) copy-start(f32[2048]{0:T(1024)} %copy-done.24) | copy-start | bytes 24580
  832.1 112.4 %copy-start.36 = (f32[1024]{0:T(1024)S(1)}, f32[1024]{0:T(1024)}, u32[]{:S(2)}) copy-start(f32[1024]{0:T(1024)} %copy-done.35) | copy-start | bytes 12292
  944.5 12.0 %copy-start.44 = (s32[8]{0:T(128)S(1)}, s32[8]{0:T(128)}, u32[]{:S(2)}) copy-start(s32[8]{0:T(128)} %bitcast_convert_fusion) | copy-start | bytes 100
  957.5 8.2 slice-start
  960.4 5.3 copy-start.32
  960.5 5.3 slice-start.1
  960.5 5.3 copy-start.34
  960.5 11.5 %slice-start.2 = ((s8[8388608]{0:T(1024)(128)(4,1)}), s8[4194304]{0:T(1024)(128)(4,1)S(1)}, s32[]{:S(2)}) async-start(s8[8388608]{0:T(1024)(128)(4,1)} %bitcast.139), calls=%async_computation.5 | async-start | bytes 8388608
  965.8 6.2 slice-start.3
  965.8 6.2 copy-start.17
Sparse Core Ops, SparseCore 0:
  11.1 58.8 all-gather.5
  72.4 87.6 all-gather.7
  695.9 29.2 all-gather.9

commit v7 on v6

--- a/solution.py
+++ b/solution.py
@@ -22,9 +22,11 @@
 NARROW = 128
 MESH = pl.DeviceIdType.MESH
 SUM_CHUNKS = 16
-AHEAD = 2
+AHEAD = 1
+LEAD = 2
 SHARED = 4
-HALVES = 2
+HALVES = 1
+READY = 6
 
 
 def matmul(left_side, right_side):
@@ -240,7 +242,7 @@
             send("yx_core", piece).start()
 
     def advance(step):
-        launch(step)
+        launch(step + LEAD)
         forward(step - AHEAD)
         hand_over(step - 2 * AHEAD)
 
@@ -305,7 +307,7 @@
         chunks, wide_ref, narrow_ref, total_ref, *scratch[:5]
     )
     gather_semaphores, local_semaphores, piece_rows, open_rows = scratch[5:]
-    gather_greet, gather_advance, gather_arrive, gather_finish, own, load, load_wait, _ = (
+    gather_greet, gather_advance, gather_arrive, gather_finish, own, load, load_wait, stages = (
         plane_gather_steps(
             pieces, block_ref, whole_ref, gather_semaphores, local_semaphores.at[0]
         )
@@ -323,6 +325,10 @@
     greet(3)
     begin()
     own().start()
+
+    @pl.loop(0, LEAD)
+    def _(piece):
+        stages[0](piece)
 
     @pl.loop(0, max(chunks + 1, pieces + 3 * AHEAD + 1))
     def _(step):
@@ -724,7 +730,7 @@
     grad_mid_ref,
     up_extra_ref,
     down_extra_ref,
-    shared_up_ref,
+    ready_up_ref,
     block_ref,
     open_ref,
     grad_ref,
@@ -748,7 +754,7 @@
     )
     hidden = open_rows.shape[1]
     count = SHARED + EXPERTS
-    each = pieces // EXPERTS
+    each = pieces // (count - READY)
 
     def span(expert, rows):
         return pl.ds(pl.multiple_of(expert * rows, rows), rows)
@@ -759,10 +765,10 @@
             open_ref.at[span(expert, hidden)], open_rows.at[slot], semaphores.at[1, slot]
         )
 
-    def load_shared(expert):
+    def load_ready(expert):
         slot = expert % 2
         return pltpu.make_async_copy(
-            shared_up_ref.at[span(expert, 2 * hidden)], up_rows.at[slot], semaphores.at[2, slot]
+            ready_up_ref.at[span(expert, 2 * hidden)], up_rows.at[slot], semaphores.at[2, slot]
         )
 
     def store_act(expert):
@@ -775,24 +781,24 @@
         for part in range(each):
             launch(each * expert + part)
         for part in range(each):
-            forward(each * (expert - 2) + part + 1)
+            forward(each * (expert + 3 - READY) + part + 1)
         for part in range(each):
-            hand_over(each * (expert - 3) + part + 1)
+            hand_over(each * (expert + 1 - READY) + part + 1)
 
         @pl.when(expert + 1 < count)
         def _():
             load_open(expert + 1).start()
 
-        @pl.when(expert + 1 < SHARED)
-        def _():
-            load_shared(expert + 1).start()
-
-        @pl.when((expert + 1 >= SHARED) & (expert + 1 < count))
+        @pl.when(expert + 1 < READY)
+        def _():
+            load_ready(expert + 1).start()
+
+        @pl.when((expert + 1 >= READY) & (expert + 1 < count))
         def _():
             for part in range(each):
-                arrive(each * (expert + 1 - SHARED) + part)
+                arrive(each * (expert + 1 - READY) + part)
             slot = (expert + 1) % 2
-            first = (expert + 1 - SHARED) * 2 * hidden
+            first = (expert + 1 - READY) * 2 * hidden
             for copy in load(first, 2 * hidden, up_rows.at[slot], semaphores.at[2, slot]):
                 copy.start()
 
@@ -805,7 +811,7 @@
 
     def compute(expert, shared):
         slot = expert % 2
-        gate_up = matmul(up_rows[slot], inputs_ref[...])
+        gate_up = contract_last(up_rows[slot], inputs_ref[...])
         extra = None
         if shared:
             gate_up = gate_up + matmul(up_extra_ref[expert], mid_up_ref[...])
@@ -831,7 +837,7 @@
     greet()
     pl.semaphore_wait(pltpu.get_barrier_semaphore(), 3)
     load_open(0).start()
-    load_shared(0).start()
+    load_ready(0).start()
     grad_total[...] = jnp.zeros_like(grad_total)
     mid_down_ref[...] = jnp.zeros_like(mid_down_ref)
     grad_mid_up_ref[...] = jnp.zeros_like(grad_mid_up_ref)
@@ -855,14 +861,14 @@
 def experts_plain(inputs, gates, mid_up, grad_mid, up_extra, down_extra, up_rows, open_rows):
     count, length = gates.shape
     hidden = open_rows.shape[0] // count
-    width = inputs.shape[0]
+    width = inputs.shape[1]
     grad_total = jnp.zeros((length, width), jnp.float32)
     act_parts, gate_grads, down_parts, up_parts = [], [], [], []
     mid_down = jnp.zeros((NARROW, length), jnp.float32)
     grad_mid_up = jnp.zeros((NARROW, length), jnp.float32)
     for expert in range(count):
         weights = up_rows[2 * hidden * expert : 2 * hidden * (expert + 1)]
-        gate_up = matmul(weights, inputs)
+        gate_up = contract_last(weights, inputs)
         extra = None
         if expert < SHARED:
             gate_up = gate_up + matmul(up_extra[expert], mid_up)
@@ -894,18 +900,18 @@
 
 
 def experts_step(
-    inputs, gates, mid_up, grad_mid, up_extra, down_extra, shared_up, block, open_rows, number
+    inputs, gates, mid_up, grad_mid, up_extra, down_extra, ready_up, block, open_rows, number
 ):
-    width, length = inputs.shape
+    length, width = inputs.shape
     count = SHARED + EXPERTS
     hidden = open_rows.shape[0] // count
     if not in_plane():
         whole = lax.all_gather(block, "dp", axis=1, tiled=True)
-        up_rows = jnp.concatenate([shared_up, whole], axis=0)
+        up_rows = jnp.concatenate([ready_up, whole], axis=0)
         return experts_plain(
             inputs, gates, mid_up, grad_mid, up_extra, down_extra, up_rows, open_rows
         )
-    pieces = HALVES * EXPERTS
+    pieces = HALVES * (count - READY)
     return pl.pallas_call(
         functools.partial(experts_kernel, pieces),
         in_specs=in_vmem(6) + in_hbm(3),
@@ -918,7 +924,7 @@
             jax.ShapeDtypeStruct((SHARED, NARROW, hidden), jnp.float32),
             jax.ShapeDtypeStruct((SHARED, NARROW, 2 * hidden), jnp.float32),
             jax.ShapeDtypeStruct((count * hidden, length), jnp.bfloat16),
-            jax.ShapeDtypeStruct((EXPERTS * 2 * hidden, width), jnp.bfloat16),
+            jax.ShapeDtypeStruct(((count - READY) * 2 * hidden, width), jnp.bfloat16),
         ],
         scratch_shapes=[
             pltpu.VMEM((length, width), jnp.float32),
@@ -933,7 +939,7 @@
             collective_id=number, has_side_effects=True, vmem_limit_bytes=60 * 2**20
         ),
         cost_estimate=pl.CostEstimate(flops=0, bytes_accessed=600 * 2**20, transcendentals=0),
-    )(inputs, gates, mid_up, grad_mid, up_extra, down_extra, shared_up, block, open_rows)[:7]
+    )(inputs, gates, mid_up, grad_mid, up_extra, down_extra, ready_up, block, open_rows)[:7]
 
 
 def gathered(weight):
@@ -990,10 +996,38 @@
     tokens_f = tokens.astype(jnp.float32)
     normed = to_low(rms_scale(tokens_f, gain_attn_f))
     mid_qkv = to_low(matmul(normed, qkv_a))
+    hidden = shared_expert_down_weight.shape[1] // SHARED
+    rank = up_a.shape[1]
+
+    def fill(rows):
+        return jnp.pad(to_low(rows), ((0, NARROW - rows.shape[0]), (0, 0)))
+
+    def fill_last(rows):
+        return jnp.pad(to_low(rows), ((0, 0), (0, 0), (0, NARROW - rows.shape[2])))
+
+    cotangent_down = ADAPTER_SCALE * contract_last(cotangent, down_b)
+    up_extra = ADAPTER_SCALE * up_b.reshape(rank, 2, SHARED, hidden).transpose(2, 1, 3, 0)
+    up_extra = fill_last(up_extra.reshape(SHARED, 2 * hidden, rank))
+    down_extra = fill_last(down_a.reshape(SHARED, hidden, rank))
+    depth = routed_gate_up_weight.shape[0]
+    early = (READY - SHARED) * 2 * hidden
+    shared_block = shared_expert_gate_up_weight.reshape(-1, 2, SHARED, hidden)
+    up_block = jnp.transpose(routed_gate_up_weight, (1, 2, 3, 0)).reshape(-1, depth)
+    ready_up = lax.all_gather(
+        jnp.concatenate(
+            [shared_block.transpose(2, 1, 3, 0).reshape(-1, depth), up_block[:early]], axis=0
+        ),
+        "dp",
+        axis=1,
+        tiled=True,
+    )
     attention_rows = gathered(
         jnp.concatenate([query_key_value_weight, output_projection_weight[:, None]], axis=1)
     )
     qkv_rows, output_rows = attention_rows[:, :3], attention_rows[:, 3]
+    normed, cotangent_down, up_extra, down_extra = lax.optimization_barrier(
+        (normed, cotangent_down, up_extra, down_extra)
+    )
     qkv_sum = jnp.einsum("tr,rsf->stf", normed, qkv_rows, preferred_element_type=jnp.float32)
     qkv_sum = qkv_sum + query_key_value_bias.astype(jnp.float32)[:, None, :]
     qkv_sum = qkv_sum + ADAPTER_SCALE * jnp.einsum(
@@ -1006,7 +1040,6 @@
     query, keys, values, attended = attend(qkv_sum, *places)
     branch_part = contract_last(attended, output_rows)
     down_block = jnp.transpose(routed_down_weight, (1, 2, 0))
-    depth = down_block.shape[2]
     down_block = jnp.concatenate(
         [shared_expert_down_weight.T, down_block.reshape(-1, depth)], axis=0
     )
@@ -1035,9 +1068,11 @@
             axis=1,
         )
     )
-    router_full, gate_full = small_rows[:, :EXPERTS], small_rows[:, EXPERTS]
-    router_probs = jax.nn.softmax(matmul(normed_two, router_full), axis=-1)
-    shared_gate = jax.nn.sigmoid(matmul(normed_two, gate_full))
+    factors = jnp.concatenate([small_rows[:, : EXPERTS + 1], up_a], axis=1)
+    projected = matmul(normed_two, factors)
+    router_probs = jax.nn.softmax(projected[:, :EXPERTS], axis=-1)
+    shared_gate = jax.nn.sigmoid(projected[:, EXPERTS])
+    mid_up = to_low(projected[:, EXPERTS + 1 :])
     expert_ids = jnp.arange(EXPERTS, dtype=jnp.int32)
     chosen = jnp.sum(
         (routes[:, :, None] == expert_ids[None, None, :]).astype(jnp.float32), axis=1
@@ -1045,24 +1080,7 @@
     gates = jnp.concatenate(
         [jnp.broadcast_to(shared_gate[None], (SHARED, length)), (router_probs * chosen).T], axis=0
     )
-    hidden = shared_expert_down_weight.shape[1] // SHARED
-    rank = up_a.shape[1]
-
-    def fill(rows):
-        return jnp.pad(to_low(rows), ((0, NARROW - rows.shape[0]), (0, 0)))
-
-    def fill_last(rows):
-        return jnp.pad(to_low(rows), ((0, 0), (0, 0), (0, NARROW - rows.shape[2])))
-
-    cotangent_down = ADAPTER_SCALE * contract_last(cotangent, down_b)
-    mid_up = to_low(matmul(normed_two, up_a))
     grad_mid_down = shared_gate[:, None] * cotangent_down
-    up_extra = ADAPTER_SCALE * up_b.reshape(rank, 2, SHARED, hidden).transpose(2, 1, 3, 0)
-    shared_block = shared_expert_gate_up_weight.reshape(-1, 2, SHARED, hidden)
-    shared_up = lax.all_gather(
-        shared_block.transpose(2, 1, 3, 0).reshape(-1, depth), "dp", axis=1, tiled=True
-    )
-    up_block = jnp.transpose(routed_gate_up_weight, (1, 2, 3, 0))
     (
         normed_two_part,
         gate_grads,
@@ -1072,14 +1090,14 @@
         grad_up_b_parts,
         act_rows,
     ) = experts_step(
-        normed_two.T,
+        normed_two,
         gates,
         fill(mid_up.T),
         fill(grad_mid_down.T),
-        fill_last(up_extra.reshape(SHARED, 2 * hidden, rank)),
-        fill_last(down_a.reshape(SHARED, hidden, rank)),
-        shared_up,
-        up_block.reshape(-1, depth),
+        up_extra,
+        down_extra,
+        ready_up,
+        up_block[early:],
         open_rows,
         5,
     )
@@ -1114,7 +1132,7 @@
     grad_gate_logit = to_low(shared_gate_grad * shared_gate * (1.0 - shared_gate))
     grad_normed_two = grad_normed_two + contract_last(
         jnp.concatenate([grad_logits, grad_gate_logit[:, None], grad_mid_up], axis=1),
-        jnp.concatenate([router_full, gate_full[:, None], up_a], axis=1),
+        factors,
     )
     grad_hidden = cot_f + norm_ffn_pull(grad_normed_two)[0]
     grad_branch = to_low(grad_hidden)
@@ -1122,17 +1140,33 @@
     grad_attended = to_low(
         matmul(grad_branch, output_rows) + contract_last(grad_mid_out, out_a)
     )
-    combined_here, grad_qkv = summed_and_attended_back(
-        combined_part, (query, keys, values, grad_attended) + places, 3
-    )
-    extra_here = ADAPTER_SCALE * matmul(mid_down, down_b)
-    output = to_low(hidden_here + combined_here + shared_gate[:, None] * extra_here)
     grad_down_b_local = ADAPTER_SCALE * contract_first(
         to_low(shared_gate[:, None] * mid_down.astype(jnp.float32)), cotangent
     )
     grad_up_a_local = contract_first(grad_mid_up, normed_two)
     grad_out_b_local = ADAPTER_SCALE * contract_first(mid_out, grad_branch)
     grad_out_a_local = contract_first(grad_mid_out, attended)
+
+    def side_by_side(local_grads):
+        return jnp.concatenate([to_low(local_grad) for local_grad in local_grads], axis=1)
+
+    early_grads = [
+        grad_out_a_local,
+        grad_up_a_local,
+        grad_up_b_local.reshape(grad_up_b_local.shape[0], -1),
+        grad_down_a_local,
+        grad_down_b_local,
+    ]
+    grad_attended, early_flat = lax.optimization_barrier(
+        (grad_attended, side_by_side(early_grads))
+    )
+    early_rows = lax.all_gather(early_flat, "dp", axis=0, tiled=False)
+    combined_here, grad_qkv = summed_and_attended_back(
+        combined_part, (query, keys, values, grad_attended) + places, 3
+    )
+    extra_here = ADAPTER_SCALE * matmul(mid_down, down_b)
+    output = to_low(hidden_here + combined_here + shared_gate[:, None] * extra_here)
+    grad_qkv, early_rows = lax.optimization_barrier((grad_qkv, early_rows))
     grad_mid_qkv_part = ADAPTER_SCALE * jnp.einsum(
         "stf,rsf->tr", grad_qkv, qkv_b, preferred_element_type=jnp.float32
     )
@@ -1157,14 +1191,18 @@
         jnp.arange(ADAPTER_SETS, dtype=jnp.int32)[:, None] == everyone.astype(jnp.int32)[None, :]
     )
 
-    def adapter_sums(local_grads):
-        sizes = [local_grad.shape[1] for local_grad in local_grads]
-        flat = jnp.concatenate([to_low(local_grad) for local_grad in local_grads], axis=1)
-        rows = lax.all_gather(flat, "dp", axis=0, tiled=False)
-        totals = jnp.einsum("cj,jrn->crn", marker, rows, preferred_element_type=jnp.float32)
+    def adapter_sums(local_grads, rows):
         results, start = [], 0
-        for size in sizes:
-            results.append(totals[:, :, start : start + size])
+        for local_grad in local_grads:
+            size = local_grad.shape[1]
+            results.append(
+                jnp.einsum(
+                    "cj,jrn->crn",
+                    marker,
+                    rows[:, :, start : start + size],
+                    preferred_element_type=jnp.float32,
+                )
+            )
             start += size
         return results
 
@@ -1174,18 +1212,16 @@
     def opened(total, count):
         return total.reshape(total.shape[0], total.shape[1], count, -1)
 
-    total_out_a, total_out_b, total_up_a, total_up_b, total_down_a, total_down_b = adapter_sums(
-        [
-            grad_out_a_local,
-            grad_out_b_local,
-            grad_up_a_local,
-            grad_up_b_local.reshape(grad_up_b_local.shape[0], -1),
-            grad_down_a_local,
-            grad_down_b_local,
-        ]
-    )
-    total_qkv_b, total_qkv_a = adapter_sums(
-        [grad_qkv_b_local.reshape(grad_qkv_b_local.shape[0], -1), grad_qkv_a_local]
+    total_out_a, total_up_a, total_up_b, total_down_a, total_down_b = adapter_sums(
+        early_grads, early_rows
+    )
+    late_grads = [
+        grad_qkv_b_local.reshape(grad_qkv_b_local.shape[0], -1),
+        grad_qkv_a_local,
+        grad_out_b_local,
+    ]
+    total_qkv_b, total_qkv_a, total_out_b = adapter_sums(
+        late_grads, lax.all_gather(side_by_side(late_grads), "dp", axis=0, tiled=False)
     )
     return (
         output,

time: 1000 us -> 1010 us (1.010)
  local copies, waits for them, and re-layouts: 61.3 us -> 78.3 us
    pallas_call x1, Pallas kernels: 156 us -> 180 us  [summed_and_gathered(): pl.pallas_call(functools.partial(sum_gather_kernel, SUM_CHUNKS, pieces),...]
    pallas_call x1, Pallas kernels: 231 us -> 208 us  [experts_step(): pl.pallas_call(functools.partial(experts_kernel, pieces), in_specs=in_vme...]
    all_gather x1, waiting for transfers between devices: 17 us -> 3.56 us  [gathered(): return lax.all_gather(weight, 'dp', axis=0, tiled=True)]
    unnamed x117 -> x130, local copies, waits for them, and re-layouts: 32.5 us -> 45.4 us
    all_gather x1 -> x0, blocking collectives: 10.8 us -> none  [adapter_sums(): rows = lax.all_gather(flat, 'dp', axis=0, tiled=False)]
    dot_general x8 -> x6, matrix products: 27.5 us -> 24.8 us  [matmul(): return jnp.dot(left_side, right_side, preferred_element_type=jnp.float32)]
  transfers between devices with their start and end apart: 3 -> 4, of which waited for: 1 -> 2; matrix products, arithmetic and copies ran while one was open for 13% -> 12% of each run, Pallas kernels for 40% -> 31%
where the time goes in v7:
time: 1010 us; the launch traced here: 1000 us
  Pallas kernels  751 us (74%)
  matrix products  98.9 us (10%)
  local copies, waits for them, and re-layouts  78.3 us (8%)
  other arithmetic  40.3 us (4%)
  between operations  15.8 us (2%)
  blocking collectives  11.8 us (1%)
    pallas_call x1, Pallas kernels, experts_step(): pl.pallas_call(functools.partial(experts_kernel, pieces), in_specs=in_vme...  208 us
    pallas_call x1, Pallas kernels, summed_and_gathered(): pl.pallas_call(functools.partial(sum_gather_kernel, SUM_CHUNKS, pieces),...  180 us
    pallas_call x1, Pallas kernels, summed_and_down(): pl.pallas_call(functools.partial(sum_down_kernel, SUM_CHUNKS), out_shape=...  120 us
    pallas_call x1, Pallas kernels, summed_and_attended_back(): pl.pallas_call(functools.partial(attend_back_sum_kernel, SUM_CHUNKS), out...  114 us
    pallas_call x1, Pallas kernels, summed(): pl.pallas_call(functools.partial(line_sum_kernel, SUM_CHUNKS), out_shape=...  114 us
    unnamed x130, local copies, waits for them, and re-layouts  45.4 us
    dot_general x6, matrix products, contract_last(): lax.dot_general(left_side, right_side, (((1,), (1,)), ((), ())), preferre...  29.4 us
    dot_general x6, matrix products, matmul(): return jnp.dot(left_side, right_side, preferred_element_type=jnp.float32)  24.8 us
  transfers between devices with their start and end apart: 4, of which 2 were waited for; matrix products, arithmetic and copies ran while one was open for 12% of the time, Pallas kernels for 31%

profile of v7, /device:TPU:0, one launch (start us, length us, event | category | flops | bytes accessed | tf_op | source)
XLA Modules:
  0.0 1004.1 jit_solution(2608481081486896081)
XLA Ops:
  7.2 1.5 copy.210
  8.7 1.1 copy.209
  10.9 1.2 slice.164
  12.1 3.7 copy.228
  15.9 1.5 pad_maximum_fusion.1
  17.5 5.0 slice.165
  27.6 6.4 copy.220
  34.0 3.2 fusion.3
  37.4 3.1 fusion.23
  40.6 3.0 fusion.5
  45.6 11.8 %all_gather.22 = bf16[2048,18]{0,1:T(8,128)(2,1)S(1)} all-gather(bf16[256,18]{0,1:T(8,128)(2,1)S(1)} %maximum_maximum_fusion), channel_id=1, replica_groups=mesh['dp'=8,'tensor'=4] {'dp'}, dimensions={0}, use_global_device_ids=true | all-gather | bytes 82944 | tf_op jit(solution)/shard_map/all_gather | solution.py:946
  58.3 1.9 fusion.41
  60.6 3.8 fusion.28
  64.4 2.0 pad_maximum_fusion.block_ref
  66.4 3.6 all-gather.7.cloned.1.call-done
  69.9 10.4 %fusion.14 = f32[3,512,1024]{1,2,0:T(8,128)S(1)} fusion(bf16[2048,4,512]{0,2,1:T(8,128)(2,1)} %all-gather.7.cloned.1.call-done, bf16[1024,2048]{1,0:T(8,128)(2,1)} %fusion.5), kind=kOutput, calls=%fused_computation.26 | convolution fusion | flops 6442450944 | bytes 18874368 | tf_op jit(solution)/shard_map/tr,rsf->stf/dot_general | solution.py:1031
  80.4 4.6 add_bitcast_fusion.qkv_ref
  85.0 14.8 %shard_map.303 = (bf16[1024,512]{1,0:T(8,128)(2,1)S(1)}, bf16[1024,512]{1,0:T(8,128)(2,1)S(1)}, bf16[1024,512]{1,0:T(8,128)(2,1)S(1)}, bf16[1024,512]{1,0:T(8,128)(2,1)S(1)}) custom-call(f32[3,1024,512]{2,1,0:T(8,128)} %add_bitcast_fusion.qkv_ref, f32[1024,128]{1,0:T(8,128)S(1)} %get-tuple-element.126.cosine_ref.refs_4_, ...), custom_call_target="tpu_custom_call" | custom-call | flops 2147483648 | bytes 16777216 | tf_op jit(solution)/shard_map/pallas_call | solution.py:604
  102.7 1.1 convolution_convert_fusion.2
  104.7 7.2 fusion.21.wide_ref
  111.9 180.5 %shard_map.304 = (bf16[1024,2176]{1,0:T(8,128)(2,1)}, bf16[7040,2048]{1,0:T(8,128)(2,1)}, bf16[7040,1024]{1,0:T(8,128)(2,1)}) custom-call(f32[1024,2048]{1,0:T(8,128)} %fusion.21.wide_ref, bf16[1024,128]{1,0:T(8,128)(2,1)} %concatenate.49.narrow_ref, bf16[7040,256]{1,0:T(8,128)(2,1)} %pad_maximum_fusion.block_ref, bf16[2048,1024]{1,0:T(8,128)(2,1)} %bitcast.147), custom_call_target="tpu_custom_call" | custom-call | bytes 377487360 | tf_op jit(solution)/shard_map/pallas_call | solution.py:498
  292.4 4.9 multiply_reduce_fusion.1
  298.2 2.5 copy-done.10
  300.7 2.0 copy-done.12
  302.7 1.4 fusion.59
  306.0 1.5 pad.21.clone.grad_mid_ref
  309.5 1.1 multiply_bitcast_fusion
  310.6 1.2 copy.227
  314.1 207.8 %shard_map.305 = (bf16[1024,2048]{1,0:T(8,128)(2,1)}, f32[20,1024]{1,0:T(8,128)}, f32[128,1024]{1,0:T(8,128)}, f32[128,1024]{1,0:T(8,128)}, f32[4,128,352]{2,1,0...) custom-call(bf16[1024,2048]{1,0:T(8,128)(2,1)} %copy-done.12, ...), custom_call_target="tpu_custom_call" | custom-call | bytes 629145600 | tf_op jit(solution)/shard_map/pallas_call | solution.py:915
  527.8 119.9 %shard_map.306 = (bf16[1024,2176]{1,0:T(8,128)(2,1)}, bf16[1024,2048]{1,0:T(8,128)(2,1)}) custom-call(bf16[1024,2048]{1,0:T(8,128)(2,1)} %get-tuple-element.43.wide_ref, bf16[1024,128]{1,0:T(8,128)(2,1)} %concatenate.56.narrow_ref, bf16[7040,1024]{1,0:T(8,128)(2,1)} %get-tuple-element.47.act_ref, bf16[7040,2048]{1,0:T(8,128)(2,1)} %get-tuple-element.48.down_ref), custom_call_target="tpu_custom_call" | custom-call | bytes 314572800 | tf_op jit(solution)/shard_map/pallas_call | solution.py:529
  647.8 2.8 convert_element_type.158
  650.6 2.6 fusion.32
  653.2 2.1 slice.144
  658.0 2.0 broadcast_subtract_fusion
  660.0 1.2 copy.236
  662.6 10.4 %multiply_reduce_fusion = (f32[1024]{0:T(1024)S(1)}, f32[1024,2048]{1,0:T(8,128)}) fusion(f32[1024,2048]{1,0:T(8,128)} %copy-done.10, f32[2048]{0:T(1024)} %copy-done.34, bf16[2048,16]{0,1:T(8,128)(2,1)} %copy-done.30, bf16[2048,17]{0,1:T(8,128)(2,1)S(1)} %bitcast.165, bf16[1024,16]{0,1:T(8,128)(2,1)S(1)} %copy.238, ...), kind=kOutput, calls=%fused_computation.19 | convolution fusion | flops 147272704 | bytes 25380864 | tf_op jit(solution)/shard_map/dot_general | solution.py:37
  673.5 1.5 copy-done.15
  675.1 4.4 fusion
  679.5 1.2 fusion.26
  681.0 2.8 copy-done.11
  684.7 1.7 fusion.19
  688.8 3.1 fusion.17
  691.9 6.4 fusion.20
  698.3 2.2 add_convert_fusion.1.refs_3_
  700.7 114.2 %shard_map.307 = (bf16[1024,2048]{1,0:T(8,128)(2,1)}, bf16[3,1024,512]{2,1,0:T(8,128)(2,1)}) custom-call(bf16[1024,2048]{1,0:T(8,128)(2,1)} %get-tuple-element.49.wide_ref, bf16[1024,512]{1,0:T(8,128)(2,1)} %copy-done.6, bf16[1024,512]{1,0:T(8,128)(2,1)} %copy-done.7, bf16[1024,512]{1,0:T(8,128)(2,1)} %copy-done.8, ...), custom_call_target="tpu_custom_call" | custom-call | bytes 314572800 | tf_op jit(solution)/shard_map/pallas_call | solution.py:694
  814.9 4.3 fusion.18
  819.6 7.2 add_convert_fusion
  826.8 3.0 fusion.24
  830.7 1.4 fusion.30
  832.1 1.3 convolution_bitcast_fusion.1
  833.4 1.3 fusion.34
  834.7 10.7 %fusion.11.refs_0_ = f32[1024,2048]{1,0:T(8,128)} fusion(bf16[3,1024,512]{2,1,0:T(8,128)(2,1)S(1)} %copy-done.26, bf16[2048,4,512]{0,2,1:T(8,128)(2,1)} %all-gather.7.cloned.1.call-done), kind=kOutput, calls=%fused_computation.25 | convolution fusion | flops 6442450944 | bytes 17825792 | tf_op jit(solution)/shard_map/stf,rsf->tr/dot_general | solution.py:1176
  845.4 113.6 %shard_map.308 = bf16[1024,2176]{1,0:T(8,128)(2,1)S(1)} custom-call(f32[1024,2048]{1,0:T(8,128)} %fusion.11.refs_0_, bf16[1024,128]{1,0:T(8,128)(2,1)S(1)} %concatenate.59.refs_1_), custom_call_target="tpu_custom_call" | custom-call | bytes 314572800 | tf_op jit(solution)/shard_map/pallas_call | solution.py:475
  959.0 2.1 copy-done.1
  962.6 3.4 copy.259
  965.9 3.0 copy.258
  968.9 1.6 copy.261
  972.7 5.3 fusion.7
  978.1 6.6 fusion.2
  984.7 4.4 all-gather.13.cloned.1.call-done
  989.1 1.3 fusion.124
  991.8 1.6 copy.257
  993.9 1.6 copy.254
  995.8 1.3 copy.255
  (207 shorter events, 41.1 us)
Async XLA Ops:
  7.2 285.3 %copy-start = (bf16[8,16,2048]{2,1,0:T(8,128)(2,1)S(1)}, bf16[8,16,2048]{2,1,0:T(8,128)(2,1)}, u32[]{:S(2)}) copy-start(bf16[8,16,2048]{2,1,0:T(8,128)(2,1)} %param.43) | copy-start | bytes 1572868
  7.2 62.8 %all-gather.7.cloned.1.call-start = ((), (), s32[]{:S(2)}) async-start(), calls=%async_computation | async-start | bytes 9437184 | tf_op jit(solution)/shard_map/all_gather | solution.py:946
  10.9 303.2 %all-gather.9.cloned.1.call-start = ((), (), s32[]{:S(2)}) async-start(), calls=%async_computation.1 | async-start | bytes 19464192 | tf_op jit(solution)/shard_map/all_gather | solution.py:1016
  17.4 10.1 %copy-start.47 = (bf16[2048]{0:T(1024)(128)(2,1)S(1)}, bf16[2048]{0:T(1024)(128)(2,1)}, u32[]{:S(2)}) copy-start(bf16[2048]{0:T(1024)(128)(2,1)} %param.26) | copy-start | bytes 12292
  17.5 809.3 %all-gather.11.cloned.1.call-start = ((), (), s32[]{:S(2)}) async-start(), calls=%async_computation.2 | async-start | bytes 2543616 | tf_op jit(solution)/shard_map/all_gather | solution.py:1163
  33.9 3.4 copy-start.14
  34.0 6.6 copy-start.16
  37.2 6.5 copy-start.41
  37.4 6.3 copy-start.39
  40.5 3.1 copy-start.48
  40.5 3.1 copy-start.50
  40.5 3.5 copy-start.29
  40.5 3.8 copy-start.49
  40.6 3.8 copy-start.51
  40.6 3.8 copy-start.43
  40.6 4.9 copy-start.46
  43.8 41.2 %copy-start.9 = (s32[1024]{0:T(1024)}, s32[1024]{0:T(1024)S(1)}, u32[]{:S(2)}) copy-start(s32[1024]{0:T(1024)S(1)} %broadcast_add_fusion) | copy-start | bytes 12292
  44.0 40.9 %copy-start.5 = (s32[1024,1]{1,0:T(8,128)}, s32[1024,1]{1,0:T(8,128)S(1)}, u32[]{:S(2)}) copy-start(s32[1024,1]{1,0:T(8,128)S(1)} %copy.217.row_piece_ref.refs_6_) | copy-start | bytes 12292
  44.4 253.1 %copy-start.34 = (f32[2048]{0:T(1024)}, f32[2048]{0:T(1024)S(1)}, u32[]{:S(2)}) copy-start(f32[2048]{0:T(1024)S(1)} %convert_element_type.150) | copy-start | bytes 24580
  45.5 18.9 %copy-start.27 = (bf16[256,16,352]{0,2,1:T(8,128)(2,1)S(1)}, bf16[256,16,352]{0,2,1:T(8,128)(2,1)}, u32[]{:S(2)}) copy-start(bf16[256,16,352]{0,2,1:T(8,128)(2,1)} %param.34) | copy-start | bytes 8650756
  58.3 242.4 %copy-start.30 = (bf16[2048,16]{0,1:T(8,128)(2,1)}, bf16[2048,16]{0,1:T(8,128)(2,1)S(1)}, u32[]{:S(2)}) copy-start(bf16[2048,16]{0,1:T(8,128)(2,1)S(1)} %dynamic-slice_bitcast_fusion) | copy-start | bytes 196612
  60.6 24.4 %copy-start.3 = (f32[1024,128]{1,0:T(8,128)}, f32[1024,128]{1,0:T(8,128)S(1)}, u32[]{:S(2)}) copy-start(f32[1024,128]{1,0:T(8,128)S(1)} %get-tuple-element.126.cosine_ref.refs_4_) | copy-start | bytes 1572868
  60.6 24.4 %copy-start.4 = (f32[1024,128]{1,0:T(8,128)}, f32[1024,128]{1,0:T(8,128)S(1)}, u32[]{:S(2)}) copy-start(f32[1024,128]{1,0:T(8,128)S(1)} %get-tuple-element.127.sine_ref.refs_5_) | copy-start | bytes 1572868
  99.8 1.0 copy-start.6
  100.7 1.0 copy-start.7
  101.7 1.0 copy-start.8
  297.4 3.3 copy-start.10
  297.4 3.3 copy-start.44
  297.4 3.3 copy-start.37
  300.7 2.0 copy-start.12
  300.7 4.3 copy-start.21
  302.7 6.8 copy-start.20
  304.1 0.7 copy-start.31
  304.8 3.5 copy-start.22
  308.9 0.6 copy-start.35
  647.7 7.5 copy-start.36
  650.6 5.2 copy-start.19
  653.2 4.8 copy-start.23
  657.0 5.5 copy-start.33
  662.5 10.5 %slice-start = ((s8[8388608]{0:T(1024)(128)(4,1)}), s8[4194304]{0:T(1024)(128)(4,1)S(1)}, s32[]{:S(2)}) async-start(s8[8388608]{0:T(1024)(128)(4,1)} %bitcast.142), calls=%async_computation.4 | async-start | bytes 8388608
  662.5 10.5 %copy-start.45 = (f32[1024]{0:T(1024)S(1)}, f32[1024]{0:T(1024)}, u32[]{:S(2)}) copy-start(f32[1024]{0:T(1024)} %copy-done.44) | copy-start | bytes 12292
  662.5 11.0 %slice-start.1 = ((s8[8388608]{0:T(1024)(128)(4,1)}), s8[4194304]{0:T(1024)(128)(4,1)S(1)}, s32[]{:S(2)}) async-start(s8[8388608]{0:T(1024)(128)(4,1)} %bitcast.142), calls=%async_computation.5 | async-start | bytes 8388608
  662.5 12.5 %copy-start.15 = (bf16[1024,2048]{1,0:T(8,128)(2,1)S(1)}, bf16[1024,2048]{1,0:T(8,128)(2,1)}, u32[]{:S(2)}) copy-start(bf16[1024,2048]{1,0:T(8,128)(2,1)} %param.25) | copy-start | bytes 12582916
  662.6 12.5 %copy-start.38 = (f32[1024]{0:T(1024)S(1)}, f32[1024]{0:T(1024)}, u32[]{:S(2)}) copy-start(f32[1024]{0:T(1024)} %copy-done.37) | copy-start | bytes 12292
  679.5 4.3 copy-start.11
  679.5 5.2 copy-start.13
  691.9 6.5 copy-start.32
  700.5 288.6 %all-gather.13.cloned.1.call-start = ((), (), s32[]{:S(2)}) async-start(), calls=%async_computation.3 | async-start | bytes 1622016 | tf_op jit(solution)/shard_map/all_gather | solution.py:1224
  814.9 4.7 copy-start.25
  826.7 3.0 copy-start.26
  826.7 3.5 copy-start.28
  845.4 115.8 %copy-start.18 = (bf16[1024,2048]{1,0:T(8,128)(2,1)S(1)}, bf16[1024,2048]{1,0:T(8,128)(2,1)}, u32[]{:S(2)}) copy-start(bf16[1024,2048]{1,0:T(8,128)(2,1)} %fusion.5) | copy-start | bytes 12582916
  959.0 2.1 copy-start.1
  962.5 6.3 copy-start.24
  962.6 10.2 %copy-start.17 = (bf16[1024,2048]{1,0:T(8,128)(2,1)S(1)}, bf16[1024,2048]{1,0:T(8,128)(2,1)}, u32[]{:S(2)}) copy-start(bf16[1024,2048]{1,0:T(8,128)(2,1)} %param.24) | copy-start | bytes 12582916
  965.9 6.8 copy-start.2
  970.7 7.4 slice-start.2
  972.7 5.3 copy-start.42
  972.7 5.3 slice-start.3
  972.7 5.4 copy-start.40
Sparse Core Ops, SparseCore 0:
  11.0 58.9 all-gather.6
  71.8 135.3 all-gather.8
  700.6 28.2 all-gather.10
  962.7 26.3 all-gather.12

commit v8 on v7

--- a/solution.py
+++ b/solution.py
@@ -413,28 +413,161 @@
     finish()
 
 
-def attend_back_sum_kernel(chunks, wide_ref, *refs):
-    inputs, (total_ref, grad_qkv_ref), scratch = refs[:8], refs[8:10], refs[10:]
+def attend_back_sum_kernel(chunks, wide_ref, rows_ref, upper_ref, *refs):
+    inputs, scratch = refs[:8], refs[12:]
+    total_ref, grad_qkv_ref, normed_part_ref, mid_total_ref = refs[8:12]
     greet, begin, advance, finish = line_sum_steps(
         chunks, wide_ref, None, total_ref, *scratch[:5]
     )
-    head_block = attend_back_steps(*inputs, grad_qkv_ref, *scratch[5:])
+    head_block = attend_back_steps(*inputs, grad_qkv_ref, *scratch[5:7])
+    mid_part = scratch[7]
+    _, mid_begin, mid_advance, mid_finish = line_sum_steps(
+        1, mid_part, None, mid_total_ref, *scratch[8:]
+    )
     length, heads_width = inputs[0].shape
     heads, blocks = heads_width // HEAD_SIZE, length // QUERY_ROWS
+    each = blocks // 2
     greet(0)
     begin()
 
     @pl.loop(0, heads)
     def _(head):
-        for block in range(blocks):
-            advance(head * blocks + block)
-            head_block(head, block * QUERY_ROWS)
-
-    @pl.loop(heads * blocks, max(heads * blocks, chunks + 1))
+        for step in range(each):
+            advance(head * each + step)
+            head_block(head, 2 * step * QUERY_ROWS)
+            head_block(head, (2 * step + 1) * QUERY_ROWS)
+
+    mid_part[...] = grad_mid_rows(grad_qkv_ref, upper_ref)
+    mid_begin()
+    done = heads * each
+
+    @pl.loop(0, blocks)
+    def _(block):
+        advance(done + block)
+        span = pl.ds(pl.multiple_of(block * QUERY_ROWS, QUERY_ROWS), QUERY_ROWS)
+        normed_part_ref[span] = to_low(
+            sum(contract_last(grad_qkv_ref[part, span], rows_ref[part]) for part in range(3))
+        )
+
+    mid_advance(0)
+
+    @pl.loop(done + blocks, max(done + blocks, chunks + 1))
     def _(step):
         advance(step)
 
+    mid_advance(1)
+    mid_finish()
     finish()
+
+
+def grad_mid_rows(grad_qkv_ref, upper_ref):
+    return sum(contract_last(grad_qkv_ref[part], upper_ref[part]) for part in range(3))
+
+
+def epilogue_kernel(
+    total_ref,
+    hidden_ref,
+    scale_ref,
+    cotangent_ref,
+    gain_ref,
+    probs_ref,
+    chosen_ref,
+    extra_ref,
+    gate_ref,
+    factors_ref,
+    out_b_ref,
+    out_a_ref,
+    rows_ref,
+    grad_hidden_ref,
+    grad_branch_ref,
+    grad_mid_ref,
+    grad_attended_ref,
+):
+    width = hidden_ref.shape[1]
+    narrow = total_ref[:, width:].astype(jnp.float32)
+    lane = lax.broadcasted_iota(jnp.int32, narrow.shape, 1)
+    probs = probs_ref[...]
+    grad_probs = chosen_ref[...] * narrow
+    grad_logits = probs * (grad_probs - jnp.sum(probs * grad_probs, axis=1, keepdims=True))
+    only_gate = jnp.where(lane == EXPERTS, narrow, 0.0)
+    gate_grad = jnp.sum(only_gate + narrow * extra_ref[...], axis=1, keepdims=True)
+    gate = gate_ref[...]
+    gate_logit = gate_grad * gate * (1.0 - gate)
+    rank = extra_ref.shape[1] // 8
+    rows = jnp.where(lane <= EXPERTS + rank, narrow, 0.0)
+    rows = jnp.where(lane == EXPERTS, gate_logit, rows)
+    rows = to_low(jnp.where(lane < EXPERTS, grad_logits, rows))
+    grad_normed = total_ref[:, :width].astype(jnp.float32) + contract_last(rows, factors_ref[...])
+    hidden = hidden_ref[...]
+    scale = scale_ref[...]
+    scaled = grad_normed * gain_ref[...]
+    pull = jnp.mean(hidden * scaled, axis=1, keepdims=True)
+    grad_hidden = (
+        cotangent_ref[...].astype(jnp.float32)
+        + scale * scaled
+        - hidden * (scale * scale * scale * pull)
+    )
+    grad_hidden_ref[...] = grad_hidden
+    grad_branch = to_low(grad_hidden)
+    grad_branch_ref[...] = grad_branch
+    grad_mid = to_low(ADAPTER_SCALE * contract_last(grad_branch, out_b_ref[...]))
+    grad_mid_ref[...] = grad_mid
+    grad_attended_ref[...] = to_low(
+        matmul(grad_branch, rows_ref[...]) + contract_last(grad_mid, out_a_ref[...])
+    )
+
+
+def epilogue(blocked, still):
+    length = blocked[0].shape[0]
+    width, heads_width = still[-1].shape
+    rows = min(length, 256)
+    total, hidden, scale, cotangent, probs, chosen, extra, gate = blocked
+    gain, factors, out_b, out_a, output_rows = still
+
+    def block(array):
+        return pl.BlockSpec((rows, array.shape[1]), lambda index: (index, 0))
+
+    def whole(array):
+        return pl.BlockSpec(array.shape, lambda index: (0, 0))
+
+    outs = [
+        jax.ShapeDtypeStruct((length, width), jnp.float32),
+        jax.ShapeDtypeStruct((length, width), jnp.bfloat16),
+        jax.ShapeDtypeStruct((length, NARROW), jnp.bfloat16),
+        jax.ShapeDtypeStruct((length, heads_width), jnp.bfloat16),
+    ]
+    return pl.pallas_call(
+        epilogue_kernel,
+        grid=(length // rows,),
+        in_specs=[block(array) for array in (total, hidden, scale, cotangent)]
+        + [whole(gain)]
+        + [block(array) for array in (probs, chosen, extra, gate)]
+        + [whole(array) for array in (factors, out_b, out_a, output_rows)],
+        out_specs=[block(out) for out in outs],
+        out_shape=outs,
+        compiler_params=pltpu.CompilerParams(
+            vmem_limit_bytes=56 * 2**20, dimension_semantics=("arbitrary",)
+        ),
+        cost_estimate=pl.CostEstimate(
+            flops=2 * length * width * heads_width,
+            bytes_accessed=32 * 2**20,
+            transcendentals=0,
+        ),
+    )(
+        total,
+        hidden,
+        scale,
+        cotangent,
+        gain,
+        probs,
+        chosen,
+        extra,
+        gate,
+        factors,
+        out_b,
+        out_a,
+        output_rows,
+    )
 
 
 def on_line():
@@ -462,28 +595,32 @@
     return jnp.concatenate([to_low(narrow_part), pad], axis=1)
 
 
-def parts_of(total, wide_part, narrow_part):
-    width, small = wide_part.shape[1], narrow_part.shape[1]
-    total = total.astype(jnp.float32)
-    return total[:, :width], total[:, width : width + small]
-
-
-def summed(wide_part, narrow_part, number):
+def plain_sum(wide_part, narrow_part):
+    if narrow_part is not None:
+        pad = jnp.zeros((narrow_part.shape[0], NARROW - narrow_part.shape[1]), jnp.float32)
+        wide_part = jnp.concatenate([wide_part, narrow_part, pad], axis=1)
+    return lax.psum(wide_part, "tensor")
+
+
+def plain_line_sum_kernel(chunks, wide_ref, *refs):
+    line_sum_kernel(chunks, wide_ref, None, *refs)
+
+
+def summed(wide_part, number):
     if not on_line():
-        return lax.psum((wide_part, narrow_part), "tensor")
-    shape = (wide_part.shape[0], wide_part.shape[1] + NARROW)
-    total = pl.pallas_call(
-        functools.partial(line_sum_kernel, SUM_CHUNKS),
+        return plain_sum(wide_part, None)
+    shape = wide_part.shape
+    return pl.pallas_call(
+        functools.partial(plain_line_sum_kernel, SUM_CHUNKS),
         out_shape=jax.ShapeDtypeStruct(shape, jnp.bfloat16),
-        in_specs=in_vmem(2),
+        in_specs=in_vmem(1),
         out_specs=pl.BlockSpec(memory_space=pltpu.VMEM),
         scratch_shapes=sum_scratch(shape),
         compiler_params=pltpu.CompilerParams(
             collective_id=number, has_side_effects=True, vmem_limit_bytes=48 * 2**20
         ),
         cost_estimate=pl.CostEstimate(flops=0, bytes_accessed=300 * 2**20, transcendentals=0),
-    )(wide_part, narrowed(narrow_part))
-    return parts_of(total, wide_part, narrow_part)
+    )(wide_part)
 
 
 def summed_and_gathered(wide_part, narrow_part, block, cotangents, number):
@@ -491,7 +628,7 @@
     if not (on_line() and in_plane()):
         whole = lax.all_gather(block, "dp", axis=1, tiled=True)
         open_rows = to_low(matmul(whole, cotangents))
-        return summed(wide_part, narrow_part, number) + (whole, open_rows)
+        return plain_sum(wide_part, narrow_part), whole, open_rows
     shape = (length, width + NARROW)
     pieces = SHARED + EXPERTS
     rows = block.shape[0] // pieces
@@ -516,14 +653,14 @@
         ),
         cost_estimate=pl.CostEstimate(flops=0, bytes_accessed=360 * 2**20, transcendentals=0),
     )(wide_part, narrowed(narrow_part), block, cotangents)
-    return parts_of(total, wide_part, narrow_part) + (whole, open_rows)
+    return total, whole, open_rows
 
 
 def summed_and_down(wide_part, narrow_part, act_rows, down_rows, number):
     length, width = wide_part.shape
     if not on_line():
         out = contract_first(act_rows, down_rows)
-        return summed(wide_part, narrow_part, number) + (out,)
+        return plain_sum(wide_part.astype(jnp.float32), narrow_part), out
     shape = (length, width + NARROW)
     rows = 2 * down_rows.shape[0] // (SHARED + EXPERTS)
     total, out = pl.pallas_call(
@@ -546,7 +683,7 @@
         ),
         cost_estimate=pl.CostEstimate(flops=0, bytes_accessed=300 * 2**20, transcendentals=0),
     )(wide_part, narrowed(narrow_part), act_rows, down_rows)
-    return parts_of(total, wide_part, narrow_part) + (out,)
+    return total, out
 
 
 def block_mask(first, rows, extent, row_piece_ref, col_piece_ref):
@@ -686,25 +823,35 @@
     )(query, keys, values, grads, cosine, signed_sine, row_piece, col_piece)
 
 
-def summed_and_attended_back(wide_part, attention_inputs, number):
+def summed_and_attended_back(wide_part, rows, upper, attention_inputs, number):
     if not on_line():
-        return lax.psum(wide_part, "tensor"), attend_back(*attention_inputs)
+        grad_qkv = attend_back(*attention_inputs)
+        normed_part = sum(contract_last(grad_qkv[part], rows[part]) for part in range(3))
+        mid_total = lax.psum(grad_mid_rows(grad_qkv, upper), "tensor")
+        return plain_sum(wide_part, None), grad_qkv, normed_part, mid_total
     shape = wide_part.shape
     length, heads_width = attention_inputs[0].shape
+    narrow_shape = (length, NARROW)
     return pl.pallas_call(
         functools.partial(attend_back_sum_kernel, SUM_CHUNKS),
         out_shape=[
             jax.ShapeDtypeStruct(shape, jnp.bfloat16),
             jax.ShapeDtypeStruct((3, length, heads_width), jnp.bfloat16),
+            jax.ShapeDtypeStruct(shape, jnp.bfloat16),
+            jax.ShapeDtypeStruct(narrow_shape, jnp.bfloat16),
         ],
-        in_specs=in_vmem(1 + len(attention_inputs)),
-        out_specs=in_vmem(2),
-        scratch_shapes=sum_scratch(shape) + [pltpu.VMEM((length, HEAD_SIZE), jnp.float32)] * 2,
+        in_specs=in_vmem(3 + len(attention_inputs)),
+        out_specs=in_vmem(4),
+        scratch_shapes=sum_scratch(shape)
+        + [pltpu.VMEM((length, HEAD_SIZE), jnp.float32)] * 2
+        + [pltpu.VMEM(narrow_shape, jnp.float32)]
+        + [pltpu.VMEM(narrow_shape, jnp.bfloat16)] * 4
+        + [pltpu.SemaphoreType.DMA((6, 1))],
         compiler_params=pltpu.CompilerParams(
-            collective_id=number, has_side_effects=True, vmem_limit_bytes=58 * 2**20
+            collective_id=number, has_side_effects=True, vmem_limit_bytes=60 * 2**20
         ),
         cost_estimate=pl.CostEstimate(flops=0, bytes_accessed=300 * 2**20, transcendentals=0),
-    )(wide_part, *attention_inputs)
+    )(wide_part, rows, upper, *attention_inputs)
 
 
 def hidden_step(gate_up, open_part, gate_row, extra):
@@ -1043,20 +1190,23 @@
     down_block = jnp.concatenate(
         [shared_expert_down_weight.T, down_block.reshape(-1, depth)], axis=0
     )
-    branch_here, mid_out_here_f, down_rows, open_rows = summed_and_gathered(
+    branch_total, down_rows, open_rows = summed_and_gathered(
         branch_part,
         matmul(attended, out_a),
         down_block,
         cotangent.T,
         1,
     )
-    mid_out = to_low(mid_out_here_f)
-    hidden_here = tokens_f + branch_here + ADAPTER_SCALE * matmul(mid_out, out_b)
-    normed_two_here_f, norm_ffn_pull = jax.vjp(
-        lambda rows: rms_scale(rows, gain_ffn_f), hidden_here
-    )
-    normed_two_here = to_low(normed_two_here_f)
-    normed_two = normed_two_here
+    mid_out = to_low(branch_total[:, width : width + rank])
+    hidden_here = (
+        tokens_f
+        + branch_total[:, :width].astype(jnp.float32)
+        + ADAPTER_SCALE * matmul(mid_out, out_b)
+    )
+    hidden_scale = lax.rsqrt(
+        jnp.mean(hidden_here * hidden_here, axis=1, keepdims=True) + EPSILON
+    )
+    normed_two = to_low(hidden_here * hidden_scale * gain_ffn_f)
     cot_f = cotangent.astype(jnp.float32)
     small_rows = gathered(
         jnp.concatenate(
@@ -1117,29 +1267,30 @@
         ],
         axis=0,
     ).T
-    grad_normed_two, narrow_sum, combined_part = summed_and_down(
+    second_total, combined_part = summed_and_down(
         normed_two_part, narrow_part, act_rows, down_rows, 2
     )
-    mid_down = to_low(narrow_sum[:, EXPERTS + 1 + rank :])
-    grad_mid_up = to_low(narrow_sum[:, EXPERTS + 1 : EXPERTS + 1 + rank])
-    grad_probs = chosen * narrow_sum[:, :EXPERTS]
-    grad_logits = to_low(
-        router_probs * (grad_probs - jnp.sum(router_probs * grad_probs, axis=1, keepdims=True))
-    )
-    shared_gate_grad = narrow_sum[:, EXPERTS] + jnp.sum(
-        mid_down.astype(jnp.float32) * cotangent_down, axis=1
-    )
-    grad_gate_logit = to_low(shared_gate_grad * shared_gate * (1.0 - shared_gate))
-    grad_normed_two = grad_normed_two + contract_last(
-        jnp.concatenate([grad_logits, grad_gate_logit[:, None], grad_mid_up], axis=1),
-        factors,
-    )
-    grad_hidden = cot_f + norm_ffn_pull(grad_normed_two)[0]
-    grad_branch = to_low(grad_hidden)
-    grad_mid_out = to_low(ADAPTER_SCALE * contract_last(grad_branch, out_b))
-    grad_attended = to_low(
-        matmul(grad_branch, output_rows) + contract_last(grad_mid_out, out_a)
-    )
+    up_from = width + EXPERTS + 1
+    grad_mid_up = to_low(second_total[:, up_from : up_from + rank])
+    mid_down = to_low(second_total[:, up_from + rank : up_from + 2 * rank])
+
+    def lanes(columns, first):
+        return jnp.pad(columns, ((0, 0), (first, NARROW - first - columns.shape[1])))
+
+    grad_hidden, grad_branch, grad_mid_out, grad_attended = epilogue(
+        (
+            second_total,
+            hidden_here,
+            hidden_scale,
+            cotangent,
+            lanes(router_probs, 0),
+            lanes(chosen, 0),
+            lanes(cotangent_down, EXPERTS + 1 + rank),
+            shared_gate[:, None],
+        ),
+        (gain_ffn_f[None], lanes(factors, 0), fill(out_b), lanes(out_a, 0), output_rows),
+    )
+    grad_mid_out = grad_mid_out[:, :rank]
     grad_down_b_local = ADAPTER_SCALE * contract_first(
         to_low(shared_gate[:, None] * mid_down.astype(jnp.float32)), cotangent
     )
@@ -1161,31 +1312,35 @@
         (grad_attended, side_by_side(early_grads))
     )
     early_rows = lax.all_gather(early_flat, "dp", axis=0, tiled=False)
-    combined_here, grad_qkv = summed_and_attended_back(
-        combined_part, (query, keys, values, grad_attended) + places, 3
-    )
+    upper = jnp.pad(
+        ADAPTER_SCALE * qkv_b.transpose(1, 0, 2), ((0, 0), (0, NARROW - rank), (0, 0))
+    )
+    combined_here, grad_qkv, normed_part, mid_total = summed_and_attended_back(
+        combined_part,
+        qkv_rows.transpose(1, 0, 2),
+        upper,
+        (query, keys, values, grad_attended) + places,
+        3,
+    )
+    mid_total, early_rows = lax.optimization_barrier((mid_total, early_rows))
+    grad_mid_qkv = to_low(mid_total[:, :rank])
+    late_grads = [
+        (
+            ADAPTER_SCALE
+            * jnp.einsum("tr,stf->rsf", mid_qkv, grad_qkv, preferred_element_type=jnp.float32)
+        ).reshape(rank, -1),
+        contract_first(grad_mid_qkv, normed),
+        grad_out_b_local,
+    ]
+    normed_part, late_flat = lax.optimization_barrier((normed_part, side_by_side(late_grads)))
+    late_rows = lax.all_gather(late_flat, "dp", axis=0, tiled=False)
     extra_here = ADAPTER_SCALE * matmul(mid_down, down_b)
     output = to_low(hidden_here + combined_here + shared_gate[:, None] * extra_here)
-    grad_qkv, early_rows = lax.optimization_barrier((grad_qkv, early_rows))
-    grad_mid_qkv_part = ADAPTER_SCALE * jnp.einsum(
-        "stf,rsf->tr", grad_qkv, qkv_b, preferred_element_type=jnp.float32
-    )
-    grad_qkv_b_local = ADAPTER_SCALE * jnp.einsum(
-        "tr,stf->rsf", mid_qkv, grad_qkv, preferred_element_type=jnp.float32
-    )
-    normed_part = jnp.einsum(
-        "stf,rsf->tr",
-        grad_qkv,
-        qkv_rows,
-        preferred_element_type=jnp.float32,
-    )
-    grad_normed, grad_mid_qkv_f = summed(normed_part, grad_mid_qkv_part, 4)
-    grad_mid_qkv_here = to_low(grad_mid_qkv_f)
-    grad_normed = grad_normed + contract_last(grad_mid_qkv_here, qkv_a)
+    last_total = summed(normed_part, 4)
+    last_total, late_rows = lax.optimization_barrier((last_total, late_rows))
+    grad_normed = last_total.astype(jnp.float32) + contract_last(grad_mid_qkv, qkv_a)
     norm_attn_pull = jax.vjp(lambda rows: rms_scale(rows, gain_attn_f), tokens_f)[1]
-    grad_tokens_here = to_low(grad_hidden + norm_attn_pull(grad_normed)[0])
-    grad_tokens, grad_mid_qkv = (grad_tokens_here, grad_mid_qkv_here)
-    grad_qkv_a_local = contract_first(grad_mid_qkv, normed)
+    grad_tokens = to_low(grad_hidden + norm_attn_pull(grad_normed)[0])
     everyone = small_rows[:: small_rows.shape[0] // lax.axis_size("dp"), EXPERTS + 1]
     marker = to_low(
         jnp.arange(ADAPTER_SETS, dtype=jnp.int32)[:, None] == everyone.astype(jnp.int32)[None, :]
@@ -1215,14 +1370,7 @@
     total_out_a, total_up_a, total_up_b, total_down_a, total_down_b = adapter_sums(
         early_grads, early_rows
     )
-    late_grads = [
-        grad_qkv_b_local.reshape(grad_qkv_b_local.shape[0], -1),
-        grad_qkv_a_local,
-        grad_out_b_local,
-    ]
-    total_qkv_b, total_qkv_a, total_out_b = adapter_sums(
-        late_grads, lax.all_gather(side_by_side(late_grads), "dp", axis=0, tiled=False)
-    )
+    total_qkv_b, total_qkv_a, total_out_b = adapter_sums(late_grads, late_rows)
     return (
         output,
         grad_tokens,

time: 1010 us -> 995 us (0.985)
  Pallas kernels: 751 us -> 795 us
  matrix products: 98.9 us -> 61.5 us
  other arithmetic: 40.3 us -> 28.8 us
    pallas_call x1, Pallas kernels: 114 us -> 150 us  [summed_and_attended_back(): pl.pallas_call(functools.partial(attend_back_sum_kernel, SUM_CHUNKS), out...]
    dot_general x6 -> x3, matrix products: 29.4 us -> 13.8 us  [contract_last(): lax.dot_general(left_side, right_side, (((1,), (1,)), ((), ())), preferre...]
    unnamed x130 -> x86, local copies, waits for them, and re-layouts: 45.4 us -> 31.6 us
    dot_general x2 -> x0, matrix products: 13.6 us -> none  [the longest x1 10.7 us: body(): jnp.einsum('stf,rsf->tr', grad_qkv, qkv_rows, preferred_element_type=jnp....]
    dot_general x6 -> x5, matrix products: 24.8 us -> 16.3 us  [matmul(): return jnp.dot(left_side, right_side, preferred_element_type=jnp.float32)]
    pallas_call x1 -> x2, Pallas kernels: 114 us -> 122 us  [the longest x1 104 us: summed(): pl.pallas_call(functools.partial(plain_line_sum_kernel, SUM_CHUNKS), out_...]
  transfers between devices with their start and end apart: 4 -> 4, of which waited for: 2 -> 0; matrix products, arithmetic and copies ran while one was open for 12% -> 12% of each run, Pallas kernels for 31% -> 46%
where the time goes in v8:
time: 995 us; the launch traced here: 985 us
  Pallas kernels  795 us (80%)
  local copies, waits for them, and re-layouts  72.9 us (7%)
  matrix products  61.5 us (6%)
  other arithmetic  28.8 us (3%)
  between operations  15.6 us (2%)
  blocking collectives  11.3 us (1%)
    pallas_call x1, Pallas kernels, experts_step(): pl.pallas_call(functools.partial(experts_kernel, pieces), in_specs=in_vme...  208 us
    pallas_call x1, Pallas kernels, summed_and_gathered(): pl.pallas_call(functools.partial(sum_gather_kernel, SUM_CHUNKS, pieces),...  181 us
    pallas_call x1, Pallas kernels, summed_and_attended_back(): pl.pallas_call(functools.partial(attend_back_sum_kernel, SUM_CHUNKS), out...  150 us
    pallas_call x1, Pallas kernels, summed_and_down(): pl.pallas_call(functools.partial(sum_down_kernel, SUM_CHUNKS), out_shape=...  120 us
    pallas_call x1, Pallas kernels, summed(): pl.pallas_call(functools.partial(plain_line_sum_kernel, SUM_CHUNKS), out_...  104 us
    unnamed x86, local copies, waits for them, and re-layouts  31.6 us
  transfers between devices with their start and end apart: 4, of which 0 were waited for; matrix products, arithmetic and copies ran while one was open for 12% of the time, Pallas kernels for 46%

profile of v8, /device:TPU:0, one launch (start us, length us, event | category | flops | bytes accessed | tf_op | source)
XLA Modules:
  0.0 985.3 jit_solution(16654394276781022367)
XLA Ops:
  7.2 2.3 pad_maximum_fusion.2
  9.6 1.2 slice.136
  10.8 3.7 copy.213
  14.6 1.5 pad_maximum_fusion.1
  16.2 5.1 slice.137
  22.0 1.0 dynamic-slice_multiply_fusion
  24.6 1.0 pad.44.up_extra_ref
  26.4 6.4 copy.207
  32.8 3.2 fusion.2
  36.3 2.3 fusion.14
  38.7 3.3 fusion.4
  42.3 1.1 copy.206
  43.9 11.3 %all_gather.22 = bf16[2048,18]{0,1:T(8,128)(2,1)S(1)} all-gather(bf16[256,18]{0,1:T(8,128)(2,1)S(1)} %maximum_maximum_fusion), channel_id=1, replica_groups=mesh['dp'=8,'tensor'=4] {'dp'}, dimensions={0}, use_global_device_ids=true | all-gather | bytes 82944 | tf_op jit(solution)/shard_map/all_gather | solution.py:1093
  55.2 0.8 dynamic-slice_bitcast_fusion
  56.5 0.9 pad.52.factors_ref
  57.4 0.8 dynamic-slice_bitcast_fusion.1
  60.6 1.0 pad.51.extra_ref
  62.5 1.9 fusion.27
  64.8 1.2 fusion.17
  66.0 2.0 pad_maximum_fusion.block_ref
  68.0 10.4 %fusion.7 = f32[3,512,1024]{1,2,0:T(8,128)S(1)} fusion(bf16[2048,4,512]{2,0,1:T(8,128)(2,1)} %all-gather.7.cloned.1.call-done, bf16[1024,2048]{1,0:T(8,128)(2,1)} %fusion.4), kind=kOutput, calls=%fused_computation.19 | convolution fusion | flops 6442450944 | bytes 16777216 | tf_op jit(solution)/shard_map/tr,rsf->stf/dot_general | solution.py:1178
  78.4 4.6 add_bitcast_fusion.qkv_ref
  83.0 14.8 %shard_map.303 = (bf16[1024,512]{1,0:T(8,128)(2,1)S(1)}, bf16[1024,512]{1,0:T(8,128)(2,1)S(1)}, bf16[1024,512]{1,0:T(8,128)(2,1)S(1)}, bf16[1024,512]{1,0:T(8,128)(2,1)S(1)}) custom-call(f32[3,1024,512]{2,1,0:T(8,128)} %add_bitcast_fusion.qkv_ref, f32[1024,128]{1,0:T(8,128)S(1)} %get-tuple-element.144.cosine_ref.refs_4_, ...), custom_call_target="tpu_custom_call" | custom-call | flops 2147483648 | bytes 16777216 | tf_op jit(solution)/shard_map/pallas_call | solution.py:741
  97.8 1.0 copy-done.6
  98.7 1.0 copy-done.7
  99.7 1.0 copy-done.8
  102.0 7.2 fusion.85.wide_ref
  109.3 181.1 %shard_map.304 = (bf16[1024,2176]{1,0:T(8,128)(2,1)}, bf16[7040,2048]{1,0:T(8,128)(2,1)}, bf16[7040,1024]{1,0:T(8,128)(2,1)}) custom-call(f32[1024,2048]{1,0:T(8,128)} %fusion.85.wide_ref, bf16[1024,128]{1,0:T(8,128)(2,1)} %concatenate.43.narrow_ref, bf16[7040,256]{1,0:T(8,128)(2,1)} %pad_maximum_fusion.block_ref, bf16[2048,1024]{1,0:T(8,128)(2,1)} %bitcast.131), custom_call_target="tpu_custom_call" | custom-call | bytes 377487360 | tf_op jit(solution)/shard_map/pallas_call | solution.py:635
  290.3 5.1 multiply_reduce_fusion
  296.3 2.5 copy-done.12
  298.8 2.0 copy-done.10
  300.8 1.4 fusion.84
  302.4 0.9 fusion.86
  305.0 1.1 multiply_bitcast_fusion
  307.1 1.9 pad.49.probs_ref
  308.9 1.0 copy.219.scale_ref
  310.6 3.1 slice_bitcast_fusion.1.rows_ref
  313.7 207.8 %shard_map.305 = (bf16[1024,2048]{1,0:T(8,128)(2,1)}, f32[20,1024]{1,0:T(8,128)}, f32[128,1024]{1,0:T(8,128)}, f32[128,1024]{1,0:T(8,128)}, f32[4,128,352]{2,1,0...) custom-call(bf16[1024,2048]{1,0:T(8,128)(2,1)} %copy-done.10, ...), custom_call_target="tpu_custom_call" | custom-call | bytes 629145600 | tf_op jit(solution)/shard_map/pallas_call | solution.py:1062
  521.5 0.9 slice.206
  525.9 119.8 %shard_map.306 = (bf16[1024,2176]{1,0:T(8,128)(2,1)}, bf16[1024,2048]{1,0:T(8,128)(2,1)}) custom-call(bf16[1024,2048]{1,0:T(8,128)(2,1)} %get-tuple-element.53.wide_ref, bf16[1024,128]{1,0:T(8,128)(2,1)} %concatenate.50.narrow_ref, bf16[7040,1024]{1,0:T(8,128)(2,1)} %get-tuple-element.57.act_ref, bf16[7040,2048]{1,0:T(8,128)(2,1)} %get-tuple-element.58.down_ref), custom_call_target="tpu_custom_call" | custom-call | bytes 314572800 | tf_op jit(solution)/shard_map/pallas_call | solution.py:666
  645.7 17.4 %shard_map.307 = (f32[1024,2048]{1,0:T(8,128)}, bf16[1024,2048]{1,0:T(8,128)(2,1)}, bf16[1024,128]{1,0:T(8,128)(2,1)}, bf16[1024,512]{1,0:T(8,128)(2,1)}) custom-call(bf16[1024,2176]{1,0:T(8,128)(2,1)} %get-tuple-element.63.total_ref, f32[1024,2048]{1,0:T(8,128)} %copy-done.12, f32[1024,1]{1,0:T(8,128)} %copy.219.scale_ref, ...), custom_call_target="tpu_custom_call" | custom-call | flops 2147483648 | bytes 33554432 | tf_op jit(solution)/shard_map/pallas_call | solution.py:539
  663.1 1.2 fusion.18
  664.3 1.7 fusion.13
  666.0 1.0 slice.203
  667.3 0.9 fusion.54
  668.4 3.1 fusion.11
  673.8 5.9 slice_bitcast_fusion.rows_ref
  679.7 150.0 %shard_map.308 = (bf16[1024,2048]{1,0:T(8,128)(2,1)}, bf16[3,1024,512]{2,1,0:T(8,128)(2,1)}, bf16[1024,2048]{1,0:T(8,128)(2,1)}, bf16[1024,128]{1,0:T(8,128)(2,1)}) custom-call(bf16[1024,2048]{1,0:T(8,128)(2,1)} %get-tuple-element.59.wide_ref, bf16[3,2048,512]{2,1,0:T(8,128)(2,1)} %slice_bitcast_fusion.rows_ref, bf16[3,128,512]{2,1,0:T(8,128)(2,1)} %pad.48.upper_ref, ...), custom_call_target="tpu_custom_call" | custom-call | bytes 314572800 | tf_op jit(solution)/shard_map/pallas_call | solution.py:835
  829.7 2.4 fusion.16
  832.2 3.0 fusion.12
  835.2 2.9 convolution_convert_fusion
  838.9 8.3 add_convert_fusion
  847.1 104.2 %shard_map.309 = bf16[1024,2048]{1,0:T(8,128)(2,1)S(1)} custom-call(bf16[1024,2048]{1,0:T(8,128)(2,1)} %get-tuple-element.77.wide_ref), custom_call_target="tpu_custom_call" | custom-call | bytes 314572800 | tf_op jit(solution)/shard_map/pallas_call | solution.py:613
  952.0 1.8 copy.237
  954.2 1.6 copy.236
  956.0 1.6 copy.239
  957.9 1.0 copy.238
  959.0 0.9 copy.234
  959.9 2.3 copy.224
  963.0 4.3 fusion.6
  967.3 1.6 copy.232
  968.9 1.6 copy.235
  970.5 1.3 copy.233
  971.9 6.5 fusion.1
  (156 shorter events, 22.7 us)
Async XLA Ops:
  7.2 57.6 %copy-start = (bf16[8,2048,16]{1,2,0:T(8,128)(2,1)S(1)}, bf16[8,2048,16]{1,2,0:T(8,128)(2,1)}, u32[]{:S(2)}) copy-start(bf16[8,2048,16]{1,2,0:T(8,128)(2,1)} %param.40) | copy-start | bytes 1572868
  7.2 60.8 %all-gather.7.cloned.1.call-start = ((), (), s32[]{:S(2)}) async-start(), calls=%async_computation | async-start | bytes 9437184 | tf_op jit(solution)/shard_map/all_gather | solution.py:1093
  9.6 304.1 %all-gather.9.cloned.1.call-start = ((), (), s32[]{:S(2)}) async-start(), calls=%async_computation.1 | async-start | bytes 19464192 | tf_op jit(solution)/shard_map/all_gather | solution.py:1163
  16.2 10.2 %copy-start.30 = (bf16[2048]{0:T(1024)(128)(2,1)S(1)}, bf16[2048]{0:T(1024)(128)(2,1)}, u32[]{:S(2)}) copy-start(bf16[2048]{0:T(1024)(128)(2,1)} %param.26) | copy-start | bytes 12292
  16.2 819.0 %all-gather.11.cloned.1.call-start = ((), (), s32[]{:S(2)}) async-start(), calls=%async_computation.2 | async-start | bytes 2543616 | tf_op jit(solution)/shard_map/all_gather | solution.py:1314
  32.8 3.4 copy-start.13
  32.8 5.8 copy-start.14
  38.6 22.0 %copy-start.17 = (f32[1024,16]{1,0:T(8,128)}, f32[1024,16]{1,0:T(8,128)S(1)}, u32[]{:S(2)}) copy-start(f32[1024,16]{1,0:T(8,128)S(1)} %fusion.14) | copy-start | bytes 196612
  38.6 3.3 copy-start.31
  38.6 3.3 copy-start.33
  38.6 3.7 copy-start.25
  38.6 4.9 copy-start.32
  38.7 4.8 copy-start.34
  38.7 4.9 copy-start.28
  38.7 5.2 copy-start.29
  42.1 40.9 %copy-start.9 = (s32[1024]{0:T(1024)}, s32[1024]{0:T(1024)S(1)}, u32[]{:S(2)}) copy-start(s32[1024]{0:T(1024)S(1)} %broadcast_add_fusion) | copy-start | bytes 12292
  42.3 40.6 %copy-start.5 = (s32[1024,1]{1,0:T(8,128)}, s32[1024,1]{1,0:T(8,128)S(1)}, u32[]{:S(2)}) copy-start(s32[1024,1]{1,0:T(8,128)S(1)} %copy.203.row_piece_ref.refs_6_) | copy-start | bytes 12292
  43.5 252.0 %copy-start.27 = (f32[2048]{0:T(1024)}, f32[2048]{0:T(1024)S(1)}, u32[]{:S(2)}) copy-start(f32[2048]{0:T(1024)S(1)} %convert_element_type.138) | copy-start | bytes 24580
  43.8 21.0 %copy-start.19 = (f32[1024,16]{1,0:T(8,128)}, f32[1024,16]{1,0:T(8,128)S(1)}, u32[]{:S(2)}) copy-start(f32[1024,16]{1,0:T(8,128)S(1)} %copy.211) | copy-start | bytes 196612
  59.9 4.9 copy-start.16
  62.4 3.6 copy-start.21
  62.4 3.6 copy-start.22
  64.8 18.2 %copy-start.3 = (f32[1024,128]{1,0:T(8,128)}, f32[1024,128]{1,0:T(8,128)S(1)}, u32[]{:S(2)}) copy-start(f32[1024,128]{1,0:T(8,128)S(1)} %get-tuple-element.144.cosine_ref.refs_4_) | copy-start | bytes 1572868
  64.8 18.2 %copy-start.4 = (f32[1024,128]{1,0:T(8,128)}, f32[1024,128]{1,0:T(8,128)S(1)}, u32[]{:S(2)}) copy-start(f32[1024,128]{1,0:T(8,128)S(1)} %get-tuple-element.145.sine_ref.refs_5_) | copy-start | bytes 1572868
  97.8 1.0 copy-start.6
  98.7 1.0 copy-start.7
  99.7 1.0 copy-start.8
  295.5 3.3 copy-start.12
  298.8 2.0 copy-start.10
  300.8 2.6 copy-start.18
  300.8 4.2 copy-start.20
  645.7 18.6 %copy-start.11 = (bf16[1024,2048]{1,0:T(8,128)(2,1)S(1)}, bf16[1024,2048]{1,0:T(8,128)(2,1)}, u32[]{:S(2)}) copy-start(bf16[1024,2048]{1,0:T(8,128)(2,1)} %copy-done.10) | copy-start | bytes 12582916
  671.5 0.7 copy-start.26
  672.2 287.7 %all-gather.13.cloned.1.call-start = ((), (), s32[]{:S(2)}) async-start(), calls=%async_computation.3 | async-start | bytes 1622016 | tf_op jit(solution)/shard_map/all_gather | solution.py:1336
  829.7 5.4 copy-start.24
  847.1 104.2 %copy-start.23 = (bf16[128,8832]{1,0:T(8,128)(2,1)S(1)}, bf16[128,8832]{1,0:T(8,128)(2,1)}, u32[]{:S(2)}) copy-start(bf16[128,8832]{1,0:T(8,128)(2,1)} %all-gather.11.cloned.1.call-done) | copy-start | bytes 6782980
  951.3 2.6 copy-start.1
  959.9 3.1 copy-start.2
  967.3 4.5 copy-start.15
Sparse Core Ops, SparseCore 0:
  10.5 57.3 all-gather.6
  69.8 134.9 all-gather.8
  672.3 28.2 all-gather.10
  838.9 22.2 all-gather.12

commit v9 on v8

--- a/solution.py
+++ b/solution.py
@@ -22,6 +22,7 @@
 NARROW = 128
 MESH = pl.DeviceIdType.MESH
 SUM_CHUNKS = 16
+LAG = 1
 AHEAD = 1
 LEAD = 2
 SHARED = 4
@@ -74,7 +75,16 @@
 
 
 def line_sum_steps(
-    chunks, wide_ref, narrow_ref, total_ref, part_ref, from_end, pair_sum, from_pair, semaphores
+    chunks,
+    lag,
+    wide_ref,
+    narrow_ref,
+    total_ref,
+    part_ref,
+    from_end,
+    pair_sum,
+    from_pair,
+    semaphores,
 ):
     place = lax.axis_index("tensor")
     width = wide_ref.shape[1]
@@ -129,10 +139,10 @@
         def _():
             pl.semaphore_wait(barrier, 1 + extra)
 
-    def begin():
+    def begin(first=0, last=chunks):
         @pl.when(end)
         def _():
-            @pl.loop(0, chunks)
+            @pl.loop(first, last)
             def _(chunk):
                 stage(chunk)
                 inward(chunk).start()
@@ -145,11 +155,11 @@
             add(part_ref, from_end, pair_sum, step)
             across(step).start()
 
-        @pl.when(inner & (step > 0) & (step <= chunks))
-        def _():
-            across(step - 1).wait_recv()
-            add(pair_sum, from_pair, total_ref, step - 1)
-            outward(step - 1).start()
+        @pl.when(inner & (step >= lag) & (step < chunks + lag))
+        def _():
+            across(step - lag).wait_recv()
+            add(pair_sum, from_pair, total_ref, step - lag)
+            outward(step - lag).start()
 
     def finish():
         @pl.when(end)
@@ -280,7 +290,7 @@
 
 
 def line_sum_kernel(chunks, *refs):
-    greet, begin, advance, finish = line_sum_steps(chunks, *refs)
+    greet, begin, advance, finish = line_sum_steps(chunks, 1, *refs)
     greet(0)
     begin()
 
@@ -304,7 +314,7 @@
     *scratch,
 ):
     greet, begin, advance, finish = line_sum_steps(
-        chunks, wide_ref, narrow_ref, total_ref, *scratch[:5]
+        chunks, LAG, wide_ref, narrow_ref, total_ref, *scratch[:5]
     )
     gather_semaphores, local_semaphores, piece_rows, open_rows = scratch[5:]
     gather_greet, gather_advance, gather_arrive, gather_finish, own, load, load_wait, stages = (
@@ -330,7 +340,7 @@
     def _(piece):
         stages[0](piece)
 
-    @pl.loop(0, max(chunks + 1, pieces + 3 * AHEAD + 1))
+    @pl.loop(0, max(chunks + LAG, pieces + 3 * AHEAD + 1))
     def _(step):
         gather_advance(step)
         advance(step)
@@ -367,7 +377,7 @@
     chunks, wide_ref, narrow_ref, act_ref, down_ref, total_ref, out_ref, *scratch
 ):
     greet, begin, advance, finish = line_sum_steps(
-        chunks, wide_ref, narrow_ref, total_ref, *scratch[:5]
+        chunks, LAG, wide_ref, narrow_ref, total_ref, *scratch[:5]
     )
     semaphores, act_rows, down_rows, out_rows = scratch[5:]
     rows = act_rows.shape[1]
@@ -387,7 +397,7 @@
     begin()
     out_rows[...] = jnp.zeros_like(out_rows)
 
-    @pl.loop(0, max(blocks, chunks + 1))
+    @pl.loop(0, max(blocks, chunks + LAG))
     def _(step):
         advance(step)
 
@@ -417,18 +427,22 @@
     inputs, scratch = refs[:8], refs[12:]
     total_ref, grad_qkv_ref, normed_part_ref, mid_total_ref = refs[8:12]
     greet, begin, advance, finish = line_sum_steps(
-        chunks, wide_ref, None, total_ref, *scratch[:5]
+        chunks, LAG, wide_ref, None, total_ref, *scratch[:5]
     )
     head_block = attend_back_steps(*inputs, grad_qkv_ref, *scratch[5:7])
     mid_part = scratch[7]
     _, mid_begin, mid_advance, mid_finish = line_sum_steps(
-        1, mid_part, None, mid_total_ref, *scratch[8:]
+        1, 1, mid_part, None, mid_total_ref, *scratch[8:13]
     )
     length, heads_width = inputs[0].shape
     heads, blocks = heads_width // HEAD_SIZE, length // QUERY_ROWS
     each = blocks // 2
+    rows = scratch[-2]
+    load = pltpu.make_async_copy(rows_ref.at[:3], rows, scratch[-1].at[0])
+    load.start()
+    done = heads * each
     greet(0)
-    begin()
+    begin(0, done + blocks)
 
     @pl.loop(0, heads)
     def _(head):
@@ -439,23 +453,26 @@
 
     mid_part[...] = grad_mid_rows(grad_qkv_ref, upper_ref)
     mid_begin()
-    done = heads * each
+    begin(done + blocks, chunks)
+    load.wait()
 
     @pl.loop(0, blocks)
     def _(block):
         advance(done + block)
         span = pl.ds(pl.multiple_of(block * QUERY_ROWS, QUERY_ROWS), QUERY_ROWS)
         normed_part_ref[span] = to_low(
-            sum(contract_last(grad_qkv_ref[part, span], rows_ref[part]) for part in range(3))
+            sum(contract_last(grad_qkv_ref[part, span], rows[part]) for part in range(3))
         )
 
     mid_advance(0)
 
-    @pl.loop(done + blocks, max(done + blocks, chunks + 1))
+    advance(done + blocks)
+    mid_advance(1)
+
+    @pl.loop(done + blocks + 1, max(done + blocks + 1, chunks + LAG))
     def _(step):
         advance(step)
 
-    mid_advance(1)
     mid_finish()
     finish()
 
@@ -513,16 +530,16 @@
     grad_mid = to_low(ADAPTER_SCALE * contract_last(grad_branch, out_b_ref[...]))
     grad_mid_ref[...] = grad_mid
     grad_attended_ref[...] = to_low(
-        matmul(grad_branch, rows_ref[...]) + contract_last(grad_mid, out_a_ref[...])
+        matmul(grad_branch, rows_ref[0]) + contract_last(grad_mid, out_a_ref[...])
     )
 
 
 def epilogue(blocked, still):
     length = blocked[0].shape[0]
-    width, heads_width = still[-1].shape
+    width, heads_width = still[-1].shape[1:]
     rows = min(length, 256)
     total, hidden, scale, cotangent, probs, chosen, extra, gate = blocked
-    gain, factors, out_b, out_a, output_rows = still
+    gain, factors, out_b, out_a, row_stack = still
 
     def block(array):
         return pl.BlockSpec((rows, array.shape[1]), lambda index: (index, 0))
@@ -542,7 +559,8 @@
         in_specs=[block(array) for array in (total, hidden, scale, cotangent)]
         + [whole(gain)]
         + [block(array) for array in (probs, chosen, extra, gate)]
-        + [whole(array) for array in (factors, out_b, out_a, output_rows)],
+        + [whole(array) for array in (factors, out_b, out_a)]
+        + [pl.BlockSpec((1, width, heads_width), lambda index: (3, 0, 0))],
         out_specs=[block(out) for out in outs],
         out_shape=outs,
         compiler_params=pltpu.CompilerParams(
@@ -566,7 +584,7 @@
         factors,
         out_b,
         out_a,
-        output_rows,
+        row_stack,
     )
 
 
@@ -840,13 +858,14 @@
             jax.ShapeDtypeStruct(shape, jnp.bfloat16),
             jax.ShapeDtypeStruct(narrow_shape, jnp.bfloat16),
         ],
-        in_specs=in_vmem(3 + len(attention_inputs)),
+        in_specs=in_vmem(1) + in_hbm(1) + in_vmem(1 + len(attention_inputs)),
         out_specs=in_vmem(4),
         scratch_shapes=sum_scratch(shape)
         + [pltpu.VMEM((length, HEAD_SIZE), jnp.float32)] * 2
         + [pltpu.VMEM(narrow_shape, jnp.float32)]
         + [pltpu.VMEM(narrow_shape, jnp.bfloat16)] * 4
-        + [pltpu.SemaphoreType.DMA((6, 1))],
+        + [pltpu.SemaphoreType.DMA((6, 1))]
+        + [pltpu.VMEM((3,) + rows.shape[1:], jnp.bfloat16), pltpu.SemaphoreType.DMA((1,))],
         compiler_params=pltpu.CompilerParams(
             collective_id=number, has_side_effects=True, vmem_limit_bytes=60 * 2**20
         ),
@@ -1172,6 +1191,7 @@
         jnp.concatenate([query_key_value_weight, output_projection_weight[:, None]], axis=1)
     )
     qkv_rows, output_rows = attention_rows[:, :3], attention_rows[:, 3]
+    row_stack = attention_rows.transpose(1, 0, 2)
     normed, cotangent_down, up_extra, down_extra = lax.optimization_barrier(
         (normed, cotangent_down, up_extra, down_extra)
     )
@@ -1288,7 +1308,7 @@
             lanes(cotangent_down, EXPERTS + 1 + rank),
             shared_gate[:, None],
         ),
-        (gain_ffn_f[None], lanes(factors, 0), fill(out_b), lanes(out_a, 0), output_rows),
+        (gain_ffn_f[None], lanes(factors, 0), fill(out_b), lanes(out_a, 0), row_stack),
     )
     grad_mid_out = grad_mid_out[:, :rank]
     grad_down_b_local = ADAPTER_SCALE * contract_first(
@@ -1311,13 +1331,13 @@
     grad_attended, early_flat = lax.optimization_barrier(
         (grad_attended, side_by_side(early_grads))
     )
-    early_rows = lax.all_gather(early_flat, "dp", axis=0, tiled=False)
+    early_rows = lax.all_gather(early_flat, "dp", axis=0, tiled=True)
     upper = jnp.pad(
         ADAPTER_SCALE * qkv_b.transpose(1, 0, 2), ((0, 0), (0, NARROW - rank), (0, 0))
     )
     combined_here, grad_qkv, normed_part, mid_total = summed_and_attended_back(
         combined_part,
-        qkv_rows.transpose(1, 0, 2),
+        row_stack,
         upper,
         (query, keys, values, grad_attended) + places,
         3,
@@ -1333,7 +1353,7 @@
         grad_out_b_local,
     ]
     normed_part, late_flat = lax.optimization_barrier((normed_part, side_by_side(late_grads)))
-    late_rows = lax.all_gather(late_flat, "dp", axis=0, tiled=False)
+    late_rows = lax.all_gather(late_flat, "dp", axis=0, tiled=True)
     extra_here = ADAPTER_SCALE * matmul(mid_down, down_b)
     output = to_low(hidden_here + combined_here + shared_gate[:, None] * extra_here)
     last_total = summed(normed_part, 4)
@@ -1342,22 +1362,17 @@
     norm_attn_pull = jax.vjp(lambda rows: rms_scale(rows, gain_attn_f), tokens_f)[1]
     grad_tokens = to_low(grad_hidden + norm_attn_pull(grad_normed)[0])
     everyone = small_rows[:: small_rows.shape[0] // lax.axis_size("dp"), EXPERTS + 1]
-    marker = to_low(
-        jnp.arange(ADAPTER_SETS, dtype=jnp.int32)[:, None] == everyone.astype(jnp.int32)[None, :]
-    )
+    hits = jnp.arange(ADAPTER_SETS, dtype=jnp.int32)[:, None] == everyone.astype(jnp.int32)
+    same = jnp.arange(rank)[:, None] == jnp.arange(rank)[None, :]
+    chooser = to_low(hits[:, None, :, None] & same[None, :, None, :])
+    chooser = chooser.reshape(ADAPTER_SETS * rank, -1)
 
     def adapter_sums(local_grads, rows):
         results, start = [], 0
         for local_grad in local_grads:
             size = local_grad.shape[1]
-            results.append(
-                jnp.einsum(
-                    "cj,jrn->crn",
-                    marker,
-                    rows[:, :, start : start + size],
-                    preferred_element_type=jnp.float32,
-                )
-            )
+            total = matmul(chooser, rows[:, start : start + size])
+            results.append(total.reshape(ADAPTER_SETS, rank, size))
             start += size
         return results
 

time: 995 us -> 972 us (0.977)
  Pallas kernels: 795 us -> 770 us
  local copies, waits for them, and re-layouts: 72.9 us -> 56.8 us
  matrix products: 61.5 us -> 74.1 us
    pallas_call x1, Pallas kernels: 150 us -> 122 us  [summed_and_attended_back(): pl.pallas_call(functools.partial(attend_back_sum_kernel, SUM_CHUNKS), out...]
    dot_general x5 -> x13, matrix products: 16.3 us -> 26.9 us  [matmul(): return jnp.dot(left_side, right_side, preferred_element_type=jnp.float32)]
    unnamed x86 -> x75, local copies, waits for them, and re-layouts: 31.6 us -> 24.1 us
  transfers between devices with their start and end apart: 4 -> 4, of which waited for: 0 -> 0; matrix products, arithmetic and copies ran while one was open for 12% -> 11% of each run, Pallas kernels for 46% -> 44%
where the time goes in v9:
time: 972 us; the launch traced here: 962 us
  Pallas kernels  770 us (79%)
  matrix products  74.1 us (8%)
  local copies, waits for them, and re-layouts  56.8 us (6%)
  other arithmetic  34 us (3%)
  between operations  15.5 us (2%)
  blocking collectives  11.3 us (1%)
    pallas_call x1, Pallas kernels, experts_step(): pl.pallas_call(functools.partial(experts_kernel, pieces), in_specs=in_vme...  208 us
    pallas_call x1, Pallas kernels, summed_and_gathered(): pl.pallas_call(functools.partial(sum_gather_kernel, SUM_CHUNKS, pieces),...  181 us
    pallas_call x1, Pallas kernels, summed_and_attended_back(): pl.pallas_call(functools.partial(attend_back_sum_kernel, SUM_CHUNKS), out...  122 us
    pallas_call x1, Pallas kernels, summed_and_down(): pl.pallas_call(functools.partial(sum_down_kernel, SUM_CHUNKS), out_shape=...  121 us
    pallas_call x1, Pallas kernels, summed(): pl.pallas_call(functools.partial(plain_line_sum_kernel, SUM_CHUNKS), out_...  107 us
    dot_general x13, matrix products, matmul(): return jnp.dot(left_side, right_side, preferred_element_type=jnp.float32)  26.9 us
    unnamed x75, local copies, waits for them, and re-layouts  24.1 us
  transfers between devices with their start and end apart: 4, of which 0 were waited for; matrix products, arithmetic and copies ran while one was open for 11% of the time, Pallas kernels for 44%

profile of v9, /device:TPU:0, one launch (start us, length us, event | category | flops | bytes accessed | tf_op | source)
XLA Modules:
  0.0 962.5 jit_solution(16669762505008820776)
XLA Ops:
  7.2 2.3 pad_maximum_fusion.2
  9.6 1.2 slice.136
  10.8 3.7 copy.167
  14.6 1.5 pad_maximum_fusion.1
  16.2 5.1 slice.137
  22.0 1.0 dynamic-slice_multiply_fusion
  24.6 1.0 pad.44.up_extra_ref
  26.4 6.4 copy.161
  32.8 3.2 fusion.2
  36.3 2.3 fusion.15
  38.7 3.3 fusion.4
  42.4 1.1 copy.160
  44.0 11.3 %all_gather.16 = bf16[2048,18]{0,1:T(8,128)(2,1)S(1)} all-gather(bf16[256,18]{0,1:T(8,128)(2,1)S(1)} %maximum_maximum_fusion), channel_id=1, replica_groups=mesh['dp'=8,'tensor'=4] {'dp'}, dimensions={0}, use_global_device_ids=true | all-gather | bytes 82944 | tf_op jit(solution)/shard_map/all_gather | solution.py:1112
  55.3 0.8 dynamic-slice_bitcast_fusion
  56.5 0.9 pad.52.factors_ref
  60.6 1.0 pad.51.extra_ref
  61.6 0.9 pad.50.chosen_ref
  62.5 1.9 fusion.30
  64.9 1.2 fusion.18
  66.1 2.0 pad_maximum_fusion.block_ref
  68.1 10.4 %fusion.7 = f32[3,512,1024]{1,2,0:T(8,128)S(1)} fusion(bf16[2048,4,512]{2,0,1:T(8,128)(2,1)} %all-gather.5.cloned.1.call-done, bf16[1024,2048]{1,0:T(8,128)(2,1)} %fusion.4), kind=kOutput, calls=%fused_computation.17 | convolution fusion | flops 6442450944 | bytes 16777216 | tf_op jit(solution)/shard_map/tr,rsf->stf/dot_general | solution.py:1198
  78.5 4.6 add_bitcast_fusion.qkv_ref
  83.0 14.8 %shard_map.303 = (bf16[1024,512]{1,0:T(8,128)(2,1)S(1)}, bf16[1024,512]{1,0:T(8,128)(2,1)S(1)}, bf16[1024,512]{1,0:T(8,128)(2,1)S(1)}, bf16[1024,512]{1,0:T(8,128)(2,1)S(1)}) custom-call(f32[3,1024,512]{2,1,0:T(8,128)} %add_bitcast_fusion.qkv_ref, f32[1024,128]{1,0:T(8,128)S(1)} %get-tuple-element.144.cosine_ref.refs_4_, ...), custom_call_target="tpu_custom_call" | custom-call | flops 2147483648 | bytes 16777216 | tf_op jit(solution)/shard_map/pallas_call | solution.py:759
  97.8 1.0 copy-done.5
  98.8 1.0 copy-done.6
  99.8 1.0 copy-done.7
  102.1 7.3 fusion.14.wide_ref
  109.3 181.0 %shard_map.304 = (bf16[1024,2176]{1,0:T(8,128)(2,1)}, bf16[7040,2048]{1,0:T(8,128)(2,1)}, bf16[7040,1024]{1,0:T(8,128)(2,1)}) custom-call(f32[1024,2048]{1,0:T(8,128)} %fusion.14.wide_ref, bf16[1024,128]{1,0:T(8,128)(2,1)} %concatenate.43.narrow_ref, bf16[7040,256]{1,0:T(8,128)(2,1)} %pad_maximum_fusion.block_ref, bf16[2048,1024]{1,0:T(8,128)(2,1)} %bitcast.152), custom_call_target="tpu_custom_call" | custom-call | bytes 377487360 | tf_op jit(solution)/shard_map/pallas_call | solution.py:653
  290.4 5.1 multiply_reduce_fusion
  296.3 2.5 copy-done.11
  298.8 2.0 copy-done.9
  300.8 1.4 fusion.94
  302.4 0.9 fusion.95
  305.0 1.1 multiply_bitcast_fusion
  307.1 1.9 pad.49.probs_ref
  309.0 1.0 copy.173.scale_ref
  310.7 207.8 %shard_map.305 = (bf16[1024,2048]{1,0:T(8,128)(2,1)}, f32[20,1024]{1,0:T(8,128)}, f32[128,1024]{1,0:T(8,128)}, f32[128,1024]{1,0:T(8,128)}, f32[4,128,352]{2,1,0...) custom-call(bf16[1024,2048]{1,0:T(8,128)(2,1)} %copy-done.9, ...), custom_call_target="tpu_custom_call" | custom-call | bytes 629145600 | tf_op jit(solution)/shard_map/pallas_call | solution.py:1081
  518.5 0.9 slice.207
  522.9 120.7 %shard_map.306 = (bf16[1024,2176]{1,0:T(8,128)(2,1)}, bf16[1024,2048]{1,0:T(8,128)(2,1)}) custom-call(bf16[1024,2048]{1,0:T(8,128)(2,1)} %get-tuple-element.53.wide_ref, bf16[1024,128]{1,0:T(8,128)(2,1)} %concatenate.50.narrow_ref, bf16[7040,1024]{1,0:T(8,128)(2,1)} %get-tuple-element.57.act_ref, bf16[7040,2048]{1,0:T(8,128)(2,1)} %get-tuple-element.58.down_ref), custom_call_target="tpu_custom_call" | custom-call | bytes 314572800 | tf_op jit(solution)/shard_map/pallas_call | solution.py:684
  643.6 17.4 %shard_map.307 = (f32[1024,2048]{1,0:T(8,128)}, bf16[1024,2048]{1,0:T(8,128)(2,1)}, bf16[1024,128]{1,0:T(8,128)(2,1)}, bf16[1024,512]{1,0:T(8,128)(2,1)}) custom-call(bf16[1024,2176]{1,0:T(8,128)(2,1)} %get-tuple-element.63.total_ref, f32[1024,2048]{1,0:T(8,128)} %copy-done.11, f32[1024,1]{1,0:T(8,128)} %copy.173.scale_ref, ...), custom_call_target="tpu_custom_call" | custom-call | flops 2147483648 | bytes 33554432 | tf_op jit(solution)/shard_map/pallas_call | solution.py:556
  661.0 1.2 fusion.19
  662.2 1.7 fusion.13
  663.9 1.0 slice.204
  665.3 0.9 fusion.65
  666.3 3.1 fusion.11
  672.2 122.0 %shard_map.308 = (bf16[1024,2048]{1,0:T(8,128)(2,1)}, bf16[3,1024,512]{2,1,0:T(8,128)(2,1)}, bf16[1024,2048]{1,0:T(8,128)(2,1)}, bf16[1024,128]{1,0:T(8,128)(2,1)}) custom-call(bf16[1024,2048]{1,0:T(8,128)(2,1)} %get-tuple-element.59.wide_ref, bf16[4,2048,512]{2,1,0:T(8,128)(2,1)} %bitcast.150, bf16[3,128,512]{2,1,0:T(8,128)(2,1)} %pad.48.upper_ref, ...), custom_call_target="tpu_custom_call" | custom-call | bytes 314572800 | tf_op jit(solution)/shard_map/pallas_call | solution.py:853
  794.2 2.4 fusion.17
  796.7 3.0 fusion.12
  799.7 2.9 convolution_convert_fusion
  803.3 8.2 add_convert_fusion
  811.4 106.7 %shard_map.309 = bf16[1024,2048]{1,0:T(8,128)(2,1)S(1)} custom-call(bf16[1024,2048]{1,0:T(8,128)(2,1)} %get-tuple-element.77.wide_ref), custom_call_target="tpu_custom_call" | custom-call | bytes 314572800 | tf_op jit(solution)/shard_map/pallas_call | solution.py:631
  918.1 2.0 copy-done.1
  920.1 1.2 slice_bitcast_fusion.2
  922.0 1.8 copy.180
  923.9 0.9 convolution_bitcast_fusion.3
  924.7 1.1 convolution_bitcast_fusion
  925.8 1.3 convolution_bitcast_fusion.1
  927.1 1.3 fusion.20
  928.4 1.0 slice_bitcast_fusion.3
  929.4 2.3 convolution_bitcast_fusion.2
  931.7 2.3 fusion.23
  934.0 8.4 fusion.6
  942.6 1.2 fusion.64
  943.8 11.7 %fusion.1 = bf16[1024,2048]{1,0:T(8,128)(2,1)} fusion(f32[1024,2048]{1,0:T(8,128)} %get-tuple-element.70, bf16[1024,2048]{1,0:T(8,128)(2,1)} %param.24, f32[1024,2048]{1,0:T(8,128)} %get-tuple-element.143, bf16[1024,2048]{1,0:T(8,128)(2,1)} %copy-done.1, f32[1024]{0:T(1024)S(1)} %multiply_multiply_fusion, f32[2048]{0:T(1024)S(1)} %convert_element_type.132, ...), kind=kLoop, calls=%fused_computation.7 | loop fusion | flops 20971520 | bytes 29376512 | tf_op jit(solution)/shard_map/convert_element_type | solution.py:50
  (151 shorter events, 21.5 us)
Async XLA Ops:
  7.2 57.6 %copy-start = (bf16[8,2048,16]{1,2,0:T(8,128)(2,1)S(1)}, bf16[8,2048,16]{1,2,0:T(8,128)(2,1)}, u32[]{:S(2)}) copy-start(bf16[8,2048,16]{1,2,0:T(8,128)(2,1)} %param.40) | copy-start | bytes 1572868
  7.2 60.9 %all-gather.5.cloned.1.call-start = ((), (), s32[]{:S(2)}) async-start(), calls=%async_computation | async-start | bytes 9437184 | tf_op jit(solution)/shard_map/all_gather | solution.py:1112
  9.6 301.1 %all-gather.7.cloned.1.call-start = ((), (), s32[]{:S(2)}) async-start(), calls=%async_computation.1 | async-start | bytes 19464192 | tf_op jit(solution)/shard_map/all_gather | solution.py:1182
  16.2 10.3 %copy-start.28 = (bf16[2048]{0:T(1024)(128)(2,1)S(1)}, bf16[2048]{0:T(1024)(128)(2,1)}, u32[]{:S(2)}) copy-start(bf16[2048]{0:T(1024)(128)(2,1)} %param.26) | copy-start | bytes 12292
  16.2 783.5 %all-gather.9.cloned.1.call-start = ((), (), s32[]{:S(2)}) async-start(), calls=%async_computation.2 | async-start | bytes 2543616 | tf_op jit(solution)/shard_map/all_gather | solution.py:1334
  32.8 3.4 copy-start.12
  32.8 5.8 copy-start.13
  38.6 22.0 %copy-start.15 = (f32[1024,16]{1,0:T(8,128)}, f32[1024,16]{1,0:T(8,128)S(1)}, u32[]{:S(2)}) copy-start(f32[1024,16]{1,0:T(8,128)S(1)} %fusion.15) | copy-start | bytes 196612
  38.6 3.4 copy-start.29
  38.6 3.4 copy-start.31
  38.6 3.7 copy-start.23
  38.7 4.9 copy-start.30
  38.7 4.9 copy-start.32
  38.7 4.9 copy-start.26
  38.7 5.2 copy-start.27
  42.1 40.9 %copy-start.8 = (s32[1024]{0:T(1024)}, s32[1024]{0:T(1024)S(1)}, u32[]{:S(2)}) copy-start(s32[1024]{0:T(1024)S(1)} %broadcast_add_fusion) | copy-start | bytes 12292
  42.4 40.7 %copy-start.4 = (s32[1024,1]{1,0:T(8,128)}, s32[1024,1]{1,0:T(8,128)S(1)}, u32[]{:S(2)}) copy-start(s32[1024,1]{1,0:T(8,128)S(1)} %copy.157.row_piece_ref.refs_6_) | copy-start | bytes 12292
  43.5 252.0 %copy-start.25 = (f32[2048]{0:T(1024)}, f32[2048]{0:T(1024)S(1)}, u32[]{:S(2)}) copy-start(f32[2048]{0:T(1024)S(1)} %convert_element_type.138) | copy-start | bytes 24580
  43.8 21.0 %copy-start.17 = (f32[1024,16]{1,0:T(8,128)}, f32[1024,16]{1,0:T(8,128)S(1)}, u32[]{:S(2)}) copy-start(f32[1024,16]{1,0:T(8,128)S(1)} %copy.165) | copy-start | bytes 196612
  59.9 4.9 copy-start.14
  62.5 3.6 copy-start.19
  62.5 3.6 copy-start.20
  64.8 18.2 %copy-start.2 = (f32[1024,128]{1,0:T(8,128)}, f32[1024,128]{1,0:T(8,128)S(1)}, u32[]{:S(2)}) copy-start(f32[1024,128]{1,0:T(8,128)S(1)} %get-tuple-element.144.cosine_ref.refs_4_) | copy-start | bytes 1572868
  64.8 18.2 %copy-start.3 = (f32[1024,128]{1,0:T(8,128)}, f32[1024,128]{1,0:T(8,128)S(1)}, u32[]{:S(2)}) copy-start(f32[1024,128]{1,0:T(8,128)S(1)} %get-tuple-element.145.sine_ref.refs_5_) | copy-start | bytes 1572868
  97.8 1.0 copy-start.5
  98.8 1.0 copy-start.6
  99.8 1.0 copy-start.7
  295.5 3.3 copy-start.11
  298.8 2.0 copy-start.9
  300.8 2.6 copy-start.16
  300.8 4.2 copy-start.18
  643.6 18.6 %copy-start.10 = (bf16[1024,2048]{1,0:T(8,128)(2,1)S(1)}, bf16[1024,2048]{1,0:T(8,128)(2,1)}, u32[]{:S(2)}) copy-start(bf16[1024,2048]{1,0:T(8,128)(2,1)} %copy-done.9) | copy-start | bytes 12582916
  669.4 0.7 copy-start.24
  670.1 258.2 %all-gather.11.cloned.1.call-start = ((), (), s32[]{:S(2)}) async-start(), calls=%async_computation.3 | async-start | bytes 1622016 | tf_op jit(solution)/shard_map/all_gather | solution.py:1356
  794.2 5.4 copy-start.22
  918.1 2.0 copy-start.1
  921.6 2.2 copy-start.21
Sparse Core Ops, SparseCore 0:
  10.5 57.3 all-gather.4
  69.8 134.8 all-gather.6
  670.3 27.9 all-gather.8
  803.4 24.4 all-gather.10

commit v10 on v9

--- a/solution.py
+++ b/solution.py
@@ -27,7 +27,7 @@
 LEAD = 2
 SHARED = 4
 HALVES = 1
-READY = 6
+READY = 4
 
 
 def matmul(left_side, right_side):
@@ -85,6 +85,7 @@
     pair_sum,
     from_pair,
     semaphores,
+    on_total=None,
 ):
     place = lax.axis_index("tensor")
     width = wide_ref.shape[1]
@@ -160,6 +161,8 @@
             across(step - lag).wait_recv()
             add(pair_sum, from_pair, total_ref, step - lag)
             outward(step - lag).start()
+            if on_total is not None:
+                on_total(step - lag)
 
     def finish():
         @pl.when(end)
@@ -168,6 +171,8 @@
             def _(chunk):
                 inward(chunk).wait_send()
                 outward(chunk).wait_recv()
+                if on_total is not None:
+                    on_total(chunk)
 
         @pl.when(inner)
         def _():
@@ -289,18 +294,6 @@
     return greet, advance, arrive, finish, own, load, load_wait, (launch, forward, hand_over)
 
 
-def line_sum_kernel(chunks, *refs):
-    greet, begin, advance, finish = line_sum_steps(chunks, 1, *refs)
-    greet(0)
-    begin()
-
-    @pl.loop(0, chunks + 1)
-    def _(step):
-        advance(step)
-
-    finish()
-
-
 def sum_gather_kernel(
     chunks,
     pieces,
@@ -421,6 +414,77 @@
 
     out_ref[...] = to_low(out_rows[...])
     finish()
+
+
+def last_sum_kernel(
+    chunks,
+    wide_ref,
+    streamed_refs,
+    mid_ref,
+    qkv_a_ref,
+    gain_ref,
+    mid_down_ref,
+    down_b_ref,
+    gate_ref,
+    grad_tokens_ref,
+    output_ref,
+    total_ref,
+    *scratch,
+):
+    buffers, load_semaphores = scratch[5:-1], scratch[-1]
+    rows = wide_ref.shape[0] // chunks
+
+    def span(chunk):
+        return pl.ds(pl.multiple_of(chunk * rows, rows), rows)
+
+    def loads(chunk):
+        slot = chunk % 2
+        return [
+            pltpu.make_async_copy(
+                source.at[span(chunk)], target.at[slot], load_semaphores.at[number, slot]
+            )
+            for number, (source, target) in enumerate(zip(streamed_refs, buffers))
+        ]
+
+    def on_total(chunk):
+        for load in loads(chunk):
+            load.wait()
+
+        @pl.when(chunk + 1 < chunks)
+        def _():
+            for load in loads(chunk + 1):
+                load.start()
+
+        here = span(chunk)
+        grad_hidden, tokens, hidden, combined = [buffer[chunk % 2] for buffer in buffers]
+        grad_normed = total_ref[here].astype(jnp.float32) + contract_last(
+            mid_ref[here], qkv_a_ref[...]
+        )
+        grad_tokens_ref[here] = last_grad(grad_normed, tokens, gain_ref[...], grad_hidden)
+        extra = ADAPTER_SCALE * matmul(mid_down_ref[here], down_b_ref[...])
+        output_ref[here] = to_low(hidden + combined.astype(jnp.float32) + gate_ref[here] * extra)
+
+    greet, begin, advance, finish = line_sum_steps(
+        chunks, 1, wide_ref, None, total_ref, *scratch[:5], on_total=on_total
+    )
+    for load in loads(0):
+        load.start()
+    greet(0)
+    begin()
+
+    @pl.loop(0, chunks + 1)
+    def _(step):
+        advance(step)
+
+    finish()
+
+
+def last_grad(grad_normed, tokens, gain, grad_hidden):
+    tokens_f = tokens.astype(jnp.float32)
+    scale = lax.rsqrt(jnp.mean(tokens_f * tokens_f, axis=1, keepdims=True) + EPSILON)
+    scaled = grad_normed * gain
+    pull = jnp.mean(tokens_f * scaled, axis=1, keepdims=True)
+    return to_low(grad_hidden + scale * scaled - tokens_f * (scale * scale * scale * pull))
 
 
 def attend_back_sum_kernel(chunks, wide_ref, rows_ref, upper_ref, *refs):
@@ -620,25 +684,36 @@
     return lax.psum(wide_part, "tensor")
 
 
-def plain_line_sum_kernel(chunks, wide_ref, *refs):
-    line_sum_kernel(chunks, wide_ref, None, *refs)
-
-
-def summed(wide_part, number):
+def last_step(wide_part, streamed, still, number):
+    length, width = wide_part.shape
+    mid, qkv_a, gain, mid_down, down_b, gate = still
     if not on_line():
-        return plain_sum(wide_part, None)
-    shape = wide_part.shape
+        grad_hidden, tokens, hidden, combined = streamed
+        grad_normed = plain_sum(wide_part, None).astype(jnp.float32) + contract_last(mid, qkv_a)
+        extra = ADAPTER_SCALE * matmul(mid_down, down_b)
+        return (
+            last_grad(grad_normed, tokens, gain, grad_hidden),
+            to_low(hidden + combined.astype(jnp.float32) + gate * extra),
+        )
+    rows = length // SUM_CHUNKS
+
+    def kernel(wide_ref, *refs):
+        last_sum_kernel(SUM_CHUNKS, wide_ref, refs[:4], *refs[4:])
+
     return pl.pallas_call(
-        functools.partial(plain_line_sum_kernel, SUM_CHUNKS),
-        out_shape=jax.ShapeDtypeStruct(shape, jnp.bfloat16),
-        in_specs=in_vmem(1),
-        out_specs=pl.BlockSpec(memory_space=pltpu.VMEM),
-        scratch_shapes=sum_scratch(shape),
+        kernel,
+        out_shape=[jax.ShapeDtypeStruct((length, width), jnp.bfloat16)] * 2,
+        in_specs=in_vmem(1) + in_hbm(4) + in_vmem(6),
+        out_specs=in_vmem(2),
+        scratch_shapes=[pltpu.VMEM((length, width), jnp.bfloat16)]
+        + sum_scratch((length, width))
+        + [pltpu.VMEM((2, rows, width), array.dtype) for array in streamed]
+        + [pltpu.SemaphoreType.DMA((4, 2))],
         compiler_params=pltpu.CompilerParams(
-            collective_id=number, has_side_effects=True, vmem_limit_bytes=48 * 2**20
+            collective_id=number, has_side_effects=True, vmem_limit_bytes=58 * 2**20
         ),
         cost_estimate=pl.CostEstimate(flops=0, bytes_accessed=300 * 2**20, transcendentals=0),
-    )(wide_part)
+    )(wide_part, *streamed, *still)
 
 
 def summed_and_gathered(wide_part, narrow_part, block, cotangents, number):
@@ -945,9 +1020,9 @@
 
     def advance(expert):
         for part in range(each):
-            launch(each * expert + part)
+            launch(each * (expert + 1) + part)
         for part in range(each):
-            forward(each * (expert + 3 - READY) + part + 1)
+            forward(each * (expert + 2 - READY) + part + 1)
         for part in range(each):
             hand_over(each * (expert + 1 - READY) + part + 1)
 
@@ -1004,6 +1079,11 @@
     pl.semaphore_wait(pltpu.get_barrier_semaphore(), 3)
     load_open(0).start()
     load_ready(0).start()
+
+    @pl.loop(0, each)
+    def _(piece):
+        launch(piece)
+
     grad_total[...] = jnp.zeros_like(grad_total)
     mid_down_ref[...] = jnp.zeros_like(mid_down_ref)
     grad_mid_up_ref[...] = jnp.zeros_like(grad_mid_up_ref)
@@ -1342,8 +1422,8 @@
         (query, keys, values, grad_attended) + places,
         3,
     )
-    mid_total, early_rows = lax.optimization_barrier((mid_total, early_rows))
-    grad_mid_qkv = to_low(mid_total[:, :rank])
+    mid_total, early_rows = lax.optimization_barrier((to_low(mid_total), early_rows))
+    grad_mid_qkv = mid_total[:, :rank]
     late_grads = [
         (
             ADAPTER_SCALE
@@ -1354,13 +1434,20 @@
     ]
     normed_part, late_flat = lax.optimization_barrier((normed_part, side_by_side(late_grads)))
     late_rows = lax.all_gather(late_flat, "dp", axis=0, tiled=True)
-    extra_here = ADAPTER_SCALE * matmul(mid_down, down_b)
-    output = to_low(hidden_here + combined_here + shared_gate[:, None] * extra_here)
-    last_total = summed(normed_part, 4)
-    last_total, late_rows = lax.optimization_barrier((last_total, late_rows))
-    grad_normed = last_total.astype(jnp.float32) + contract_last(grad_mid_qkv, qkv_a)
-    norm_attn_pull = jax.vjp(lambda rows: rms_scale(rows, gain_attn_f), tokens_f)[1]
-    grad_tokens = to_low(grad_hidden + norm_attn_pull(grad_normed)[0])
+    grad_tokens, output = last_step(
+        normed_part,
+        (grad_hidden, tokens, hidden_here, combined_here),
+        (
+            mid_total,
+            lanes(qkv_a, 0),
+            gain_attn_f[None],
+            lanes(mid_down, 0),
+            fill(down_b),
+            shared_gate[:, None],
+        ),
+        4,
+    )
+    output, late_rows = lax.optimization_barrier((output, late_rows))
     everyone = small_rows[:: small_rows.shape[0] // lax.axis_size("dp"), EXPERTS + 1]
     hits = jnp.arange(ADAPTER_SETS, dtype=jnp.int32)[:, None] == everyone.astype(jnp.int32)
     same = jnp.arange(rank)[:, None] == jnp.arange(rank)[None, :]

time: 972 us -> 945 us (0.972)
  matrix products: 74.1 us -> 56.8 us
  other arithmetic: 34 us -> 19.8 us
    pallas_call x1, Pallas kernels: 181 us -> 158 us  [summed_and_gathered(): pl.pallas_call(functools.partial(sum_gather_kernel, SUM_CHUNKS, pieces),...]
    pallas_call x1, Pallas kernels: 208 us -> 228 us  [experts_step(): pl.pallas_call(functools.partial(experts_kernel, pieces), in_specs=in_vme...]
    convert_element_type x4 -> x3, other arithmetic: 15.9 us -> 4.02 us  [to_low(): return values.astype(jnp.bfloat16)]
    dot_general x13 -> x12, matrix products: 26.9 us -> 18.7 us  [matmul(): return jnp.dot(left_side, right_side, preferred_element_type=jnp.float32)]
    unnamed x75 -> x79, local copies, waits for them, and re-layouts: 24.1 us -> 29.4 us
  transfers between devices with their start and end apart: 4 -> 4, of which waited for: 0 -> 1; matrix products, arithmetic and copies ran while one was open for 11% -> 10% of each run, Pallas kernels for 44% -> 43%
where the time goes in v10:
time: 945 us; the launch traced here: 936 us
  Pallas kernels  764 us (81%)
  local copies, waits for them, and re-layouts  61.1 us (6%)
  matrix products  56.8 us (6%)
  other arithmetic  19.8 us (2%)
  between operations  15.5 us (2%)
  blocking collectives  11.1 us (1%)
    pallas_call x1, Pallas kernels, experts_step(): pl.pallas_call(functools.partial(experts_kernel, pieces), in_specs=in_vme...  228 us
    pallas_call x1, Pallas kernels, summed_and_gathered(): pl.pallas_call(functools.partial(sum_gather_kernel, SUM_CHUNKS, pieces),...  158 us
    pallas_call x1, Pallas kernels, summed_and_down(): pl.pallas_call(functools.partial(sum_down_kernel, SUM_CHUNKS), out_shape=...  120 us
    pallas_call x1, Pallas kernels, summed_and_attended_back(): pl.pallas_call(functools.partial(attend_back_sum_kernel, SUM_CHUNKS), out...  119 us
    pallas_call x1, Pallas kernels, last_step(): pl.pallas_call(kernel, out_shape=[jax.ShapeDtypeStruct((length, width), j...  108 us
    unnamed x79, local copies, waits for them, and re-layouts  29.4 us
  transfers between devices with their start and end apart: 4, of which 1 were waited for; matrix products, arithmetic and copies ran while one was open for 10% of the time, Pallas kernels for 43%

profile of v10, /device:TPU:0, one launch (start us, length us, event | category | flops | bytes accessed | tf_op | source)
XLA Modules:
  0.0 935.5 jit_solution(11762937460494846003)
XLA Ops:
  7.2 2.3 pad_maximum_fusion.1
  9.6 3.7 copy.172
  13.4 1.2 copy.173
  15.3 1.0 dynamic-slice_multiply_fusion
  17.8 1.0 pad.55.up_extra_ref
  19.7 6.5 copy.166
  26.2 3.2 fusion
  29.4 1.4 dynamic-slice_bitcast_fusion.1
  30.8 1.2 fusion.12
  32.1 3.0 fusion.2
  35.5 1.6 copy.165
  37.6 11.1 %all_gather.16 = bf16[2048,18]{0,1:T(8,128)(2,1)S(1)} all-gather(bf16[256,18]{0,1:T(8,128)(2,1)S(1)} %maximum_maximum_fusion), channel_id=1, replica_groups=mesh['dp'=8,'tensor'=4] {'dp'}, dimensions={0}, use_global_device_ids=true | all-gather | bytes 82944 | tf_op jit(solution)/shard_map/all_gather | solution.py:1192
  49.0 0.9 pad.63.factors_ref
  50.0 0.9 pad.64.out_b_ref
  52.4 1.0 pad.62.extra_ref
  54.2 0.9 constant_dynamic-slice_fusion.1
  55.1 1.9 fusion.27
  57.4 1.2 fusion.15
  58.6 2.0 pad_maximum_fusion.block_ref
  60.6 7.3 all-gather.5.cloned.1.call-done
  67.9 10.4 %fusion.4 = f32[3,512,1024]{1,2,0:T(8,128)S(1)} fusion(bf16[2048,4,512]{2,0,1:T(8,128)(2,1)} %all-gather.5.cloned.1.call-done, bf16[1024,2048]{1,0:T(8,128)(2,1)} %fusion.2), kind=kOutput, calls=%fused_computation.9 | convolution fusion | flops 6442450944 | bytes 16777216 | tf_op jit(solution)/shard_map/tr,rsf->stf/dot_general | solution.py:1278
  78.3 4.5 add_bitcast_fusion.qkv_ref
  82.8 14.6 %shard_map.303 = (bf16[1024,512]{1,0:T(8,128)(2,1)S(1)}, bf16[1024,512]{1,0:T(8,128)(2,1)S(1)}, bf16[1024,512]{1,0:T(8,128)(2,1)S(1)}, bf16[1024,512]{1,0:T(8,128)(2,1)S(1)}) custom-call(f32[3,1024,512]{2,1,0:T(8,128)} %add_bitcast_fusion.qkv_ref, f32[1024,128]{1,0:T(8,128)S(1)} %get-tuple-element.148.cosine_ref.refs_4_, ...), custom_call_target="tpu_custom_call" | custom-call | flops 2147483648 | bytes 16777216 | tf_op jit(solution)/shard_map/pallas_call | solution.py:834
  97.5 1.0 copy-done.5
  98.4 1.0 copy-done.6
  99.4 1.0 copy-done.7
  101.7 7.6 fusion.11.wide_ref
  109.3 157.7 %shard_map.304 = (bf16[1024,2176]{1,0:T(8,128)(2,1)}, bf16[7040,2048]{1,0:T(8,128)(2,1)}, bf16[7040,1024]{1,0:T(8,128)(2,1)}) custom-call(f32[1024,2048]{1,0:T(8,128)} %fusion.11.wide_ref, bf16[1024,128]{1,0:T(8,128)(2,1)} %concatenate.40.narrow_ref, bf16[7040,256]{1,0:T(8,128)(2,1)} %pad_maximum_fusion.block_ref, bf16[2048,1024]{1,0:T(8,128)(2,1)} %bitcast.147), custom_call_target="tpu_custom_call" | custom-call | bytes 377487360 | tf_op jit(solution)/shard_map/pallas_call | solution.py:728
  267.1 5.1 multiply_reduce_fusion
  273.0 2.5 copy-done.11
  275.5 2.0 copy-done.9
  277.5 1.4 fusion.76
  279.1 0.9 fusion.77
  282.3 0.9 fusion.55
  284.7 1.0 copy.178.scale_ref
  286.4 227.7 %shard_map.305 = (bf16[1024,2048]{1,0:T(8,128)(2,1)}, f32[20,1024]{1,0:T(8,128)}, f32[128,1024]{1,0:T(8,128)}, f32[128,1024]{1,0:T(8,128)}, f32[4,128,352]{2,1,0...) custom-call(bf16[1024,2048]{1,0:T(8,128)(2,1)} %copy-done.9, ...), custom_call_target="tpu_custom_call" | custom-call | bytes 629145600 | tf_op jit(solution)/shard_map/pallas_call | solution.py:1161
  514.2 0.9 slice.185
  515.8 0.8 slice.183
  518.5 119.6 %shard_map.306 = (bf16[1024,2176]{1,0:T(8,128)(2,1)}, bf16[1024,2048]{1,0:T(8,128)(2,1)}) custom-call(bf16[1024,2048]{1,0:T(8,128)(2,1)} %get-tuple-element.55.wide_ref, bf16[1024,128]{1,0:T(8,128)(2,1)} %concatenate.46.narrow_ref, bf16[7040,1024]{1,0:T(8,128)(2,1)} %get-tuple-element.59.act_ref, bf16[7040,2048]{1,0:T(8,128)(2,1)} %get-tuple-element.60.down_ref), custom_call_target="tpu_custom_call" | custom-call | bytes 314572800 | tf_op jit(solution)/shard_map/pallas_call | solution.py:759
  638.1 17.4 %shard_map.307 = (f32[1024,2048]{1,0:T(8,128)}, bf16[1024,2048]{1,0:T(8,128)(2,1)}, bf16[1024,128]{1,0:T(8,128)(2,1)}, bf16[1024,512]{1,0:T(8,128)(2,1)}) custom-call(bf16[1024,2176]{1,0:T(8,128)(2,1)} %get-tuple-element.65.total_ref, f32[1024,2048]{1,0:T(8,128)} %copy-done.11, f32[1024,1]{1,0:T(8,128)} %copy.178.scale_ref, ...), custom_call_target="tpu_custom_call" | custom-call | flops 2147483648 | bytes 33554432 | tf_op jit(solution)/shard_map/pallas_call | solution.py:620
  655.5 1.2 fusion.16
  656.7 1.7 fusion.10
  658.4 1.0 slice.182
  659.8 0.9 fusion.51
  660.8 3.1 fusion.8
  667.5 0.9 pad.66.refs_5_
  668.4 118.9 %shard_map.308 = (bf16[1024,2048]{1,0:T(8,128)(2,1)}, bf16[3,1024,512]{2,1,0:T(8,128)(2,1)}, bf16[1024,2048]{1,0:T(8,128)(2,1)}, bf16[1024,128]{1,0:T(8,128)(2,1)}) custom-call(bf16[1024,2048]{1,0:T(8,128)(2,1)} %get-tuple-element.61.wide_ref, bf16[4,2048,512]{2,1,0:T(8,128)(2,1)} %bitcast.146, bf16[3,128,512]{2,1,0:T(8,128)(2,1)} %pad.59.upper_ref, ...), custom_call_target="tpu_custom_call" | custom-call | bytes 314572800 | tf_op jit(solution)/shard_map/pallas_call | solution.py:928
  787.3 2.4 fusion.14
  789.8 3.0 fusion.9
  792.8 2.9 convolution_convert_fusion
  796.7 1.1 slice.103
  798.5 107.8 %shard_map.309 = (bf16[1024,2048]{1,0:T(8,128)(2,1)}, bf16[1024,2048]{1,0:T(8,128)(2,1)}) custom-call(bf16[1024,2048]{1,0:T(8,128)(2,1)} %get-tuple-element.77.wide_ref, f32[1024,2048]{1,0:T(8,128)} %get-tuple-element.78.refs_0_, bf16[1024,2048]{1,0:T(8,128)(2,1)} %refs_1_.1, f32[1024,2048]{1,0:T(8,128)} %copy-done.11, ...), custom_call_target="tpu_custom_call" | custom-call | bytes 314572800 | tf_op jit(solution)/shard_map/pallas_call | solution.py:703
  906.3 1.2 slice_bitcast_fusion.2
  908.2 1.8 copy.185
  910.1 0.9 convolution_bitcast_fusion.3
  911.0 1.1 convolution_bitcast_fusion
  912.1 1.3 convolution_bitcast_fusion.1
  913.3 1.3 fusion.17
  914.6 1.0 slice_bitcast_fusion.3
  915.6 2.3 convolution_bitcast_fusion.2
  917.9 2.3 fusion.20
  920.5 1.2 fusion.50
  921.6 4.9 copy.204
  926.6 2.0 copy.205
  (153 shorter events, 22.5 us)
Async XLA Ops:
  7.2 41.5 %copy-start = (bf16[8,2048,16]{1,2,0:T(8,128)(2,1)S(1)}, bf16[8,2048,16]{1,2,0:T(8,128)(2,1)}, u32[]{:S(2)}) copy-start(bf16[8,2048,16]{1,2,0:T(8,128)(2,1)} %param.44) | copy-start | bytes 1572868
  7.2 60.7 %all-gather.5.cloned.1.call-start = ((), (), s32[]{:S(2)}) async-start(), calls=%async_computation | async-start | bytes 9437184 | tf_op jit(solution)/shard_map/all_gather | solution.py:1192
  9.6 276.8 %all-gather.7.cloned.1.call-start = ((), (), s32[]{:S(2)}) async-start(), calls=%async_computation.1 | async-start | bytes 12976128 | tf_op jit(solution)/shard_map/all_gather | solution.py:1262
  13.3 6.3 copy-start.29
  14.6 778.2 %all-gather.9.cloned.1.call-start = ((), (), s32[]{:S(2)}) async-start(), calls=%async_computation.2 | async-start | bytes 2543616 | tf_op jit(solution)/shard_map/all_gather | solution.py:1414
  19.7 12.4 %copy-start.25 = (f32[2048]{0:T(1024)}, f32[2048]{0:T(1024)S(1)}, u32[]{:S(2)}) copy-start(f32[2048]{0:T(1024)S(1)} %convert_element_type.125) | copy-start | bytes 24580
  26.2 4.6 copy-start.12
  26.2 5.9 copy-start.14
  32.0 3.1 copy-start.30
  32.1 3.1 copy-start.32
  32.1 5.0 copy-start.31
  32.1 5.1 copy-start.33
  32.1 5.1 copy-start.27
  32.1 5.4 copy-start.28
  35.3 47.5 %copy-start.8 = (s32[1024]{0:T(1024)}, s32[1024]{0:T(1024)S(1)}, u32[]{:S(2)}) copy-start(s32[1024]{0:T(1024)S(1)} %broadcast_add_fusion) | copy-start | bytes 12292
  35.5 47.3 %copy-start.4 = (s32[1024,1]{1,0:T(8,128)}, s32[1024,1]{1,0:T(8,128)S(1)}, u32[]{:S(2)}) copy-start(s32[1024,1]{1,0:T(8,128)S(1)} %copy.162.row_piece_ref.refs_6_) | copy-start | bytes 12292
  37.1 235.1 %copy-start.26 = (f32[2048]{0:T(1024)}, f32[2048]{0:T(1024)S(1)}, u32[]{:S(2)}) copy-start(f32[2048]{0:T(1024)S(1)} %convert_element_type.131) | copy-start | bytes 24580
  37.4 19.6 %copy-start.15 = (f32[1024,16]{1,0:T(8,128)}, f32[1024,16]{1,0:T(8,128)S(1)}, u32[]{:S(2)}) copy-start(f32[1024,16]{1,0:T(8,128)S(1)} %copy.170) | copy-start | bytes 196612
  51.5 2.7 copy-start.23
  51.7 5.7 copy-start.13
  55.1 3.5 copy-start.18
  57.4 25.5 %copy-start.2 = (f32[1024,128]{1,0:T(8,128)}, f32[1024,128]{1,0:T(8,128)S(1)}, u32[]{:S(2)}) copy-start(f32[1024,128]{1,0:T(8,128)S(1)} %get-tuple-element.148.cosine_ref.refs_4_) | copy-start | bytes 1572868
  57.4 25.5 %copy-start.3 = (f32[1024,128]{1,0:T(8,128)}, f32[1024,128]{1,0:T(8,128)S(1)}, u32[]{:S(2)}) copy-start(f32[1024,128]{1,0:T(8,128)S(1)} %get-tuple-element.149.sine_ref.refs_5_) | copy-start | bytes 1572868
  82.8 17.5 %copy-start.24 = (bf16[1,512,16]{1,2,0:T(8,128)(2,1)S(1)}, bf16[1,512,16]{1,2,0:T(8,128)(2,1)}, u32[]{:S(2)}) copy-start(bf16[1,512,16]{1,2,0:T(8,128)(2,1)} %copy-done.23) | copy-start | bytes 49156
  97.4 1.0 copy-start.5
  98.4 1.0 copy-start.6
  99.4 1.0 copy-start.7
  272.2 3.3 copy-start.11
  275.5 2.0 copy-start.9
  277.5 4.3 copy-start.16
  278.9 2.5 copy-start.21
  638.1 18.6 %copy-start.10 = (bf16[1024,2048]{1,0:T(8,128)(2,1)S(1)}, bf16[1024,2048]{1,0:T(8,128)(2,1)}, u32[]{:S(2)}) copy-start(bf16[1024,2048]{1,0:T(8,128)(2,1)} %copy-done.9) | copy-start | bytes 12582916
  663.9 0.7 copy-start.22
  664.6 250.0 %all-gather.11.cloned.1.call-start = ((), (), s32[]{:S(2)}) async-start(), calls=%async_computation.3 | async-start | bytes 1622016 | tf_op jit(solution)/shard_map/all_gather | solution.py:1436
  787.3 5.4 copy-start.20
  907.9 2.2 copy-start.19
  921.6 4.9 copy-start.17
  921.6 7.0 copy-start.1
Sparse Core Ops, SparseCore 0:
  10.5 57.3 all-gather.4
  70.3 88.2 all-gather.6
  664.8 28.8 all-gather.8
  796.5 26.2 all-gather.10

commit v11 on v10

--- a/solution.py
+++ b/solution.py
@@ -297,8 +297,9 @@
 def sum_gather_kernel(
     chunks,
     pieces,
-    wide_ref,
+    attended_ref,
     narrow_ref,
+    row_stack_ref,
     block_ref,
     cotangent_ref,
     total_ref,
@@ -306,10 +307,11 @@
     open_ref,
     *scratch,
 ):
+    wide_ref, projection, projection_semaphore = scratch[-3:]
     greet, begin, advance, finish = line_sum_steps(
         chunks, LAG, wide_ref, narrow_ref, total_ref, *scratch[:5]
     )
-    gather_semaphores, local_semaphores, piece_rows, open_rows = scratch[5:]
+    gather_semaphores, local_semaphores, piece_rows, open_rows = scratch[5:-3]
     gather_greet, gather_advance, gather_arrive, gather_finish, own, load, load_wait, stages = (
         plane_gather_steps(
             pieces, block_ref, whole_ref, gather_semaphores, local_semaphores.at[0]
@@ -324,14 +326,25 @@
             open_rows.at[slot], open_ref.at[span], local_semaphores.at[3 + slot]
         )
 
+    load_projection = pltpu.make_async_copy(
+        row_stack_ref.at[3], projection, projection_semaphore.at[0]
+    )
+    load_projection.start()
     gather_greet()
     greet(3)
-    begin()
-    own().start()
 
     @pl.loop(0, LEAD)
     def _(piece):
         stages[0](piece)
+
+    load_projection.wait()
+    blocks = 4
+    size = wide_ref.shape[0] // blocks
+    for block in range(blocks):
+        span = slice(block * size, (block + 1) * size)
+        wide_ref[span] = contract_last(attended_ref[span], projection[...])
+        begin(block * chunks // blocks, (block + 1) * chunks // blocks)
+    own().start()
 
     @pl.loop(0, max(chunks + LAG, pieces + 3 * AHEAD + 1))
     def _(step):
@@ -543,6 +556,62 @@
 
 def grad_mid_rows(grad_qkv_ref, upper_ref):
     return sum(contract_last(grad_qkv_ref[part], upper_ref[part]) for part in range(3))
+
+
+def hidden_kernel(
+    total_ref,
+    tokens_ref,
+    out_b_ref,
+    gain_ref,
+    factors_ref,
+    hidden_ref,
+    scale_ref,
+    normed_ref,
+    projected_ref,
+):
+    width = tokens_ref.shape[1]
+    total = total_ref[...]
+    hidden = (
+        tokens_ref[...].astype(jnp.float32)
+        + total[:, :width].astype(jnp.float32)
+        + ADAPTER_SCALE * matmul(to_low(total[:, width:]), out_b_ref[...])
+    )
+    scale = lax.rsqrt(jnp.mean(hidden * hidden, axis=1, keepdims=True) + EPSILON)
+    normed = to_low(hidden * scale * gain_ref[...])
+    hidden_ref[...] = hidden
+    scale_ref[...] = scale
+    normed_ref[...] = normed
+    projected_ref[...] = matmul(normed, factors_ref[...])
+
+
+def hidden_rows(total, tokens, out_b, gain, factors):
+    length, width = tokens.shape
+    rows = min(length, 128)
+
+    def block(columns):
+        return pl.BlockSpec((rows, columns), lambda index: (index, 0))
+
+    def whole(array):
+        return pl.BlockSpec(array.shape, lambda index: (0, 0))
+
+    return pl.pallas_call(
+        hidden_kernel,
+        grid=(length // rows,),
+        in_specs=[block(total.shape[1]), block(width), whole(out_b), whole(gain), whole(factors)],
+        out_specs=[block(width), block(1), block(width), block(NARROW)],
+        out_shape=[
+            jax.ShapeDtypeStruct((length, width), jnp.float32),
+            jax.ShapeDtypeStruct((length, 1), jnp.float32),
+            jax.ShapeDtypeStruct((length, width), jnp.bfloat16),
+            jax.ShapeDtypeStruct((length, NARROW), jnp.float32),
+        ],
+        compiler_params=pltpu.CompilerParams(
+            vmem_limit_bytes=40 * 2**20, dimension_semantics=("arbitrary",)
+        ),
+        cost_estimate=pl.CostEstimate(
+            flops=4 * length * width * NARROW, bytes_accessed=20 * 2**20, transcendentals=0
+        ),
+    )(total, tokens, out_b, gain, factors)
 
 
 def epilogue_kernel(
@@ -716,11 +785,12 @@
     )(wide_part, *streamed, *still)
 
 
-def summed_and_gathered(wide_part, narrow_part, block, cotangents, number):
-    length, width = wide_part.shape
+def summed_and_gathered(attended, narrow_part, row_stack, block, cotangents, number):
+    length, width = attended.shape[0], row_stack.shape[1]
     if not (on_line() and in_plane()):
         whole = lax.all_gather(block, "dp", axis=1, tiled=True)
         open_rows = to_low(matmul(whole, cotangents))
+        wide_part = contract_last(attended, row_stack[3])
         return plain_sum(wide_part, narrow_part), whole, open_rows
     shape = (length, width + NARROW)
     pieces = SHARED + EXPERTS
@@ -732,7 +802,7 @@
             jax.ShapeDtypeStruct((block.shape[0], width), jnp.bfloat16),
             jax.ShapeDtypeStruct((block.shape[0], length), jnp.bfloat16),
         ],
-        in_specs=in_vmem(2) + in_hbm(1) + in_vmem(1),
+        in_specs=in_vmem(2) + in_hbm(2) + in_vmem(1),
         out_specs=in_vmem(1) + in_hbm(2),
         scratch_shapes=sum_scratch(shape)
         + [
@@ -740,12 +810,15 @@
             pltpu.SemaphoreType.DMA((5,)),
             pltpu.VMEM((2, rows, width), jnp.bfloat16),
             pltpu.VMEM((2, rows, length), jnp.bfloat16),
+            pltpu.VMEM((length, width), jnp.float32),
+            pltpu.VMEM(row_stack.shape[1:], jnp.bfloat16),
+            pltpu.SemaphoreType.DMA((1,)),
         ],
         compiler_params=pltpu.CompilerParams(
             collective_id=number, has_side_effects=True, vmem_limit_bytes=58 * 2**20
         ),
         cost_estimate=pl.CostEstimate(flops=0, bytes_accessed=360 * 2**20, transcendentals=0),
-    )(wide_part, narrowed(narrow_part), block, cotangents)
+    )(attended, narrowed(narrow_part), row_stack, block, cotangents)
     return total, whole, open_rows
 
 
@@ -799,6 +872,9 @@
 
 def attend_kernel(
     qkv_ref,
+    mid_ref,
+    upper_ref,
+    bias_ref,
     cosine_ref,
     sine_ref,
     row_piece_ref,
@@ -810,13 +886,17 @@
 ):
     length = qkv_ref.shape[1]
 
+    def whole(source, column):
+        extra = matmul(mid_ref[...], upper_ref[source, :, column])
+        return qkv_ref[source, :, column] + extra + bias_ref[source, :, column]
+
     @pl.loop(0, qkv_ref.shape[2] // HEAD_SIZE)
     def _(head):
         column = pl.ds(pl.multiple_of(head * HEAD_SIZE, HEAD_SIZE), HEAD_SIZE)
         for source, target in ((0, query_ref), (1, keys_ref)):
-            raw = qkv_ref[source, :, column]
+            raw = whole(source, column)
             target[:, column] = to_low(raw * cosine_ref[...] + half_turn(raw, sine_ref[...]))
-        values_ref[:, column] = to_low(qkv_ref[2, :, column])
+        values_ref[:, column] = to_low(whole(2, column))
         for first in range(0, length, QUERY_ROWS):
             extent = min(length, first + QUERY_ROWS + PIECE)
             allowed = block_mask(first, QUERY_ROWS, extent, row_piece_ref, col_piece_ref)
@@ -828,13 +908,13 @@
             )
 
 
-def attend(qkv, cosine, signed_sine, row_piece, col_piece):
+def attend(qkv, mid, upper, bias, cosine, signed_sine, row_piece, col_piece):
     length, heads_width = qkv.shape[1:]
     shape = jax.ShapeDtypeStruct((length, heads_width), jnp.bfloat16)
     return pl.pallas_call(
         attend_kernel,
         out_shape=[shape] * 4,
-        in_specs=[pl.BlockSpec(memory_space=pltpu.VMEM)] * 5,
+        in_specs=[pl.BlockSpec(memory_space=pltpu.VMEM)] * 8,
         out_specs=[pl.BlockSpec(memory_space=pltpu.VMEM)] * 4,
         compiler_params=pltpu.CompilerParams(vmem_limit_bytes=48 * 2**20),
         cost_estimate=pl.CostEstimate(
@@ -842,7 +922,7 @@
             bytes_accessed=16 * 2**20,
             transcendentals=length * length * heads_width // HEAD_SIZE,
         ),
-    )(qkv, cosine, signed_sine, row_piece, col_piece)
+    )(qkv, mid, upper, bias, cosine, signed_sine, row_piece, col_piece)
 
 
 def attend_back_steps(
@@ -1255,6 +1335,12 @@
     up_extra = ADAPTER_SCALE * up_b.reshape(rank, 2, SHARED, hidden).transpose(2, 1, 3, 0)
     up_extra = fill_last(up_extra.reshape(SHARED, 2 * hidden, rank))
     down_extra = fill_last(down_a.reshape(SHARED, hidden, rank))
+    def lanes(columns, first):
+        return jnp.pad(columns, ((0, 0), (first, NARROW - first - columns.shape[1])))
+
+    upper = jnp.pad(
+        ADAPTER_SCALE * qkv_b.transpose(1, 0, 2), ((0, 0), (0, NARROW - rank), (0, 0))
+    )
     depth = routed_gate_up_weight.shape[0]
     early = (READY - SHARED) * 2 * hidden
     shared_block = shared_expert_gate_up_weight.reshape(-1, 2, SHARED, hidden)
@@ -1270,44 +1356,36 @@
     attention_rows = gathered(
         jnp.concatenate([query_key_value_weight, output_projection_weight[:, None]], axis=1)
     )
-    qkv_rows, output_rows = attention_rows[:, :3], attention_rows[:, 3]
+    qkv_rows = attention_rows[:, :3]
     row_stack = attention_rows.transpose(1, 0, 2)
     normed, cotangent_down, up_extra, down_extra = lax.optimization_barrier(
         (normed, cotangent_down, up_extra, down_extra)
     )
     qkv_sum = jnp.einsum("tr,rsf->stf", normed, qkv_rows, preferred_element_type=jnp.float32)
-    qkv_sum = qkv_sum + query_key_value_bias.astype(jnp.float32)[:, None, :]
-    qkv_sum = qkv_sum + ADAPTER_SCALE * jnp.einsum(
-        "tr,rsf->stf", mid_qkv, qkv_b, preferred_element_type=jnp.float32
-    )
     cosine, sine_table = rope_tables(length)
     signs = jnp.where(jnp.arange(HEAD_SIZE) < HEAD_SIZE // 2, -1.0, 1.0)
     piece_ids = piece_index(jnp.arange(length, dtype=jnp.int32), starts)
     places = (cosine, sine_table * signs[None, :], piece_ids[:, None], piece_ids[None, :])
-    query, keys, values, attended = attend(qkv_sum, *places)
-    branch_part = contract_last(attended, output_rows)
+    query, keys, values, attended = attend(
+        qkv_sum,
+        lanes(mid_qkv, 0),
+        upper,
+        query_key_value_bias.astype(jnp.float32)[:, None, :],
+        *places,
+    )
     down_block = jnp.transpose(routed_down_weight, (1, 2, 0))
     down_block = jnp.concatenate(
         [shared_expert_down_weight.T, down_block.reshape(-1, depth)], axis=0
     )
     branch_total, down_rows, open_rows = summed_and_gathered(
-        branch_part,
+        attended,
         matmul(attended, out_a),
+        row_stack,
         down_block,
         cotangent.T,
         1,
     )
     mid_out = to_low(branch_total[:, width : width + rank])
-    hidden_here = (
-        tokens_f
-        + branch_total[:, :width].astype(jnp.float32)
-        + ADAPTER_SCALE * matmul(mid_out, out_b)
-    )
-    hidden_scale = lax.rsqrt(
-        jnp.mean(hidden_here * hidden_here, axis=1, keepdims=True) + EPSILON
-    )
-    normed_two = to_low(hidden_here * hidden_scale * gain_ffn_f)
-    cot_f = cotangent.astype(jnp.float32)
     small_rows = gathered(
         jnp.concatenate(
             [
@@ -1319,10 +1397,12 @@
         )
     )
     factors = jnp.concatenate([small_rows[:, : EXPERTS + 1], up_a], axis=1)
-    projected = matmul(normed_two, factors)
+    hidden_here, hidden_scale, normed_two, projected = hidden_rows(
+        branch_total, tokens, fill(out_b), gain_ffn_f[None], lanes(factors, 0)
+    )
     router_probs = jax.nn.softmax(projected[:, :EXPERTS], axis=-1)
     shared_gate = jax.nn.sigmoid(projected[:, EXPERTS])
-    mid_up = to_low(projected[:, EXPERTS + 1 :])
+    mid_up = to_low(projected[:, EXPERTS + 1 : EXPERTS + 1 + rank])
     expert_ids = jnp.arange(EXPERTS, dtype=jnp.int32)
     chosen = jnp.sum(
         (routes[:, :, None] == expert_ids[None, None, :]).astype(jnp.float32), axis=1
@@ -1374,9 +1454,6 @@
     grad_mid_up = to_low(second_total[:, up_from : up_from + rank])
     mid_down = to_low(second_total[:, up_from + rank : up_from + 2 * rank])
 
-    def lanes(columns, first):
-        return jnp.pad(columns, ((0, 0), (first, NARROW - first - columns.shape[1])))
-
     grad_hidden, grad_branch, grad_mid_out, grad_attended = epilogue(
         (
             second_total,
@@ -1412,9 +1489,6 @@
         (grad_attended, side_by_side(early_grads))
     )
     early_rows = lax.all_gather(early_flat, "dp", axis=0, tiled=True)
-    upper = jnp.pad(
-        ADAPTER_SCALE * qkv_b.transpose(1, 0, 2), ((0, 0), (0, NARROW - rank), (0, 0))
-    )
     combined_here, grad_qkv, normed_part, mid_total = summed_and_attended_back(
         combined_part,
         row_stack,

time: 945 us -> 942 us (level)
  Pallas kernels: 764 us -> 776 us
  matrix products: 56.8 us -> 45.4 us
    unnamed x79 -> x89, local copies, waits for them, and re-layouts: 29.4 us -> 28.5 us
  transfers between devices with their start and end apart: 4 -> 4, of which waited for: 1 -> 0; matrix products, arithmetic and copies ran while one was open for 10% -> 9% of each run, Pallas kernels for 43% -> 44%
where the time goes in v11:
time: 942 us; the launch traced here: 932 us
  Pallas kernels  776 us (82%)
  local copies, waits for them, and re-layouts  61.5 us (7%)
  matrix products  45.4 us (5%)
  other arithmetic  21.1 us (2%)
  between operations  15.3 us (2%)
  blocking collectives  12.3 us (1%)
    pallas_call x1, Pallas kernels, experts_step(): pl.pallas_call(functools.partial(experts_kernel, pieces), in_specs=in_vme...  228 us
    pallas_call x1, Pallas kernels, summed_and_gathered(): pl.pallas_call(functools.partial(sum_gather_kernel, SUM_CHUNKS, pieces),...  161 us
    pallas_call x1, Pallas kernels, summed_and_attended_back(): pl.pallas_call(functools.partial(attend_back_sum_kernel, SUM_CHUNKS), out...  119 us
    pallas_call x1, Pallas kernels, summed_and_down(): pl.pallas_call(functools.partial(sum_down_kernel, SUM_CHUNKS), out_shape=...  118 us
    pallas_call x1, Pallas kernels, last_step(): pl.pallas_call(kernel, out_shape=[jax.ShapeDtypeStruct((length, width), j...  107 us
    unnamed x89, local copies, waits for them, and re-layouts  28.5 us
  transfers between devices with their start and end apart: 4, of which 0 were waited for; matrix products, arithmetic and copies ran while one was open for 9% of the time, Pallas kernels for 44%

profile of v11, /device:TPU:0, one launch (start us, length us, event | category | flops | bytes accessed | tf_op | source)
XLA Modules:
  0.0 931.8 jit_solution(17638740349830513393)
XLA Ops:
  7.2 2.3 pad_maximum_fusion.1
  9.6 3.7 copy.169
  13.4 1.2 copy.170
  15.3 1.0 dynamic-slice_multiply_fusion
  17.8 1.0 pad.60.up_extra_ref
  19.7 6.5 copy.163
  26.2 3.2 fusion
  29.4 1.5 dynamic-slice_bitcast_fusion.1
  31.5 3.4 fusion.15
  35.0 3.0 fusion.2
  38.7 3.4 convolution_convert_fusion.3
  43.6 1.6 copy.162
  45.3 12.3 %all_gather.16 = bf16[2048,18]{0,1:T(8,128)(2,1)S(1)} all-gather(bf16[256,18]{0,1:T(8,128)(2,1)S(1)} %maximum_maximum_fusion), channel_id=1, replica_groups=mesh['dp'=8,'tensor'=4] {'dp'}, dimensions={0}, use_global_device_ids=true | all-gather | bytes 82944 | tf_op jit(solution)/shard_map/all_gather | solution.py:1272
  57.6 0.9 dynamic-slice_bitcast_fusion
  58.9 0.9 pad.65.factors_ref
  59.8 0.9 pad.64.out_b_ref
  61.4 1.0 copy.166
  64.0 1.7 pad.71.out_a_ref
  65.7 1.0 pad.70.extra_ref
  67.6 1.9 fusion.29
  70.0 2.1 pad_maximum_fusion.block_ref
  72.0 11.7 %fusion.6.qkv_ref = f32[3,1024,512]{2,1,0:T(8,128)} fusion(bf16[2048,4,512]{2,0,1:T(8,128)(2,1)} %all-gather.5.cloned.1.call-done, bf16[1024,2048]{1,0:T(8,128)(2,1)} %fusion.2), kind=kOutput, calls=%fused_computation.9 | convolution fusion | flops 6442450944 | bytes 16777216 | tf_op jit(solution)/shard_map/tr,rsf->stf/dot_general | solution.py:1364
  83.8 15.9 %shard_map.303 = (bf16[1024,512]{1,0:T(8,128)(2,1)S(1)}, bf16[1024,512]{1,0:T(8,128)(2,1)S(1)}, bf16[1024,512]{1,0:T(8,128)(2,1)S(1)}, bf16[1024,512]{1,0:T(8,128)(2,1)}) custom-call(f32[3,1024,512]{2,1,0:T(8,128)} %fusion.6.qkv_ref, bf16[1024,128]{1,0:T(8,128)(2,1)S(1)} %pad.62.mid_ref, bf16[3,128,512]{2,1,0:T(8,128)(2,1)S(1)} %pad.63.upper_ref, ...), custom_call_target="tpu_custom_call" | custom-call | flops 2147483648 | bytes 16777216 | tf_op jit(solution)/shard_map/pallas_call | solution.py:914
  99.7 1.0 copy-done.12
  100.7 1.0 copy-done.13
  101.7 1.0 copy-done.14
  102.6 1.9 convolution_convert_fusion.2
  105.5 161.5 %shard_map.304 = (bf16[1024,2176]{1,0:T(8,128)(2,1)}, bf16[7040,2048]{1,0:T(8,128)(2,1)}, bf16[7040,1024]{1,0:T(8,128)(2,1)}) custom-call(bf16[1024,512]{1,0:T(8,128)(2,1)} %get-tuple-element.53.attended_ref, bf16[1024,128]{1,0:T(8,128)(2,1)} %concatenate.40.narrow_ref, bf16[4,2048,512]{2,1,0:T(8,128)(2,1)} %bitcast.137, ...), custom_call_target="tpu_custom_call" | custom-call | bytes 377487360 | tf_op jit(solution)/shard_map/pallas_call | solution.py:798
  267.0 9.3 shard_map.305
  276.3 2.0 copy-done.4
  279.3 1.0 fusion.74
  280.3 1.2 fusion.35
  284.2 0.9 pad.68.probs_ref
  285.8 227.7 %shard_map.306 = (bf16[1024,2048]{1,0:T(8,128)(2,1)}, f32[20,1024]{1,0:T(8,128)}, f32[128,1024]{1,0:T(8,128)}, f32[128,1024]{1,0:T(8,128)}, f32[4,128,352]{2,1,0...) custom-call(bf16[1024,2048]{1,0:T(8,128)(2,1)} %copy-done.4, ...), custom_call_target="tpu_custom_call" | custom-call | bytes 629145600 | tf_op jit(solution)/shard_map/pallas_call | solution.py:1241
  513.5 0.9 slice.177
  515.1 0.8 slice.175
  516.0 0.8 slice.176
  517.8 118.5 %shard_map.307 = (bf16[1024,2176]{1,0:T(8,128)(2,1)}, bf16[1024,2048]{1,0:T(8,128)(2,1)}) custom-call(bf16[1024,2048]{1,0:T(8,128)(2,1)} %get-tuple-element.61.wide_ref, bf16[1024,128]{1,0:T(8,128)(2,1)} %concatenate.46.narrow_ref, bf16[7040,1024]{1,0:T(8,128)(2,1)} %get-tuple-element.65.act_ref, bf16[7040,2048]{1,0:T(8,128)(2,1)} %get-tuple-element.66.down_ref), custom_call_target="tpu_custom_call" | custom-call | bytes 314572800 | tf_op jit(solution)/shard_map/pallas_call | solution.py:832
  636.3 17.4 %shard_map.308 = (f32[1024,2048]{1,0:T(8,128)}, bf16[1024,2048]{1,0:T(8,128)(2,1)}, bf16[1024,128]{1,0:T(8,128)(2,1)}, bf16[1024,512]{1,0:T(8,128)(2,1)}) custom-call(bf16[1024,2176]{1,0:T(8,128)(2,1)} %get-tuple-element.71.total_ref, f32[1024,2048]{1,0:T(8,128)} %get-tuple-element.72.hidden_ref.refs_2_, f32[1024,1]{1,0:T(8,128)} %copy-done.15, ...), custom_call_target="tpu_custom_call" | custom-call | flops 2147483648 | bytes 33554432 | tf_op jit(solution)/shard_map/pallas_call | solution.py:689
  653.7 1.2 fusion.18
  654.9 1.7 fusion.14
  656.6 1.0 slice.174
  658.0 0.9 fusion.52
  659.0 3.1 fusion.12
  664.0 0.9 slice.97
  664.9 0.9 pad.72.refs_5_
  665.8 118.6 %shard_map.309 = (bf16[1024,2048]{1,0:T(8,128)(2,1)}, bf16[3,1024,512]{2,1,0:T(8,128)(2,1)}, bf16[1024,2048]{1,0:T(8,128)(2,1)}, bf16[1024,128]{1,0:T(8,128)(2,1)}) custom-call(bf16[1024,2048]{1,0:T(8,128)(2,1)} %get-tuple-element.67.wide_ref, bf16[4,2048,512]{2,1,0:T(8,128)(2,1)} %bitcast.139, bf16[3,128,512]{2,1,0:T(8,128)(2,1)} %copy-done.11, ...), custom_call_target="tpu_custom_call" | custom-call | bytes 314572800 | tf_op jit(solution)/shard_map/pallas_call | solution.py:1008
  784.4 2.4 fusion.17
  786.8 3.0 fusion.13
  789.8 2.9 convolution_convert_fusion
  793.7 1.1 slice.94
  795.6 107.2 %shard_map.310 = (bf16[1024,2048]{1,0:T(8,128)(2,1)}, bf16[1024,2048]{1,0:T(8,128)(2,1)}) custom-call(bf16[1024,2048]{1,0:T(8,128)(2,1)} %get-tuple-element.85.wide_ref, f32[1024,2048]{1,0:T(8,128)} %get-tuple-element.86.refs_0_, bf16[1024,2048]{1,0:T(8,128)(2,1)} %refs_1_.1, f32[1024,2048]{1,0:T(8,128)} %get-tuple-element.72.hidden_ref.refs_2_, ...), custom_call_target="tpu_custom_call" | custom-call | bytes 314572800 | tf_op jit(solution)/shard_map/pallas_call | solution.py:772
  902.8 1.2 slice_bitcast_fusion
  904.7 1.8 copy.180
  906.5 0.9 convolution_bitcast_fusion.3
  907.4 1.1 convolution_bitcast_fusion
  908.5 1.3 convolution_bitcast_fusion.1
  909.8 1.3 fusion.19
  911.0 1.0 slice_bitcast_fusion.1
  912.1 2.3 convolution_bitcast_fusion.2
  914.4 2.3 fusion.22
  916.9 1.2 fusion.51
  918.1 4.9 copy.195
  923.0 2.0 copy.196
  (159 shorter events, 21.4 us)
Async XLA Ops:
  7.2 30.9 %copy-start = (bf16[8,2048,16]{1,2,0:T(8,128)(2,1)S(1)}, bf16[8,2048,16]{1,2,0:T(8,128)(2,1)}, u32[]{:S(2)}) copy-start(bf16[8,2048,16]{1,2,0:T(8,128)(2,1)} %param.40) | copy-start | bytes 1572868
  7.2 64.9 %all-gather.5.cloned.1.call-start = ((), (), s32[]{:S(2)}) async-start(), calls=%async_computation | async-start | bytes 9437184 | tf_op jit(solution)/shard_map/all_gather | solution.py:1272
  9.6 276.2 %all-gather.7.cloned.1.call-start = ((), (), s32[]{:S(2)}) async-start(), calls=%async_computation.1 | async-start | bytes 12976128 | tf_op jit(solution)/shard_map/all_gather | solution.py:1348
  13.3 6.3 copy-start.35
  14.6 775.2 %all-gather.9.cloned.1.call-start = ((), (), s32[]{:S(2)}) async-start(), calls=%async_computation.2 | async-start | bytes 2543616 | tf_op jit(solution)/shard_map/all_gather | solution.py:1491
  19.7 15.3 %copy-start.32 = (f32[2048]{0:T(1024)}, f32[2048]{0:T(1024)S(1)}, u32[]{:S(2)}) copy-start(f32[2048]{0:T(1024)S(1)} %convert_element_type.118) | copy-start | bytes 24580
  26.2 8.8 copy-start.2
  30.9 0.6 copy-start.26
  35.0 30.8 %copy-start.19 = (f32[1024,16]{1,0:T(8,128)}, f32[1024,16]{1,0:T(8,128)S(1)}, u32[]{:S(2)}) copy-start(f32[1024,16]{1,0:T(8,128)S(1)} %fusion.15) | copy-start | bytes 196612
  38.0 5.2 copy-start.38
  38.0 5.5 copy-start.37
  38.1 0.6 copy-start.28
  38.7 6.5 copy-start.39
  38.7 6.6 copy-start.34
  42.1 18.6 %copy-start.36 = (bf16[2048]{0:T(1024)(128)(2,1)S(1)}, bf16[2048]{0:T(1024)(128)(2,1)}, u32[]{:S(2)}) copy-start(bf16[2048]{0:T(1024)(128)(2,1)} %param.30) | copy-start | bytes 12292
  42.1 18.6 %copy-start.33 = (s32[1024,4]{0,1:T(4,128)S(1)}, s32[1024,4]{0,1:T(4,128)}, u32[]{:S(2)}) copy-start(s32[1024,4]{0,1:T(4,128)} %param.37) | copy-start | bytes 49156
  43.2 40.6 %copy-start.11 = (bf16[3,128,512]{2,1,0:T(8,128)(2,1)}, bf16[3,128,512]{2,1,0:T(8,128)(2,1)S(1)}, u32[]{:S(2)}) copy-start(bf16[3,128,512]{2,1,0:T(8,128)(2,1)S(1)} %pad.63.upper_ref) | copy-start | bytes 1179652
  43.3 40.5 %copy-start.17 = (s32[1024]{0:T(1024)}, s32[1024]{0:T(1024)S(1)}, u32[]{:S(2)}) copy-start(s32[1024]{0:T(1024)S(1)} %broadcast_add_fusion) | copy-start | bytes 12292
  43.6 40.2 %copy-start.10 = (s32[1024,1]{1,0:T(8,128)}, s32[1024,1]{1,0:T(8,128)S(1)}, u32[]{:S(2)}) copy-start(s32[1024,1]{1,0:T(8,128)S(1)} %copy.159.row_piece_ref.refs_6_) | copy-start | bytes 12292
  57.6 2.1 copy-start.30
  60.7 206.3 %copy-start.6 = (bf16[128,2048]{1,0:T(8,128)(2,1)}, bf16[128,2048]{1,0:T(8,128)(2,1)S(1)}, u32[]{:S(2)}) copy-start(bf16[128,2048]{1,0:T(8,128)(2,1)S(1)} %pad.64.out_b_ref) | copy-start | bytes 1572868
  60.7 206.3 %copy-start.16 = (f32[2048]{0:T(1024)}, f32[2048]{0:T(1024)S(1)}, u32[]{:S(2)}) copy-start(f32[2048]{0:T(1024)S(1)} %broadcast_in_dim.90) | copy-start | bytes 24580
  62.5 7.1 copy-start.20
  64.0 5.9 copy-start.23
  69.9 13.9 %copy-start.8 = (f32[1024,128]{1,0:T(8,128)}, f32[1024,128]{1,0:T(8,128)S(1)}, u32[]{:S(2)}) copy-start(f32[1024,128]{1,0:T(8,128)S(1)} %get-tuple-element.152.cosine_ref.refs_4_) | copy-start | bytes 1572868
  69.9 13.9 %copy-start.9 = (f32[1024,128]{1,0:T(8,128)}, f32[1024,128]{1,0:T(8,128)S(1)}, u32[]{:S(2)}) copy-start(f32[1024,128]{1,0:T(8,128)S(1)} %get-tuple-element.153.sine_ref.refs_5_) | copy-start | bytes 1572868
  99.7 1.0 copy-start.12
  100.7 1.0 copy-start.13
  101.7 1.0 copy-start.14
  105.5 161.5 %copy-start.3 = (bf16[1024,2048]{1,0:T(8,128)(2,1)S(1)}, bf16[1024,2048]{1,0:T(8,128)(2,1)}, u32[]{:S(2)}) copy-start(bf16[1024,2048]{1,0:T(8,128)(2,1)} %refs_1_.1) | copy-start | bytes 12582916
  105.5 161.5 %copy-start.7 = (bf16[2048,128]{1,0:T(8,128)(2,1)S(1)}, bf16[2048,128]{1,0:T(8,128)(2,1)}, u32[]{:S(2)}) copy-start(bf16[2048,128]{1,0:T(8,128)(2,1)} %pad.65.factors_ref) | copy-start | bytes 1572868
  276.3 2.0 copy-start.4
  278.3 0.8 copy-start.15
  279.1 3.8 copy-start.21
  636.3 17.4 %copy-start.18 = (bf16[1024,512]{1,0:T(8,128)(2,1)S(1)}, bf16[1024,512]{1,0:T(8,128)(2,1)}, u32[]{:S(2)}) copy-start(bf16[1024,512]{1,0:T(8,128)(2,1)} %get-tuple-element.53.attended_ref) | copy-start | bytes 3145732
  636.3 18.6 %copy-start.5 = (bf16[1024,2048]{1,0:T(8,128)(2,1)S(1)}, bf16[1024,2048]{1,0:T(8,128)(2,1)}, u32[]{:S(2)}) copy-start(bf16[1024,2048]{1,0:T(8,128)(2,1)} %copy-done.4) | copy-start | bytes 12582916
  656.6 6.3 copy-start.27
  656.6 7.1 copy-start.29
  662.1 0.7 copy-start.31
  662.8 248.2 %all-gather.11.cloned.1.call-start = ((), (), s32[]{:S(2)}) async-start(), calls=%async_computation.3 | async-start | bytes 1622016 | tf_op jit(solution)/shard_map/all_gather | solution.py:1510
  784.4 5.4 copy-start.25
  904.3 2.2 copy-start.24
  918.1 4.9 copy-start.22
  918.1 7.0 copy-start.1
Sparse Core Ops, SparseCore 0:
  10.5 57.3 all-gather.4
  70.3 93.9 all-gather.6
  663.0 28.5 all-gather.8
  793.5 25.4 all-gather.10
